TPU v7x, 32 devices: a whole 2x2x4 slice. The times are simulated.
32 devices in a mesh: section: 2 (over x), dp: 16 (over z, y, core).
Axes of the slice: x: 2, y: 2, z: 4, core: 2. Of those that a mesh axis runs over, the one named last changes fastest.
Arguments:
- inputs: bfloat16 [2, 32, 256, 768], P(None, 'dp')
- keep_mask: int32 [2, 32, 256], P(None, 'dp'), may hold values 0 or 1
- lengths: int32 [2, 32], P(None, 'dp'), may hold values from 128 to 256, as said below
- slot_order: int32 [32], P('dp'), may hold values from 0 to 1, as said below
- cotangent: bfloat16 [32, 256, 768], P('dp'), may hold values from -6 to 6
- query_projection: bfloat16 [2, 768, 2304], P('section', 'dp')
- query_output: bfloat16 [2, 768, 768], P('section', 'dp'), may hold values from -0.4375 to 0.4375
- query_expand: bfloat16 [2, 768, 3072], P('section', 'dp'), may hold values from -0.21875 to 0.21875
- query_contract: bfloat16 [2, 3072, 768], P('section', 'dp'), may hold values from -0.109375 to 0.109375
- query_gains: bfloat16 [2, 2, 768], P('section', None, 'dp'), may hold values from 0.5 to 1.5
- query_biases: bfloat16 [2, 6, 768], P('section', None, 'dp'), may hold values from -1.75 to 1.75
- query_offsets: bfloat16 [2, 3072], P('section', 'dp'), may hold values from -1.75 to 1.75
- momentum_projection: bfloat16 [2, 768, 2304], P('section', 'dp')
- momentum_output: bfloat16 [2, 768, 768], P('section', 'dp'), may hold values from -0.4375 to 0.4375
- momentum_expand: bfloat16 [2, 768, 3072], P('section', 'dp'), may hold values from -0.21875 to 0.21875
- momentum_contract: bfloat16 [2, 3072, 768], P('section', 'dp'), may hold values from -0.109375 to 0.109375
- momentum_gains: bfloat16 [2, 2, 768], P('section', None, 'dp'), may hold values from 0.5 to 1.5
- momentum_biases: bfloat16 [2, 6, 768], P('section', None, 'dp'), may hold values from -1.75 to 1.75
- momentum_offsets: bfloat16 [2, 3072], P('section', 'dp'), may hold values from -1.75 to 1.75
Outputs:
- pooled: float32 [2, 2, 32, 768], P('section')
- grad_input: float32 [2, 32, 256, 768], P('section', 'dp')
- grad_projection: float32 [2, 768, 2304], P('section', 'dp')
- grad_output: float32 [2, 768, 768], P('section', 'dp')
- grad_expand: float32 [2, 768, 3072], P('section', 'dp')
- grad_contract: float32 [2, 3072, 768], P('section', 'dp')
- grad_gains: float32 [2, 2, 768], P('section', None, 'dp')
- grad_biases: float32 [2, 6, 768], P('section', None, 'dp')
- grad_offsets: float32 [2, 3072], P('section', 'dp')
Inputs may be any that keep to these rules, and one draw needn't show every extreme that they name: `lengths`: one crop of each view has all 256 positions. `slot_order`: each aligned block of 2 entries, one device's crops, is a permutation of 0 to 1.
All inputs are finite; a program needn't handle non-finite values. No bound on the sum of `keep_mask` on one device may be relied on, other than what follows from the above.
Results may differ from a plain program's by a relative error of at most 0.02.
Values may be sent and summed in bfloat16 or wider, within the bound.
No kernel may reach another device: no remote copies, remote signals or barrier semaphores. Data moves between devices by JAX's collectives and lax.ppermute only.
A program may use at most 256 MiB of HBM per device.

v0:
```python
import jax
import jax.numpy as jnp
from jax import lax
from jax.sharding import PartitionSpec as P

HD = 64
MB = 2


epsilon = 1e-12
highest_level = lax.Precision.HIGHEST


def passed_along(block, axis, distance):
    devices = range(lax.axis_size(axis))
    route = [(i - distance, i) for i in devices if i - distance in devices]
    return lax.ppermute(block, axis, route)


def layer_norm(values, norm_gain, norm_offset_vector):
    centred = values - jnp.mean(values, axis=-1, keepdims=True)
    variance = jnp.mean(centred * centred, axis=-1, keepdims=True)
    return centred * lax.rsqrt(variance + epsilon) * norm_gain + norm_offset_vector


def exact_gelu(values):
    return jax.nn.gelu(values, approximate=False)


def take_micro(array, position, count, axis):
    return lax.dynamic_slice_in_dim(array, position * count, count, axis)


def split_heads(matrix, crop_count, length):
    return matrix.reshape(crop_count, length, -1, HD)


def attention_scores(queries, key_rows, validity):
    scores = jnp.einsum(
        "clhd,cmhd->chlm", queries, key_rows, preferred_element_type=jnp.float32
    ) * HD ** (-0.5)
    return jnp.where(validity[:, None, None, :] > 0, scores, -1e30)


def column_sum(matrix):
    return jnp.sum(matrix.astype(jnp.float32), axis=0)


def pool_rows(result, validity):
    summed = jnp.sum(result * validity[..., None], axis=1)
    return summed / jnp.sum(validity, axis=1)[:, None]


def forward_block(block_in, validity, params):
    w_proj, w_out, w_expand, w_contract, norm_gains, biases, offsets = params
    norm_gains = norm_gains.astype(jnp.float32)
    biases = biases.astype(jnp.float32)
    offsets = offsets.astype(jnp.float32)
    crop_count, length, features = block_in.shape
    rows_flat = block_in.reshape(crop_count * length, features)
    mixture = jnp.dot(rows_flat, w_proj, preferred_element_type=jnp.float32)
    queries = (mixture[:, :features] + biases[0]).astype(jnp.bfloat16)
    key_rows = mixture[:, features : 2 * features].astype(jnp.bfloat16)
    values = (mixture[:, 2 * features :] + biases[1]).astype(jnp.bfloat16)
    scores = attention_scores(
        split_heads(queries, crop_count, length),
        split_heads(key_rows, crop_count, length),
        validity,
    )
    top_score = jnp.max(scores, axis=-1, keepdims=True)
    exponent = jnp.exp(scores - top_score)
    denominator = jnp.sum(exponent, axis=-1, keepdims=True)
    attn_weights = (exponent / denominator).astype(jnp.bfloat16)
    log_total = top_score + jnp.log(denominator)
    attended = jnp.einsum(
        "chlm,cmhd->clhd",
        attn_weights,
        split_heads(values, crop_count, length),
        preferred_element_type=jnp.float32,
    )
    attended = attended.reshape(crop_count * length, features).astype(jnp.bfloat16)
    pre_first = (
        rows_flat.astype(jnp.float32)
        + jnp.dot(attended, w_out, preferred_element_type=jnp.float32)
        + biases[2]
    )
    hidden = layer_norm(pre_first, norm_gains[0], biases[3])
    upward = (
        jnp.dot(hidden.astype(jnp.bfloat16), w_expand, preferred_element_type=jnp.float32) + offsets
    )
    active = exact_gelu(upward).astype(jnp.bfloat16)
    pre_second = (
        hidden + jnp.dot(active, w_contract, preferred_element_type=jnp.float32) + biases[4]
    )
    result = layer_norm(pre_second, norm_gains[1], biases[5])
    saved_activations = (
        rows_flat,
        queries,
        key_rows,
        values,
        log_total,
        attended,
        pre_first,
        upward,
        active,
        pre_second,
    )
    return (result.reshape(crop_count, length, features), saved_activations)


def backward_block(grad_result, validity, params, saved_activations):
    w_proj, w_out, w_expand, w_contract, norm_gains, biases, offsets = params
    (
        rows_flat,
        queries,
        key_rows,
        values,
        log_total,
        attended,
        pre_first,
        upward,
        active,
        pre_second,
    ) = saved_activations
    norm_gains = norm_gains.astype(jnp.float32)
    biases = biases.astype(jnp.float32)
    crop_count, length, features = grad_result.shape
    row_total = crop_count * length
    grad_flat = grad_result.reshape(row_total, features)
    second_pull = jax.vjp(layer_norm, pre_second, norm_gains[1], biases[5])[1]
    grad_pre2, grad_gain2, grad_shift2 = second_pull(grad_flat)
    grad_branch = grad_pre2.astype(jnp.bfloat16)
    grad_contract = jnp.einsum("rf,rd->fd", active, grad_branch, preferred_element_type=jnp.float32)
    grad_active = jnp.einsum(
        "rd,fd->rf", grad_branch, w_contract, preferred_element_type=jnp.float32
    )
    grad_upward = jax.vjp(exact_gelu, upward)[1](grad_active)[0].astype(jnp.bfloat16)
    hidden, first_pull = jax.vjp(layer_norm, pre_first, norm_gains[0], biases[3])
    grad_expand = jnp.einsum(
        "rd,rf->df", hidden.astype(jnp.bfloat16), grad_upward, preferred_element_type=jnp.float32
    )
    grad_hidden = grad_pre2 + jnp.einsum(
        "rf,df->rd", grad_upward, w_expand, preferred_element_type=jnp.float32
    )
    grad_pre1, grad_gain1, grad_shift1 = first_pull(grad_hidden)
    grad_output = grad_pre1.astype(jnp.bfloat16)
    grad_w_out = jnp.einsum("rd,re->de", attended, grad_output, preferred_element_type=jnp.float32)
    grad_attended = jnp.einsum(
        "re,de->rd", grad_output, w_out, preferred_element_type=jnp.float32
    ).astype(jnp.bfloat16)
    heads_q = split_heads(queries, crop_count, length)
    heads_k = split_heads(key_rows, crop_count, length)
    heads_v = split_heads(values, crop_count, length)
    heads_grad = split_heads(grad_attended, crop_count, length)
    scores = attention_scores(heads_q, heads_k, validity)
    chances = jnp.exp(scores - log_total)
    grad_values = jnp.einsum(
        "chlm,clhd->cmhd",
        chances.astype(jnp.bfloat16),
        heads_grad,
        preferred_element_type=jnp.float32,
    )
    grad_chances = jnp.einsum(
        "clhd,cmhd->chlm", heads_grad, heads_v, preferred_element_type=jnp.float32
    )
    inner_sum = jnp.sum(grad_chances * chances, axis=-1, keepdims=True)
    grad_scores = (chances * (grad_chances - inner_sum)).astype(jnp.bfloat16)
    grad_queries = jnp.einsum(
        "chlm,cmhd->clhd", grad_scores, heads_k, preferred_element_type=jnp.float32
    ) * HD ** (-0.5)
    grad_keys = jnp.einsum(
        "chlm,clhd->cmhd", grad_scores, heads_q, preferred_element_type=jnp.float32
    ) * HD ** (-0.5)
    grad_mixture = jnp.concatenate(
        [
            grad_queries.reshape(row_total, features),
            grad_keys.reshape(row_total, features),
            grad_values.reshape(row_total, features),
        ],
        axis=1,
    ).astype(jnp.bfloat16)
    grad_proj = jnp.einsum("rd,re->de", rows_flat, grad_mixture, preferred_element_type=jnp.float32)
    grad_in = grad_pre1 + jnp.einsum(
        "re,de->rd", grad_mixture, w_proj, preferred_element_type=jnp.float32
    )
    grad_biases = jnp.stack(
        [
            column_sum(grad_mixture[:, :features]),
            column_sum(grad_mixture[:, 2 * features :]),
            column_sum(grad_output),
            grad_shift1,
            column_sum(grad_branch),
            grad_shift2,
        ]
    )
    grad_gains = jnp.stack([grad_gain1, grad_gain2])
    grad_offsets = column_sum(grad_upward)
    return (
        grad_in.reshape(crop_count, length, features),
        (grad_proj, grad_w_out, grad_expand, grad_contract, grad_gains, grad_biases, grad_offsets),
    )


def shards(
    inputs,
    keep_mask,
    lengths,
    slot_order,
    cotangent,
    query_projection,
    query_output,
    query_expand,
    query_contract,
    query_gains,
    query_biases,
    query_offsets,
    momentum_projection,
    momentum_output,
    momentum_expand,
    momentum_contract,
    momentum_gains,
    momentum_biases,
    momentum_offsets,
):
    section_index = lax.axis_index("section")
    first_section = section_index == 0
    crop_count = inputs.shape[1]
    crop_len = inputs.shape[2]
    features = inputs.shape[3]
    per_micro = crop_count // MB
    gathered = (
        lax.all_gather(query_projection, "dp", axis=1, tiled=True),
        lax.all_gather(query_output, "dp", axis=1, tiled=True),
        lax.all_gather(query_expand, "dp", axis=1, tiled=True),
        lax.all_gather(query_contract, "dp", axis=1, tiled=True),
        lax.all_gather(query_gains, "dp", axis=2, tiled=True),
        lax.all_gather(query_biases, "dp", axis=2, tiled=True),
        lax.all_gather(query_offsets, "dp", axis=1, tiled=True),
        lax.all_gather(momentum_projection, "dp", axis=1, tiled=True),
        lax.all_gather(momentum_output, "dp", axis=1, tiled=True),
        lax.all_gather(momentum_expand, "dp", axis=1, tiled=True),
        lax.all_gather(momentum_contract, "dp", axis=1, tiled=True),
        lax.all_gather(momentum_gains, "dp", axis=2, tiled=True),
        lax.all_gather(momentum_biases, "dp", axis=2, tiled=True),
        lax.all_gather(momentum_offsets, "dp", axis=1, tiled=True),
    )
    query_params = tuple((member[0] for member in gathered[:7]))
    momentum_params = tuple((member[0] for member in gathered[7:]))
    selector = slot_order[:, None] == jnp.arange(crop_count, dtype=jnp.int32)[None, :]
    lower_selection = selector.astype(jnp.bfloat16)
    full_selection = selector.astype(jnp.float32)
    positions = lax.broadcasted_iota(jnp.int32, keep_mask.shape, 2)
    validity = ((positions < lengths[:, :, None]) & ((keep_mask > 0) | (positions == 0))).astype(
        jnp.float32
    )
    slot_inputs = jnp.einsum(
        "sc,vcld->vsld", lower_selection, inputs, preferred_element_type=jnp.float32
    ).astype(jnp.bfloat16)
    slot_valid = jnp.einsum("sc,vcl->vsl", full_selection, validity, precision=highest_level)
    slot_cotangent = jnp.einsum(
        "yj,jgf->ygf", lower_selection, cotangent, preferred_element_type=jnp.float32
    ).astype(jnp.bfloat16)
    received = jnp.zeros((2, per_micro, crop_len, features), jnp.bfloat16)
    stored_ticks = []
    pooled_ticks = []
    for moment in range(MB + 1):
        micro_index = jnp.clip(moment - section_index, 0, MB - 1)
        local_in = take_micro(slot_inputs, micro_index, per_micro, 1)
        valid_now = take_micro(slot_valid, micro_index, per_micro, 1)
        block_in = jnp.where(first_section, local_in, received)
        query_out, saved_activations = forward_block(block_in[0], valid_now[0], query_params)
        momentum_out = forward_block(block_in[1], valid_now[1], momentum_params)[0]
        stored_ticks.append(saved_activations)
        pooled_ticks.append(
            jnp.stack([pool_rows(query_out, valid_now[0]), pool_rows(momentum_out, valid_now[1])])
        )
        if moment < MB:
            received = passed_along(
                jnp.stack([query_out, momentum_out]).astype(jnp.bfloat16), "section", 1
            )
    pooled_all = jnp.stack(pooled_ticks)
    pooled_live = lax.dynamic_slice_in_dim(pooled_all, section_index, MB, 0)
    pooled_slots = jnp.moveaxis(pooled_live, 1, 0).reshape(2, crop_count, features)
    pooled = lax.all_gather(pooled_slots, "dp", axis=1, tiled=True)[None]
    stored_stack = jax.tree.map(lambda *members: jnp.stack(members), *stored_ticks)
    back_received = jnp.zeros((per_micro, crop_len, features), jnp.bfloat16)
    grad_ticks = []
    totals = None
    pending = None
    for moment in range(MB + 1):
        micro_index = moment - 1 + section_index
        is_live = (micro_index >= 0) & (micro_index < MB)
        clipped = jnp.clip(micro_index, 0, MB - 1)
        valid_now = take_micro(slot_valid[0], clipped, per_micro, 0)
        own_grad = (
            take_micro(slot_cotangent, clipped, per_micro, 0).astype(jnp.float32)
            * valid_now[..., None]
        )
        incoming = jnp.where(first_section, back_received.astype(jnp.float32), own_grad)
        incoming = jnp.where(is_live, incoming, 0.0)
        forward_tick = jnp.clip(moment - 1 + 2 * section_index, 0, MB)
        saved_activations = jax.tree.map(
            lambda stacked: lax.dynamic_index_in_dim(stacked, forward_tick, 0, False), stored_stack
        )
        grad_in, grad_terms = backward_block(incoming, valid_now, query_params, saved_activations)
        grad_ticks.append(grad_in)
        pending = (
            grad_terms
            if pending is None
            else tuple((before + addend for before, addend in zip(pending, grad_terms)))
        )
        if moment < MB:
            back_received = passed_along(grad_in.astype(jnp.bfloat16), "section", -1)
    totals = (
        lax.psum_scatter(pending[0], "dp", scatter_dimension=0, tiled=True),
        lax.psum_scatter(pending[1], "dp", scatter_dimension=0, tiled=True),
        lax.psum_scatter(pending[2], "dp", scatter_dimension=0, tiled=True),
        lax.psum_scatter(pending[3], "dp", scatter_dimension=0, tiled=True),
        lax.psum_scatter(pending[4], "dp", scatter_dimension=1, tiled=True),
        lax.psum_scatter(pending[5], "dp", scatter_dimension=1, tiled=True),
        lax.psum_scatter(pending[6], "dp", scatter_dimension=0, tiled=True),
    )
    grad_all = jnp.stack(grad_ticks)
    live_gradient = lax.dynamic_slice_in_dim(grad_all, 1 - section_index, MB, 0).reshape(
        crop_count, crop_len, features
    )
    crop_gradients = jnp.einsum(
        "ka,kxo->axo", full_selection, live_gradient, precision=highest_level
    )
    grad_input = crop_gradients[None]
    return (
        pooled,
        grad_input,
        totals[0][None],
        totals[1][None],
        totals[2][None],
        totals[3][None],
        totals[4][None],
        totals[5][None],
        totals[6][None],
    )


def solution(mesh):
    in_specs = (
        P(None, "dp", None, None),
        P(None, "dp", None),
        P(None, "dp"),
        P("dp"),
        P("dp", None, None),
        P("section", "dp", None),
        P("section", "dp", None),
        P("section", "dp", None),
        P("section", "dp", None),
        P("section", None, "dp"),
        P("section", None, "dp"),
        P("section", "dp"),
        P("section", "dp", None),
        P("section", "dp", None),
        P("section", "dp", None),
        P("section", "dp", None),
        P("section", None, "dp"),
        P("section", None, "dp"),
        P("section", "dp"),
    )
    out_specs = (
        P("section", None, None, None),
        P("section", "dp", None, None),
        P("section", "dp", None),
        P("section", "dp", None),
        P("section", "dp", None),
        P("section", "dp", None),
        P("section", None, "dp"),
        P("section", None, "dp"),
        P("section", "dp"),
    )
    return jax.shard_map(shards, mesh=mesh, in_specs=in_specs, out_specs=out_specs, check_vma=False)
```

profile of v0, /device:TPU:2, one launch (start us, length us, event | category | flops | bytes accessed | tf_op | source)
XLA Modules:
  0.0 1212.3 jit_solution(16262190069257578221)
XLA Ops:
  13.6 23.4 %all_gather.53 = bf16[1,6,768]{1,0,2:T(2,128)(2,1)S(1)} all-gather(bf16[1,6,48]{1,0,2:T(2,128)(2,1)S(1)} %copy.255), channel_id=1, replica_groups=mesh['section'=2,'dp'=16] {'dp'}, dimensions={2}, use_global_device_ids=true | all-gather | bytes 9792 | tf_op jit(solution)/shard_map/all_gather | solution.py:244
  37.4 13.4 %slice_reduce_fusion = (f32[768]{0:T(1024)S(1)}, f32[768]{0:T(1024)}, f32[768]{0:T(1024)}, f32[768]{0:T(1024)}, f32[768]{0:T(1024)}, /*index=5*/f32[768]{0:T(1024)}) fusion(f32[1,6,768]{1,0,2:T(1,128)S(1)} %convert_element_type.472), kind=kLoop, calls=%fused_computation.686 | loop fusion | bytes 36864 | tf_op jit(solution)/shard_map/slice | solution.py:95
  52.6 58.6 %all-reduce.3 = (bf16[3072]{0:T(1024)(128)(2,1)S(1)}, bf16[3072]{0:T(1024)(128)(2,1)S(1)}) all-reduce(bf16[3072]{0:T(1024)(128)(2,1)S(1)} %dynamic-update-slice.1, bf16[3072]{0:T(1024)(128)(2,1)S(1)} %dynamic-update-slice), channel_id=1, replica_groups=mesh['section'=2,'dp'=16] {'dp'}, use_global_device_ids=true, to_apply=%add.1 | all-reduce | flops 6144 | bytes 24576
  111.8 2.6 convolution_convert_fusion
  114.4 6.1 constant_dynamic-slice_fusion.16
  120.5 2.5 fusion.783
  124.6 19.2 %all_gather.55 = bf16[1,2,768]{1,0,2:T(2,128)(2,1)S(1)} all-gather(bf16[1,2,48]{1,0,2:T(2,128)(2,1)S(1)} %copy.260), channel_id=1, replica_groups=mesh['section'=2,'dp'=16] {'dp'}, dimensions={2}, use_global_device_ids=true | all-gather | bytes 3264 | tf_op jit(solution)/shard_map/all_gather | solution.py:243
  144.2 5.1 slice_reduce_fusion.1
  149.5 19.7 %all_gather.46 = bf16[1,6,768]{1,0,2:T(2,128)(2,1)S(1)} all-gather(bf16[1,6,48]{1,0,2:T(2,128)(2,1)S(1)} %copy.248), channel_id=1, replica_groups=mesh['section'=2,'dp'=16] {'dp'}, dimensions={2}, use_global_device_ids=true | all-gather | bytes 9792 | tf_op jit(solution)/shard_map/all_gather | solution.py:237
  169.6 13.4 %slice_reduce_fusion.8 = (f32[768]{0:T(1024)}, f32[768]{0:T(1024)}, f32[768]{0:T(1024)S(1)}, f32[768]{0:T(1024)}, f32[768]{0:T(1024)}, /*index=5*/f32[768]{0:T(1024)}) fusion(f32[1,6,768]{1,0,2:T(1,128)S(1)} %convert_element_type.460), kind=kLoop, calls=%fused_computation.694 | loop fusion | bytes 36864 | tf_op jit(solution)/shard_map/slice | solution.py:95
  184.2 19.7 %all_gather.48 = bf16[1,2,768]{1,0,2:T(2,128)(2,1)S(1)} all-gather(bf16[1,2,48]{1,0,2:T(2,128)(2,1)S(1)} %copy.254), channel_id=1, replica_groups=mesh['section'=2,'dp'=16] {'dp'}, dimensions={2}, use_global_device_ids=true | all-gather | bytes 3264 | tf_op jit(solution)/shard_map/all_gather | solution.py:236
  204.3 4.5 slice_reduce_fusion.9
  211.7 3.3 fusion.61
  218.0 3.1 fusion.73
  225.9 4.6 fusion.785
  230.5 3.2 fusion.453
  239.2 2.2 fusion.792
  243.6 53.7 %all-gather.22.cloned.1.call-done = bf16[1,768,3072]{2,1,0:T(8,128)(2,1)} async-done(((bf16[1,48,3072]{2,1,0:T(8,128)(2,1)}), bf16[1,768,3072]{2,1,0:T(8,128)(2,1)}) %all-gather.22.cloned.1.call-update) | async-done | bytes 4718608 | tf_op jit(solution)/shard_map/all_gather | solution.py:241
  297.3 14.0 %fusion.787 = (f32[256]{0:T(256)}, f32[256,768]{1,0:T(8,128)S(1)}) fusion(f32[768]{0:T(1024)} %get-tuple-element.93, bf16[1,3072,768]{2,1,0:T(8,128)(2,1)} %all-gather.24.cloned.1.call-done, bf16[1,768,3072]{2,1,0:T(8,128)(2,1)} %all-gather.22.cloned.1.call-done, f32[3072]{0:T(1024)} %add.853, f32[256,768]{1,0:T(8,128)} %copy-done.118, ...), kind=kOutput, calls=%fused_computation.1037 | convolution fusion | flops 2470182656 | bytes 11034624 | tf_op jit(solution)/shard_map/dot_general | solution.py:93
  312.2 39.4 %all-gather.14.cloned.1.call-done = bf16[1,768,3072]{2,1,0:T(8,128)(2,1)} async-done(((bf16[1,48,3072]{2,1,0:T(8,128)(2,1)}), bf16[1,768,3072]{2,1,0:T(8,128)(2,1)}) %all-gather.14.cloned.1.call-update) | async-done | bytes 4718608 | tf_op jit(solution)/shard_map/all_gather | solution.py:234
  351.5 11.4 fusion.77
  362.9 42.9 %all-gather.16.cloned.1.call-done = bf16[1,3072,768]{2,1,0:T(8,128)(2,1)} async-done(((bf16[1,192,768]{2,1,0:T(8,128)(2,1)}), bf16[1,3072,768]{2,1,0:T(8,128)(2,1)}) %all-gather.16.cloned.1.call-update) | async-done | bytes 4718608 | tf_op jit(solution)/shard_map/all_gather | solution.py:235
  405.8 4.5 fusion.793
  414.2 2.6 fusion.507
  416.8 16.0 %collective-permute-done = bf16[2,1,256,768]{3,2,1,0:T(8,128)(2,1)S(1)} collective-permute-done((bf16[2,1,256,768]{3,2,1,0:T(8,128)(2,1)S(1)}, bf16[2,1,256,768]{3,2,1,0:T(8,128)(2,1)S(1)}, u32[]{:S(2)}, u32[]{:S(2)}) %collective-permute-start) | collective-permute-done | bytes 786464 | tf_op jit(solution)/shard_map/ppermute | solution.py:17
  438.3 3.5 fusion.794
  441.8 2.4 fusion.452
  450.7 13.9 %fusion.795 = (f32[256]{0:T(256)S(1)}, f32[256,768]{1,0:T(8,128)S(1)}) fusion(f32[768]{0:T(1024)S(1)} %copy-done.241, bf16[1,3072,768]{2,1,0:T(8,128)(2,1)} %all-gather.24.cloned.1.call-done, bf16[1,768,3072]{2,1,0:T(8,128)(2,1)} %all-gather.22.cloned.1.call-done, f32[3072]{0:T(1024)S(1)} %copy-done.204, f32[256]{0:T(256)S(1)} %add_rsqrt_fusion.5, ...), kind=kOutput, calls=%fused_computation.1041 | convolution fusion | flops 2471362304 | bytes 12628992 | tf_op jit(solution)/shard_map/dot_general | solution.py:93
  465.4 11.5 fusion.83
  484.0 2.2 slice_bitcast_fusion.6
  488.1 12.9 %collective-permute-done.1 = bf16[2,1,256,768]{3,2,1,0:T(8,128)(2,1)} collective-permute-done((bf16[2,1,256,768]{3,2,1,0:T(8,128)(2,1)}, bf16[2,1,256,768]{3,2,1,0:T(8,128)(2,1)}, u32[]{:S(2)}, u32[]{:S(2)}) %collective-permute-start.1) | collective-permute-done | bytes 786464 | tf_op jit(solution)/shard_map/ppermute | solution.py:17
  514.5 4.5 fusion.801
  519.0 2.4 fusion.451
  533.1 9.9 fusion.89
  543.0 2.1 fusion.807
  548.0 3.5 pad_maximum_fusion
  551.6 12.9 %convert_reduce_fusion.2 = (f32[3072]{0:T(1024)}, bf16[256,3072]{1,0:T(8,128)(2,1)S(1)}) fusion(bf16[1,3072,768]{2,1,0:T(8,128)(2,1)} %all-gather.16.cloned.1.call-done, f32[256]{0:T(256)S(1)} %negate_multiply_fusion.14, f32[256]{0:T(256)S(1)} %multiply_multiply_fusion.35, f32[256]{0:T(256)S(1)} %broadcast_multiply_fusion.5, ...), kind=kOutput, calls=%fused_computation.142 | convolution fusion | flops 1268511744 | bytes 10640896 | tf_op jit(solution)/shard_map/rd,fd->rf/dot_general | solution.py:134
  564.6 5.3 multiply_reduce_fusion.5
  615.5 3.2 fusion.543
  620.6 2.6 subtract_exponential_fusion.1
  625.8 2.5 subtract_exponential_fusion
  630.2 12.2 %convert_reduce_fusion.1 = (f32[3072]{0:T(1024)}, bf16[256,3072]{1,0:T(8,128)(2,1)S(1)}) fusion(bf16[1,3072,768]{2,1,0:T(8,128)(2,1)} %all-gather.16.cloned.1.call-done, f32[3,256,768]{2,1,0:T(8,128)S(1)} %pad_maximum_fusion.2, s32[]{:T(128)S(6)} %min.34, f32[256]{0:T(256)S(1)} %negate_multiply_fusion.12, f32[256]{0:T(256)S(1)} %multiply_multiply_fusion.33, ...), kind=kOutput, calls=%fused_computation.141 | convolution fusion | flops 1268708352 | bytes 11034112 | tf_op jit(solution)/shard_map/rd,fd->rf/dot_general | solution.py:134
  642.5 2.4 multiply_reduce_fusion.4
  649.3 2.6 fusion.457
  663.8 2.9 fusion.541
  669.2 12.8 %convert_reduce_fusion = (f32[3072]{0:T(1024)}, bf16[256,3072]{1,0:T(8,128)(2,1)S(1)}) fusion(bf16[1,3072,768]{2,1,0:T(8,128)(2,1)S(1)} %bitcast.1070, f32[3,256,768]{2,1,0:T(8,128)S(1)} %pad_maximum_fusion.2, s32[]{:T(128)S(6)} %min.36, f32[256]{0:T(256)S(1)} %negate_multiply_fusion.10, f32[256]{0:T(256)S(1)} %multiply_multiply_fusion.31, ...), kind=kOutput, calls=%fused_computation.140 | convolution fusion | flops 1268708352 | bytes 11034112 | tf_op jit(solution)/shard_map/rd,fd->rf/dot_general | solution.py:134
  682.0 2.3 multiply_reduce_fusion.3
  690.2 3.5 fusion.460
  716.9 4.5 add_add_fusion.3
  729.3 4.1 add_add_fusion.2
  734.1 3.4 fusion.534
  737.5 5.2 fusion.535
  742.7 9.2 add_add_fusion.1
  752.1 2.8 pad_maximum_fusion.1
  759.0 7.0 add_add_fusion
  767.6 14.6 %fusion.802 = (f32[256]{0:T(256)S(1)}, f32[256,768]{1,0:T(8,128)}) fusion(f32[768]{0:T(1024)S(1)} %copy-done.242, bf16[1,3072,768]{2,1,0:T(8,128)(2,1)} %all-gather.24.cloned.1.call-done, bf16[1,768,3072]{2,1,0:T(8,128)(2,1)} %all-gather.22.cloned.1.call-done, f32[3072]{0:T(1024)S(1)} %copy-done.205, f32[256]{0:T(256)S(1)} %add_rsqrt_fusion.1, ...), kind=kOutput, calls=%fused_computation.1044 | convolution fusion | flops 2471362304 | bytes 12628992 | tf_op jit(solution)/shard_map/dot_general | solution.py:93
  784.0 2.1 multiply_reduce_fusion.30
  790.8 19.5 %all-gather = f32[2,32,1,768]{3,0,2,1:T(2,128)S(1)} all-gather(f32[2,2,1,768]{3,0,2,1:T(2,128)S(1)} %fusion.631), channel_id=2, replica_groups=mesh['section'=2,'dp'=16] {'dp'}, dimensions={1}, use_global_device_ids=true | all-gather | bytes 208896 | tf_op jit(solution)/shard_map/all_gather | solution.py:284
  811.0 2.4 fusion.421
  814.1 3.6 fusion.365
  818.9 58.3 %all-reduce.2 = f32[3072]{0:T(1024)S(1)} all-reduce(f32[3072]{0:T(1024)S(1)} %add_add_fusion.22), channel_id=9, replica_groups=mesh['section'=2,'dp'=16] {'dp'}, use_global_device_ids=true, to_apply=%region_108.109.clone | all-reduce | flops 3072 | bytes 24576
  880.6 92.9 %reduce-scatter.11.cloned.1.call-done = f32[48,2304]{1,0:T(8,128)} async-done(((f32[768,2304]{1,0:T(8,128)}), f32[48,2304]{1,0:T(8,128)}) %reduce-scatter.11.cloned.1.call-update) | async-done | bytes 442384 | tf_op jit(solution)/shard_map/reduce_scatter | solution.py:315
  973.6 115.6 %reduce-scatter.15.cloned.1.call-done = f32[48,3072]{1,0:T(8,128)} async-done(((f32[768,3072]{1,0:T(8,128)}), f32[48,3072]{1,0:T(8,128)}) %reduce-scatter.15.cloned.1.call-update) | async-done | bytes 589840 | tf_op jit(solution)/shard_map/reduce_scatter | solution.py:317
  1089.1 116.2 %reduce-scatter.17.cloned.1.call-done = f32[192,768]{1,0:T(8,128)} async-done(((f32[3072,768]{1,0:T(8,128)}), f32[192,768]{1,0:T(8,128)}) %reduce-scatter.17.cloned.1.call-update) | async-done | bytes 589840 | tf_op jit(solution)/shard_map/reduce_scatter | solution.py:318
  (990 shorter events, 207.6 us)
Async XLA Ops:
  7.2 104.6 %copy-start = (bf16[2,2,256,768]{3,2,1,0:T(8,128)(2,1)S(1)}, bf16[2,2,256,768]{3,2,1,0:T(8,128)(2,1)}, u32[]{:S(2)}) copy-start(bf16[2,2,256,768]{3,2,1,0:T(8,128)(2,1)} %param.19) | copy-start | bytes 4718596
  7.2 43.6 %copy-start.290 = (u32[32]{0:T(128)S(1)}, u32[32]{0:T(128)}, u32[]{:S(2)}) copy-start(u32[32]{0:T(128)} %constant.251) | copy-start | bytes 388
  7.2 43.6 %copy-start.295 = (bf16[1,192]{1,0:T(2,128)(2,1)S(1)}, bf16[1,192]{1,0:T(2,128)(2,1)}, u32[]{:S(2)}) copy-start(bf16[1,192]{1,0:T(2,128)(2,1)} %param.37) | copy-start | bytes 1156
  7.2 43.6 %copy-start.296 = (bf16[1,192]{1,0:T(2,128)(2,1)S(1)}, bf16[1,192]{1,0:T(2,128)(2,1)}, u32[]{:S(2)}) copy-start(bf16[1,192]{1,0:T(2,128)(2,1)} %param.30) | copy-start | bytes 1156
  7.2 104.6 %copy-start.306 = (s32[2]{0:T(128)S(1)}, s32[2]{0:T(128)}, u32[]{:S(2)}) copy-start(s32[2]{0:T(128)} %param.22) | copy-start | bytes 28
  7.2 204.5 %all-gather.18.cloned.1.call-start = ((), (), s32[]{:S(2)}) async-start(), calls=%async_computation.10 | async-start | bytes 3760128 | tf_op jit(solution)/shard_map/all_gather | solution.py:239
  8.0 210.1 %all-gather.10.cloned.1.call-start = ((), (), s32[]{:S(2)}) async-start(), calls=%async_computation.6 | async-start | bytes 3760128 | tf_op jit(solution)/shard_map/all_gather | solution.py:232
  8.7 224.9 %all-gather.20.cloned.1.call-start = ((), (), s32[]{:S(2)}) async-start(), calls=%async_computation.11 | async-start | bytes 1253376 | tf_op jit(solution)/shard_map/all_gather | solution.py:240
  9.5 229.7 %all-gather.12.cloned.1.call-start = ((), (), s32[]{:S(2)}) async-start(), calls=%async_computation.7 | async-start | bytes 1253376 | tf_op jit(solution)/shard_map/all_gather | solution.py:233
  10.0 233.5 %all-gather.24.cloned.1.call-start = ((), (), s32[]{:S(2)}) async-start(), calls=%async_computation.13 | async-start | bytes 5013504 | tf_op jit(solution)/shard_map/all_gather | solution.py:242
  10.6 286.7 %all-gather.22.cloned.1.call-start = ((), (), s32[]{:S(2)}) async-start(), calls=%async_computation.12 | async-start | bytes 5013504 | tf_op jit(solution)/shard_map/all_gather | solution.py:241
  11.2 340.3 %all-gather.14.cloned.1.call-start = ((), (), s32[]{:S(2)}) async-start(), calls=%async_computation.8 | async-start | bytes 5013504 | tf_op jit(solution)/shard_map/all_gather | solution.py:234
  11.9 393.9 %all-gather.16.cloned.1.call-start = ((), (), s32[]{:S(2)}) async-start(), calls=%async_computation.9 | async-start | bytes 5013504 | tf_op jit(solution)/shard_map/all_gather | solution.py:235
  12.7 865.2 %reduce-scatter.19.cloned.1.call-start = ((), (), s32[]{:S(2)}) async-start(), calls=%async_computation.18 | async-start | bytes 417792
  50.8 414.1 %copy-start.130 = (f32[768]{0:T(1024)}, f32[768]{0:T(1024)S(1)}, u32[]{:S(2)}) copy-start(f32[768]{0:T(1024)S(1)} %get-tuple-element.92) | copy-start | bytes 9220
  120.5 28.9 %copy-start.291 = (bf16[1,6,48]{2,1,0:T(8,128)(2,1)S(1)}, bf16[1,6,48]{2,1,0:T(8,128)(2,1)}, u32[]{:S(2)}) copy-start(bf16[1,6,48]{2,1,0:T(8,128)(2,1)} %param.29) | copy-start | bytes 1732
  123.0 116.1 %copy-start.39 = (bf16[1,1,256,768]{3,0,2,1:T(2,128)(2,1)}, bf16[1,1,256,768]{3,0,2,1:T(2,128)(2,1)S(1)}, u32[]{:S(2)}) copy-start(bf16[1,1,256,768]{3,0,2,1:T(2,128)(2,1)S(1)} %get-tuple-element.155) | copy-start | bytes 1179652
  123.1 61.0 %copy-start.305 = (bf16[1,2,48]{2,1,0:T(2,128)(2,1)S(1)}, bf16[1,2,48]{2,1,0:T(2,128)(2,1)}, u32[]{:S(2)}) copy-start(bf16[1,2,48]{2,1,0:T(2,128)(2,1)} %param.28) | copy-start | bytes 580
  124.0 80.4 %copy-start.262 = (f32[1,256,1]{1,2,0:T(1,128)}, f32[1,256,1]{1,2,0:T(1,128)S(1)}, u32[]{:S(2)}) copy-start(f32[1,256,1]{1,2,0:T(1,128)S(1)} %get-tuple-element.174) | copy-start | bytes 3076
  124.0 80.4 %copy-start.268 = (f32[1,256,1]{1,2,0:T(1,128)}, f32[1,256,1]{1,2,0:T(1,128)S(1)}, u32[]{:S(2)}) copy-start(f32[1,256,1]{1,2,0:T(1,128)S(1)} %get-tuple-element.180) | copy-start | bytes 3076
  124.0 84.9 %copy-start.266 = (f32[1,256,1]{1,2,0:T(1,128)}, f32[1,256,1]{1,2,0:T(1,128)S(1)}, u32[]{:S(2)}) copy-start(f32[1,256,1]{1,2,0:T(1,128)S(1)} %get-tuple-element.178) | copy-start | bytes 3076
  124.0 85.5 %copy-start.260 = (f32[1,256,1]{1,2,0:T(1,128)}, f32[1,256,1]{1,2,0:T(1,128)S(1)}, u32[]{:S(2)}) copy-start(f32[1,256,1]{1,2,0:T(1,128)S(1)} %get-tuple-element.172) | copy-start | bytes 3076
  124.0 86.1 %copy-start.264 = (f32[1,256,1]{1,2,0:T(1,128)}, f32[1,256,1]{1,2,0:T(1,128)S(1)}, u32[]{:S(2)}) copy-start(f32[1,256,1]{1,2,0:T(1,128)S(1)} %get-tuple-element.176) | copy-start | bytes 3076
  124.0 86.6 %copy-start.258 = (f32[1,256,1]{1,2,0:T(1,128)}, f32[1,256,1]{1,2,0:T(1,128)S(1)}, u32[]{:S(2)}) copy-start(f32[1,256,1]{1,2,0:T(1,128)S(1)} %get-tuple-element.133) | copy-start | bytes 3076
  183.0 360.0 %copy-start.119 = (f32[768]{0:T(1024)}, f32[768]{0:T(1024)S(1)}, u32[]{:S(2)}) copy-start(f32[768]{0:T(1024)S(1)} %get-tuple-element.86) | copy-start | bytes 9220
  239.1 72.1 %copy-start.121 = (bf16[12,64,256]{2,1,0:T(8,128)(2,1)}, bf16[12,64,256]{2,1,0:T(8,128)(2,1)S(1)}, u32[]{:S(2)}) copy-start(bf16[12,64,256]{2,1,0:T(8,128)(2,1)S(1)} %fusion.471) | copy-start | bytes 1179652
  241.4 55.9 %copy-start.71 = (f32[256,768]{1,0:T(8,128)}, f32[256,768]{1,0:T(8,128)S(1)}, u32[]{:S(2)}) copy-start(f32[256,768]{1,0:T(8,128)S(1)} %get-tuple-element.195) | copy-start | bytes 2359300
  297.3 54.3 %copy-start.72 = (f32[256,768]{1,0:T(8,128)S(1)}, f32[256,768]{1,0:T(8,128)}, u32[]{:S(2)}) copy-start(f32[256,768]{1,0:T(8,128)} %copy-done.71) | copy-start | bytes 2359300
  311.2 99.4 %copy-start.33 = (f32[256,768]{1,0:T(8,128)}, f32[256,768]{1,0:T(8,128)S(1)}, u32[]{:S(2)}) copy-start(f32[256,768]{1,0:T(8,128)S(1)} %get-tuple-element.191) | copy-start | bytes 2359300
  311.9 98.7 %copy-start.174 = (f32[256]{0:T(256)}, f32[256]{0:T(256)S(1)}, u32[]{:S(2)}) copy-start(f32[256]{0:T(256)S(1)} %broadcast_multiply_fusion.14) | copy-start | bytes 3076
  312.2 98.5 %copy-start.222 = (f32[256]{0:T(256)}, f32[256]{0:T(256)S(1)}, u32[]{:S(2)}) copy-start(f32[256]{0:T(256)S(1)} %add_rsqrt_fusion.8) | copy-start | bytes 3076
  351.5 54.3 %copy-start.253 = (f32[768]{0:T(1024)S(1)}, f32[768]{0:T(1024)}, u32[]{:S(2)}) copy-start(f32[768]{0:T(1024)} %get-tuple-element.85) | copy-start | bytes 9220
  351.5 54.3 %copy-start.274 = (f32[256]{0:T(256)S(1)}, f32[256]{0:T(256)}, u32[]{:S(2)}) copy-start(f32[256]{0:T(256)} %copy-done.273) | copy-start | bytes 3076
  351.5 54.3 %copy-start.301 = (f32[256]{0:T(256)S(1)}, f32[256]{0:T(256)}, u32[]{:S(2)}) copy-start(f32[256]{0:T(256)} %add_rsqrt_fusion.11) | copy-start | bytes 3076
  411.2 21.6 %collective-permute-start = (bf16[2,1,256,768]{3,2,1,0:T(8,128)(2,1)S(1)}, bf16[2,1,256,768]{3,2,1,0:T(8,128)(2,1)S(1)}, u32[]{:S(2)}, u32[]{:S(2)}) collective-permute-start(bf16[2,1,256,768]{3,2,1,0:T(8,128)(2,1)S(1)} %pad_maximum_fusion.12), channel_id=1, source_target_pairs={{0,16},{1,17},{2,18},{3,19},{4,20},{5,21},{6,22},{7,23},{8,24},{9,... | collective-permute-start | bytes 2359304 | tf_op jit(solution)/shard_map/ppermute | solution.py:17
  413.0 19.7 %copy-start.155 = (f32[1,1,256]{2,1,0:T(1,128)}, f32[1,1,256]{2,1,0:T(1,128)S(1)}, u32[]{:S(2)}) copy-start(f32[1,1,256]{2,1,0:T(1,128)S(1)} %get-tuple-element.182) | copy-start | bytes 3076
  413.0 19.7 %copy-start.158 = (f32[1,1,256]{2,1,0:T(1,128)}, f32[1,1,256]{2,1,0:T(1,128)S(1)}, u32[]{:S(2)}) copy-start(f32[1,1,256]{2,1,0:T(1,128)S(1)} %get-tuple-element.183) | copy-start | bytes 3076
  414.2 18.7 %copy-start.11 = (bf16[1,768,2304]{2,1,0:T(8,128)(2,1)S(1)}, bf16[1,768,2304]{2,1,0:T(8,128)(2,1)}, u32[]{:S(2)}) copy-start(bf16[1,768,2304]{2,1,0:T(8,128)(2,1)} %all-gather.18.cloned.1.call-done) | copy-start | bytes 10616836
  450.6 26.3 %copy-start.74 = (f32[256,768]{1,0:T(8,128)}, f32[256,768]{1,0:T(8,128)S(1)}, u32[]{:S(2)}) copy-start(f32[256,768]{1,0:T(8,128)S(1)} %get-tuple-element.139) | copy-start | bytes 2359300
  478.8 24.1 %copy-start.228 = (f32[256]{0:T(256)}, f32[256]{0:T(256)S(1)}, u32[]{:S(2)}) copy-start(f32[256]{0:T(256)S(1)} %add_rsqrt_fusion.6) | copy-start | bytes 3076
  480.0 21.1 %collective-permute-start.1 = (bf16[2,1,256,768]{3,2,1,0:T(8,128)(2,1)}, bf16[2,1,256,768]{3,2,1,0:T(8,128)(2,1)}, u32[]{:S(2)}, u32[]{:S(2)}) collective-permute-start(bf16[2,1,256,768]{3,2,1,0:T(8,128)(2,1)} %pad_maximum_fusion.13), channel_id=1, source_target_pairs={{0,16},{1,17},{2,18},{3,19},{4,20},{5,21},{6,22},{7,23},{8,24},{9,... | collective-permute-start | bytes 2359304 | tf_op jit(solution)/shard_map/ppermute | solution.py:17
  483.3 19.5 %copy-start.12 = (bf16[1,768,2304]{2,1,0:T(8,128)(2,1)S(1)}, bf16[1,768,2304]{2,1,0:T(8,128)(2,1)}, u32[]{:S(2)}) copy-start(bf16[1,768,2304]{2,1,0:T(8,128)(2,1)} %all-gather.18.cloned.1.call-done) | copy-start | bytes 10616836
  502.9 27.5 %copy-start.41 = (bf16[2,1,256,768]{3,2,1,0:T(8,128)(2,1)}, bf16[2,1,256,768]{3,2,1,0:T(8,128)(2,1)S(1)}, u32[]{:S(2)}) copy-start(bf16[2,1,256,768]{3,2,1,0:T(8,128)(2,1)S(1)} %bitcast_select_fusion) | copy-start | bytes 2359300
  507.1 17.3 %copy-start.59 = (bf16[256,768]{1,0:T(8,128)(2,1)}, bf16[256,768]{1,0:T(8,128)(2,1)S(1)}, u32[]{:S(2)}) copy-start(bf16[256,768]{1,0:T(8,128)(2,1)S(1)} %get-tuple-element.140) | copy-start | bytes 1179652
  532.3 37.6 %copy-start.2 = (f32[3,256,768]{2,1,0:T(8,128)}, f32[3,256,768]{2,1,0:T(8,128)S(1)}, u32[]{:S(2)}) copy-start(f32[3,256,768]{2,1,0:T(8,128)S(1)} %pad_maximum_fusion.3) | copy-start | bytes 7077892
  533.0 36.9 %copy-start.169 = (f32[256]{0:T(256)}, f32[256]{0:T(256)S(1)}, u32[]{:S(2)}) copy-start(f32[256]{0:T(256)S(1)} %broadcast_multiply_fusion.4) | copy-start | bytes 3076
  546.3 23.6 %copy-start.196 = (f32[256]{0:T(256)}, f32[256]{0:T(256)S(1)}, u32[]{:S(2)}) copy-start(f32[256]{0:T(256)S(1)} %fusion.643) | copy-start | bytes 3076
  546.4 18.2 %copy-start.193 = (f32[256]{0:T(256)}, f32[256]{0:T(256)S(1)}, u32[]{:S(2)}) copy-start(f32[256]{0:T(256)S(1)} %broadcast_multiply_fusion.2) | copy-start | bytes 3076
  548.0 16.6 %copy-start.78 = (f32[256,768]{1,0:T(8,128)}, f32[256,768]{1,0:T(8,128)S(1)}, u32[]{:S(2)}) copy-start(f32[256,768]{1,0:T(8,128)S(1)} %get-tuple-element.123) | copy-start | bytes 2359300
  600.5 27.8 %collective-permute-start.2 = (bf16[1,256,768]{2,1,0:T(8,128)(2,1)}, bf16[1,256,768]{2,1,0:T(8,128)(2,1)S(1)}, u32[]{:S(2)}, u32[]{:S(2)}) collective-permute-start(bf16[1,256,768]{2,1,0:T(8,128)(2,1)} %convert_bitcast_fusion.1), channel_id=1, source_target_pairs={{16,0},{17,1},{18,2},{19,3},{20,4},{21,5},{22,6},{23,7},{24,8},{25... | collective-permute-start | bytes 1179656 | tf_op jit(solution)/shard_map/ppermute | solution.py:17
  625.8 16.6 %slice-start.2 = ((s8[4718592]{0:T(1024)(128)(4,1)}), s8[4194304]{0:T(1024)(128)(4,1)S(1)}, s32[]{:S(2)}) async-start(s8[4718592]{0:T(1024)(128)(4,1)} %bitcast.1061), calls=%async_computation.22 | async-start | bytes 8388608
  654.9 29.4 %copy-start.214 = (f32[256]{0:T(256)}, f32[256]{0:T(256)S(1)}, u32[]{:S(2)}) copy-start(f32[256]{0:T(256)S(1)} %fusion.647) | copy-start | bytes 3076
  657.7 9.1 collective-permute-start.3
  699.7 179.5 %reduce-scatter.21.cloned.1.call-start = ((), (), s32[]{:S(2)}) async-start(), calls=%async_computation.19 | async-start | bytes 417792
  716.9 163.8 %reduce-scatter.13.cloned.1.call-start = ((), (), s32[]{:S(2)}) async-start(), calls=%async_computation.15 | async-start | bytes 2506752 | tf_op jit(solution)/shard_map/reduce_scatter | solution.py:316
  721.5 252.1 %reduce-scatter.11.cloned.1.call-start = ((), (), s32[]{:S(2)}) async-start(), calls=%async_computation.14 | async-start | bytes 7520256 | tf_op jit(solution)/shard_map/reduce_scatter | solution.py:315
  733.4 355.7 %reduce-scatter.15.cloned.1.call-start = ((), (), s32[]{:S(2)}) async-start(), calls=%async_computation.16 | async-start | bytes 10027008 | tf_op jit(solution)/shard_map/reduce_scatter | solution.py:317
  752.0 453.4 %reduce-scatter.17.cloned.1.call-start = ((), (), s32[]{:S(2)}) async-start(), calls=%async_computation.17 | async-start | bytes 10027008 | tf_op jit(solution)/shard_map/reduce_scatter | solution.py:318
  782.3 28.7 %copy-start.10 = (bf16[1,768,2304]{2,1,0:T(8,128)(2,1)S(1)}, bf16[1,768,2304]{2,1,0:T(8,128)(2,1)}, u32[]{:S(2)}) copy-start(bf16[1,768,2304]{2,1,0:T(8,128)(2,1)} %all-gather.10.cloned.1.call-done) | copy-start | bytes 10616836
  782.3 28.7 %copy-start.62 = (bf16[12,64,256]{2,1,0:T(8,128)(2,1)S(1)}, bf16[12,64,256]{2,1,0:T(8,128)(2,1)}, u32[]{:S(2)}) copy-start(bf16[12,64,256]{2,1,0:T(8,128)(2,1)} %fusion.467) | copy-start | bytes 1179652
  782.3 28.7 %copy-start.69 = (bf16[12,64,256]{2,1,0:T(8,128)(2,1)S(1)}, bf16[12,64,256]{2,1,0:T(8,128)(2,1)}, u32[]{:S(2)}) copy-start(bf16[12,64,256]{2,1,0:T(8,128)(2,1)} %fusion.460) | copy-start | bytes 1179652
  782.3 28.7 %copy-start.117 = (bf16[12,64,256]{2,1,0:T(8,128)(2,1)S(1)}, bf16[12,64,256]{2,1,0:T(8,128)(2,1)}, u32[]{:S(2)}) copy-start(bf16[12,64,256]{2,1,0:T(8,128)(2,1)} %copy-done.116) | copy-start | bytes 1179652
  782.3 28.6 %copy-start.285 = (f32[256]{0:T(256)S(1)}, f32[256]{0:T(256)}, u32[]{:S(2)}) copy-start(f32[256]{0:T(256)} %copy-done.284) | copy-start | bytes 3076
  813.4 391.9 %copy-start.1 = (bf16[2,2,256,768]{3,2,1,0:T(8,128)(2,1)S(1)}, bf16[2,2,256,768]{3,2,1,0:T(8,128)(2,1)}, u32[]{:S(2)}) copy-start(bf16[2,2,256,768]{3,2,1,0:T(8,128)(2,1)} %param.19) | copy-start | bytes 4718596
  (285 other events, 1401.2 us)
Sparse Core Ops, SparseCore 0:
  10.4 49.1 all-gather.17
  61.8 46.2 all-gather.9
  110.3 38.7 all-gather.19
  151.3 37.4 all-gather.11
  190.8 52.2 all-gather.23
  245.3 51.9 all-gather.21
  299.6 51.9 all-gather.13
  353.8 51.9 all-gather.15
  699.8 54.8 reduce-scatter.18
  758.4 54.5 reduce-scatter.20
  817.4 62.0 reduce-scatter.12
  884.5 89.0 reduce-scatter.10
  978.3 110.8 reduce-scatter.14
  1094.2 111.0 reduce-scatter.16
where the time goes:
time: 1220 us; the launch traced here: 1210 us
  waiting for transfers between devices  495 us (41%)
  matrix products  260 us (21%)
  blocking collectives  218 us (18%)
  local copies, waits for them, and re-layouts  138 us (11%)
  other arithmetic  74.7 us (6%)
  between operations  20 us (2%)
    unnamed x2, blocking collectives  117 us
    reduce_scatter x1, waiting for transfers between devices, shards(): lax.psum_scatter(pending[3], 'dp', scatter_dimension=0, tiled=True)  116 us
    reduce_scatter x1, waiting for transfers between devices, shards(): lax.psum_scatter(pending[2], 'dp', scatter_dimension=0, tiled=True)  116 us
    reduce_scatter x1, waiting for transfers between devices, shards(): lax.psum_scatter(pending[0], 'dp', scatter_dimension=0, tiled=True)  92.9 us
    all_gather x1, waiting for transfers between devices, shards(): lax.all_gather(momentum_expand, 'dp', axis=1, tiled=True)  53.7 us
    dot_general x6, matrix products, forward_block(): jnp.dot(active, w_contract, preferred_element_type=jnp.float32)  50.6 us
    all_gather x1, waiting for transfers between devices, shards(): lax.all_gather(query_contract, 'dp', axis=1, tiled=True)  42.9 us
    all_gather x1, waiting for transfers between devices, shards(): lax.all_gather(query_expand, 'dp', axis=1, tiled=True)  39.4 us
  transfers between devices with their start and end apart: 18, of which 8 were waited for; matrix products, arithmetic and copies ran while one was open for 21% of the time, Pallas kernels for 0%

commit v1 on v0

--- a/solution.py
+++ b/solution.py
@@ -198,6 +198,101 @@
     return (
         grad_in.reshape(crop_count, length, features),
         (grad_proj, grad_w_out, grad_expand, grad_contract, grad_gains, grad_biases, grad_offsets),
+    )
+
+
+def pack_columns(w_proj, w_out, w_expand, w_contract, norm_gains, biases, offsets):
+    rows, features = w_out.shape
+    folded = w_contract.reshape(-1, rows, features)
+    groups = folded.shape[0]
+    vectors = jnp.concatenate([norm_gains, biases, offsets.reshape(groups, rows)], axis=0)
+    vectors = jnp.pad(vectors, ((0, 128 - vectors.shape[0]), (0, 0)))
+    return jnp.concatenate(
+        [
+            w_proj,
+            w_out,
+            w_expand,
+            jnp.moveaxis(folded, 0, 1).reshape(rows, groups * features),
+            vectors.T,
+        ],
+        axis=1,
+    )
+
+
+def unpack_columns(packed, shards_of):
+    features = packed.shape[0]
+    rows = features // shards_of
+    w_proj = packed[:, : 3 * features]
+    w_out = packed[:, 3 * features : 4 * features]
+    w_expand = packed[:, 4 * features : 8 * features]
+    folded = packed[:, 8 * features : 12 * features].reshape(shards_of, rows, -1, features)
+    w_contract = jnp.moveaxis(folded, 2, 1).reshape(-1, features)
+    vectors = packed[:, 12 * features :]
+    lines = vectors[:, :8].T
+    offsets = jnp.moveaxis(vectors[:, 8:12].reshape(shards_of, rows, -1), 2, 1).reshape(-1)
+    return (w_proj, w_out, w_expand, w_contract, lines[:2], lines[2:8], offsets)
+
+
+def halving_sum(block, shards_of):
+    here = lax.axis_index("dp")
+    levels = shards_of.bit_length() - 1
+    current = block.reshape((2,) * levels + block.shape[1:])
+    for level in range(levels):
+        axis = levels - 1 - level
+        mine = (here >> level) & 1
+        send = lax.dynamic_index_in_dim(current, 1 - mine, axis, keepdims=False)
+        keep = lax.dynamic_index_in_dim(current, mine, axis, keepdims=False)
+        route = [(i, i ^ (1 << level)) for i in range(shards_of)]
+        got = lax.ppermute(send, "dp", route)
+        current = (keep.astype(jnp.float32) + got.astype(jnp.float32)).astype(jnp.bfloat16)
+    return current
+
+
+def scatter_sum(terms, shards_of):
+    grad_proj, grad_out, grad_expand, grad_contract, grad_gains, grad_biases, grad_offsets = terms
+    features = grad_out.shape[0]
+    rows = features // shards_of
+    groups = grad_contract.shape[0] // features
+
+    def folded(matrix):
+        return matrix.astype(jnp.bfloat16).reshape(shards_of, rows, -1)
+
+    contract = grad_contract.astype(jnp.bfloat16).reshape(shards_of, groups, rows, features)
+    contract = jnp.moveaxis(contract, 1, 2).reshape(shards_of, rows, groups * features)
+    lines = jnp.concatenate([grad_gains, grad_biases], axis=0).T.reshape(shards_of, rows, 8)
+    marks = jnp.moveaxis(grad_offsets.reshape(shards_of, groups, rows), 1, 2)
+    vectors = jnp.concatenate([lines, marks], axis=2)
+    coarse = vectors.astype(jnp.bfloat16)
+    fine = (vectors - coarse.astype(jnp.float32)).astype(jnp.bfloat16)
+    vectors = jnp.concatenate([coarse, fine], axis=2)
+    vectors = jnp.pad(vectors, ((0, 0), (0, 0), (0, 128 - vectors.shape[2])))
+    half = 2 * features
+    expand = folded(grad_expand)
+    proj = folded(grad_proj)
+    chunks = [
+        contract[:, :, :half],
+        contract[:, :, half:],
+        expand[:, :, :half],
+        expand[:, :, half:],
+        jnp.concatenate([folded(grad_out), proj[:, :, :features]], axis=2),
+        jnp.concatenate([proj[:, :, features:], vectors], axis=2),
+    ]
+    sums = [halving_sum(chunk, shards_of).astype(jnp.float32) for chunk in chunks]
+    contract_sum = jnp.concatenate(sums[:2], axis=1).reshape(rows, groups, features)
+    contract_sum = jnp.moveaxis(contract_sum, 1, 0).reshape(groups * rows, features)
+    expand_sum = jnp.concatenate(sums[2:4], axis=1)
+    out_sum = sums[4][:, :features]
+    proj_sum = jnp.concatenate([sums[4][:, features:], sums[5][:, :half]], axis=1)
+    vector_sum = sums[5][:, half : half + 12] + sums[5][:, half + 12 : half + 24]
+    lines = vector_sum.T
+    return (
+        proj_sum,
+        out_sum,
+        expand_sum,
+        contract_sum,
+        lines[:2],
+        lines[2:8],
+        lines[8:].reshape(groups * rows),
     )
 
 
@@ -228,24 +323,39 @@
     crop_len = inputs.shape[2]
     features = inputs.shape[3]
     per_micro = crop_count // MB
-    gathered = (
-        lax.all_gather(query_projection, "dp", axis=1, tiled=True),
-        lax.all_gather(query_output, "dp", axis=1, tiled=True),
-        lax.all_gather(query_expand, "dp", axis=1, tiled=True),
-        lax.all_gather(query_contract, "dp", axis=1, tiled=True),
-        lax.all_gather(query_gains, "dp", axis=2, tiled=True),
-        lax.all_gather(query_biases, "dp", axis=2, tiled=True),
-        lax.all_gather(query_offsets, "dp", axis=1, tiled=True),
-        lax.all_gather(momentum_projection, "dp", axis=1, tiled=True),
-        lax.all_gather(momentum_output, "dp", axis=1, tiled=True),
-        lax.all_gather(momentum_expand, "dp", axis=1, tiled=True),
-        lax.all_gather(momentum_contract, "dp", axis=1, tiled=True),
-        lax.all_gather(momentum_gains, "dp", axis=2, tiled=True),
-        lax.all_gather(momentum_biases, "dp", axis=2, tiled=True),
-        lax.all_gather(momentum_offsets, "dp", axis=1, tiled=True),
-    )
-    query_params = tuple((member[0] for member in gathered[:7]))
-    momentum_params = tuple((member[0] for member in gathered[7:]))
+    n_dp = lax.axis_size("dp")
+    share = features // n_dp
+    query_all = pack_columns(
+        query_projection[0],
+        query_output[0],
+        query_expand[0],
+        query_contract[0],
+        query_gains[0],
+        query_biases[0],
+        query_offsets[0],
+    )
+    momentum_all = pack_columns(
+        momentum_projection[0],
+        momentum_output[0],
+        momentum_expand[0],
+        momentum_contract[0],
+        momentum_gains[0],
+        momentum_biases[0],
+        momentum_offsets[0],
+    )
+    width = query_all.shape[1]
+    early = 3 * features
+    momentum_early = momentum_all[:, :early]
+    momentum_late = momentum_all[:, early:]
+    gathered_first = lax.all_gather(
+        jnp.concatenate([query_all, momentum_early], axis=1), "dp", axis=0, tiled=True
+    )
+    momentum_late, gathered_first = lax.optimization_barrier((momentum_late, gathered_first))
+    gathered_second = lax.all_gather(momentum_late, "dp", axis=0, tiled=True)
+    query_params = unpack_columns(gathered_first[:, :width], n_dp)
+    momentum_params = unpack_columns(
+        jnp.concatenate([gathered_first[:, width:], gathered_second], axis=1), n_dp
+    )
     selector = slot_order[:, None] == jnp.arange(crop_count, dtype=jnp.int32)[None, :]
     lower_selection = selector.astype(jnp.bfloat16)
     full_selection = selector.astype(jnp.float32)
@@ -285,7 +395,6 @@
     stored_stack = jax.tree.map(lambda *members: jnp.stack(members), *stored_ticks)
     back_received = jnp.zeros((per_micro, crop_len, features), jnp.bfloat16)
     grad_ticks = []
-    totals = None
     pending = None
     for moment in range(MB + 1):
         micro_index = moment - 1 + section_index
@@ -311,15 +420,7 @@
         )
         if moment < MB:
             back_received = passed_along(grad_in.astype(jnp.bfloat16), "section", -1)
-    totals = (
-        lax.psum_scatter(pending[0], "dp", scatter_dimension=0, tiled=True),
-        lax.psum_scatter(pending[1], "dp", scatter_dimension=0, tiled=True),
-        lax.psum_scatter(pending[2], "dp", scatter_dimension=0, tiled=True),
-        lax.psum_scatter(pending[3], "dp", scatter_dimension=0, tiled=True),
-        lax.psum_scatter(pending[4], "dp", scatter_dimension=1, tiled=True),
-        lax.psum_scatter(pending[5], "dp", scatter_dimension=1, tiled=True),
-        lax.psum_scatter(pending[6], "dp", scatter_dimension=0, tiled=True),
-    )
+    totals = scatter_sum(pending, n_dp)
     grad_all = jnp.stack(grad_ticks)
     live_gradient = lax.dynamic_slice_in_dim(grad_all, 1 - section_index, MB, 0).reshape(
         crop_count, crop_len, features

time: 1220 us -> 894 us (0.73)
  waiting for transfers between devices: 495 us -> 247 us
  blocking collectives: 218 us -> 19 us
  local copies, waits for them, and re-layouts: 138 us -> 183 us
  matrix products: 260 us -> 303 us
  starting transfers between devices: 6.66 us -> 21.4 us
  other arithmetic: 74.7 us -> 88.3 us
    reduce_scatter x4 -> x0, waiting for transfers between devices: 325 us -> none  [the longest x1 116 us: shards(): lax.psum_scatter(pending[3], 'dp', scatter_dimension=0, tiled=True)]
    unnamed x2 -> x0, blocking collectives: 117 us -> none
    ppermute x0 -> x24, waiting for transfers between devices: none -> 102 us  [halving_sum(): got = lax.ppermute(send, 'dp', route)]
    all_gather x4 -> x0, blocking collectives: 82.1 us -> none  [the longest x1 23.4 us: shards(): lax.all_gather(momentum_biases, 'dp', axis=2, tiled=True)]
    reshape x0 -> x7, local copies, waits for them, and re-layouts: none -> 35.4 us  [the longest x2 20.2 us: unpack_columns(): packed[:, 8 * features:12 * features].reshape(shards_of, rows, -1, features)]
    slice x4, local copies, waits for them, and re-layouts: 36.4 us -> 4.8 us  [forward_block(): result = layer_norm(pre_second, norm_gains[1], biases[5])]
    all_gather x8 -> x2, waiting for transfers between devices: 136 us -> 113 us  [the longest x1 93.6 us: shards(): lax.all_gather(jnp.concatenate([query_all, momentum_early], axis=1), 'dp'...]
    slice x0 -> x12, local copies, waits for them, and re-layouts: none -> 18.7 us  [the longest x2 9.69 us: unpack_columns(): packed[:, 8 * features:12 * features].reshape(shards_of, rows, -1, features)]
  transfers between devices with their start and end apart: 18 -> 30, of which waited for: 8 -> 15; matrix products, arithmetic and copies ran while one was open for 21% -> 21% of each run, Pallas kernels for 0% -> 0%
where the time goes in v1:
time: 894 us; the launch traced here: 880 us
  matrix products  303 us (34%)
  waiting for transfers between devices  247 us (28%)
  local copies, waits for them, and re-layouts  183 us (20%)
  other arithmetic  88.3 us (10%)
  starting transfers between devices  21.4 us (2%)
  blocking collectives  19 us (2%)
  between operations  19 us (2%)
    ppermute x24, waiting for transfers between devices, halving_sum(): got = lax.ppermute(send, 'dp', route)  102 us
    all_gather x1, waiting for transfers between devices, shards(): lax.all_gather(jnp.concatenate([query_all, momentum_early], axis=1), 'dp'...  93.6 us
    dot_general x6, matrix products, forward_block(): jnp.dot(active, w_contract, preferred_element_type=jnp.float32)  48.2 us
    dot_general x3, matrix products, backward_block(): jnp.einsum('rd,fd->rf', grad_branch, w_contract, preferred_element_type=j...  39.3 us
    dot_general x3, matrix products, forward_block(): jnp.dot(hidden.astype(jnp.bfloat16), w_expand, preferred_element_type=jnp...  32.5 us
    ppermute x4, waiting for transfers between devices, passed_along(): return lax.ppermute(block, axis, route)  31.7 us
    unnamed x610, local copies, waits for them, and re-layouts  28.3 us
    reshape x2, local copies, waits for them, and re-layouts, unpack_columns(): packed[:, 8 * features:12 * features].reshape(shards_of, rows, -1, features)  20.2 us
  transfers between devices with their start and end apart: 30, of which 15 were waited for; matrix products, arithmetic and copies ran while one was open for 21% of the time, Pallas kernels for 0%

profile of v1, /device:TPU:2, one launch (start us, length us, event | category | flops | bytes accessed | tf_op | source)
XLA Modules:
  0.0 880.4 jit_solution(14555514066519623027)
XLA Ops:
  17.0 93.6 %all-gather.4.cloned.1.call-done = bf16[768,11648]{1,0:T(8,128)(2,1)} async-done(((bf16[48,11648]{1,0:T(8,128)(2,1)}), bf16[768,11648]{1,0:T(8,128)(2,1)}) %all-gather.4.cloned.1.call-update) | async-done | bytes 17891344 | tf_op jit(solution)/shard_map/all_gather | solution.py:350
  113.3 6.1 constant_dynamic-slice_fusion.28
  128.7 4.8 slice.329
  133.6 3.1 fusion.146
  139.9 3.1 fusion.224
  150.6 10.0 %reshape.1622 = bf16[16,48,4,768]{3,2,1,0:T(4,128)(2,1)} reshape(bf16[768,3072]{1,0:T(8,128)(2,1)} %slice.329) | data formatting | bytes 9437184 | tf_op jit(solution)/shard_map/reshape | solution.py:228
  160.7 3.3 copy.397
  170.0 10.8 %fusion.9 = (bf16[256,3072]{1,0:T(8,128)(2,1)S(1)}, f32[256,3072]{1,0:T(8,128)}) fusion(f32[3072]{0:T(1024)S(1)} %copy-done.207, bf16[768,11648]{1,0:T(8,128)(2,1)} %all-gather.4.cloned.1.call-done, f32[256,768]{1,0:T(8,128)S(1)} %get-tuple-element.210, f32[768]{0:T(1024)S(1)} %get-tuple-element.99, f32[768]{0:T(1024)S(1)} %get-tuple-element.96, ...), kind=kOutput, calls=%fused_computation.31 | convolution fusion | flops 1260847104 | bytes 10244096 | tf_op jit(solution)/shard_map/dot_general | solution.py:89
  183.4 19.2 %all-gather.6.cloned.1.call-done = bf16[768,7040]{1,0:T(8,128)(2,1)} async-done(((bf16[48,7040]{1,0:T(8,128)(2,1)}), bf16[768,7040]{1,0:T(8,128)(2,1)}) %all-gather.6.cloned.1.call-update) | async-done | bytes 10813456 | tf_op jit(solution)/shard_map/all_gather | solution.py:354
  205.6 4.9 slice.418
  210.5 10.2 %reshape.1627 = bf16[16,48,4,768]{3,2,1,0:T(4,128)(2,1)} reshape(bf16[768,3072]{1,0:T(8,128)(2,1)} %slice.418) | data formatting | bytes 9437184 | tf_op jit(solution)/shard_map/reshape | solution.py:228
  220.7 5.3 copy.403
  231.5 3.5 fusion.670
  240.3 13.5 %fusion.672 = (f32[256]{0:T(256)S(1)}, f32[256,768]{1,0:T(8,128)S(1)}) fusion(f32[768]{0:T(1024)S(1)} %copy-done.240, bf16[3072,768]{1,0:T(8,128)(2,1)} %bitcast.975, f32[3072]{0:T(1024)S(1)} %copy-done.205, bf16[768,7040]{1,0:T(8,128)(2,1)} %all-gather.6.cloned.1.call-done, f32[256,768]{1,0:T(8,128)} %copy-done.120, f32[768]{0:T(1024)S(1)} %copy-done.241, ...), kind=kOutput, calls=%fused_computation.1062 | convolution fusion | flops 2470182656 | bytes 11834368 | tf_op jit(solution)/shard_map/dot_general | solution.py:93
  259.4 17.7 %collective-permute-done = bf16[2,1,256,768]{3,2,1,0:T(8,128)(2,1)} collective-permute-done((bf16[2,1,256,768]{3,2,1,0:T(8,128)(2,1)}, bf16[2,1,256,768]{3,2,1,0:T(8,128)(2,1)}, u32[]{:S(2)}, u32[]{:S(2)}) %collective-permute-start) | collective-permute-done | bytes 786464 | tf_op jit(solution)/shard_map/ppermute | solution.py:17
  278.4 3.4 fusion.144
  282.0 3.1 fusion.222
  287.9 3.5 fusion.679
  297.2 14.4 %fusion.680 = (f32[256]{0:T(256)}, f32[256,768]{1,0:T(8,128)S(1)}) fusion(f32[768]{0:T(1024)} %get-tuple-element.106, bf16[3072,768]{1,0:T(8,128)(2,1)} %bitcast.976, f32[3072]{0:T(1024)} %reshape.1691, bf16[768,7040]{1,0:T(8,128)(2,1)} %all-gather.6.cloned.1.call-done, f32[256]{0:T(256)} %add_rsqrt_fusion.5, f32[256]{0:T(256)} %copy-done.261, ...), kind=kOutput, calls=%fused_computation.1066 | convolution fusion | flops 2471362304 | bytes 12628992 | tf_op jit(solution)/shard_map/dot_general | solution.py:93
  321.3 10.9 %fusion.15 = (bf16[256,3072]{1,0:T(8,128)(2,1)S(1)}, f32[256,3072]{1,0:T(8,128)}) fusion(f32[3072]{0:T(1024)S(1)} %copy-done.208, bf16[768,11648]{1,0:T(8,128)(2,1)} %all-gather.4.cloned.1.call-done, f32[256,768]{1,0:T(8,128)S(1)} %get-tuple-element.224, f32[256]{0:T(256)S(1)} %add_rsqrt_fusion.7, f32[256]{0:T(256)S(1)} %broadcast_multiply_fusion.13, ...), kind=kOutput, calls=%fused_computation.37 | convolution fusion | flops 1260847104 | bytes 10244096 | tf_op jit(solution)/shard_map/dot_general | solution.py:89
  341.2 14.0 %collective-permute-done.1 = bf16[2,1,256,768]{3,2,1,0:T(8,128)(2,1)S(1)} collective-permute-done((bf16[2,1,256,768]{3,2,1,0:T(8,128)(2,1)S(1)}, bf16[2,1,256,768]{3,2,1,0:T(8,128)(2,1)S(1)}, u32[]{:S(2)}, u32[]{:S(2)}) %collective-permute-start.1) | collective-permute-done | bytes 786464 | tf_op jit(solution)/shard_map/ppermute | solution.py:17
  355.5 3.4 fusion.142
  360.6 3.1 fusion.220
  371.4 10.9 %fusion.21 = (bf16[256,3072]{1,0:T(8,128)(2,1)S(1)}, f32[256,3072]{1,0:T(8,128)}) fusion(f32[3072]{0:T(1024)S(1)} %copy-done.209, bf16[768,11648]{1,0:T(8,128)(2,1)} %all-gather.4.cloned.1.call-done, f32[256,768]{1,0:T(8,128)S(1)} %get-tuple-element.238, f32[256]{0:T(256)S(1)} %add_rsqrt_fusion.3, f32[256]{0:T(256)S(1)} %broadcast_multiply_fusion.9, ...), kind=kOutput, calls=%fused_computation.43 | convolution fusion | flops 1260847104 | bytes 10244096 | tf_op jit(solution)/shard_map/dot_general | solution.py:89
  389.9 3.5 pad_maximum_fusion
  393.5 13.2 %convert_reduce_fusion.2 = (f32[3072]{0:T(1024)}, bf16[256,3072]{1,0:T(8,128)(2,1)S(1)}) fusion(bf16[3072,768]{1,0:T(8,128)(2,1)} %bitcast.962, f32[256]{0:T(256)S(1)} %negate_multiply_fusion.14, f32[256]{0:T(256)S(1)} %multiply_multiply_fusion.35, f32[256]{0:T(256)S(1)} %broadcast_multiply_fusion.5, f32[3,256,768]{2,1,0:T(8,128)S(1)} %pad_maximum_fusion.2, ...), kind=kOutput, calls=%fused_computation.94 | convolution fusion | flops 1268511744 | bytes 10640896 | tf_op jit(solution)/shard_map/rd,fd->rf/dot_general | solution.py:134
  406.7 5.3 multiply_reduce_fusion.5
  441.2 6.4 fusion.385
  453.3 4.5 fusion.687
  463.6 15.2 %fusion.688 = (f32[256]{0:T(256)}, f32[256,768]{1,0:T(8,128)}) fusion(f32[768]{0:T(1024)} %get-tuple-element.106, bf16[3072,768]{1,0:T(8,128)(2,1)} %bitcast.977, f32[3072]{0:T(1024)} %reshape.1691, bf16[768,7040]{1,0:T(8,128)(2,1)} %all-gather.6.cloned.1.call-done, f32[256]{0:T(256)} %add_rsqrt_fusion.1, f32[256]{0:T(256)} %copy-done.260, ...), kind=kOutput, calls=%fused_computation.1070 | convolution fusion | flops 2471362304 | bytes 12628992 | tf_op jit(solution)/shard_map/dot_general | solution.py:93
  488.3 19.0 %all-gather = f32[2,32,1,768]{3,0,2,1:T(2,128)S(1)} all-gather(f32[2,2,1,768]{3,0,2,1:T(2,128)S(1)} %fusion.510), channel_id=2, replica_groups=mesh['section'=2,'dp'=16] {'dp'}, dimensions={1}, use_global_device_ids=true | all-gather | bytes 208896 | tf_op jit(solution)/shard_map/all_gather | solution.py:394
  510.5 3.1 fusion.228
  531.3 5.7 fusion.365
  541.4 5.5 fusion.176
  557.8 13.3 %convert_reduce_fusion.1 = (f32[3072]{0:T(1024)}, bf16[256,3072]{1,0:T(8,128)(2,1)S(1)}) fusion(bf16[3072,768]{1,0:T(8,128)(2,1)S(1)} %bitcast.971, f32[3,256,768]{2,1,0:T(8,128)S(1)} %pad_maximum_fusion.2, s32[]{:T(128)S(6)} %min.34, f32[256]{0:T(256)S(1)} %negate_multiply_fusion.12, f32[256]{0:T(256)S(1)} %multiply_multiply_fusion.33, ...), kind=kOutput, calls=%fused_computation.93 | convolution fusion | flops 1268708352 | bytes 11034112 | tf_op jit(solution)/shard_map/rd,fd->rf/dot_general | solution.py:134
  571.2 5.2 multiply_reduce_fusion.4
  583.0 2.8 fusion.277
  589.5 3.1 fusion.231
  592.6 5.5 fusion.364
  598.1 3.0 fusion.395
  601.3 5.1 fusion.386
  612.0 6.8 fusion.174
  620.6 12.8 %convert_reduce_fusion = (f32[3072]{0:T(1024)}, bf16[256,3072]{1,0:T(8,128)(2,1)S(1)}) fusion(bf16[3072,768]{1,0:T(8,128)(2,1)S(1)} %bitcast.974, f32[3,256,768]{2,1,0:T(8,128)S(1)} %pad_maximum_fusion.2, s32[]{:T(128)S(6)} %min.36, f32[256]{0:T(256)S(1)} %negate_multiply_fusion.10, f32[256]{0:T(256)S(1)} %multiply_multiply_fusion.31, ...), kind=kOutput, calls=%fused_computation.92 | convolution fusion | flops 1268708352 | bytes 11034112 | tf_op jit(solution)/shard_map/rd,fd->rf/dot_general | solution.py:134
  633.5 5.3 multiply_reduce_fusion.3
  645.9 3.5 fusion.280
  672.6 3.8 fusion.237
  676.4 6.3 add_convert_fusion.2
  685.8 3.8 fusion.211
  698.8 8.3 add_convert_fusion.1
  713.1 6.1 add_convert_fusion
  719.3 4.6 copy.531
  723.9 9.5 %reshape.1686 = bf16[16,48,3072]{2,1,0:T(8,128)(2,1)} reshape(bf16[16,48,4,768]{3,2,1,0:T(4,128)(2,1)} %bitcast.942) | data formatting | bytes 9437184 | tf_op jit(solution)/shard_map/reshape | solution.py:261
  750.8 5.4 collective-permute-done.5
  757.0 11.8 %collective-permute-done.17 = bf16[2,2,48,1536]{3,2,0,1:T(8,128)(2,1)S(1)} collective-permute-done((bf16[2,2,48,1536]{3,2,0,1:T(8,128)(2,1)S(1)}, bf16[2,2,48,1536]{3,2,0,1:T(8,128)(2,1)S(1)}, u32[]{:S(2)}, u32[]{:S(2)}) %collective-permute-start.17) | collective-permute-done | bytes 589856 | tf_op jit(solution)/shard_map/ppermute | solution.py:246
  769.0 12.4 %collective-permute-done.13 = bf16[2,2,48,1536]{3,2,1,0:T(8,128)(2,1)S(1)} collective-permute-done((bf16[2,2,48,1536]{3,2,1,0:T(8,128)(2,1)S(1)}, bf16[2,2,48,1536]{3,2,1,0:T(8,128)(2,1)S(1)}, u32[]{:S(2)}, u32[]{:S(2)}) %collective-permute-start.13) | collective-permute-done | bytes 589856 | tf_op jit(solution)/shard_map/ppermute | solution.py:246
  781.7 12.4 %collective-permute-done.25 = bf16[2,2,48,1536]{3,2,0,1:T(8,128)(2,1)S(1)} collective-permute-done((bf16[2,2,48,1536]{3,2,0,1:T(8,128)(2,1)S(1)}, bf16[2,2,48,1536]{3,2,0,1:T(8,128)(2,1)S(1)}, u32[]{:S(2)}, u32[]{:S(2)}) %collective-permute-start.25) | collective-permute-done | bytes 589856 | tf_op jit(solution)/shard_map/ppermute | solution.py:246
  794.3 12.4 %collective-permute-done.21 = bf16[2,2,48,1536]{3,2,0,1:T(8,128)(2,1)S(1)} collective-permute-done((bf16[2,2,48,1536]{3,2,0,1:T(8,128)(2,1)S(1)}, bf16[2,2,48,1536]{3,2,0,1:T(8,128)(2,1)S(1)}, u32[]{:S(2)}, u32[]{:S(2)}) %collective-permute-start.21) | collective-permute-done | bytes 589856 | tf_op jit(solution)/shard_map/ppermute | solution.py:246
  806.9 12.8 %collective-permute-done.9 = bf16[2,2,48,1664]{3,2,1,0:T(8,128)(2,1)S(1)} collective-permute-done((bf16[2,2,48,1664]{3,2,1,0:T(8,128)(2,1)S(1)}, bf16[2,2,48,1664]{3,2,1,0:T(8,128)(2,1)S(1)}, u32[]{:S(2)}, u32[]{:S(2)}) %collective-permute-start.9) | collective-permute-done | bytes 639008 | tf_op jit(solution)/shard_map/ppermute | solution.py:246
  823.1 3.0 collective-permute-start.19
  826.9 10.6 %collective-permute-done.22 = bf16[2,48,1536]{2,1,0:T(8,128)(2,1)S(1)} collective-permute-done((bf16[2,48,1536]{2,1,0:T(8,128)(2,1)S(1)}, bf16[2,48,1536]{2,1,0:T(8,128)(2,1)S(1)}, u32[]{:S(2)}, u32[]{:S(2)}) %collective-permute-start.22) | collective-permute-done | bytes 294944 | tf_op jit(solution)/shard_map/ppermute | solution.py:246
  837.6 3.1 collective-permute-start.23
  840.7 8.4 collective-permute-done.19
  849.2 6.2 collective-permute-done.27
  862.0 8.1 collective-permute-done.11
  (1027 shorter events, 288.6 us)
Async XLA Ops:
  7.2 103.4 %copy-start = (bf16[2,2,256,768]{3,2,1,0:T(8,128)(2,1)S(1)}, bf16[2,2,256,768]{3,2,1,0:T(8,128)(2,1)}, u32[]{:S(2)}) copy-start(bf16[2,2,256,768]{3,2,1,0:T(8,128)(2,1)} %param.19) | copy-start | bytes 4718596
  7.2 103.3 %all-gather.4.cloned.1.call-start = ((), (), s32[]{:S(2)}) async-start(), calls=%async_computation | async-start | bytes 19009536 | tf_op jit(solution)/shard_map/all_gather | solution.py:350
  8.4 102.3 %copy-start.282 = (s32[2]{0:T(128)S(1)}, s32[2]{0:T(128)}, u32[]{:S(2)}) copy-start(s32[2]{0:T(128)} %param.22) | copy-start | bytes 28
  14.8 187.8 %all-gather.6.cloned.1.call-start = ((), (), s32[]{:S(2)}) async-start(), calls=%async_computation.1 | async-start | bytes 11489280 | tf_op jit(solution)/shard_map/all_gather | solution.py:354
  123.3 42.0 %copy-start.278 = (pred[256]{0:T(512)(128)(4,1)}, pred[256]{0:T(512)(128)(4,1)S(1)}, u32[]{:S(2)}) copy-start(pred[256]{0:T(512)(128)(4,1)S(1)} %broadcast_compare_fusion.8) | copy-start | bytes 772
  164.0 16.8 %copy-start.34 = (bf16[16,4,48,768]{3,2,1,0:T(8,128)(2,1)}, bf16[16,4,48,768]{3,2,1,0:T(8,128)(2,1)S(1)}, u32[]{:S(2)}) copy-start(bf16[16,4,48,768]{3,2,1,0:T(8,128)(2,1)S(1)} %copy.397) | copy-start | bytes 14155780
  182.4 28.1 %copy-start.182 = (f32[256]{0:T(256)}, f32[256]{0:T(256)S(1)}, u32[]{:S(2)}) copy-start(f32[256]{0:T(256)S(1)} %broadcast_multiply_fusion.16) | copy-start | bytes 3076
  182.6 27.9 %copy-start.218 = (f32[256]{0:T(256)}, f32[256]{0:T(256)S(1)}, u32[]{:S(2)}) copy-start(f32[256]{0:T(256)S(1)} %add_rsqrt_fusion.10) | copy-start | bytes 3076
  253.7 24.6 %copy-start.27 = (f32[256,768]{1,0:T(8,128)}, f32[256,768]{1,0:T(8,128)S(1)}, u32[]{:S(2)}) copy-start(f32[256,768]{1,0:T(8,128)S(1)} %get-tuple-element.206) | copy-start | bytes 2359300
  255.2 21.9 %collective-permute-start = (bf16[2,1,256,768]{3,2,1,0:T(8,128)(2,1)}, bf16[2,1,256,768]{3,2,1,0:T(8,128)(2,1)}, u32[]{:S(2)}, u32[]{:S(2)}) collective-permute-start(bf16[2,1,256,768]{3,2,1,0:T(8,128)(2,1)} %pad_maximum_fusion.12), channel_id=1, source_target_pairs={{0,16},{1,17},{2,18},{3,19},{4,20},{5,21},{6,22},{7,23},{8,24},{9,... | collective-permute-start | bytes 2359304 | tf_op jit(solution)/shard_map/ppermute | solution.py:17
  257.8 24.0 %copy-start.160 = (f32[1,1,256]{2,1,0:T(1,128)}, f32[1,1,256]{2,1,0:T(1,128)S(1)}, u32[]{:S(2)}) copy-start(f32[1,1,256]{2,1,0:T(1,128)S(1)} %get-tuple-element.198) | copy-start | bytes 3076
  257.8 24.0 %copy-start.162 = (f32[1,1,256]{2,1,0:T(1,128)}, f32[1,1,256]{2,1,0:T(1,128)S(1)}, u32[]{:S(2)}) copy-start(f32[1,1,256]{2,1,0:T(1,128)S(1)} %get-tuple-element.199) | copy-start | bytes 3076
  257.8 24.0 %copy-start.165 = (f32[1,1,256]{2,1,0:T(1,128)}, f32[1,1,256]{2,1,0:T(1,128)S(1)}, u32[]{:S(2)}) copy-start(f32[1,1,256]{2,1,0:T(1,128)S(1)} %get-tuple-element.200) | copy-start | bytes 3076
  286.6 27.8 %copy-start.41 = (bf16[256,768]{1,0:T(8,128)(2,1)}, bf16[256,768]{1,0:T(8,128)(2,1)S(1)}, u32[]{:S(2)}) copy-start(bf16[256,768]{1,0:T(8,128)(2,1)S(1)} %get-tuple-element.162) | copy-start | bytes 1179652
  286.6 28.7 %copy-start.40 = (bf16[256,768]{1,0:T(8,128)(2,1)}, bf16[256,768]{1,0:T(8,128)(2,1)S(1)}, u32[]{:S(2)}) copy-start(bf16[256,768]{1,0:T(8,128)(2,1)S(1)} %get-tuple-element.161) | copy-start | bytes 1179652
  333.7 21.7 %copy-start.11 = (f32[256,768]{1,0:T(8,128)}, f32[256,768]{1,0:T(8,128)S(1)}, u32[]{:S(2)}) copy-start(f32[256,768]{1,0:T(8,128)S(1)} %get-tuple-element.228) | copy-start | bytes 2359300
  333.8 21.5 %copy-start.29 = (bf16[1,2,256,768]{3,0,2,1:T(2,128)(2,1)S(1)}, bf16[1,2,256,768]{3,0,2,1:T(2,128)(2,1)}, u32[]{:S(2)}) copy-start(bf16[1,2,256,768]{3,0,2,1:T(2,128)(2,1)} %get-tuple-element.169) | copy-start | bytes 2359300
  333.8 21.6 %copy-start.186 = (f32[256]{0:T(256)}, f32[256]{0:T(256)S(1)}, u32[]{:S(2)}) copy-start(f32[256]{0:T(256)S(1)} %broadcast_multiply_fusion.12) | copy-start | bytes 3076
  334.0 21.4 %copy-start.225 = (f32[256]{0:T(256)}, f32[256]{0:T(256)S(1)}, u32[]{:S(2)}) copy-start(f32[256]{0:T(256)S(1)} %add_rsqrt_fusion.6) | copy-start | bytes 3076
  334.3 20.9 %collective-permute-start.1 = (bf16[2,1,256,768]{3,2,1,0:T(8,128)(2,1)S(1)}, bf16[2,1,256,768]{3,2,1,0:T(8,128)(2,1)S(1)}, u32[]{:S(2)}, u32[]{:S(2)}) collective-permute-start(bf16[2,1,256,768]{3,2,1,0:T(8,128)(2,1)S(1)} %pad_maximum_fusion.13), channel_id=1, source_target_pairs={{0,16},{1,17},{2,18},{3,19},{4,20},{5,21},{6,22},{7,23},{8,24},{9,... | collective-permute-start | bytes 2359304 | tf_op jit(solution)/shard_map/ppermute | solution.py:17
  384.6 27.3 %copy-start.2 = (f32[3,256,768]{2,1,0:T(8,128)}, f32[3,256,768]{2,1,0:T(8,128)S(1)}, u32[]{:S(2)}) copy-start(f32[3,256,768]{2,1,0:T(8,128)S(1)} %pad_maximum_fusion.3) | copy-start | bytes 7077892
  385.3 26.7 %copy-start.176 = (f32[256]{0:T(256)}, f32[256]{0:T(256)S(1)}, u32[]{:S(2)}) copy-start(f32[256]{0:T(256)S(1)} %broadcast_multiply_fusion.4) | copy-start | bytes 3076
  388.2 23.8 %copy-start.203 = (f32[256]{0:T(256)}, f32[256]{0:T(256)S(1)}, u32[]{:S(2)}) copy-start(f32[256]{0:T(256)S(1)} %fusion.523) | copy-start | bytes 3076
  388.2 18.5 %copy-start.198 = (f32[256]{0:T(256)}, f32[256]{0:T(256)S(1)}, u32[]{:S(2)}) copy-start(f32[256]{0:T(256)S(1)} %broadcast_multiply_fusion.2) | copy-start | bytes 3076
  389.8 16.8 %copy-start.60 = (f32[256,768]{1,0:T(8,128)}, f32[256,768]{1,0:T(8,128)S(1)}, u32[]{:S(2)}) copy-start(f32[256,768]{1,0:T(8,128)S(1)} %get-tuple-element.134) | copy-start | bytes 2359300
  389.9 16.8 %copy-start.227 = (f32[256]{0:T(256)}, f32[256]{0:T(256)S(1)}, u32[]{:S(2)}) copy-start(f32[256]{0:T(256)S(1)} %negate_multiply_fusion.14) | copy-start | bytes 3076
  439.7 70.8 %copy-start.36 = (bf16[12,64,256]{2,1,0:T(8,128)(2,1)}, bf16[12,64,256]{2,1,0:T(8,128)(2,1)S(1)}, u32[]{:S(2)}) copy-start(bf16[12,64,256]{2,1,0:T(8,128)(2,1)S(1)} %fusion.283) | copy-start | bytes 1179652
  481.0 26.9 %copy-start.266 = (f32[256]{0:T(256)S(1)}, f32[256]{0:T(256)}, u32[]{:S(2)}) copy-start(f32[256]{0:T(256)} %get-tuple-element.81) | copy-start | bytes 3076
  481.1 27.5 %copy-start.259 = (f32[256]{0:T(256)S(1)}, f32[256]{0:T(256)}, u32[]{:S(2)}) copy-start(f32[256]{0:T(256)} %get-tuple-element.83) | copy-start | bytes 3076
  481.1 28.1 %copy-start.237 = (f32[256]{0:T(256)S(1)}, f32[256]{0:T(256)}, u32[]{:S(2)}) copy-start(f32[256]{0:T(256)} %get-tuple-element.82) | copy-start | bytes 3076
  481.1 29.4 %copy-start.42 = (bf16[12,64,256]{2,1,0:T(8,128)(2,1)S(1)}, bf16[12,64,256]{2,1,0:T(8,128)(2,1)}, u32[]{:S(2)}) copy-start(bf16[12,64,256]{2,1,0:T(8,128)(2,1)} %fusion.274) | copy-start | bytes 1179652
  481.1 29.4 %copy-start.67 = (f32[256,768]{1,0:T(8,128)S(1)}, f32[256,768]{1,0:T(8,128)}, u32[]{:S(2)}) copy-start(f32[256,768]{1,0:T(8,128)} %copy-done.66) | copy-start | bytes 2359300
  481.1 29.4 %copy-start.82 = (bf16[12,64,256]{2,1,0:T(8,128)(2,1)S(1)}, bf16[12,64,256]{2,1,0:T(8,128)(2,1)}, u32[]{:S(2)}) copy-start(bf16[12,64,256]{2,1,0:T(8,128)(2,1)} %fusion.284) | copy-start | bytes 1179652
  481.1 29.4 %copy-start.270 = (f32[256]{0:T(256)S(1)}, f32[256]{0:T(256)}, u32[]{:S(2)}) copy-start(f32[256]{0:T(256)} %copy-done.269) | copy-start | bytes 3076
  515.4 40.7 %collective-permute-start.2 = (bf16[1,256,768]{2,1,0:T(8,128)(2,1)}, bf16[1,256,768]{2,1,0:T(8,128)(2,1)S(1)}, u32[]{:S(2)}, u32[]{:S(2)}) collective-permute-start(bf16[1,256,768]{2,1,0:T(8,128)(2,1)} %convert_bitcast_fusion.1), channel_id=1, source_target_pairs={{16,0},{17,1},{18,2},{19,3},{20,4},{21,5},{22,6},{23,7},{24,8},{25... | collective-permute-start | bytes 1179656 | tf_op jit(solution)/shard_map/ppermute | solution.py:17
  517.1 39.0 %copy-start.171 = (f32[256]{0:T(256)}, f32[256]{0:T(256)S(1)}, u32[]{:S(2)}) copy-start(f32[256]{0:T(256)S(1)} %broadcast_multiply_fusion.1) | copy-start | bytes 3076
  541.4 16.4 %slice-start.7 = ((s8[4718592]{0:T(1024)(128)(4,1)}), s8[524288]{0:T(1024)(128)(4,1)S(1)}, s32[]{:S(2)}) async-start(s8[4718592]{0:T(1024)(128)(4,1)} %bitcast.969), calls=%async_computation.9 | async-start | bytes 1048576
  601.3 19.3 %slice-start.9 = ((s8[4718592]{0:T(1024)(128)(4,1)}), s8[4194304]{0:T(1024)(128)(4,1)S(1)}, s32[]{:S(2)}) async-start(s8[4718592]{0:T(1024)(128)(4,1)} %bitcast.972), calls=%async_computation.11 | async-start | bytes 8388608
  606.4 32.3 %copy-start.230 = (f32[256]{0:T(256)}, f32[256]{0:T(256)S(1)}, u32[]{:S(2)}) copy-start(f32[256]{0:T(256)S(1)} %fusion.527) | copy-start | bytes 3076
  606.5 12.3 %collective-permute-start.3 = (bf16[1,256,768]{2,1,0:T(8,128)(2,1)S(1)}, bf16[1,256,768]{2,1,0:T(8,128)(2,1)S(1)}, u32[]{:S(2)}, u32[]{:S(2)}) collective-permute-start(bf16[1,256,768]{2,1,0:T(8,128)(2,1)S(1)} %convert_bitcast_fusion), channel_id=1, source_target_pairs={{16,0},{17,1},{18,2},{19,3},{20,4},{21,5},{22,6},{23,7},{24,8},{25... | collective-permute-start | bytes 1179656 | tf_op jit(solution)/shard_map/ppermute | solution.py:17
  694.3 54.1 %collective-permute-start.8 = (bf16[2,2,2,48,1664]{4,3,2,1,0:T(8,128)(2,1)}, bf16[2,2,2,48,1664]{4,3,2,1,0:T(8,128)(2,1)}, u32[]{:S(2)}, u32[]{:S(2)}) collective-permute-start(bf16[2,2,2,48,1664]{4,3,2,1,0:T(8,128)(2,1)} %dynamic-slice_bitcast_fusion), channel_id=1, source_target_pairs={{0,1},{1,0},{2,3},{3,2},{4,5},{5,4},{6,7},{7,6},{8,9},{9,8},{10,11... | collective-permute-start | bytes 3833864 | tf_op jit(solution)/shard_map/ppermute | solution.py:246
  697.9 39.1 %collective-permute-start.4 = (bf16[2,2,2,48,1536]{4,3,2,1,0:T(8,128)(2,1)}, bf16[2,2,2,48,1536]{4,3,2,1,0:T(8,128)(2,1)}, u32[]{:S(2)}, u32[]{:S(2)}) collective-permute-start(bf16[2,2,2,48,1536]{4,3,2,1,0:T(8,128)(2,1)} %fusion.293), channel_id=1, source_target_pairs={{0,1},{1,0},{2,3},{3,2},{4,5},{5,4},{6,7},{7,6},{8,9},{9,8},{10,11... | collective-permute-start | bytes 3538952 | tf_op jit(solution)/shard_map/ppermute | solution.py:246
  710.0 30.0 %collective-permute-start.16 = (bf16[2,2,2,48,1536]{4,3,0,1,2:T(8,128)(2,1)}, bf16[2,2,2,48,1536]{4,3,0,1,2:T(8,128)(2,1)}, u32[]{:S(2)}, u32[]{:S(2)}) collective-permute-start(bf16[2,2,2,48,1536]{4,3,0,1,2:T(8,128)(2,1)} %bitcast.934), channel_id=1, source_target_pairs={{0,1},{1,0},{2,3},{3,2},{4,5},{5,4},{6,7},{7,6},{8,9},{9,8},{10,11... | collective-permute-start | bytes 3538952 | tf_op jit(solution)/shard_map/ppermute | solution.py:246
  711.3 31.0 %collective-permute-start.12 = (bf16[2,2,2,48,1536]{4,3,2,1,0:T(8,128)(2,1)}, bf16[2,2,2,48,1536]{4,3,2,1,0:T(8,128)(2,1)}, u32[]{:S(2)}, u32[]{:S(2)}) collective-permute-start(bf16[2,2,2,48,1536]{4,3,2,1,0:T(8,128)(2,1)} %dynamic-slice_bitcast_fusion.1), channel_id=1, source_target_pairs={{0,1},{1,0},{2,3},{3,2},{4,5},{5,4},{6,7},{7,6},{8,9},{9,8},{10,11... | collective-permute-start | bytes 3538952 | tf_op jit(solution)/shard_map/ppermute | solution.py:246
  736.4 9.0 %collective-permute-start.24 = (bf16[2,2,2,48,1536]{4,3,0,1,2:T(8,128)(2,1)S(1)}, bf16[2,2,2,48,1536]{4,3,0,1,2:T(8,128)(2,1)S(1)}, u32[]{:S(2)}, u32[]{:S(2)}) collective-permute-start(bf16[2,2,2,48,1536]{4,3,0,1,2:T(8,128)(2,1)S(1)} %bitcast.1043), channel_id=1, source_target_pairs={{0,1},{1,0},{2,3},{3,2},{4,5},{5,4},{6,7},{7,6},{8,9},{9,8},{10,11... | collective-permute-start | bytes 3538952 | tf_op jit(solution)/shard_map/ppermute | solution.py:246
  737.0 9.5 %collective-permute-start.20 = (bf16[2,2,2,48,1536]{4,3,0,1,2:T(8,128)(2,1)S(1)}, bf16[2,2,2,48,1536]{4,3,0,1,2:T(8,128)(2,1)S(1)}, u32[]{:S(2)}, u32[]{:S(2)}) collective-permute-start(bf16[2,2,2,48,1536]{4,3,0,1,2:T(8,128)(2,1)S(1)} %bitcast.1042), channel_id=1, source_target_pairs={{0,1},{1,0},{2,3},{3,2},{4,5},{5,4},{6,7},{7,6},{8,9},{9,8},{10,11... | collective-permute-start | bytes 3538952 | tf_op jit(solution)/shard_map/ppermute | solution.py:246
  740.0 16.2 %collective-permute-start.5 = (bf16[2,2,48,1536]{3,2,1,0:T(8,128)(2,1)S(1)}, bf16[2,2,48,1536]{3,2,1,0:T(8,128)(2,1)S(1)}, u32[]{:S(2)}, u32[]{:S(2)}) collective-permute-start(bf16[2,2,48,1536]{3,2,1,0:T(8,128)(2,1)S(1)} %dynamic-slice_bitcast_fusion.7), channel_id=1, source_target_pairs={{0,2},{1,3},{2,0},{3,1},{4,6},{5,7},{6,4},{7,5},{8,10},{9,11},{10,... | collective-permute-start | bytes 1769480 | tf_op jit(solution)/shard_map/ppermute | solution.py:246
  742.3 26.5 %collective-permute-start.17 = (bf16[2,2,48,1536]{3,2,0,1:T(8,128)(2,1)S(1)}, bf16[2,2,48,1536]{3,2,0,1:T(8,128)(2,1)S(1)}, u32[]{:S(2)}, u32[]{:S(2)}) collective-permute-start(bf16[2,2,48,1536]{3,2,0,1:T(8,128)(2,1)S(1)} %dynamic-slice_bitcast_fusion.5), channel_id=1, source_target_pairs={{0,2},{1,3},{2,0},{3,1},{4,6},{5,7},{6,4},{7,5},{8,10},{9,11},{10,... | collective-permute-start | bytes 1769480 | tf_op jit(solution)/shard_map/ppermute | solution.py:246
  745.5 36.0 %collective-permute-start.13 = (bf16[2,2,48,1536]{3,2,1,0:T(8,128)(2,1)S(1)}, bf16[2,2,48,1536]{3,2,1,0:T(8,128)(2,1)S(1)}, u32[]{:S(2)}, u32[]{:S(2)}) collective-permute-start(bf16[2,2,48,1536]{3,2,1,0:T(8,128)(2,1)S(1)} %dynamic-slice_bitcast_fusion.6), channel_id=1, source_target_pairs={{0,2},{1,3},{2,0},{3,1},{4,6},{5,7},{6,4},{7,5},{8,10},{9,11},{10,... | collective-permute-start | bytes 1769480 | tf_op jit(solution)/shard_map/ppermute | solution.py:246
  746.5 47.6 %collective-permute-start.25 = (bf16[2,2,48,1536]{3,2,0,1:T(8,128)(2,1)S(1)}, bf16[2,2,48,1536]{3,2,0,1:T(8,128)(2,1)S(1)}, u32[]{:S(2)}, u32[]{:S(2)}) collective-permute-start(bf16[2,2,48,1536]{3,2,0,1:T(8,128)(2,1)S(1)} %dynamic-slice_bitcast_fusion.3), channel_id=1, source_target_pairs={{0,2},{1,3},{2,0},{3,1},{4,6},{5,7},{6,4},{7,5},{8,10},{9,11},{10,... | collective-permute-start | bytes 1769480 | tf_op jit(solution)/shard_map/ppermute | solution.py:246
  748.4 58.4 %collective-permute-start.21 = (bf16[2,2,48,1536]{3,2,0,1:T(8,128)(2,1)S(1)}, bf16[2,2,48,1536]{3,2,0,1:T(8,128)(2,1)S(1)}, u32[]{:S(2)}, u32[]{:S(2)}) collective-permute-start(bf16[2,2,48,1536]{3,2,0,1:T(8,128)(2,1)S(1)} %dynamic-slice_bitcast_fusion.4), channel_id=1, source_target_pairs={{0,2},{1,3},{2,0},{3,1},{4,6},{5,7},{6,4},{7,5},{8,10},{9,11},{10,... | collective-permute-start | bytes 1769480 | tf_op jit(solution)/shard_map/ppermute | solution.py:246
  756.2 63.6 %collective-permute-start.9 = (bf16[2,2,48,1664]{3,2,1,0:T(8,128)(2,1)S(1)}, bf16[2,2,48,1664]{3,2,1,0:T(8,128)(2,1)S(1)}, u32[]{:S(2)}, u32[]{:S(2)}) collective-permute-start(bf16[2,2,48,1664]{3,2,1,0:T(8,128)(2,1)S(1)} %dynamic-slice_bitcast_fusion.2), channel_id=1, source_target_pairs={{0,2},{1,3},{2,0},{3,1},{4,6},{5,7},{6,4},{7,5},{8,10},{9,11},{10,... | collective-permute-start | bytes 1916936 | tf_op jit(solution)/shard_map/ppermute | solution.py:246
  768.8 51.9 %collective-permute-start.6 = (bf16[2,48,1536]{2,1,0:T(8,128)(2,1)S(1)}, bf16[2,48,1536]{2,1,0:T(8,128)(2,1)S(1)}, u32[]{:S(2)}, u32[]{:S(2)}) collective-permute-start(bf16[2,48,1536]{2,1,0:T(8,128)(2,1)S(1)} %dynamic-slice_bitcast_fusion.13), channel_id=1, source_target_pairs={{0,4},{1,5},{2,6},{3,7},{4,0},{5,1},{6,2},{7,3},{8,12},{9,13},{10,... | collective-permute-start | bytes 884744 | tf_op jit(solution)/shard_map/ppermute | solution.py:246
  781.5 41.4 %collective-permute-start.18 = (bf16[2,48,1536]{2,1,0:T(8,128)(2,1)S(1)}, bf16[2,48,1536]{2,1,0:T(8,128)(2,1)S(1)}, u32[]{:S(2)}, u32[]{:S(2)}) collective-permute-start(bf16[2,48,1536]{2,1,0:T(8,128)(2,1)S(1)} %dynamic-slice_bitcast_fusion.11), channel_id=1, source_target_pairs={{0,4},{1,5},{2,6},{3,7},{4,0},{5,1},{6,2},{7,3},{8,12},{9,13},{10,... | collective-permute-start | bytes 884744 | tf_op jit(solution)/shard_map/ppermute | solution.py:246
  794.1 29.0 %collective-permute-start.14 = (bf16[2,48,1536]{2,1,0:T(8,128)(2,1)S(1)}, bf16[2,48,1536]{2,1,0:T(8,128)(2,1)S(1)}, u32[]{:S(2)}, u32[]{:S(2)}) collective-permute-start(bf16[2,48,1536]{2,1,0:T(8,128)(2,1)S(1)} %dynamic-slice_bitcast_fusion.12), channel_id=1, source_target_pairs={{0,4},{1,5},{2,6},{3,7},{4,0},{5,1},{6,2},{7,3},{8,12},{9,13},{10,... | collective-permute-start | bytes 884744 | tf_op jit(solution)/shard_map/ppermute | solution.py:246
  806.8 20.1 %collective-permute-start.26 = (bf16[2,48,1536]{2,1,0:T(8,128)(2,1)S(1)}, bf16[2,48,1536]{2,1,0:T(8,128)(2,1)S(1)}, u32[]{:S(2)}, u32[]{:S(2)}) collective-permute-start(bf16[2,48,1536]{2,1,0:T(8,128)(2,1)S(1)} %dynamic-slice_bitcast_fusion.9), channel_id=1, source_target_pairs={{0,4},{1,5},{2,6},{3,7},{4,0},{5,1},{6,2},{7,3},{8,12},{9,13},{10,... | collective-permute-start | bytes 884744 | tf_op jit(solution)/shard_map/ppermute | solution.py:246
  819.8 17.7 %collective-permute-start.22 = (bf16[2,48,1536]{2,1,0:T(8,128)(2,1)S(1)}, bf16[2,48,1536]{2,1,0:T(8,128)(2,1)S(1)}, u32[]{:S(2)}, u32[]{:S(2)}) collective-permute-start(bf16[2,48,1536]{2,1,0:T(8,128)(2,1)S(1)} %dynamic-slice_bitcast_fusion.10), channel_id=1, source_target_pairs={{0,4},{1,5},{2,6},{3,7},{4,0},{5,1},{6,2},{7,3},{8,12},{9,13},{10,... | collective-permute-start | bytes 884744 | tf_op jit(solution)/shard_map/ppermute | solution.py:246
  820.7 39.4 %collective-permute-start.10 = (bf16[2,48,1664]{2,1,0:T(8,128)(2,1)}, bf16[2,48,1664]{2,1,0:T(8,128)(2,1)}, u32[]{:S(2)}, u32[]{:S(2)}) collective-permute-start(bf16[2,48,1664]{2,1,0:T(8,128)(2,1)} %dynamic-slice_bitcast_fusion.8), channel_id=1, source_target_pairs={{0,4},{1,5},{2,6},{3,7},{4,0},{5,1},{6,2},{7,3},{8,12},{9,13},{10,... | collective-permute-start | bytes 958472 | tf_op jit(solution)/shard_map/ppermute | solution.py:246
  822.9 14.7 %collective-permute-start.7 = (bf16[48,1536]{1,0:T(8,128)(2,1)S(1)}, bf16[48,1536]{1,0:T(8,128)(2,1)S(1)}, u32[]{:S(2)}, u32[]{:S(2)}) collective-permute-start(bf16[48,1536]{1,0:T(8,128)(2,1)S(1)} %dynamic-slice_bitcast_fusion.19), channel_id=1, source_target_pairs={{0,8},{1,9},{2,10},{3,11},{4,12},{5,13},{6,14},{7,15},{8,0},{9,1},... | collective-permute-start | bytes 442376 | tf_op jit(solution)/shard_map/ppermute | solution.py:246
  823.1 26.1 %collective-permute-start.19 = (bf16[48,1536]{1,0:T(8,128)(2,1)S(1)}, bf16[48,1536]{1,0:T(8,128)(2,1)S(1)}, u32[]{:S(2)}, u32[]{:S(2)}) collective-permute-start(bf16[48,1536]{1,0:T(8,128)(2,1)S(1)} %dynamic-slice_bitcast_fusion.17), channel_id=1, source_target_pairs={{0,8},{1,9},{2,10},{3,11},{4,12},{5,13},{6,14},{7,15},{8,0},{9,1},... | collective-permute-start | bytes 442376 | tf_op jit(solution)/shard_map/ppermute | solution.py:246
  826.8 31.5 %collective-permute-start.15 = (bf16[48,1536]{1,0:T(8,128)(2,1)}, bf16[48,1536]{1,0:T(8,128)(2,1)}, u32[]{:S(2)}, u32[]{:S(2)}) collective-permute-start(bf16[48,1536]{1,0:T(8,128)(2,1)} %dynamic-slice_bitcast_fusion.18), channel_id=1, source_target_pairs={{0,8},{1,9},{2,10},{3,11},{4,12},{5,13},{6,14},{7,15},{8,0},{9,1},... | collective-permute-start | bytes 442376 | tf_op jit(solution)/shard_map/ppermute | solution.py:246
  837.5 17.9 %collective-permute-start.27 = (bf16[48,1536]{1,0:T(8,128)(2,1)S(1)}, bf16[48,1536]{1,0:T(8,128)(2,1)S(1)}, u32[]{:S(2)}, u32[]{:S(2)}) collective-permute-start(bf16[48,1536]{1,0:T(8,128)(2,1)S(1)} %dynamic-slice_bitcast_fusion.15), channel_id=1, source_target_pairs={{0,8},{1,9},{2,10},{3,11},{4,12},{5,13},{6,14},{7,15},{8,0},{9,1},... | collective-permute-start | bytes 442376 | tf_op jit(solution)/shard_map/ppermute | solution.py:246
  837.6 19.4 %collective-permute-start.23 = (bf16[48,1536]{1,0:T(8,128)(2,1)S(1)}, bf16[48,1536]{1,0:T(8,128)(2,1)S(1)}, u32[]{:S(2)}, u32[]{:S(2)}) collective-permute-start(bf16[48,1536]{1,0:T(8,128)(2,1)S(1)} %dynamic-slice_bitcast_fusion.16), channel_id=1, source_target_pairs={{0,8},{1,9},{2,10},{3,11},{4,12},{5,13},{6,14},{7,15},{8,0},{9,1},... | collective-permute-start | bytes 442376 | tf_op jit(solution)/shard_map/ppermute | solution.py:246
  861.2 8.9 %collective-permute-start.11 = (bf16[48,1664]{1,0:T(8,128)(2,1)S(1)}, bf16[48,1664]{1,0:T(8,128)(2,1)S(1)}, u32[]{:S(2)}, u32[]{:S(2)}) collective-permute-start(bf16[48,1664]{1,0:T(8,128)(2,1)S(1)} %dynamic-slice_bitcast_fusion.14), channel_id=1, source_target_pairs={{0,8},{1,9},{2,10},{3,11},{4,12},{5,13},{6,14},{7,15},{8,0},{9,1},... | collective-permute-start | bytes 479240 | tf_op jit(solution)/shard_map/ppermute | solution.py:246
  (266 other events, 1339.0 us)
Sparse Core Ops, SparseCore 0:
  15.0 95.5 all-gather.3
  112.7 89.8 all-gather.5

commit v2 on v0

v2 whole, which is shorter than its diff:
```python
import functools

import jax
import jax.numpy as jnp
from jax import lax
from jax.experimental import pallas as pl
from jax.experimental.pallas import tpu as pltpu
from jax.sharding import PartitionSpec as P

HD = 64
BLOCK = 48
STRIP = 32
VMEM_LIMIT = 56 * 1024 * 1024

epsilon = 1e-12
SCALE = HD ** (-0.5)

ANY = pl.BlockSpec(memory_space=pl.ANY)
VMEM = pl.BlockSpec(memory_space=pltpu.VMEM)
SMEM = pl.BlockSpec(memory_space=pltpu.SMEM)


def dot_nn(a, b):
    return jnp.dot(a, b, preferred_element_type=jnp.float32)


def dot_nt(a, b):
    return lax.dot_general(a, b, (((1,), (1,)), ((), ())), preferred_element_type=jnp.float32)


def dot_tn(a, b):
    return lax.dot_general(a, b, (((0,), (0,)), ((), ())), preferred_element_type=jnp.float32)


def gelu_parts(values):
    size = jnp.abs(values)
    inverse = 1.0 / (1.0 + (0.3275911 * 0.5**0.5) * size)
    series = 0.5 * 1.061405429
    for factor in (-1.453152027, 1.421413741, -0.284496736, 0.254829592):
        series = series * inverse + 0.5 * factor
    bell = jnp.exp(-0.5 * (values * values))
    tail = series * inverse * bell
    phi = jnp.where(values >= 0, 1.0 - tail, tail)
    return values * phi, phi + values * bell * 0.3989422804014327


def each_strip(rows, body, carry=None):
    def step(i, held):
        return body(pl.ds(pl.multiple_of(i * STRIP, STRIP), STRIP), held)

    return lax.fori_loop(0, rows // STRIP, step, carry)


def by_eights(values):
    return jnp.sum(values.reshape(-1, 8, values.shape[-1]), axis=0)


def normalised(values):
    centred = values - jnp.mean(values, axis=-1, keepdims=True)
    variance = jnp.mean(centred * centred, axis=-1, keepdims=True)
    scale = lax.rsqrt(variance + epsilon)
    return centred * scale, scale


def weight_copies(layout, packs, buffers, sems):
    copies = {}
    for at, (name, pack, source, width, target) in enumerate(layout):
        block = packs[pack].at[:, :, pl.ds(source, width)]
        if name == "contract":
            place = buffers[name].at[:, target]
        else:
            place = buffers[name].at[:, :, pl.ds(target, width)]
        copies.setdefault(name, []).append(pltpu.make_async_copy(block, place, sems.at[at]))
    return copies


def flat(block):
    return block.reshape(-1, block.shape[-1])


def forward_kernel(layout, pack_count, crops, saved_count, kept_count, *refs):
    flag, vrow, vcol, lines, offs, x_hbm = refs[:6]
    packs = refs[6 : 6 + pack_count]
    refs = refs[6 + pack_count + kept_count :]
    y_out, pooled_out = refs[:2]
    saved = refs[2 : 2 + saved_count]
    (
        x_buf, w_proj, w_out, w_expand, w_contract, mix, probs, att, low, hat1, hat2,
        rstd1, rstd2, act, slope, wide, hidden, w_sems, io_sems,
    ) = refs[2 + saved_count :]
    rows, features = x_buf.shape
    buffers = {"proj": w_proj, "out": w_out, "expand": w_expand, "contract": w_contract}

    @pl.when(flag[0] == 1)
    def _():
        copies = weight_copies(layout, packs, buffers, w_sems)
        for name in ("proj", "out", "expand", "contract"):
            for copy in copies[name]:
                copy.start()

        def arrive(name):
            for copy in copies[name]:
                copy.wait()

        for crop in range(crops):
            fetch = pltpu.make_async_copy(x_hbm.at[crop], x_buf, io_sems.at[0])
            fetch.start()
            fetch.wait()
            if crop == 0:
                arrive("proj")
            for third in range(3):
                columns = pl.ds(third * features, features)
                part = dot_nn(x_buf[...], flat(w_proj[:, :, columns]))
                if third != 1:
                    part = part + lines[2 + third // 2 : 3 + third // 2, :]
                mix[:, columns] = part.astype(jnp.bfloat16)
            head_low = lax.broadcasted_iota(jnp.int32, (rows, 2 * HD), 1) < HD
            valid = jnp.broadcast_to(vrow[crop] > 0, (rows, rows))

            def pair_step(pair, _):
                at = pl.multiple_of(pair * 2 * HD, 2 * HD)
                q = mix[:, pl.ds(at, 2 * HD)]
                k = mix[:, pl.ds(at + features, 2 * HD)]
                v = mix[:, pl.ds(at + 2 * features, 2 * HD)]
                outs = []
                for side in range(2):
                    lanes = head_low if side == 0 else jnp.logical_not(head_low)
                    own = jnp.where(lanes, q.astype(jnp.float32) * SCALE, 0.0).astype(jnp.bfloat16)
                    scores = jnp.where(valid, dot_nt(own, k), -1e30)
                    top = jnp.max(scores, axis=-1, keepdims=True)
                    weights = jnp.exp(scores - top)
                    total = jnp.sum(weights, axis=-1, keepdims=True)
                    weights = (weights * (1.0 / total)).astype(jnp.bfloat16)
                    if saved_count:
                        probs[2 * pair + side] = weights
                    outs.append(dot_nn(weights, v))
                att[:, pl.ds(at, 2 * HD)] = jnp.where(head_low, outs[0], outs[1]).astype(jnp.bfloat16)

            lax.fori_loop(0, features // (2 * HD), pair_step, None)
            sends = []

            def keep(index, source):
                if saved_count:
                    copy = pltpu.make_async_copy(source, saved[index], io_sems.at[1 + index])
                    copy.start()
                    sends.append(copy)

            keep(0, mix)
            keep(1, probs)
            keep(2, att)
            if crop == 0:
                arrive("out")
            wide[...] = dot_nn(att[...], flat(w_out[...]))

            def first_norm(at, _):
                total = x_buf[at, :].astype(jnp.float32) + wide[at, :] + lines[4:5, :]
                hat, scale = normalised(total)
                value = hat * lines[0:1, :] + lines[5:6, :]
                hidden[at, :] = value
                low[at, :] = value.astype(jnp.bfloat16)
                if saved_count:
                    hat1[at, :] = hat.astype(jnp.bfloat16)
                    rstd1[at, :] = jnp.broadcast_to(scale, (STRIP, 128))

            each_strip(rows, first_norm)
            keep(3, low)
            keep(4, hat1)
            keep(5, rstd1)
            if crop == 0:
                arrive("expand")
            groups = w_expand.shape[2] // features
            ahead = None
            for group in range(groups):
                columns = pl.ds(group * features, features)
                wide[...] = dot_nn(low[...], flat(w_expand[:, :, columns]))

                def activate(at, _):
                    value, gradient = gelu_parts(wide[at, :] + offs[:, columns])
                    act[at, columns] = value.astype(jnp.bfloat16)
                    if saved_count:
                        slope[at, columns] = gradient.astype(jnp.bfloat16)

                each_strip(rows, activate)
                if crop == 0 and group == 0:
                    arrive("contract")
                stack = w_contract.shape[0] // groups
                hidden[...] += dot_nn(
                    act[:, columns], flat(w_contract[group * stack : (group + 1) * stack])
                )
            keep(6, act)
            keep(7, slope)

            def second_norm(at, held):
                hat, scale = normalised(hidden[at, :] + lines[6:7, :])
                value = hat * lines[1:2, :] + lines[7:8, :]
                y_out[crop, at, :] = value.astype(jnp.bfloat16)
                if saved_count:
                    hat2[at, :] = hat.astype(jnp.bfloat16)
                    rstd2[at, :] = jnp.broadcast_to(scale, (STRIP, 128))
                return held + by_eights(value * vcol[crop, at, :])

            total = each_strip(rows, second_norm, jnp.zeros((8, features), jnp.float32))
            count = jnp.sum(vrow[crop], axis=-1, keepdims=True)
            pooled_out[crop] = jnp.sum(total, axis=0, keepdims=True) / count
            keep(8, hat2)
            keep(9, rstd2)
            for copy in sends:
                copy.wait()


def forward_block(flag, x, vrow, vcol, lines, offs, packs, layout, save, kept=()):
    crops, rows, features = x.shape
    hidden_size = offs.shape[-1]
    heads = features // HD
    blocks = features // BLOCK
    bf16, f32 = jnp.bfloat16, jnp.float32
    shapes = []
    if save:
        shapes = [
            ((rows, 3 * features), bf16),
            ((heads, rows, rows), bf16),
            ((rows, features), bf16),
            ((rows, features), bf16),
            ((rows, features), bf16),
            ((rows, 128), f32),
            ((rows, hidden_size), bf16),
            ((rows, hidden_size), bf16),
            ((rows, features), bf16),
            ((rows, 128), f32),
        ]
    kept = tuple(kept)
    out_shape = [
        jax.ShapeDtypeStruct((crops, rows, features), bf16),
        jax.ShapeDtypeStruct((crops, 1, features), f32),
    ] + [jax.ShapeDtypeStruct(*shape) for shape in shapes]
    flops = 2 * crops * rows * (4 * features * features + 2 * features * hidden_size)
    first_kept = 6 + len(packs)
    result = pl.pallas_call(
        functools.partial(forward_kernel, layout, len(packs), crops, len(shapes), len(kept)),
        out_shape=out_shape,
        in_specs=[SMEM] + [VMEM] * 4 + [ANY] * (1 + len(packs) + len(kept)),
        out_specs=[VMEM, VMEM] + [ANY] * len(shapes),
        scratch_shapes=[
            pltpu.VMEM((rows, features), bf16),
            pltpu.VMEM((blocks, BLOCK, 3 * features), bf16),
            pltpu.VMEM((blocks, BLOCK, features), bf16),
            pltpu.VMEM((blocks, BLOCK, hidden_size), bf16),
            pltpu.VMEM((blocks, hidden_size // features, BLOCK, features), bf16),
            pltpu.VMEM((rows, 3 * features), bf16),
            pltpu.VMEM((heads, rows, rows) if save else (8, 128), bf16),
            pltpu.VMEM((rows, features), bf16),
            pltpu.VMEM((rows, features), bf16),
            pltpu.VMEM((rows, features), bf16),
            pltpu.VMEM((rows, features), bf16),
            pltpu.VMEM((rows, 128), f32),
            pltpu.VMEM((rows, 128), f32),
            pltpu.VMEM((rows, hidden_size), bf16),
            pltpu.VMEM((rows, hidden_size) if save else (8, 128), bf16),
            pltpu.VMEM((rows, features), f32),
            pltpu.VMEM((rows, features), f32),
            pltpu.SemaphoreType.DMA((len(layout),)),
            pltpu.SemaphoreType.DMA((11,)),
        ],
        input_output_aliases={first_kept + i: 2 + i for i in range(len(kept))},
        compiler_params=pltpu.CompilerParams(vmem_limit_bytes=VMEM_LIMIT),
        cost_estimate=pl.CostEstimate(flops=flops, bytes_accessed=20_000_000, transcendentals=0),
        name="forward_save" if save else "forward_only",
    )(flag, vrow, vcol, lines, offs, x, *packs, *kept)
    return result[0], result[1], tuple(result[2:])


def backward_kernel(layout, pack_count, kept_count, *refs):
    flag, vcol, lines, g_hbm = refs[:4]
    packs = refs[4 : 4 + pack_count]
    saved = refs[4 + pack_count : 14 + pack_count]
    refs = refs[14 + pack_count + kept_count :]
    vec_out, offs_out, dx_low = refs[:3]
    dx_out, branch_out, upward_out, output_out, mixture_out = refs[3:8]
    (
        g_buf, w_proj, w_out, w_expand, w_contract, mix, probs, hat1, hat2, rstd1, rstd2, slope,
        dbranch, dupward, doutput, datt, dmix, wide, total, w_sems, in_sems, out_sems,
    ) = refs[8:]
    rows, features = g_buf.shape
    groups = w_expand.shape[2] // features
    buffers = {"proj": w_proj, "out": w_out, "expand": w_expand, "contract": w_contract}

    @pl.when(flag[0] == 1)
    def _():
        copies = weight_copies(layout, packs, buffers, w_sems)
        fetches = {}
        for at, (name, source, place) in enumerate(
            (
                ("g", g_hbm, g_buf),
                ("hat2", saved[8], hat2),
                ("rstd2", saved[9], rstd2),
                ("slope", saved[7], slope),
                ("hat1", saved[4], hat1),
                ("rstd1", saved[5], rstd1),
                ("mix", saved[0], mix),
                ("probs", saved[1], probs),
            )
        ):
            fetches[name] = [pltpu.make_async_copy(source, place, in_sems.at[at])]
        fetches.update(copies)
        for name in (
            "g", "hat2", "rstd2", "contract", "slope", "expand", "hat1", "rstd1", "out", "mix",
            "probs", "proj",
        ):
            for copy in fetches[name]:
                copy.start()

        def arrive(*names):
            for name in names:
                for copy in fetches[name]:
                    copy.wait()

        sends = []

        def send(index, source, place):
            copy = pltpu.make_async_copy(source, place, out_sems.at[index])
            copy.start()
            sends.append(copy)

        zero = jnp.zeros((8, features), jnp.float32)

        def norm_back(gradient, hat, scale, gain):
            weighted = gradient * gain
            mean = jnp.mean(weighted, axis=-1, keepdims=True)
            slant = jnp.mean(weighted * hat, axis=-1, keepdims=True)
            return scale * (weighted - mean - hat * slant)

        arrive("g", "hat2", "rstd2")

        def second_norm(at, held):
            gradient = g_buf[at, :].astype(jnp.float32) * vcol[at, :]
            hat = hat2[at, :].astype(jnp.float32)
            moved = norm_back(gradient, hat, rstd2[at, 0:1], lines[1:2, :])
            total[at, :] = moved
            rounded = moved.astype(jnp.bfloat16)
            dbranch[at, :] = rounded
            return (
                held[0] + by_eights(gradient * hat),
                held[1] + by_eights(gradient),
                held[2] + by_eights(rounded.astype(jnp.float32)),
            )

        sums = each_strip(rows, second_norm, (zero, zero, zero))
        for line, partial in zip((1, 7, 6), sums):
            vec_out[line : line + 1, :] = jnp.sum(partial, axis=0, keepdims=True)
        send(0, dbranch, branch_out)
        arrive("contract", "slope")
        stack = w_contract.shape[0] // groups
        for group in range(groups):
            columns = pl.ds(group * features, features)
            wide[...] = dot_nt(
                dbranch[...], flat(w_contract[group * stack : (group + 1) * stack])
            )

            def through(at, held):
                rounded = (wide[at, :] * slope[at, columns].astype(jnp.float32)).astype(jnp.bfloat16)
                dupward[at, columns] = rounded
                return held + by_eights(rounded.astype(jnp.float32))

            partial = each_strip(rows, through, zero)
            offs_out[:, columns] = jnp.sum(partial, axis=0, keepdims=True)
            if group == 0:
                arrive("expand")
            total[...] += dot_nt(dupward[:, columns], flat(w_expand[:, :, columns]))
        send(1, dupward, upward_out)
        arrive("hat1", "rstd1")

        def first_norm(at, held):
            gradient = total[at, :]
            hat = hat1[at, :].astype(jnp.float32)
            moved = norm_back(gradient, hat, rstd1[at, 0:1], lines[0:1, :])
            total[at, :] = moved
            rounded = moved.astype(jnp.bfloat16)
            doutput[at, :] = rounded
            return (
                held[0] + by_eights(gradient * hat),
                held[1] + by_eights(gradient),
                held[2] + by_eights(rounded.astype(jnp.float32)),
            )

        sums = each_strip(rows, first_norm, (zero, zero, zero))
        for line, partial in zip((0, 5, 4), sums):
            vec_out[line : line + 1, :] = jnp.sum(partial, axis=0, keepdims=True)
        send(2, doutput, output_out)
        arrive("out")
        datt[...] = dot_nt(doutput[...], flat(w_out[...])).astype(jnp.bfloat16)
        arrive("mix", "probs")
        head_low = lax.broadcasted_iota(jnp.int32, (rows, 2 * HD), 1) < HD

        def pair_step(pair, _):
            at = pl.multiple_of(pair * 2 * HD, 2 * HD)
            q = mix[:, pl.ds(at, 2 * HD)]
            k = mix[:, pl.ds(at + features, 2 * HD)]
            v = mix[:, pl.ds(at + 2 * features, 2 * HD)]
            pull = datt[:, pl.ds(at, 2 * HD)]
            parts = []
            for side in range(2):
                lanes = head_low if side == 0 else jnp.logical_not(head_low)
                own = jnp.where(lanes, pull, jnp.zeros_like(pull))
                weights = probs[2 * pair + side]
                dweights = dot_nt(own, v)
                wide_weights = weights.astype(jnp.float32)
                product = dweights * wide_weights
                inner = jnp.sum(product, axis=-1, keepdims=True)
                dscores = (product - wide_weights * inner).astype(jnp.bfloat16)
                parts.append((dot_nn(dscores, k), dot_tn(dscores, q), dot_tn(weights, pull)))
            for place, (first, second) in enumerate(zip(*parts)):
                merged = jnp.where(head_low, first, second)
                if place < 2:
                    merged = merged * SCALE
                dmix[:, pl.ds(at + place * features, 2 * HD)] = merged.astype(jnp.bfloat16)

        lax.fori_loop(0, features // (2 * HD), pair_step, None)
        send(3, dmix, mixture_out)

        def mixture_sums(at, held):
            return (
                held[0] + by_eights(dmix[at, 0:features].astype(jnp.float32)),
                held[1] + by_eights(dmix[at, 2 * features : 3 * features].astype(jnp.float32)),
            )

        sums = each_strip(rows, mixture_sums, (zero, zero))
        for line, partial in zip((2, 3), sums):
            vec_out[line : line + 1, :] = jnp.sum(partial, axis=0, keepdims=True)
        arrive("proj")
        for third in range(3):
            columns = pl.ds(third * features, features)
            total[...] += dot_nt(dmix[:, columns], flat(w_proj[:, :, columns]))
        dx_low[...] = total[...].astype(jnp.bfloat16)
        send(4, total, dx_out)
        for copy in sends:
            copy.wait()


def backward_block(flag, gradient, vcol, lines, packs, layout, saved, kept=()):
    rows, features = gradient.shape
    hidden_size = saved[6].shape[-1]
    heads = features // HD
    blocks = features // BLOCK
    bf16, f32 = jnp.bfloat16, jnp.float32
    kept = tuple(kept)
    out_shape = [
        jax.ShapeDtypeStruct((8, features), f32),
        jax.ShapeDtypeStruct((1, hidden_size), f32),
        jax.ShapeDtypeStruct((rows, features), bf16),
        jax.ShapeDtypeStruct((rows, features), f32),
        jax.ShapeDtypeStruct((rows, features), bf16),
        jax.ShapeDtypeStruct((rows, hidden_size), bf16),
        jax.ShapeDtypeStruct((rows, features), bf16),
        jax.ShapeDtypeStruct((rows, 3 * features), bf16),
    ]
    flops = 2 * rows * (4 * features * features + 2 * features * hidden_size)
    first_kept = 4 + len(packs) + 10
    result = pl.pallas_call(
        functools.partial(backward_kernel, layout, len(packs), len(kept)),
        out_shape=out_shape,
        in_specs=[SMEM] + [VMEM] * 2 + [ANY] * (1 + len(packs) + 10 + len(kept)),
        out_specs=[VMEM] * 3 + [ANY] * 5,
        scratch_shapes=[
            pltpu.VMEM((rows, features), bf16),
            pltpu.VMEM((blocks, BLOCK, 3 * features), bf16),
            pltpu.VMEM((blocks, BLOCK, features), bf16),
            pltpu.VMEM((blocks, BLOCK, hidden_size), bf16),
            pltpu.VMEM((blocks, hidden_size // features, BLOCK, features), bf16),
            pltpu.VMEM((rows, 3 * features), bf16),
            pltpu.VMEM((heads, rows, rows), bf16),
            pltpu.VMEM((rows, features), bf16),
            pltpu.VMEM((rows, features), bf16),
            pltpu.VMEM((rows, 128), f32),
            pltpu.VMEM((rows, 128), f32),
            pltpu.VMEM((rows, hidden_size), bf16),
            pltpu.VMEM((rows, features), bf16),
            pltpu.VMEM((rows, hidden_size), bf16),
            pltpu.VMEM((rows, features), bf16),
            pltpu.VMEM((rows, features), bf16),
            pltpu.VMEM((rows, 3 * features), bf16),
            pltpu.VMEM((rows, features), f32),
            pltpu.VMEM((rows, features), f32),
            pltpu.SemaphoreType.DMA((len(layout),)),
            pltpu.SemaphoreType.DMA((8,)),
            pltpu.SemaphoreType.DMA((5,)),
        ],
        input_output_aliases={first_kept + i: 3 + i for i in range(len(kept))},
        compiler_params=pltpu.CompilerParams(vmem_limit_bytes=VMEM_LIMIT),
        cost_estimate=pl.CostEstimate(flops=flops, bytes_accessed=25_000_000, transcendentals=0),
        name="backward_data",
    )(flag, vcol, lines, gradient, *packs, *saved, *kept)
    return result[:3], tuple(result[3:])


def contract_kernel(core, act0, act1, grad0, grad1, *refs):
    outs, (piece,) = refs[:4], refs[4:]
    features = grad0.shape[1]
    groups = act0.shape[1] // features
    span = outs[0].shape[2] // features
    stack = 2 * outs[0].shape[0] // groups
    for part in range(groups):
        columns = pl.ds(part * features, features)
        piece[...] = (
            dot_tn(act0[:, columns], grad0[...]) + dot_tn(act1[:, columns], grad1[...])
        ).astype(jnp.bfloat16)
        for block in range(stack):
            place = (part * stack + block) // 2
            for group in range(groups):
                rows = pl.ds((block * groups + group) * BLOCK, BLOCK)
                at = pl.ds((group % span) * features, features)
                keep, send = outs[2 * (group // span)], outs[2 * (group // span) + 1]

                @pl.when(core[0] == block % 2)
                def _():
                    keep[place, :, at] = piece[rows, :]

                @pl.when(core[0] != block % 2)
                def _():
                    send[place, :, at] = piece[rows, :]


def row_kernel(plan, core, *refs):
    count = len({source for entry in plan for source in entry[:2]})
    sources, outs, (piece,) = refs[: 2 * count], refs[2 * count : -1], refs[-1:]
    features = piece.shape[0]
    width = piece.shape[1]
    for left, right, column, target, to in plan:
        columns = pl.ds(column, width)
        piece[...] = (
            dot_tn(sources[2 * left][...], sources[2 * right][:, columns])
            + dot_tn(sources[2 * left + 1][...], sources[2 * right + 1][:, columns])
        ).astype(jnp.bfloat16)
        keep, send = outs[2 * target], outs[2 * target + 1]
        for block in range(features // BLOCK):
            rows = pl.ds(block * BLOCK, BLOCK)

            @pl.when(core[0] == block % 2)
            def _():
                keep[block // 2, :, pl.ds(to, width)] = piece[rows, :]

            @pl.when(core[0] != block % 2)
            def _():
                send[block // 2, :, pl.ds(to, width)] = piece[rows, :]


def weight_gradient(kernel, core, operands, targets, features, width, name):
    blocks = features // BLOCK // 2
    shape = jax.ShapeDtypeStruct((blocks, BLOCK, 2 * features), jnp.bfloat16)
    return pl.pallas_call(
        kernel,
        out_shape=[shape] * (2 * targets),
        in_specs=[SMEM] + [VMEM] * len(operands),
        out_specs=[VMEM] * (2 * targets),
        scratch_shapes=[pltpu.VMEM((features, width), jnp.bfloat16)],
        compiler_params=pltpu.CompilerParams(vmem_limit_bytes=VMEM_LIMIT),
        cost_estimate=pl.CostEstimate(
            flops=4 * targets * features * features * 512, bytes_accessed=9_000_000, transcendentals=0
        ),
        name=name,
    )(core, *operands)


def pack_vectors(norm_gains, biases, offsets, rows):
    vectors = jnp.concatenate([norm_gains, biases, offsets.reshape(-1, rows)], axis=0)
    return jnp.pad(vectors, ((0, 128 - vectors.shape[0]), (0, 0))).T


def fold_rows(matrix, rows):
    folded = matrix.reshape(-1, rows, matrix.shape[-1])
    return jnp.moveaxis(folded, 0, 1).reshape(rows, -1)


def refold(columns, shards_of, features):
    rows = features // shards_of
    if rows == BLOCK:
        return columns
    natural = jnp.moveaxis(columns.reshape(shards_of, rows, -1, features), 2, 1)
    natural = natural.reshape(features // BLOCK, -1, BLOCK, features)
    return jnp.moveaxis(natural, 1, 2).reshape(features, -1)


def unfold(blocks, shards_of, features):
    rows = features // shards_of
    if rows == BLOCK:
        return blocks
    natural = jnp.moveaxis(blocks.reshape(features // BLOCK, BLOCK, -1, features), 2, 1)
    natural = natural.reshape(shards_of, -1, rows, features)
    return jnp.moveaxis(natural, 1, 2).reshape(shards_of, rows, -1)


def vector_rows(columns, shards_of):
    features = columns.shape[0]
    lines = columns[:, :8].astype(jnp.float32).T
    offsets = columns[:, 8:12].astype(jnp.float32).reshape(shards_of, features // shards_of, -1)
    return lines, jnp.moveaxis(offsets, 2, 1).reshape(1, -1)


def swapped(block, level):
    route = [(i, i ^ (1 << level)) for i in range(lax.axis_size("dp"))]
    return lax.ppermute(block, "dp", route)


def added(first, second):
    return (first.astype(jnp.float32) + second.astype(jnp.float32)).astype(jnp.bfloat16)


def halving_sum(current, first_level, levels):
    here = lax.axis_index("dp")
    current = current.reshape((2,) * (levels - first_level) + current.shape[1:])
    for level in range(first_level, levels):
        axis = levels - 1 - level
        mine = (here >> level) & 1
        send = lax.dynamic_index_in_dim(current, 1 - mine, axis, keepdims=False)
        keep = lax.dynamic_index_in_dim(current, mine, axis, keepdims=False)
        current = added(keep, swapped(send, level))
    return current


def scattered(keep, send, shards_of, features, contracted):
    levels = shards_of.bit_length() - 1
    if features == BLOCK * shards_of:
        return halving_sum(added(keep, swapped(send, 0)), 1, levels)
    blocks = jnp.stack([keep, send], axis=1).reshape(-1, BLOCK, keep.shape[-1])
    if contracted:
        blocks = unfold(blocks, shards_of, features)
    else:
        blocks = blocks.reshape(shards_of, features // shards_of, -1)
    return halving_sum(blocks, 0, levels)


def doubled(block):
    here = lax.axis_index("dp")
    for level in range(lax.axis_size("dp").bit_length() - 1):
        other = swapped(block, level)
        upper = ((here >> level) & 1) == 1
        block = jnp.concatenate(
            [jnp.where(upper, other, block), jnp.where(upper, block, other)], axis=0
        )
    return block


def shards(
    inputs,
    keep_mask,
    lengths,
    slot_order,
    cotangent,
    query_projection,
    query_output,
    query_expand,
    query_contract,
    query_gains,
    query_biases,
    query_offsets,
    momentum_projection,
    momentum_output,
    momentum_expand,
    momentum_contract,
    momentum_gains,
    momentum_biases,
    momentum_offsets,
):
    first_section = lax.axis_index("section") == 0
    shards_of = lax.axis_size("dp")
    crop_count, crop_len, features = inputs.shape[1:]
    rows = features // shards_of
    hidden_size = query_expand.shape[2]
    groups = hidden_size // features
    blocks = features // BLOCK

    own = jnp.concatenate(
        [
            query_projection[0],
            query_output[0],
            query_expand[0],
            fold_rows(query_contract[0], rows),
            pack_vectors(query_gains[0], query_biases[0], query_offsets[0], rows),
            pack_vectors(momentum_gains[0], momentum_biases[0], momentum_offsets[0], rows),
            momentum_output[0],
            momentum_projection[0, :, features : 2 * features],
        ],
        axis=1,
    )
    gathered = lax.all_gather(own, "dp", axis=0, tiled=True)
    rest = jnp.concatenate(
        [
            momentum_projection[0, :, :features],
            momentum_projection[0, :, 2 * features :],
            momentum_expand[0],
            fold_rows(momentum_contract[0], rows),
        ],
        axis=1,
    )
    rest, gathered = lax.optimization_barrier((rest, gathered))
    late = lax.all_gather(rest, "dp", axis=0, tiled=True)

    inner = 4 * features + hidden_size
    vectors_at = inner + groups * features
    query_lines, query_offs = vector_rows(gathered[:, vectors_at : vectors_at + 128], shards_of)
    momentum_lines, momentum_offs = vector_rows(
        gathered[:, vectors_at + 128 : vectors_at + 256], shards_of
    )
    if rows != BLOCK:
        gathered = jnp.concatenate(
            [
                gathered[:, :inner],
                refold(gathered[:, inner:vectors_at], shards_of, features),
                gathered[:, vectors_at:],
            ],
            axis=1,
        )
        split = 2 * features + hidden_size
        late = jnp.concatenate(
            [late[:, :split], refold(late[:, split:], shards_of, features)], axis=1
        )
    gathered = gathered.reshape(blocks, BLOCK, -1)
    late = late.reshape(blocks, BLOCK, -1)
    query_layout = (
        ("proj", 0, 0, 3 * features, 0),
        ("out", 0, 3 * features, features, 0),
        ("expand", 0, 4 * features, hidden_size, 0),
    ) + tuple(("contract", 0, inner + i * features, features, i) for i in range(groups))
    early_at = vectors_at + 256
    momentum_layout = (
        ("proj", 0, early_at + features, features, features),
        ("proj", 1, 0, features, 0),
        ("proj", 1, features, features, 2 * features),
        ("out", 0, early_at, features, 0),
        ("expand", 1, 2 * features, hidden_size, 0),
    ) + tuple(
        ("contract", 1, 2 * features + hidden_size + i * features, features, i)
        for i in range(groups)
    )

    positions = lax.broadcasted_iota(jnp.int32, keep_mask.shape, 2)
    validity = ((positions < lengths[:, :, None]) & ((keep_mask > 0) | (positions == 0))).astype(
        jnp.float32
    )
    across = validity[:, :, None, :]
    down = validity[:, :, :, None]
    in_first = first_section.astype(jnp.int32).reshape(1)
    in_second = 1 - in_first

    def query_forward(flag, block_in, crop, kept=()):
        return forward_block(
            flag,
            block_in,
            across[0, crop : crop + 1],
            down[0, crop : crop + 1],
            query_lines,
            query_offs,
            (gathered,),
            query_layout,
            True,
            kept,
        )

    def query_backward(flag, gradient, weight, saved, kept=()):
        return backward_block(
            flag, gradient, weight, query_lines, (gathered,), query_layout, saved, kept
        )

    def momentum_forward(flag, block_in):
        return forward_block(
            flag,
            block_in,
            across[1],
            down[1],
            momentum_lines,
            momentum_offs,
            (gathered, late),
            momentum_layout,
            False,
        )[:2]

    crops = range(crop_count)
    started = [query_forward(in_first, inputs[0, c : c + 1], c) for c in crops]
    passed = [lax.ppermute(started[c][0], "section", [(0, 1)]) for c in crops]
    pools, saved, pulled, returned = [], [], [], []
    for c in crops:
        _, pool, kept = query_forward(in_second, passed[c], c, started[c][2])
        pools.append(jnp.where(first_section, started[c][1], pool))
        saved.append(kept)
        pulled.append(query_backward(in_second, cotangent[c], down[0, c], kept))
        returned.append(lax.ppermute(pulled[c][0][2], "section", [(1, 0)]))
    ones = jnp.ones((crop_len, 1), jnp.float32)
    vectors, marks, terms = 0.0, 0.0, []
    for c in crops:
        ends, kept = query_backward(in_first, returned[c], ones, saved[c], pulled[c][1])
        terms.append(kept)
        vectors = vectors + jnp.where(first_section, ends[0], pulled[c][0][0])
        marks = marks + jnp.where(first_section, ends[1], pulled[c][0][1])
    grad_input = jnp.stack([term[0] for term in terms])[None]

    core = lax.axis_index("dp") & 1 if rows == BLOCK else jnp.int32(0)
    core = jnp.asarray(core, jnp.int32).reshape(1)
    block_ins = [jnp.where(first_section, inputs[0, c], passed[c][0]) for c in crops]
    contract_sums = weight_gradient(
        contract_kernel,
        core,
        [kept[6] for kept in saved] + [term[1] for term in terms],
        groups // 2,
        features,
        features,
        "grad_contract",
    )
    expand_sums = weight_gradient(
        functools.partial(
            row_kernel,
            tuple((0, 1, i * features, i // 2, i % 2 * features) for i in range(groups)),
        ),
        core,
        [kept[3] for kept in saved] + [term[2] for term in terms],
        groups // 2,
        features,
        features,
        "grad_expand",
    )
    project_sums = weight_gradient(
        functools.partial(
            row_kernel,
            (
                (0, 1, 0, 0, 0),
                (2, 3, 0, 0, features),
                (2, 3, features, 1, 0),
                (2, 3, 2 * features, 1, features),
            ),
        ),
        core,
        [kept[2] for kept in saved]
        + [term[3] for term in terms]
        + block_ins
        + [term[4] for term in terms],
        2,
        features,
        features,
        "grad_projection",
    )

    def halves(sums, contracted=False):
        return [
            scattered(sums[2 * i], sums[2 * i + 1], shards_of, features, contracted)
            for i in range(len(sums) // 2)
        ]

    contract_parts = halves(contract_sums, True)
    expand_parts = halves(expand_sums)
    project_parts = halves(project_sums)
    columns = jnp.concatenate(
        [
            vectors.T.reshape(shards_of, rows, 8),
            jnp.moveaxis(marks.reshape(shards_of, groups, rows), 1, 2),
        ],
        axis=2,
    )
    coarse = columns.astype(jnp.bfloat16)
    fine = (columns - coarse.astype(jnp.float32)).astype(jnp.bfloat16)
    both = jnp.concatenate([coarse, fine], axis=2)
    both = jnp.pad(both, ((0, 0), (0, 0), (0, 128 - both.shape[2])))
    both = halving_sum(both, 0, shards_of.bit_length() - 1).astype(jnp.float32)
    small = (both[:, :12] + both[:, 12:24]).T

    key_out, key_pool = momentum_forward(in_first, inputs[1])
    key_in = lax.ppermute(key_out, "section", [(0, 1)])
    key_pool_second = momentum_forward(in_second, key_in)[1]
    key_pool = jnp.where(first_section, key_pool, key_pool_second)
    pooled = jnp.concatenate([jnp.concatenate(pools, axis=0)[:, None], key_pool[:, None]], axis=1)
    order = (slot_order[:, None] == jnp.arange(crop_count, dtype=jnp.int32)[None, :])[..., None]
    pooled = pooled.reshape(crop_count, -1)
    pooled = jnp.sum(jnp.where(order, pooled[None], 0.0), axis=1)
    pooled = doubled(pooled).reshape(-1, 2, features)
    pooled = jnp.moveaxis(pooled, 1, 0)[None]

    def wide(parts):
        return jnp.concatenate(parts, axis=1).astype(jnp.float32)

    contract_sum = jnp.moveaxis(wide(contract_parts).reshape(rows, groups, features), 1, 0)
    project_sum = wide(project_parts)
    return (
        pooled,
        grad_input,
        project_sum[None, :, features:],
        project_sum[None, :, :features],
        wide(expand_parts)[None],
        contract_sum.reshape(1, groups * rows, features),
        small[None, :2],
        small[None, 2:8],
        small[8:].reshape(1, groups * rows),
    )


def solution(mesh):
    in_specs = (
        P(None, "dp", None, None),
        P(None, "dp", None),
        P(None, "dp"),
        P("dp"),
        P("dp", None, None),
        P("section", "dp", None),
        P("section", "dp", None),
        P("section", "dp", None),
        P("section", "dp", None),
        P("section", None, "dp"),
        P("section", None, "dp"),
        P("section", "dp"),
        P("section", "dp", None),
        P("section", "dp", None),
        P("section", "dp", None),
        P("section", "dp", None),
        P("section", None, "dp"),
        P("section", None, "dp"),
        P("section", "dp"),
    )
    out_specs = (
        P("section", None, None, None),
        P("section", "dp", None, None),
        P("section", "dp", None),
        P("section", "dp", None),
        P("section", "dp", None),
        P("section", "dp", None),
        P("section", None, "dp"),
        P("section", None, "dp"),
        P("section", "dp"),
    )
    return jax.shard_map(shards, mesh=mesh, in_specs=in_specs, out_specs=out_specs, check_vma=False)
```

time: 1220 us -> 597 us (0.49)
  matrix products: 260 us -> 0 us
  blocking collectives: 218 us -> 0 us
  waiting for transfers between devices: 495 us -> 302 us
  Pallas kernels: 0 us -> 171 us
  local copies, waits for them, and re-layouts: 138 us -> 50.7 us
  other arithmetic: 74.7 us -> 16 us
  starting transfers between devices: 6.66 us -> 32.4 us
    reduce_scatter x4 -> x0, waiting for transfers between devices: 325 us -> none  [the longest x1 116 us: shards(): lax.psum_scatter(pending[3], 'dp', scatter_dimension=0, tiled=True)]
    dot_general x73 -> x0, matrix products: 247 us -> none  [the longest x6 50.6 us: forward_block(): jnp.dot(active, w_contract, preferred_element_type=jnp.float32)]
    ppermute x4 -> x37, waiting for transfers between devices: 28.9 us -> 217 us  [the longest x32 109 us: swapped(): return lax.ppermute(block, 'dp', route)]
    pallas_call x0 -> x13, Pallas kernels: none -> 171 us  [the longest x6 98.2 us: forward_block(): pl.pallas_call(functools.partial(forward_kernel, layout, len(packs), crop...]
    unnamed x2 -> x0, blocking collectives: 117 us -> none
    all_gather x5 -> x0, blocking collectives: 102 us -> none  [the longest x1 23.4 us: shards(): lax.all_gather(momentum_biases, 'dp', axis=2, tiled=True)]
    all_gather x8 -> x2, waiting for transfers between devices: 136 us -> 84.8 us  [the longest x1 84.8 us: shards(): gathered = lax.all_gather(own, 'dp', axis=0, tiled=True)]
    slice x18 -> x5, local copies, waits for them, and re-layouts: 48.5 us -> 4.66 us  [the longest x2 1.5 us: shards(): small[8:].reshape(1, groups * rows)]
  transfers between devices with their start and end apart: 18 -> 39, of which waited for: 8 -> 20; matrix products, arithmetic and copies ran while one was open for 21% -> 5% of each run, Pallas kernels for 0% -> 21%
where the time goes in v2:
time: 597 us; the launch traced here: 588 us
  waiting for transfers between devices  302 us (51%)
  Pallas kernels  171 us (29%)
  local copies, waits for them, and re-layouts  50.7 us (8%)
  starting transfers between devices  32.4 us (5%)
  other arithmetic  16 us (3%)
  between operations  15.8 us (3%)
    ppermute x32, waiting for transfers between devices, swapped(): return lax.ppermute(block, 'dp', route)  109 us
    pallas_call x6, Pallas kernels, forward_block(): pl.pallas_call(functools.partial(forward_kernel, layout, len(packs), crop...  98.2 us
    all_gather x1, waiting for transfers between devices, shards(): gathered = lax.all_gather(own, 'dp', axis=0, tiled=True)  84.8 us
    ppermute x1, waiting for transfers between devices, shards(): key_in = lax.ppermute(key_out, 'section', [(0, 1)])  78.3 us
    pallas_call x4, Pallas kernels, backward_block(): pl.pallas_call(functools.partial(backward_kernel, layout, len(packs), len...  43.5 us
    pallas_call x3, Pallas kernels, weight_gradient(): pl.pallas_call(kernel, out_shape=[shape] * (2 * targets), in_specs=[SMEM]...  28.9 us
    ppermute x32, starting transfers between devices, swapped(): return lax.ppermute(block, 'dp', route)  25.8 us
    ppermute x2, waiting for transfers between devices, shards(): passed = [lax.ppermute(started[c][0], 'section', [(0, 1)]) for c in crops]  25.4 us
  transfers between devices with their start and end apart: 39, of which 20 were waited for; matrix products, arithmetic and copies ran while one was open for 5% of the time, Pallas kernels for 21%

profile of v2, /device:TPU:2, one launch (start us, length us, event | category | flops | bytes accessed | tf_op | source)
XLA Modules:
  0.0 587.7 jit_solution(10217559948356587359)
XLA Ops:
  7.3 1.0 bitcast_dynamic-update-slice_fusion.1
  8.3 1.1 copy.301
  10.5 1.0 copy-done.7
  14.8 1.0 slice_bitcast_fusion.3
  17.7 84.8 %all-gather.3.cloned.1.call-done = bf16[768,11008]{1,0:T(8,128)(2,1)} async-done(((bf16[48,11008]{1,0:T(8,128)(2,1)}), bf16[768,11008]{1,0:T(8,128)(2,1)}) %all-gather.3.cloned.1.call-update) | async-done | bytes 16908304 | tf_op jit(solution)/shard_map/all_gather | solution.py:684
  102.5 22.4 %copy.304 = bf16[768,11008]{0,1:T(8,128)(2,1)} copy(bf16[768,11008]{1,0:T(8,128)(2,1)} %all-gather.3.cloned.1.call-done) | data formatting | bytes 33816576 | tf_op jit(solution)/shard_map/optimization_barrier | solution.py:694
  125.0 1.2 fusion.42
  126.2 1.3 convert_bitcast_fusion.2
  128.4 1.9 forward_save.4
  130.3 1.3 collective-permute-start
  134.9 2.3 forward_save.6
  137.2 1.3 collective-permute-start.1
  139.4 25.4 %collective-permute-done.refs_5_ = bf16[1,256,768]{2,1,0:T(8,128)(2,1)S(1)} collective-permute-done((bf16[1,256,768]{2,1,0:T(8,128)(2,1)}, bf16[1,256,768]{2,1,0:T(8,128)(2,1)S(1)}, u32[]{:S(2)}, u32[]{:S(2)}) %collective-permute-start) | collective-permute-done | bytes 393248 | tf_op jit(solution)/shard_map/ppermute | solution.py:778
  165.5 24.8 %forward_save.5 = (bf16[1,256,768]{2,1,0:T(8,128)(2,1)}, f32[1,1,768]{2,1,0:T(1,128)}, bf16[256,2304]{1,0:T(8,128)(2,1)}, bf16[12,256,256]{2,1,0:T(8,128)(2,1)},...) custom-call(s32[1]{0:T(128)S(6)} %sub.12.refs_0_, ...), custom_call_target="tpu_custom_call", output_to_operand_aliasing={{2}: (7, {}), {3}: (8, {}), {4}: (9, {}), {5}: (10, {}), {6... | custom-call | flops 3623878656 | bytes 20000000 | tf_op jit(solution)/shard_map/forward_save/pallas_call | solution.py:238
  190.3 19.6 %backward_data.4 = (f32[8,768]{1,0:T(8,128)}, f32[1,3072]{1,0:T(1,128)}, bf16[256,768]{1,0:T(8,128)(2,1)}, f32[256,768]{1,0:T(8,128)}, bf16[256,768]{1,0:T(8,128...) custom-call(s32[1]{0:T(128)S(6)} %sub.12.refs_0_, ...), custom_call_target="tpu_custom_call" | custom-call | flops 3623878656 | bytes 25000000 | tf_op jit(solution)/shard_map/backward_data/pallas_call | solution.py:458
  210.0 1.3 collective-permute-start.7
  212.0 25.0 %forward_save.7 = (bf16[1,256,768]{2,1,0:T(8,128)(2,1)}, f32[1,1,768]{2,1,0:T(1,128)}, bf16[256,2304]{1,0:T(8,128)(2,1)}, bf16[12,256,256]{2,1,0:T(8,128)(2,1)},...) custom-call(s32[1]{0:T(128)S(6)} %sub.12.refs_0_, ...), custom_call_target="tpu_custom_call", output_to_operand_aliasing={{2}: (7, {}), {3}: (8, {}), {4}: (9, {}), {5}: (10, {}), {6... | custom-call | flops 3623878656 | bytes 20000000 | tf_op jit(solution)/shard_map/forward_save/pallas_call | solution.py:238
  237.1 19.9 %backward_data.6 = (f32[8,768]{1,0:T(8,128)}, f32[1,3072]{1,0:T(1,128)}, bf16[256,768]{1,0:T(8,128)(2,1)}, f32[256,768]{1,0:T(8,128)}, bf16[256,768]{1,0:T(8,128...) custom-call(s32[1]{0:T(128)S(6)} %sub.12.refs_0_, ...), custom_call_target="tpu_custom_call" | custom-call | flops 3623878656 | bytes 25000000 | tf_op jit(solution)/shard_map/backward_data/pallas_call | solution.py:458
  257.0 1.3 collective-permute-start.8
  258.4 1.0 bitcast_select_fusion
  260.2 2.1 backward_data.5
  262.2 5.1 collective-permute-done.8.refs_3_
  268.1 1.9 backward_data.7
  270.7 9.7 %grad_contract.1 = (bf16[8,48,1536]{2,1,0:T(8,128)(2,1)}, bf16[8,48,1536]{2,1,0:T(8,128)(2,1)}, bf16[8,48,1536]{2,1,0:T(8,128)(2,1)}, bf16[8,48,1536]{2,1,0:T(8,128)(2,1)}) custom-call(s32[1]{0:T(128)} %bitcast.48.core, bf16[256,3072]{1,0:T(8,128)(2,1)} %get-tuple-element.139.refs_11_.act0, bf16[256,3072]{1,0:T(8,128)(2,1)} %get-tuple-element.156.refs_11_.act1, ...), custom_call_target="tpu_custom_call" | custom-call | flops 2415919104 | bytes 9000000 | tf_op jit(solution)/shard_map/grad_contract/pallas_call | solution.py:549
  281.0 1.3 collective-permute-start.34
  282.3 9.3 %grad_expand.1 = (bf16[8,48,1536]{2,1,0:T(8,128)(2,1)}, bf16[8,48,1536]{2,1,0:T(8,128)(2,1)}, bf16[8,48,1536]{2,1,0:T(8,128)(2,1)}, bf16[8,48,1536]{2,1,0:T(8,128)(2,1)}) custom-call(s32[1]{0:T(128)} %bitcast.48.core, bf16[256,768]{1,0:T(8,128)(2,1)} %get-tuple-element.136.refs_8_.refs_0_, bf16[256,768]{1,0:T(8,128)(2,1)} %get-tuple-element.153.refs_8_.refs_1_, ...), custom_call_target="tpu_custom_call" | custom-call | flops 2415919104 | bytes 9000000 | tf_op jit(solution)/shard_map/grad_expand/pallas_call | solution.py:549
  292.2 1.6 collective-permute-start.35
  293.8 9.9 %grad_projection.1 = (bf16[8,48,1536]{2,1,0:T(8,128)(2,1)}, bf16[8,48,1536]{2,1,0:T(8,128)(2,1)}, bf16[8,48,1536]{2,1,0:T(8,128)(2,1)}, bf16[8,48,1536]{2,1,0:T(8,128)(2,1)}) custom-call(s32[1]{0:T(128)} %bitcast.48.core, bf16[256,768]{1,0:T(8,128)(2,1)} %get-tuple-element.135.refs_7_.refs_0_, bf16[256,768]{1,0:T(8,128)(2,1)} %get-tuple-element.152.refs_7_.refs_1_, ...), custom_call_target="tpu_custom_call" | custom-call | flops 2415919104 | bytes 9000000 | tf_op jit(solution)/shard_map/grad_projection/pallas_call | solution.py:549
  303.7 1.9 collective-permute-start.36
  305.6 1.2 maximum_bitcast_fusion
  306.8 1.6 collective-permute-done.36
  309.9 1.4 copy.331
  312.8 1.4 copy.328
  316.6 1.0 collective-permute-start.30
  317.8 1.7 add_convert_fusion.3
  319.5 1.6 add_convert_fusion.2
  321.4 1.0 collective-permute-start.18
  322.4 1.2 collective-permute-start.22
  323.6 1.7 add_convert_fusion.5
  325.9 1.0 collective-permute-start.10
  326.9 4.4 collective-permute-done.26
  332.2 11.7 %collective-permute-done.30 = bf16[2,2,48,1536]{3,2,1,0:T(8,128)(2,1)S(1)} collective-permute-done((bf16[2,2,48,1536]{3,2,1,0:T(8,128)(2,1)S(1)}, bf16[2,2,48,1536]{3,2,1,0:T(8,128)(2,1)S(1)}, u32[]{:S(2)}, u32[]{:S(2)}) %collective-permute-start.30) | collective-permute-done | bytes 589856 | tf_op jit(solution)/shard_map/ppermute | solution.py:600
  344.5 12.0 %collective-permute-done.18 = bf16[2,2,48,1536]{3,2,0,1:T(8,128)(2,1)S(1)} collective-permute-done((bf16[2,2,48,1536]{3,2,0,1:T(8,128)(2,1)S(1)}, bf16[2,2,48,1536]{3,2,0,1:T(8,128)(2,1)S(1)}, u32[]{:S(2)}, u32[]{:S(2)}) %collective-permute-start.18) | collective-permute-done | bytes 589856 | tf_op jit(solution)/shard_map/ppermute | solution.py:600
  357.2 12.0 %collective-permute-done.22 = bf16[2,2,48,1536]{3,2,0,1:T(8,128)(2,1)S(1)} collective-permute-done((bf16[2,2,48,1536]{3,2,0,1:T(8,128)(2,1)S(1)}, bf16[2,2,48,1536]{3,2,0,1:T(8,128)(2,1)S(1)}, u32[]{:S(2)}, u32[]{:S(2)}) %collective-permute-start.22) | collective-permute-done | bytes 589856 | tf_op jit(solution)/shard_map/ppermute | solution.py:600
  369.8 12.0 %collective-permute-done.10 = bf16[2,2,48,1536]{3,2,0,1:T(8,128)(2,1)S(1)} collective-permute-done((bf16[2,2,48,1536]{3,2,0,1:T(8,128)(2,1)S(1)}, bf16[2,2,48,1536]{3,2,0,1:T(8,128)(2,1)S(1)}, u32[]{:S(2)}, u32[]{:S(2)}) %collective-permute-start.10) | collective-permute-done | bytes 589856 | tf_op jit(solution)/shard_map/ppermute | solution.py:600
  382.5 11.1 %collective-permute-done.14 = bf16[2,2,48,1536]{3,2,0,1:T(8,128)(2,1)S(1)} collective-permute-done((bf16[2,2,48,1536]{3,2,0,1:T(8,128)(2,1)S(1)}, bf16[2,2,48,1536]{3,2,0,1:T(8,128)(2,1)S(1)}, u32[]{:S(2)}, u32[]{:S(2)}) %collective-permute-start.14) | collective-permute-done | bytes 589856 | tf_op jit(solution)/shard_map/ppermute | solution.py:600
  394.2 1.7 collective-permute-start.15
  395.9 1.8 collective-permute-start.28
  397.8 1.3 collective-permute-start.32
  399.2 1.8 collective-permute-start.20
  401.1 11.8 %collective-permute-done.11 = bf16[2,48,1536]{2,1,0:T(8,128)(2,1)S(1)} collective-permute-done((bf16[2,48,1536]{2,1,0:T(8,128)(2,1)S(1)}, bf16[2,48,1536]{2,1,0:T(8,128)(2,1)S(1)}, u32[]{:S(2)}, u32[]{:S(2)}) %collective-permute-start.11) | collective-permute-done | bytes 294944 | tf_op jit(solution)/shard_map/ppermute | solution.py:600
  413.5 4.0 collective-permute-done.15
  418.0 2.6 collective-permute-start.16
  420.8 10.5 %collective-permute-done.24 = bf16[48,1536]{1,0:T(8,128)(2,1)S(1)} collective-permute-done((bf16[48,1536]{1,0:T(8,128)(2,1)S(1)}, bf16[48,1536]{1,0:T(8,128)(2,1)S(1)}, u32[]{:S(2)}, u32[]{:S(2)}) %collective-permute-start.24) | collective-permute-done | bytes 147488 | tf_op jit(solution)/shard_map/ppermute | solution.py:600
  431.3 3.1 collective-permute-done.12
  434.5 3.0 collective-permute-done.16
  437.6 2.2 forward_only.2
  439.8 1.3 collective-permute-start.2
  441.9 78.3 %collective-permute-done.2.refs_5_ = bf16[2,256,768]{2,1,0:T(8,128)(2,1)S(1)} collective-permute-done((bf16[2,256,768]{2,1,0:T(8,128)(2,1)}, bf16[2,256,768]{2,1,0:T(8,128)(2,1)S(1)}, u32[]{:S(2)}, u32[]{:S(2)}) %collective-permute-start.2) | collective-permute-done | bytes 786464 | tf_op jit(solution)/shard_map/ppermute | solution.py:864
  521.1 42.0 %forward_only.3 = (bf16[2,256,768]{2,1,0:T(8,128)(2,1)}, f32[2,1,768]{2,1,0:T(1,128)}) custom-call(s32[1]{0:T(128)S(6)} %sub.12.refs_0_, f32[2,1,256]{2,1,0:T(1,128)} %get-tuple-element.293.refs_1_, f32[2,256,1]{2,1,0:T(8,128)} %squeeze.239.refs_2_, f32[8,768]{1,0:T(8,128)} %get-tuple-element.261.refs_3_, f32[1,3072]{1,0:T(1,128)} %reshape.229.refs_4_, ...), custom_call_target="tpu_custom_call" | custom-call | flops 7247757312 | bytes 20000000 | tf_op jit(solution)/shard_map/forward_only/pallas_call | solution.py:238
  565.3 1.4 collective-permute-start.4
  566.8 2.4 collective-permute-done.4
  570.2 3.2 collective-permute-done.5
  574.2 5.3 collective-permute-done.6
  (258 shorter events, 34.7 us)
Async XLA Ops:
  7.2 2.3 copy-start.39
  7.2 2.5 copy-start.42
  7.2 2.4 copy-start.37
  7.2 2.5 copy-start.40
  7.2 2.7 copy-start.43
  7.2 2.6 copy-start.38
  7.2 2.7 copy-start.23
  7.2 2.8 copy-start.19
  7.3 95.3 %all-gather.3.cloned.1.call-start = ((), (), s32[]{:S(2)}) async-start(), calls=%async_computation | async-start | bytes 17965056 | tf_op jit(solution)/shard_map/all_gather | solution.py:684
  10.4 3.5 copy-start
  11.4 426.1 %all-gather.5.cloned.1.call-start = ((), (), s32[]{:S(2)}) async-start(), calls=%async_computation.1 | async-start | bytes 12533760 | tf_op jit(solution)/shard_map/all_gather | solution.py:695
  11.5 3.3 copy-start.14
  128.4 3.2 copy-start.44
  130.3 34.5 %collective-permute-start = (bf16[1,256,768]{2,1,0:T(8,128)(2,1)}, bf16[1,256,768]{2,1,0:T(8,128)(2,1)S(1)}, u32[]{:S(2)}, u32[]{:S(2)}) collective-permute-start(bf16[1,256,768]{2,1,0:T(8,128)(2,1)} %get-tuple-element.104), channel_id=1, source_target_pairs={{0,16},{1,17},{2,18},{3,19},{4,20},{5,21},{6,22},{7,23},{8,24},{9,... | collective-permute-start | bytes 1179656 | tf_op jit(solution)/shard_map/ppermute | solution.py:778
  137.2 74.1 %collective-permute-start.1 = (bf16[1,256,768]{2,1,0:T(8,128)(2,1)}, bf16[1,256,768]{2,1,0:T(8,128)(2,1)S(1)}, u32[]{:S(2)}, u32[]{:S(2)}) collective-permute-start(bf16[1,256,768]{2,1,0:T(8,128)(2,1)} %get-tuple-element.117), channel_id=1, source_target_pairs={{0,16},{1,17},{2,18},{3,19},{4,20},{5,21},{6,22},{7,23},{8,24},{9,... | collective-permute-start | bytes 1179656 | tf_op jit(solution)/shard_map/ppermute | solution.py:778
  210.0 49.4 %collective-permute-start.7 = (bf16[256,768]{1,0:T(8,128)(2,1)}, bf16[256,768]{1,0:T(8,128)(2,1)S(1)}, u32[]{:S(2)}, u32[]{:S(2)}) collective-permute-start(bf16[256,768]{1,0:T(8,128)(2,1)} %get-tuple-element.143), channel_id=1, source_target_pairs={{16,0},{17,1},{18,2},{19,3},{20,4},{21,5},{22,6},{23,7},{24,8},{25... | collective-permute-start | bytes 1179656 | tf_op jit(solution)/shard_map/ppermute | solution.py:785
  237.0 21.3 %copy-start.33 = (f32[1,1,768]{2,1,0:T(1,128)S(1)}, f32[1,1,768]{2,1,0:T(1,128)}, u32[]{:S(2)}) copy-start(f32[1,1,768]{2,1,0:T(1,128)} %get-tuple-element.103) | copy-start | bytes 9220
  237.0 21.3 %copy-start.34 = (f32[1,1,768]{2,1,0:T(1,128)S(1)}, f32[1,1,768]{2,1,0:T(1,128)}, u32[]{:S(2)}) copy-start(f32[1,1,768]{2,1,0:T(1,128)} %get-tuple-element.116) | copy-start | bytes 9220
  237.0 21.3 %copy-start.35 = (f32[1,1,768]{2,1,0:T(1,128)S(1)}, f32[1,1,768]{2,1,0:T(1,128)}, u32[]{:S(2)}) copy-start(f32[1,1,768]{2,1,0:T(1,128)} %get-tuple-element.115) | copy-start | bytes 9220
  237.1 21.3 %copy-start.36 = (f32[1,1,768]{2,1,0:T(1,128)S(1)}, f32[1,1,768]{2,1,0:T(1,128)}, u32[]{:S(2)}) copy-start(f32[1,1,768]{2,1,0:T(1,128)} %get-tuple-element.128) | copy-start | bytes 9220
  237.1 21.3 %copy-start.4 = (bf16[1,256,768]{2,1,0:T(8,128)(2,1)S(1)}, bf16[1,256,768]{2,1,0:T(8,128)(2,1)}, u32[]{:S(2)}) copy-start(bf16[1,256,768]{2,1,0:T(8,128)(2,1)} %copy-done.3) | copy-start | bytes 1179652
  237.1 21.3 %copy-start.6 = (bf16[1,256,768]{2,1,0:T(8,128)(2,1)S(1)}, bf16[1,256,768]{2,1,0:T(8,128)(2,1)}, u32[]{:S(2)}) copy-start(bf16[1,256,768]{2,1,0:T(8,128)(2,1)} %copy-done.5) | copy-start | bytes 1179652
  257.0 10.3 %collective-permute-start.8 = (bf16[256,768]{1,0:T(8,128)(2,1)}, bf16[256,768]{1,0:T(8,128)(2,1)S(1)}, u32[]{:S(2)}, u32[]{:S(2)}) collective-permute-start(bf16[256,768]{1,0:T(8,128)(2,1)} %get-tuple-element.160), channel_id=1, source_target_pairs={{16,0},{17,1},{18,2},{19,3},{20,4},{21,5},{22,6},{23,7},{24,8},{25... | collective-permute-start | bytes 1179656 | tf_op jit(solution)/shard_map/ppermute | solution.py:785
  268.0 2.1 copy-start.29
  268.1 2.1 copy-start.30
  268.1 2.1 copy-start.31
  270.7 10.3 %collective-permute-start.33 = (bf16[2,2,2,48,128]{4,3,2,1,0:T(8,128)(2,1)S(1)}, bf16[2,2,2,48,128]{4,3,2,1,0:T(8,128)(2,1)S(1)}, u32[]{:S(2)}, u32[]{:S(2)}) collective-permute-start(bf16[2,2,2,48,128]{4,3,2,1,0:T(8,128)(2,1)S(1)} %dynamic-slice_bitcast_fusion.14), channel_id=1, source_target_pairs={{0,1},{1,0},{2,3},{3,2},{4,5},{5,4},{6,7},{7,6},{8,9},{9,8},{10,11... | collective-permute-start | bytes 294920 | tf_op jit(solution)/shard_map/ppermute | solution.py:600
  280.4 33.7 %collective-permute-start.25 = (bf16[8,48,1536]{2,1,0:T(8,128)(2,1)}, bf16[8,48,1536]{2,1,0:T(8,128)(2,1)S(1)}, u32[]{:S(2)}, u32[]{:S(2)}) collective-permute-start(bf16[8,48,1536]{2,1,0:T(8,128)(2,1)} %get-tuple-element.184), channel_id=1, source_target_pairs={{0,1},{1,0},{2,3},{3,2},{4,5},{5,4},{6,7},{7,6},{8,9},{9,8},{10,11... | collective-permute-start | bytes 3538952 | tf_op jit(solution)/shard_map/ppermute | solution.py:600
  280.9 34.1 %collective-permute-start.29 = (bf16[8,48,1536]{2,1,0:T(8,128)(2,1)}, bf16[8,48,1536]{2,1,0:T(8,128)(2,1)S(1)}, u32[]{:S(2)}, u32[]{:S(2)}) collective-permute-start(bf16[8,48,1536]{2,1,0:T(8,128)(2,1)} %get-tuple-element.186), channel_id=1, source_target_pairs={{0,1},{1,0},{2,3},{3,2},{4,5},{5,4},{6,7},{7,6},{8,9},{9,8},{10,11... | collective-permute-start | bytes 3538952 | tf_op jit(solution)/shard_map/ppermute | solution.py:600
  281.0 11.2 %collective-permute-start.34 = (bf16[2,2,48,128]{3,2,1,0:T(8,128)(2,1)S(1)}, bf16[2,2,48,128]{3,2,1,0:T(8,128)(2,1)S(1)}, u32[]{:S(2)}, u32[]{:S(2)}) collective-permute-start(bf16[2,2,48,128]{3,2,1,0:T(8,128)(2,1)S(1)} %dynamic-slice_bitcast_fusion.15), channel_id=1, source_target_pairs={{0,2},{1,3},{2,0},{3,1},{4,6},{5,7},{6,4},{7,5},{8,10},{9,11},{10,... | collective-permute-start | bytes 147464 | tf_op jit(solution)/shard_map/ppermute | solution.py:600
  291.6 25.0 %collective-permute-start.17 = (bf16[8,48,1536]{2,1,0:T(8,128)(2,1)}, bf16[8,48,1536]{2,1,0:T(8,128)(2,1)}, u32[]{:S(2)}, u32[]{:S(2)}) collective-permute-start(bf16[8,48,1536]{2,1,0:T(8,128)(2,1)} %get-tuple-element.178), channel_id=1, source_target_pairs={{0,1},{1,0},{2,3},{3,2},{4,5},{5,4},{6,7},{7,6},{8,9},{9,8},{10,11... | collective-permute-start | bytes 3538952 | tf_op jit(solution)/shard_map/ppermute | solution.py:600
  291.9 27.6 %collective-permute-start.21 = (bf16[8,48,1536]{2,1,0:T(8,128)(2,1)}, bf16[8,48,1536]{2,1,0:T(8,128)(2,1)}, u32[]{:S(2)}, u32[]{:S(2)}) collective-permute-start(bf16[8,48,1536]{2,1,0:T(8,128)(2,1)} %get-tuple-element.180), channel_id=1, source_target_pairs={{0,1},{1,0},{2,3},{3,2},{4,5},{5,4},{6,7},{7,6},{8,9},{9,8},{10,11... | collective-permute-start | bytes 3538952 | tf_op jit(solution)/shard_map/ppermute | solution.py:600
  292.2 11.5 %collective-permute-start.35 = (bf16[2,48,128]{2,1,0:T(8,128)(2,1)S(1)}, bf16[2,48,128]{2,1,0:T(8,128)(2,1)S(1)}, u32[]{:S(2)}, u32[]{:S(2)}) collective-permute-start(bf16[2,48,128]{2,1,0:T(8,128)(2,1)S(1)} %dynamic-slice_bitcast_fusion.16), channel_id=1, source_target_pairs={{0,4},{1,5},{2,6},{3,7},{4,0},{5,1},{6,2},{7,3},{8,12},{9,13},{10,... | collective-permute-start | bytes 73736 | tf_op jit(solution)/shard_map/ppermute | solution.py:600
  293.8 11.8 %copy-start.1 = (f32[256,768]{1,0:T(8,128)S(1)}, f32[256,768]{1,0:T(8,128)}, u32[]{:S(2)}) copy-start(f32[256,768]{1,0:T(8,128)} %get-tuple-element.149) | copy-start | bytes 2359300
  293.8 11.8 %copy-start.2 = (f32[256,768]{1,0:T(8,128)S(1)}, f32[256,768]{1,0:T(8,128)}, u32[]{:S(2)}) copy-start(f32[256,768]{1,0:T(8,128)} %get-tuple-element.166) | copy-start | bytes 2359300
  303.7 4.7 collective-permute-start.36
  305.6 9.1 %copy-start.10 = (bf16[8,48,1536]{2,1,0:T(8,128)(2,1)S(1)}, bf16[8,48,1536]{2,1,0:T(8,128)(2,1)}, u32[]{:S(2)}) copy-start(bf16[8,48,1536]{2,1,0:T(8,128)(2,1)} %get-tuple-element.183) | copy-start | bytes 3538948
  308.4 13.9 %collective-permute-start.9 = (bf16[8,48,1536]{2,1,0:T(8,128)(2,1)}, bf16[8,48,1536]{2,1,0:T(8,128)(2,1)}, u32[]{:S(2)}, u32[]{:S(2)}) collective-permute-start(bf16[8,48,1536]{2,1,0:T(8,128)(2,1)} %get-tuple-element.172), channel_id=1, source_target_pairs={{0,1},{1,0},{2,3},{3,2},{4,5},{5,4},{6,7},{7,6},{8,9},{9,8},{10,11... | collective-permute-start | bytes 3538952 | tf_op jit(solution)/shard_map/ppermute | solution.py:600
  314.1 11.1 %collective-permute-start.13 = (bf16[8,48,1536]{2,1,0:T(8,128)(2,1)}, bf16[8,48,1536]{2,1,0:T(8,128)(2,1)S(1)}, u32[]{:S(2)}, u32[]{:S(2)}) collective-permute-start(bf16[8,48,1536]{2,1,0:T(8,128)(2,1)} %get-tuple-element.174), channel_id=1, source_target_pairs={{0,1},{1,0},{2,3},{3,2},{4,5},{5,4},{6,7},{7,6},{8,9},{9,8},{10,11... | collective-permute-start | bytes 3538952 | tf_op jit(solution)/shard_map/ppermute | solution.py:600
  315.0 16.3 %collective-permute-start.26 = (bf16[2,2,48,1536]{3,2,1,0:T(8,128)(2,1)S(1)}, bf16[2,2,48,1536]{3,2,1,0:T(8,128)(2,1)S(1)}, u32[]{:S(2)}, u32[]{:S(2)}) collective-permute-start(bf16[2,2,48,1536]{3,2,1,0:T(8,128)(2,1)S(1)} %dynamic-slice_bitcast_fusion.1), channel_id=1, source_target_pairs={{0,2},{1,3},{2,0},{3,1},{4,6},{5,7},{6,4},{7,5},{8,10},{9,11},{10,... | collective-permute-start | bytes 1769480 | tf_op jit(solution)/shard_map/ppermute | solution.py:600
  316.6 27.3 %collective-permute-start.30 = (bf16[2,2,48,1536]{3,2,1,0:T(8,128)(2,1)S(1)}, bf16[2,2,48,1536]{3,2,1,0:T(8,128)(2,1)S(1)}, u32[]{:S(2)}, u32[]{:S(2)}) collective-permute-start(bf16[2,2,48,1536]{3,2,1,0:T(8,128)(2,1)S(1)} %dynamic-slice_bitcast_fusion), channel_id=1, source_target_pairs={{0,2},{1,3},{2,0},{3,1},{4,6},{5,7},{6,4},{7,5},{8,10},{9,11},{10,... | collective-permute-start | bytes 1769480 | tf_op jit(solution)/shard_map/ppermute | solution.py:600
  321.3 2.3 copy-start.12
  321.4 35.2 %collective-permute-start.18 = (bf16[2,2,48,1536]{3,2,0,1:T(8,128)(2,1)S(1)}, bf16[2,2,48,1536]{3,2,0,1:T(8,128)(2,1)S(1)}, u32[]{:S(2)}, u32[]{:S(2)}) collective-permute-start(bf16[2,2,48,1536]{3,2,0,1:T(8,128)(2,1)S(1)} %bitcast.288), channel_id=1, source_target_pairs={{0,2},{1,3},{2,0},{3,1},{4,6},{5,7},{6,4},{7,5},{8,10},{9,11},{10,... | collective-permute-start | bytes 1769480 | tf_op jit(solution)/shard_map/ppermute | solution.py:600
  322.4 46.8 %collective-permute-start.22 = (bf16[2,2,48,1536]{3,2,0,1:T(8,128)(2,1)S(1)}, bf16[2,2,48,1536]{3,2,0,1:T(8,128)(2,1)S(1)}, u32[]{:S(2)}, u32[]{:S(2)}) collective-permute-start(bf16[2,2,48,1536]{3,2,0,1:T(8,128)(2,1)S(1)} %bitcast.287), channel_id=1, source_target_pairs={{0,2},{1,3},{2,0},{3,1},{4,6},{5,7},{6,4},{7,5},{8,10},{9,11},{10,... | collective-permute-start | bytes 1769480 | tf_op jit(solution)/shard_map/ppermute | solution.py:600
  325.9 56.0 %collective-permute-start.10 = (bf16[2,2,48,1536]{3,2,0,1:T(8,128)(2,1)S(1)}, bf16[2,2,48,1536]{3,2,0,1:T(8,128)(2,1)S(1)}, u32[]{:S(2)}, u32[]{:S(2)}) collective-permute-start(bf16[2,2,48,1536]{3,2,0,1:T(8,128)(2,1)S(1)} %bitcast.291), channel_id=1, source_target_pairs={{0,2},{1,3},{2,0},{3,1},{4,6},{5,7},{6,4},{7,5},{8,10},{9,11},{10,... | collective-permute-start | bytes 1769480 | tf_op jit(solution)/shard_map/ppermute | solution.py:600
  331.3 62.2 %collective-permute-start.14 = (bf16[2,2,48,1536]{3,2,0,1:T(8,128)(2,1)S(1)}, bf16[2,2,48,1536]{3,2,0,1:T(8,128)(2,1)S(1)}, u32[]{:S(2)}, u32[]{:S(2)}) collective-permute-start(bf16[2,2,48,1536]{3,2,0,1:T(8,128)(2,1)S(1)} %bitcast.290), channel_id=1, source_target_pairs={{0,2},{1,3},{2,0},{3,1},{4,6},{5,7},{6,4},{7,5},{8,10},{9,11},{10,... | collective-permute-start | bytes 1769480 | tf_op jit(solution)/shard_map/ppermute | solution.py:600
  343.9 50.2 %collective-permute-start.27 = (bf16[2,48,1536]{2,1,0:T(8,128)(2,1)S(1)}, bf16[2,48,1536]{2,1,0:T(8,128)(2,1)S(1)}, u32[]{:S(2)}, u32[]{:S(2)}) collective-permute-start(bf16[2,48,1536]{2,1,0:T(8,128)(2,1)S(1)} %dynamic-slice_bitcast_fusion.3), channel_id=1, source_target_pairs={{0,4},{1,5},{2,6},{3,7},{4,0},{5,1},{6,2},{7,3},{8,12},{9,13},{10,... | collective-permute-start | bytes 884744 | tf_op jit(solution)/shard_map/ppermute | solution.py:600
  356.6 39.4 %collective-permute-start.31 = (bf16[2,48,1536]{2,1,0:T(8,128)(2,1)S(1)}, bf16[2,48,1536]{2,1,0:T(8,128)(2,1)S(1)}, u32[]{:S(2)}, u32[]{:S(2)}) collective-permute-start(bf16[2,48,1536]{2,1,0:T(8,128)(2,1)S(1)} %dynamic-slice_bitcast_fusion.2), channel_id=1, source_target_pairs={{0,4},{1,5},{2,6},{3,7},{4,0},{5,1},{6,2},{7,3},{8,12},{9,13},{10,... | collective-permute-start | bytes 884744 | tf_op jit(solution)/shard_map/ppermute | solution.py:600
  369.2 28.6 %collective-permute-start.19 = (bf16[2,48,1536]{2,1,0:T(8,128)(2,1)S(1)}, bf16[2,48,1536]{2,1,0:T(8,128)(2,1)S(1)}, u32[]{:S(2)}, u32[]{:S(2)}) collective-permute-start(bf16[2,48,1536]{2,1,0:T(8,128)(2,1)S(1)} %dynamic-slice_bitcast_fusion.5), channel_id=1, source_target_pairs={{0,4},{1,5},{2,6},{3,7},{4,0},{5,1},{6,2},{7,3},{8,12},{9,13},{10,... | collective-permute-start | bytes 884744 | tf_op jit(solution)/shard_map/ppermute | solution.py:600
  381.8 17.4 %collective-permute-start.23 = (bf16[2,48,1536]{2,1,0:T(8,128)(2,1)S(1)}, bf16[2,48,1536]{2,1,0:T(8,128)(2,1)S(1)}, u32[]{:S(2)}, u32[]{:S(2)}) collective-permute-start(bf16[2,48,1536]{2,1,0:T(8,128)(2,1)S(1)} %dynamic-slice_bitcast_fusion.4), channel_id=1, source_target_pairs={{0,4},{1,5},{2,6},{3,7},{4,0},{5,1},{6,2},{7,3},{8,12},{9,13},{10,... | collective-permute-start | bytes 884744 | tf_op jit(solution)/shard_map/ppermute | solution.py:600
  393.5 19.4 %collective-permute-start.11 = (bf16[2,48,1536]{2,1,0:T(8,128)(2,1)S(1)}, bf16[2,48,1536]{2,1,0:T(8,128)(2,1)S(1)}, u32[]{:S(2)}, u32[]{:S(2)}) collective-permute-start(bf16[2,48,1536]{2,1,0:T(8,128)(2,1)S(1)} %dynamic-slice_bitcast_fusion.7), channel_id=1, source_target_pairs={{0,4},{1,5},{2,6},{3,7},{4,0},{5,1},{6,2},{7,3},{8,12},{9,13},{10,... | collective-permute-start | bytes 884744 | tf_op jit(solution)/shard_map/ppermute | solution.py:600
  394.2 23.3 %collective-permute-start.15 = (bf16[2,48,1536]{2,1,0:T(8,128)(2,1)S(1)}, bf16[2,48,1536]{2,1,0:T(8,128)(2,1)S(1)}, u32[]{:S(2)}, u32[]{:S(2)}) collective-permute-start(bf16[2,48,1536]{2,1,0:T(8,128)(2,1)S(1)} %dynamic-slice_bitcast_fusion.6), channel_id=1, source_target_pairs={{0,4},{1,5},{2,6},{3,7},{4,0},{5,1},{6,2},{7,3},{8,12},{9,13},{10,... | collective-permute-start | bytes 884744 | tf_op jit(solution)/shard_map/ppermute | solution.py:600
  395.9 22.1 %collective-permute-start.28 = (bf16[48,1536]{1,0:T(8,128)(2,1)S(1)}, bf16[48,1536]{1,0:T(8,128)(2,1)S(1)}, u32[]{:S(2)}, u32[]{:S(2)}) collective-permute-start(bf16[48,1536]{1,0:T(8,128)(2,1)S(1)} %dynamic-slice_bitcast_fusion.9), channel_id=1, source_target_pairs={{0,8},{1,9},{2,10},{3,11},{4,12},{5,13},{6,14},{7,15},{8,0},{9,1},... | collective-permute-start | bytes 442376 | tf_op jit(solution)/shard_map/ppermute | solution.py:600
  397.8 22.8 %collective-permute-start.32 = (bf16[48,1536]{1,0:T(8,128)(2,1)S(1)}, bf16[48,1536]{1,0:T(8,128)(2,1)S(1)}, u32[]{:S(2)}, u32[]{:S(2)}) collective-permute-start(bf16[48,1536]{1,0:T(8,128)(2,1)S(1)} %dynamic-slice_bitcast_fusion.8), channel_id=1, source_target_pairs={{0,8},{1,9},{2,10},{3,11},{4,12},{5,13},{6,14},{7,15},{8,0},{9,1},... | collective-permute-start | bytes 442376 | tf_op jit(solution)/shard_map/ppermute | solution.py:600
  399.2 21.5 %collective-permute-start.20 = (bf16[48,1536]{1,0:T(8,128)(2,1)S(1)}, bf16[48,1536]{1,0:T(8,128)(2,1)S(1)}, u32[]{:S(2)}, u32[]{:S(2)}) collective-permute-start(bf16[48,1536]{1,0:T(8,128)(2,1)S(1)} %dynamic-slice_bitcast_fusion.11), channel_id=1, source_target_pairs={{0,8},{1,9},{2,10},{3,11},{4,12},{5,13},{6,14},{7,15},{8,0},{9,1},... | collective-permute-start | bytes 442376 | tf_op jit(solution)/shard_map/ppermute | solution.py:600
  413.0 18.3 %collective-permute-start.24 = (bf16[48,1536]{1,0:T(8,128)(2,1)S(1)}, bf16[48,1536]{1,0:T(8,128)(2,1)S(1)}, u32[]{:S(2)}, u32[]{:S(2)}) collective-permute-start(bf16[48,1536]{1,0:T(8,128)(2,1)S(1)} %dynamic-slice_bitcast_fusion.10), channel_id=1, source_target_pairs={{0,8},{1,9},{2,10},{3,11},{4,12},{5,13},{6,14},{7,15},{8,0},{9,1},... | collective-permute-start | bytes 442376 | tf_op jit(solution)/shard_map/ppermute | solution.py:600
  417.5 16.9 %collective-permute-start.12 = (bf16[48,1536]{1,0:T(8,128)(2,1)S(1)}, bf16[48,1536]{1,0:T(8,128)(2,1)S(1)}, u32[]{:S(2)}, u32[]{:S(2)}) collective-permute-start(bf16[48,1536]{1,0:T(8,128)(2,1)S(1)} %dynamic-slice_bitcast_fusion.13), channel_id=1, source_target_pairs={{0,8},{1,9},{2,10},{3,11},{4,12},{5,13},{6,14},{7,15},{8,0},{9,1},... | collective-permute-start | bytes 442376 | tf_op jit(solution)/shard_map/ppermute | solution.py:600
  418.0 19.5 %collective-permute-start.16 = (bf16[48,1536]{1,0:T(8,128)(2,1)S(1)}, bf16[48,1536]{1,0:T(8,128)(2,1)S(1)}, u32[]{:S(2)}, u32[]{:S(2)}) collective-permute-start(bf16[48,1536]{1,0:T(8,128)(2,1)S(1)} %dynamic-slice_bitcast_fusion.12), channel_id=1, source_target_pairs={{0,8},{1,9},{2,10},{3,11},{4,12},{5,13},{6,14},{7,15},{8,0},{9,1},... | collective-permute-start | bytes 442376 | tf_op jit(solution)/shard_map/ppermute | solution.py:600
  439.8 80.5 %collective-permute-start.2 = (bf16[2,256,768]{2,1,0:T(8,128)(2,1)}, bf16[2,256,768]{2,1,0:T(8,128)(2,1)S(1)}, u32[]{:S(2)}, u32[]{:S(2)}) collective-permute-start(bf16[2,256,768]{2,1,0:T(8,128)(2,1)} %get-tuple-element.131), channel_id=1, source_target_pairs={{0,16},{1,17},{2,18},{3,19},{4,20},{5,21},{6,22},{7,23},{8,24},{9,... | collective-permute-start | bytes 2359304 | tf_op jit(solution)/shard_map/ppermute | solution.py:864
  441.9 121.3 %copy-start.32 = (f32[2,1,768]{2,1,0:T(1,128)S(1)}, f32[2,1,768]{2,1,0:T(1,128)}, u32[]{:S(2)}) copy-start(f32[2,1,768]{2,1,0:T(1,128)} %get-tuple-element.130) | copy-start | bytes 18436
  564.1 1.2 collective-permute-start.3
  565.3 3.9 collective-permute-start.4
  569.3 4.2 collective-permute-start.5
  573.5 6.1 %collective-permute-start.6 = (f32[16,1536]{1,0:T(8,128)S(1)}, f32[16,1536]{1,0:T(8,128)S(1)}, u32[]{:S(2)}, u32[]{:S(2)}) collective-permute-start(f32[16,1536]{1,0:T(8,128)S(1)} %pad_maximum_fusion.2), channel_id=1, source_target_pairs={{0,8},{1,9},{2,10},{3,11},{4,12},{5,13},{6,14},{7,15},{8,0},{9,1},... | collective-permute-start | bytes 294920 | tf_op jit(solution)/shard_map/ppermute | solution.py:600
  (20 other events, 24.8 us)
Sparse Core Ops, SparseCore 0:
  11.6 90.9 all-gather.2
  135.0 117.9 all-gather.4

commit v3 on v2

--- a/solution.py
+++ b/solution.py
@@ -78,7 +78,7 @@
     return block.reshape(-1, block.shape[-1])
 
 
-def forward_kernel(layout, pack_count, crops, saved_count, kept_count, *refs):
+def forward_kernel(layout, pack_count, view, first, crops, saved_count, kept_count, *refs):
     flag, vrow, vcol, lines, offs, x_hbm = refs[:6]
     packs = refs[6 : 6 + pack_count]
     refs = refs[6 + pack_count + kept_count :]
@@ -103,7 +103,8 @@
                 copy.wait()
 
         for crop in range(crops):
-            fetch = pltpu.make_async_copy(x_hbm.at[crop], x_buf, io_sems.at[0])
+            source = x_hbm.at[view, first + crop] if len(x_hbm.shape) == 4 else x_hbm.at[crop]
+            fetch = pltpu.make_async_copy(source, x_buf, io_sems.at[0])
             fetch.start()
             fetch.wait()
             if crop == 0:
@@ -115,7 +116,7 @@
                     part = part + lines[2 + third // 2 : 3 + third // 2, :]
                 mix[:, columns] = part.astype(jnp.bfloat16)
             head_low = lax.broadcasted_iota(jnp.int32, (rows, 2 * HD), 1) < HD
-            valid = jnp.broadcast_to(vrow[crop] > 0, (rows, rows))
+            valid = jnp.broadcast_to(vrow[view, first + crop] > 0, (rows, rows))
 
             def pair_step(pair, _):
                 at = pl.multiple_of(pair * 2 * HD, 2 * HD)
@@ -197,10 +198,10 @@
                 if saved_count:
                     hat2[at, :] = hat.astype(jnp.bfloat16)
                     rstd2[at, :] = jnp.broadcast_to(scale, (STRIP, 128))
-                return held + by_eights(value * vcol[crop, at, :])
+                return held + by_eights(value * vcol[view, first + crop, at, :])
 
             total = each_strip(rows, second_norm, jnp.zeros((8, features), jnp.float32))
-            count = jnp.sum(vrow[crop], axis=-1, keepdims=True)
+            count = jnp.sum(vrow[view, first + crop], axis=-1, keepdims=True)
             pooled_out[crop] = jnp.sum(total, axis=0, keepdims=True) / count
             keep(8, hat2)
             keep(9, rstd2)
@@ -208,8 +209,8 @@
                 copy.wait()
 
 
-def forward_block(flag, x, vrow, vcol, lines, offs, packs, layout, save, kept=()):
-    crops, rows, features = x.shape
+def forward_block(flag, x, vrow, vcol, lines, offs, packs, layout, save, view, first, crops, kept=()):
+    rows, features = x.shape[-2:]
     hidden_size = offs.shape[-1]
     heads = features // HD
     blocks = features // BLOCK
@@ -236,7 +237,9 @@
     flops = 2 * crops * rows * (4 * features * features + 2 * features * hidden_size)
     first_kept = 6 + len(packs)
     result = pl.pallas_call(
-        functools.partial(forward_kernel, layout, len(packs), crops, len(shapes), len(kept)),
+        functools.partial(
+            forward_kernel, layout, len(packs), view, first, crops, len(shapes), len(kept)
+        ),
         out_shape=out_shape,
         in_specs=[SMEM] + [VMEM] * 4 + [ANY] * (1 + len(packs) + len(kept)),
         out_specs=[VMEM, VMEM] + [ANY] * len(shapes),
@@ -269,7 +272,7 @@
     return result[0], result[1], tuple(result[2:])
 
 
-def backward_kernel(layout, pack_count, kept_count, *refs):
+def backward_kernel(layout, pack_count, crop, kept_count, *refs):
     flag, vcol, lines, g_hbm = refs[:4]
     packs = refs[4 : 4 + pack_count]
     saved = refs[4 + pack_count : 14 + pack_count]
@@ -290,7 +293,7 @@
         fetches = {}
         for at, (name, source, place) in enumerate(
             (
-                ("g", g_hbm, g_buf),
+                ("g", g_hbm.at[crop] if len(g_hbm.shape) == 3 else g_hbm, g_buf),
                 ("hat2", saved[8], hat2),
                 ("rstd2", saved[9], rstd2),
                 ("slope", saved[7], slope),
@@ -332,7 +335,9 @@
         arrive("g", "hat2", "rstd2")
 
         def second_norm(at, held):
-            gradient = g_buf[at, :].astype(jnp.float32) * vcol[at, :]
+            gradient = g_buf[at, :].astype(jnp.float32)
+            if len(g_hbm.shape) == 3:
+                gradient = gradient * vcol[0, crop, at, :]
             hat = hat2[at, :].astype(jnp.float32)
             moved = norm_back(gradient, hat, rstd2[at, 0:1], lines[1:2, :])
             total[at, :] = moved
@@ -436,8 +441,8 @@
             copy.wait()
 
 
-def backward_block(flag, gradient, vcol, lines, packs, layout, saved, kept=()):
-    rows, features = gradient.shape
+def backward_block(flag, gradient, vcol, lines, packs, layout, saved, crop, kept=()):
+    rows, features = gradient.shape[-2:]
     hidden_size = saved[6].shape[-1]
     heads = features // HD
     blocks = features // BLOCK
@@ -456,7 +461,7 @@
     flops = 2 * rows * (4 * features * features + 2 * features * hidden_size)
     first_kept = 4 + len(packs) + 10
     result = pl.pallas_call(
-        functools.partial(backward_kernel, layout, len(packs), len(kept)),
+        functools.partial(backward_kernel, layout, len(packs), crop, len(kept)),
         out_shape=out_shape,
         in_specs=[SMEM] + [VMEM] * 2 + [ANY] * (1 + len(packs) + 10 + len(kept)),
         out_specs=[VMEM] * 3 + [ANY] * 5,
@@ -560,14 +565,37 @@
     )(core, *operands)
 
 
-def pack_vectors(norm_gains, biases, offsets, rows):
-    vectors = jnp.concatenate([norm_gains, biases, offsets.reshape(-1, rows)], axis=0)
-    return jnp.pad(vectors, ((0, 128 - vectors.shape[0]), (0, 0))).T
-
-
-def fold_rows(matrix, rows):
-    folded = matrix.reshape(-1, rows, matrix.shape[-1])
-    return jnp.moveaxis(folded, 0, 1).reshape(rows, -1)
+def pack_kernel(plan, *refs):
+    sems = refs[-1]
+    target = refs[-2]
+    copies = []
+    for at, (source, row, column, width, place) in enumerate(plan):
+        block = refs[source].at[0, pl.ds(row, target.shape[0]), pl.ds(column, width)]
+        copy = pltpu.make_async_copy(block, target.at[:, pl.ds(place, width)], sems.at[at])
+        copy.start()
+        copies.append(copy)
+    for copy in copies:
+        copy.wait()
+
+
+def packed(arrays, pieces, rows):
+    width = sum(piece[3] for piece in pieces)
+    if rows % 16:
+        return jnp.concatenate(
+            [arrays[i][0, r : r + rows, c : c + w] for i, r, c, w in pieces], axis=1
+        )
+    plan, place = [], 0
+    for piece in pieces:
+        plan.append(piece + (place,))
+        place += piece[3]
+    return pl.pallas_call(
+        functools.partial(pack_kernel, tuple(plan)),
+        out_shape=jax.ShapeDtypeStruct((rows, width), jnp.bfloat16),
+        in_specs=[ANY] * len(arrays),
+        out_specs=ANY,
+        scratch_shapes=[pltpu.SemaphoreType.DMA((len(plan),))],
+        name="pack",
+    )(*arrays)
 
 
 def refold(columns, shards_of, features):
@@ -588,13 +616,6 @@
     return jnp.moveaxis(natural, 1, 2).reshape(shards_of, rows, -1)
 
 
-def vector_rows(columns, shards_of):
-    features = columns.shape[0]
-    lines = columns[:, :8].astype(jnp.float32).T
-    offsets = columns[:, 8:12].astype(jnp.float32).reshape(shards_of, features // shards_of, -1)
-    return lines, jnp.moveaxis(offsets, 2, 1).reshape(1, -1)
-
-
 def swapped(block, level):
     route = [(i, i ^ (1 << level)) for i in range(lax.axis_size("dp"))]
     return lax.ppermute(block, "dp", route)
@@ -604,28 +625,40 @@
     return (first.astype(jnp.float32) + second.astype(jnp.float32)).astype(jnp.bfloat16)
 
 
-def halving_sum(current, first_level, levels):
-    here = lax.axis_index("dp")
-    current = current.reshape((2,) * (levels - first_level) + current.shape[1:])
-    for level in range(first_level, levels):
-        axis = levels - 1 - level
-        mine = (here >> level) & 1
-        send = lax.dynamic_index_in_dim(current, 1 - mine, axis, keepdims=False)
-        keep = lax.dynamic_index_in_dim(current, mine, axis, keepdims=False)
-        current = added(keep, swapped(send, level))
-    return current
-
-
-def scattered(keep, send, shards_of, features, contracted):
+def tied(value, *others):
+    return lax.optimization_barrier((value,) + others)[0]
+
+
+def split(block, level):
+    levels = lax.axis_size("dp").bit_length() - 1
+    mine = (lax.axis_index("dp") >> level) & 1
+    axis = levels - 1 - level
+    keep = lax.dynamic_index_in_dim(block, mine, axis, keepdims=False)
+    return keep, lax.dynamic_index_in_dim(block, 1 - mine, axis, keepdims=False)
+
+
+def by_bits(block, levels):
+    return block.reshape((2,) * levels + block.shape[1:])
+
+
+def halved(pair, level):
+    keep, send = pair
+    total = added(keep, swapped(send, level))
+    if level + 1 == lax.axis_size("dp").bit_length() - 1:
+        return total
+    return split(total, level + 1)
+
+
+def first_pair(keep, send, shards_of, features, contracted):
     levels = shards_of.bit_length() - 1
     if features == BLOCK * shards_of:
-        return halving_sum(added(keep, swapped(send, 0)), 1, levels)
+        return by_bits(keep, levels - 1), by_bits(send, levels - 1)
     blocks = jnp.stack([keep, send], axis=1).reshape(-1, BLOCK, keep.shape[-1])
     if contracted:
         blocks = unfold(blocks, shards_of, features)
     else:
         blocks = blocks.reshape(shards_of, features // shards_of, -1)
-    return halving_sum(blocks, 0, levels)
+    return split(by_bits(blocks, levels), 0)
 
 
 def doubled(block):
@@ -668,38 +701,54 @@
     groups = hidden_size // features
     blocks = features // BLOCK
 
-    own = jnp.concatenate(
-        [
-            query_projection[0],
-            query_output[0],
-            query_expand[0],
-            fold_rows(query_contract[0], rows),
-            pack_vectors(query_gains[0], query_biases[0], query_offsets[0], rows),
-            pack_vectors(momentum_gains[0], momentum_biases[0], momentum_offsets[0], rows),
-            momentum_output[0],
-            momentum_projection[0, :, features : 2 * features],
-        ],
-        axis=1,
+    def folded(which):
+        return [(which, i * rows, 0, features) for i in range(groups)]
+
+    late_from, late_to = 2 * features // 3, 2 * features
+    own = packed(
+        (query_projection, query_output, query_expand, query_contract)
+        + (momentum_output, momentum_projection),
+        [(0, 0, 0, 3 * features), (1, 0, 0, features), (2, 0, 0, hidden_size)]
+        + folded(3)
+        + [(4, 0, 0, features), (5, 0, late_from, late_to - late_from)],
+        rows,
     )
     gathered = lax.all_gather(own, "dp", axis=0, tiled=True)
-    rest = jnp.concatenate(
-        [
-            momentum_projection[0, :, :features],
-            momentum_projection[0, :, 2 * features :],
-            momentum_expand[0],
-            fold_rows(momentum_contract[0], rows),
-        ],
-        axis=1,
-    )
-    rest, gathered = lax.optimization_barrier((rest, gathered))
+    rest = packed(
+        (tied(momentum_projection, own), momentum_expand, momentum_contract),
+        [(0, 0, 0, late_from), (0, 0, late_to, 3 * features - late_to), (1, 0, 0, hidden_size)]
+        + folded(2),
+        rows,
+    )
     late = lax.all_gather(rest, "dp", axis=0, tiled=True)
+
+    sizes = (2 * rows, 6 * rows, groups * rows)
+    vectors = doubled(
+        jnp.concatenate(
+            [
+                array[0].reshape(-1)
+                for array in (
+                    query_gains,
+                    query_biases,
+                    query_offsets,
+                    momentum_gains,
+                    momentum_biases,
+                    momentum_offsets,
+                )
+            ]
+        )[None]
+    ).astype(jnp.float32)
+
+    def vector_rows(start):
+        lines = vectors[:, start : start + 8 * rows].reshape(shards_of, 8, rows)
+        marks = vectors[:, start + 8 * rows : start + sum(sizes)]
+        return jnp.moveaxis(lines, 1, 0).reshape(8, features), marks.reshape(1, hidden_size)
+
+    query_lines, query_offs = vector_rows(0)
+    momentum_lines, momentum_offs = vector_rows(sum(sizes))
 
     inner = 4 * features + hidden_size
     vectors_at = inner + groups * features
-    query_lines, query_offs = vector_rows(gathered[:, vectors_at : vectors_at + 128], shards_of)
-    momentum_lines, momentum_offs = vector_rows(
-        gathered[:, vectors_at + 128 : vectors_at + 256], shards_of
-    )
     if rows != BLOCK:
         gathered = jnp.concatenate(
             [
@@ -709,9 +758,9 @@
             ],
             axis=1,
         )
-        split = 2 * features + hidden_size
+        late_end = late.shape[1] - groups * features
         late = jnp.concatenate(
-            [late[:, :split], refold(late[:, split:], shards_of, features)], axis=1
+            [late[:, :late_end], refold(late[:, late_end:], shards_of, features)], axis=1
         )
     gathered = gathered.reshape(blocks, BLOCK, -1)
     late = late.reshape(blocks, BLOCK, -1)
@@ -720,15 +769,15 @@
         ("out", 0, 3 * features, features, 0),
         ("expand", 0, 4 * features, hidden_size, 0),
     ) + tuple(("contract", 0, inner + i * features, features, i) for i in range(groups))
-    early_at = vectors_at + 256
+    late_expand = 3 * features - (late_to - late_from)
     momentum_layout = (
-        ("proj", 0, early_at + features, features, features),
-        ("proj", 1, 0, features, 0),
-        ("proj", 1, features, features, 2 * features),
-        ("out", 0, early_at, features, 0),
-        ("expand", 1, 2 * features, hidden_size, 0),
+        ("proj", 0, vectors_at + features, late_to - late_from, late_from),
+        ("proj", 1, 0, late_from, 0),
+        ("proj", 1, late_from, 3 * features - late_to, late_to),
+        ("out", 0, vectors_at, features, 0),
+        ("expand", 1, late_expand, hidden_size, 0),
     ) + tuple(
-        ("contract", 1, 2 * features + hidden_size + i * features, features, i)
+        ("contract", 1, late_expand + hidden_size + i * features, features, i)
         for i in range(groups)
     )
 
@@ -745,48 +794,53 @@
         return forward_block(
             flag,
             block_in,
-            across[0, crop : crop + 1],
-            down[0, crop : crop + 1],
+            across,
+            down,
             query_lines,
             query_offs,
             (gathered,),
             query_layout,
             True,
+            0,
+            crop,
+            1,
             kept,
         )
 
-    def query_backward(flag, gradient, weight, saved, kept=()):
+    def query_backward(flag, gradient, crop, saved, kept=()):
         return backward_block(
-            flag, gradient, weight, query_lines, (gathered,), query_layout, saved, kept
+            flag, gradient, down, query_lines, (gathered,), query_layout, saved, crop, kept
         )
 
     def momentum_forward(flag, block_in):
         return forward_block(
             flag,
             block_in,
-            across[1],
-            down[1],
+            across,
+            down,
             momentum_lines,
             momentum_offs,
             (gathered, late),
             momentum_layout,
             False,
+            1,
+            0,
+            crop_count,
         )[:2]
 
     crops = range(crop_count)
-    started = [query_forward(in_first, inputs[0, c : c + 1], c) for c in crops]
+    started = [query_forward(in_first, inputs, c) for c in crops]
     passed = [lax.ppermute(started[c][0], "section", [(0, 1)]) for c in crops]
     pools, saved, pulled, returned = [], [], [], []
     for c in crops:
         _, pool, kept = query_forward(in_second, passed[c], c, started[c][2])
         pools.append(jnp.where(first_section, started[c][1], pool))
         saved.append(kept)
-        pulled.append(query_backward(in_second, cotangent[c], down[0, c], kept))
+        pulled.append(query_backward(in_second, cotangent, c, kept))
         returned.append(lax.ppermute(pulled[c][0][2], "section", [(1, 0)]))
-    ones = jnp.ones((crop_len, 1), jnp.float32)
     vectors, marks, terms = 0.0, 0.0, []
     for c in crops:
-        ends, kept = query_backward(in_first, returned[c], ones, saved[c], pulled[c][1])
+        ends, kept = query_backward(in_first, returned[c], c, saved[c], pulled[c][1])
         terms.append(kept)
         vectors = vectors + jnp.where(first_section, ends[0], pulled[c][0][0])
         marks = marks + jnp.where(first_section, ends[1], pulled[c][0][1])
@@ -795,57 +849,62 @@
     core = lax.axis_index("dp") & 1 if rows == BLOCK else jnp.int32(0)
     core = jnp.asarray(core, jnp.int32).reshape(1)
     block_ins = [jnp.where(first_section, inputs[0, c], passed[c][0]) for c in crops]
-    contract_sums = weight_gradient(
-        contract_kernel,
-        core,
-        [kept[6] for kept in saved] + [term[1] for term in terms],
-        groups // 2,
-        features,
-        features,
-        "grad_contract",
-    )
-    expand_sums = weight_gradient(
-        functools.partial(
-            row_kernel,
-            tuple((0, 1, i * features, i // 2, i % 2 * features) for i in range(groups)),
-        ),
-        core,
-        [kept[3] for kept in saved] + [term[2] for term in terms],
-        groups // 2,
-        features,
-        features,
-        "grad_expand",
-    )
-    project_sums = weight_gradient(
-        functools.partial(
-            row_kernel,
-            (
-                (0, 1, 0, 0, 0),
-                (2, 3, 0, 0, features),
-                (2, 3, features, 1, 0),
-                (2, 3, 2 * features, 1, features),
-            ),
-        ),
-        core,
-        [kept[2] for kept in saved]
-        + [term[3] for term in terms]
-        + block_ins
-        + [term[4] for term in terms],
-        2,
-        features,
-        features,
-        "grad_projection",
-    )
-
-    def halves(sums, contracted=False):
+
+    def pairs(sums, contracted=False):
         return [
-            scattered(sums[2 * i], sums[2 * i + 1], shards_of, features, contracted)
+            first_pair(sums[2 * i], sums[2 * i + 1], shards_of, features, contracted)
             for i in range(len(sums) // 2)
         ]
 
-    contract_parts = halves(contract_sums, True)
-    expand_parts = halves(expand_sums)
-    project_parts = halves(project_sums)
+    contract_pairs = pairs(
+        weight_gradient(
+            contract_kernel,
+            core,
+            [kept[6] for kept in saved] + [term[1] for term in terms],
+            groups // 2,
+            features,
+            features,
+            "grad_contract",
+        ),
+        True,
+    )
+    expand_pairs = pairs(
+        weight_gradient(
+            functools.partial(
+                row_kernel,
+                tuple((0, 1, i * features, i // 2, i % 2 * features) for i in range(groups)),
+            ),
+            core,
+            [kept[3] for kept in saved] + [term[2] for term in terms],
+            groups // 2,
+            features,
+            features,
+            "grad_expand",
+        )
+    )
+    contract_pairs = [halved(pair, 0) for pair in contract_pairs]
+    project_pairs = pairs(
+        weight_gradient(
+            functools.partial(
+                row_kernel,
+                (
+                    (0, 1, 0, 0, 0),
+                    (2, 3, 0, 0, features),
+                    (2, 3, features, 1, 0),
+                    (2, 3, 2 * features, 1, features),
+                ),
+            ),
+            tied(core, *[pair[1] for pair in contract_pairs]),
+            [kept[2] for kept in saved]
+            + [term[3] for term in terms]
+            + block_ins
+            + [term[4] for term in terms],
+            2,
+            features,
+            features,
+            "grad_projection",
+        )
+    )
     columns = jnp.concatenate(
         [
             vectors.T.reshape(shards_of, rows, 8),
@@ -857,11 +916,21 @@
     fine = (columns - coarse.astype(jnp.float32)).astype(jnp.bfloat16)
     both = jnp.concatenate([coarse, fine], axis=2)
     both = jnp.pad(both, ((0, 0), (0, 0), (0, 128 - both.shape[2])))
-    both = halving_sum(both, 0, shards_of.bit_length() - 1).astype(jnp.float32)
-    small = (both[:, :12] + both[:, 12:24]).T
-
-    key_out, key_pool = momentum_forward(in_first, inputs[1])
+    levels = shards_of.bit_length() - 1
+    small = split(by_bits(both, levels), 0)
+    chunks = contract_pairs + [halved(pair, 0) for pair in expand_pairs + project_pairs]
+    small = halved(small, 0)
+
+    key_out, key_pool = momentum_forward(tied(in_first, *[pair[1] for pair in chunks]), inputs)
     key_in = lax.ppermute(key_out, "section", [(0, 1)])
+    chunks = [halved((tied(keep, key_pool), send), 1) for keep, send in chunks]
+    small = halved(small, 1)
+    for level in range(2, levels):
+        chunks = [halved(pair, level) for pair in chunks]
+        small = halved(small, level)
+    small = small.astype(jnp.float32)
+    small = (small[:, :12] + small[:, 12:24]).T
+
     key_pool_second = momentum_forward(in_second, key_in)[1]
     key_pool = jnp.where(first_section, key_pool, key_pool_second)
     pooled = jnp.concatenate([jnp.concatenate(pools, axis=0)[:, None], key_pool[:, None]], axis=1)
@@ -874,14 +943,16 @@
     def wide(parts):
         return jnp.concatenate(parts, axis=1).astype(jnp.float32)
 
-    contract_sum = jnp.moveaxis(wide(contract_parts).reshape(rows, groups, features), 1, 0)
-    project_sum = wide(project_parts)
+    half = groups // 2
+    contract_sum = jnp.moveaxis(wide(chunks[:half]).reshape(rows, groups, features), 1, 0)
+    expand_sum = wide(chunks[half : 2 * half])
+    project_sum = wide(chunks[2 * half :])
     return (
         pooled,
         grad_input,
         project_sum[None, :, features:],
         project_sum[None, :, :features],
-        wide(expand_parts)[None],
+        expand_sum[None],
         contract_sum.reshape(1, groups * rows, features),
         small[None, :2],
         small[None, 2:8],

time: 597 us -> 529 us (0.89)
  waiting for transfers between devices: 302 us -> 196 us
  Pallas kernels: 171 us -> 228 us
  local copies, waits for them, and re-layouts: 50.7 us -> 25.6 us
    pallas_call x10 -> x12, Pallas kernels: 142 us -> 199 us  [the longest x6 99.3 us: forward_block(): pl.pallas_call(functools.partial(forward_kernel, layout, len(packs), view...]
    ppermute x1, waiting for transfers between devices: 78.3 us -> 30.1 us  [shards(): key_in = lax.ppermute(key_out, 'section', [(0, 1)])]
    all_gather x1, waiting for transfers between devices: 84.8 us -> 52.5 us  [shards(): gathered = lax.all_gather(own, 'dp', axis=0, tiled=True)]
    ppermute x32 -> x36, waiting for transfers between devices: 109 us -> 80 us  [swapped(): return lax.ppermute(block, 'dp', route)]
    optimization_barrier x1 -> x0, local copies, waits for them, and re-layouts: 22.4 us -> none  [shards(): rest, gathered = lax.optimization_barrier((rest, gathered))]
    squeeze x29 -> x16, local copies, waits for them, and re-layouts: 7.87 us -> 0.33 us  [split(): lax.dynamic_index_in_dim(block, 1 - mine, axis, keepdims=False)]
    ppermute x32 -> x36, starting transfers between devices: 25.8 us -> 29.7 us  [swapped(): return lax.ppermute(block, 'dp', route)]
  transfers between devices with their start and end apart: 39 -> 43, of which waited for: 20 -> 26; matrix products, arithmetic and copies ran while one was open for 5% -> 7% of each run, Pallas kernels for 21% -> 38%
where the time goes in v3:
time: 529 us; the launch traced here: 519 us
  Pallas kernels  228 us (43%)
  waiting for transfers between devices  196 us (37%)
  starting transfers between devices  36.4 us (7%)
  local copies, waits for them, and re-layouts  25.6 us (5%)
  other arithmetic  18.1 us (3%)
  between operations  15.6 us (3%)
    pallas_call x6, Pallas kernels, forward_block(): pl.pallas_call(functools.partial(forward_kernel, layout, len(packs), view...  99.3 us
    ppermute x36, waiting for transfers between devices, swapped(): return lax.ppermute(block, 'dp', route)  80 us
    pallas_call x2, Pallas kernels, packed(): pl.pallas_call(functools.partial(pack_kernel, tuple(plan)), out_shape=jax...  56 us
    all_gather x1, waiting for transfers between devices, shards(): gathered = lax.all_gather(own, 'dp', axis=0, tiled=True)  52.5 us
    pallas_call x4, Pallas kernels, backward_block(): pl.pallas_call(functools.partial(backward_kernel, layout, len(packs), cro...  43.9 us
    ppermute x1, waiting for transfers between devices, shards(): key_in = lax.ppermute(key_out, 'section', [(0, 1)])  30.1 us
    ppermute x36, starting transfers between devices, swapped(): return lax.ppermute(block, 'dp', route)  29.7 us
    pallas_call x3, Pallas kernels, weight_gradient(): pl.pallas_call(kernel, out_shape=[shape] * (2 * targets), in_specs=[SMEM]...  29 us
  transfers between devices with their start and end apart: 43, of which 26 were waited for; matrix products, arithmetic and copies ran while one was open for 7% of the time, Pallas kernels for 38%

profile of v3, /device:TPU:2, one launch (start us, length us, event | category | flops | bytes accessed | tf_op | source)
XLA Modules:
  0.0 519.4 jit_solution(5316645227772727060)
XLA Ops:
  7.2 33.2 %pack.2 = bf16[48,11008]{1,0:T(8,128)(2,1)} custom-call(bf16[1,48,2304]{2,1,0:T(8,128)(2,1)} %refs_0_.1, bf16[1,48,768]{2,1,0:T(8,128)(2,1)} %refs_1_.2, bf16[1,48,3072]{2,1,0:T(8,128)(2,1)} %refs_2_.2, bf16[1,192,768]{2,1,0:T(8,128)(2,1)} %refs_3_.3, bf16[1,48,768]{2,1,0:T(8,128)(2,1)} %refs_4_.1, bf16[1,48,2304]{2,1,0:T(8,128)(2,1)} %refs_0_.2), custom_call_target="tpu_custom_call" | custom-call | tf_op jit(solution)/shard_map/pack/pallas_call | solution.py:591
  40.6 22.8 %pack.3 = bf16[48,7424]{1,0:T(8,128)(2,1)} custom-call(bf16[1,48,2304]{2,1,0:T(8,128)(2,1)} %refs_0_.2, bf16[1,48,3072]{2,1,0:T(8,128)(2,1)} %refs_1_.3, bf16[1,192,768]{2,1,0:T(8,128)(2,1)} %refs_2_.3), custom_call_target="tpu_custom_call" | custom-call | tf_op jit(solution)/shard_map/pack/pallas_call | solution.py:591
  64.0 1.1 collective-permute-done
  65.2 1.6 collective-permute-start.1
  66.8 2.2 collective-permute-done.1
  69.0 1.6 collective-permute-start.2
  70.6 2.2 collective-permute-done.2
  72.9 2.6 collective-permute-start.3
  79.7 52.5 %all-gather.3.cloned.1.call-done = bf16[768,11008]{1,0:T(8,128)(2,1)} async-done(((bf16[48,11008]{1,0:T(8,128)(2,1)}), bf16[768,11008]{1,0:T(8,128)(2,1)}) %all-gather.3.cloned.1.call-update) | async-done | bytes 16908304 | tf_op jit(solution)/shard_map/all_gather | solution.py:716
  132.1 2.0 forward_save.6
  134.1 1.3 collective-permute-start.5
  137.0 2.0 forward_save.4
  139.0 1.3 collective-permute-start.4
  140.3 28.3 %collective-permute-done.5.refs_5_ = bf16[1,256,768]{2,1,0:T(8,128)(2,1)S(1)} collective-permute-done((bf16[1,256,768]{2,1,0:T(8,128)(2,1)}, bf16[1,256,768]{2,1,0:T(8,128)(2,1)S(1)}, u32[]{:S(2)}, u32[]{:S(2)}) %collective-permute-start.5) | collective-permute-done | bytes 393248 | tf_op jit(solution)/shard_map/ppermute | solution.py:833
  169.3 25.9 %forward_save.7 = (bf16[1,256,768]{2,1,0:T(8,128)(2,1)}, f32[1,1,768]{2,1,0:T(1,128)}, bf16[256,2304]{1,0:T(8,128)(2,1)}, bf16[12,256,256]{2,1,0:T(8,128)(2,1)},...) custom-call(s32[1]{0:T(128)S(6)} %sub.12.refs_0_, ...), custom_call_target="tpu_custom_call", output_to_operand_aliasing={{2}: (7, {}), {3}: (8, {}), {4}: (9, {}), {5}: (10, {}), {6... | custom-call | flops 3623878656 | bytes 20000000 | tf_op jit(solution)/shard_map/forward_save/pallas_call | solution.py:239
  195.3 19.8 %backward_data.6 = (f32[8,768]{1,0:T(8,128)}, f32[1,3072]{1,0:T(1,128)}, bf16[256,768]{1,0:T(8,128)(2,1)}, f32[256,768]{1,0:T(8,128)}, bf16[256,768]{1,0:T(8,128...) custom-call(s32[1]{0:T(128)S(6)} %sub.12.refs_0_, ...), custom_call_target="tpu_custom_call" | custom-call | flops 3623878656 | bytes 25000000 | tf_op jit(solution)/shard_map/backward_data/pallas_call | solution.py:463
  215.0 1.3 collective-permute-start.7
  217.1 25.4 %forward_save.5 = (bf16[1,256,768]{2,1,0:T(8,128)(2,1)}, f32[1,1,768]{2,1,0:T(1,128)}, bf16[256,2304]{1,0:T(8,128)(2,1)}, bf16[12,256,256]{2,1,0:T(8,128)(2,1)},...) custom-call(s32[1]{0:T(128)S(6)} %sub.12.refs_0_, ...), custom_call_target="tpu_custom_call", output_to_operand_aliasing={{2}: (7, {}), {3}: (8, {}), {4}: (9, {}), {5}: (10, {}), {6... | custom-call | flops 3623878656 | bytes 20000000 | tf_op jit(solution)/shard_map/forward_save/pallas_call | solution.py:239
  242.5 19.9 %backward_data.4 = (f32[8,768]{1,0:T(8,128)}, f32[1,3072]{1,0:T(1,128)}, bf16[256,768]{1,0:T(8,128)(2,1)}, f32[256,768]{1,0:T(8,128)}, bf16[256,768]{1,0:T(8,128...) custom-call(s32[1]{0:T(128)S(6)} %sub.12.refs_0_, ...), custom_call_target="tpu_custom_call" | custom-call | flops 3623878656 | bytes 25000000 | tf_op jit(solution)/shard_map/backward_data/pallas_call | solution.py:463
  262.5 1.3 collective-permute-start.6
  265.6 2.1 backward_data.7
  267.8 4.7 collective-permute-done.6.refs_3_
  273.2 2.0 backward_data.5
  276.1 1.3 collective-permute-done.37
  277.4 1.3 collective-permute-start.38
  278.6 9.7 %grad_contract.1 = (bf16[8,48,1536]{2,1,0:T(8,128)(2,1)}, bf16[8,48,1536]{2,1,0:T(8,128)(2,1)}, bf16[8,48,1536]{2,1,0:T(8,128)(2,1)}, bf16[8,48,1536]{2,1,0:T(8,128)(2,1)}) custom-call(s32[1]{0:T(128)} %bitcast.5.core, bf16[256,3072]{1,0:T(8,128)(2,1)} %get-tuple-element.135.refs_11_.act0, bf16[256,3072]{1,0:T(8,128)(2,1)} %get-tuple-element.136.refs_11_.act1, ...), custom_call_target="tpu_custom_call" | custom-call | flops 2415919104 | bytes 9000000 | tf_op jit(solution)/shard_map/grad_contract/pallas_call | solution.py:554
  288.9 2.0 collective-permute-start.39
  290.9 9.4 %grad_expand.1 = (bf16[8,48,1536]{2,1,0:T(8,128)(2,1)}, bf16[8,48,1536]{2,1,0:T(8,128)(2,1)}, bf16[8,48,1536]{2,1,0:T(8,128)(2,1)}, bf16[8,48,1536]{2,1,0:T(8,128)(2,1)}) custom-call(s32[1]{0:T(128)} %bitcast.5.core, bf16[256,768]{1,0:T(8,128)(2,1)} %get-tuple-element.140.refs_8_.refs_0_, bf16[256,768]{1,0:T(8,128)(2,1)} %get-tuple-element.156.refs_8_.refs_1_, ...), custom_call_target="tpu_custom_call" | custom-call | flops 2415919104 | bytes 9000000 | tf_op jit(solution)/shard_map/grad_expand/pallas_call | solution.py:554
  301.8 1.2 maximum_bitcast_fusion
  303.1 2.5 collective-permute-done.40
  307.0 1.4 copy.229
  309.9 1.4 copy.226
  311.2 1.7 fusion.5
  312.9 1.6 fusion.4
  318.5 9.8 %grad_projection.1 = (bf16[8,48,1536]{2,1,0:T(8,128)(2,1)}, bf16[8,48,1536]{2,1,0:T(8,128)(2,1)}, bf16[8,48,1536]{2,1,0:T(8,128)(2,1)}, bf16[8,48,1536]{2,1,0:T(8,128)(2,1)}) custom-call(s32[1]{0:T(128)} %bitcast.5.core, bf16[256,768]{1,0:T(8,128)(2,1)} %get-tuple-element.139.refs_7_.refs_0_, bf16[256,768]{1,0:T(8,128)(2,1)} %get-tuple-element.155.refs_7_.refs_1_, ...), custom_call_target="tpu_custom_call" | custom-call | flops 2415919104 | bytes 9000000 | tf_op jit(solution)/shard_map/grad_projection/pallas_call | solution.py:554
  333.5 1.2 collective-permute-start.28
  338.8 2.1 forward_only.2
  341.0 1.2 collective-permute-start.22
  342.1 1.2 add_convert_fusion.1
  343.4 2.3 collective-permute-done.34
  345.8 1.2 add_convert_fusion
  347.0 11.3 %collective-permute-done.25 = bf16[2,2,48,1536]{3,2,0,1:T(8,128)(2,1)} collective-permute-done((bf16[2,2,48,1536]{3,2,0,1:T(8,128)(2,1)}, bf16[2,2,48,1536]{3,2,0,1:T(8,128)(2,1)}, u32[]{:S(2)}, u32[]{:S(2)}) %collective-permute-start.25) | collective-permute-done | bytes 589856 | tf_op jit(solution)/shard_map/ppermute | solution.py:621
  358.4 1.2 add_convert_fusion.3
  359.7 11.3 %collective-permute-done.28 = bf16[2,2,48,1536]{3,2,0,1:T(8,128)(2,1)} collective-permute-done((bf16[2,2,48,1536]{3,2,0,1:T(8,128)(2,1)}, bf16[2,2,48,1536]{3,2,0,1:T(8,128)(2,1)}, u32[]{:S(2)}, u32[]{:S(2)}) %collective-permute-start.28) | collective-permute-done | bytes 589856 | tf_op jit(solution)/shard_map/ppermute | solution.py:621
  371.1 1.2 add_convert_fusion.2
  372.4 2.0 collective-permute-start.29
  374.5 1.5 collective-permute-start.14
  376.1 4.3 collective-permute-done.26
  381.4 4.0 collective-permute-done.29
  385.4 1.9 collective-permute-start.36
  387.3 6.7 %collective-permute-done.33 = bf16[48,1536]{1,0:T(8,128)(2,1)S(1)} collective-permute-done((bf16[48,1536]{1,0:T(8,128)(2,1)S(1)}, bf16[48,1536]{1,0:T(8,128)(2,1)S(1)}, u32[]{:S(2)}, u32[]{:S(2)}) %collective-permute-start.33) | collective-permute-done | bytes 147488 | tf_op jit(solution)/shard_map/ppermute | solution.py:621
  394.1 3.1 collective-permute-done.36
  397.2 5.1 collective-permute-done.27
  404.8 1.2 add_convert_fusion.5
  406.0 30.1 %collective-permute-done.14.refs_5_ = bf16[2,256,768]{2,1,0:T(8,128)(2,1)S(1)} collective-permute-done((bf16[2,256,768]{2,1,0:T(8,128)(2,1)}, bf16[2,256,768]{2,1,0:T(8,128)(2,1)S(1)}, u32[]{:S(2)}, u32[]{:S(2)}) %collective-permute-start.14) | collective-permute-done | bytes 786464 | tf_op jit(solution)/shard_map/ppermute | solution.py:925
  437.1 41.9 %forward_only.3 = (bf16[2,256,768]{2,1,0:T(8,128)(2,1)}, f32[2,1,768]{2,1,0:T(1,128)}) custom-call(s32[1]{0:T(128)S(6)} %sub.12.refs_0_, f32[2,2,1,256]{3,2,1,0:T(1,128)} %broadcast_in_dim.61.refs_1_, f32[2,2,256,1]{3,2,1,0:T(8,128)} %copy.200.refs_2_.refs_1_, f32[8,768]{1,0:T(8,128)} %reshape.208.refs_3_, f32[1,3072]{1,0:T(1,128)} %reshape.209.refs_4_, ...), custom_call_target="tpu_custom_call" | custom-call | flops 7247757312 | bytes 20000000 | tf_op jit(solution)/shard_map/forward_only/pallas_call | solution.py:239
  482.1 1.2 add_convert_fusion.4
  483.3 1.7 collective-permute-done.16
  487.2 3.6 collective-permute-done.17
  492.0 2.1 collective-permute-start.21
  494.1 6.2 %collective-permute-done.23 = bf16[2,48,1536]{2,1,0:T(8,128)(2,1)S(1)} collective-permute-done((bf16[2,48,1536]{2,1,0:T(8,128)(2,1)S(1)}, bf16[2,48,1536]{2,1,0:T(8,128)(2,1)S(1)}, u32[]{:S(2)}, u32[]{:S(2)}) %collective-permute-start.23) | collective-permute-done | bytes 294944 | tf_op jit(solution)/shard_map/ppermute | solution.py:621
  500.4 5.5 %collective-permute-done.18 = f32[16,1536]{1,0:T(8,128)S(1)} collective-permute-done((f32[16,1536]{1,0:T(8,128)S(1)}, f32[16,1536]{1,0:T(8,128)S(1)}, u32[]{:S(2)}, u32[]{:S(2)}) %collective-permute-start.18) | collective-permute-done | bytes 98336 | tf_op jit(solution)/shard_map/ppermute | solution.py:621
  506.8 2.2 collective-permute-done.21
  509.1 1.6 collective-permute-done.24
  (248 shorter events, 43.5 us)
Async XLA Ops:
  7.2 125.0 %all-gather.3.cloned.1.call-start = ((), (), s32[]{:S(2)}) async-start(), calls=%async_computation | async-start | bytes 17965056 | tf_op jit(solution)/shard_map/all_gather | solution.py:716
  40.5 22.9 %copy-start.30 = (bf16[1,6,48]{2,1,0:T(8,128)(2,1)S(1)}, bf16[1,6,48]{2,1,0:T(8,128)(2,1)}, u32[]{:S(2)}) copy-start(bf16[1,6,48]{2,1,0:T(8,128)(2,1)} %param.29) | copy-start | bytes 1732
  40.5 23.0 %copy-start.31 = (bf16[1,6,48]{2,1,0:T(8,128)(2,1)S(1)}, bf16[1,6,48]{2,1,0:T(8,128)(2,1)}, u32[]{:S(2)}) copy-start(bf16[1,6,48]{2,1,0:T(8,128)(2,1)} %param.36) | copy-start | bytes 1732
  40.5 23.1 %copy-start.32 = (bf16[1,192]{1,0:T(2,128)(2,1)S(1)}, bf16[1,192]{1,0:T(2,128)(2,1)}, u32[]{:S(2)}) copy-start(bf16[1,192]{1,0:T(2,128)(2,1)} %param.30) | copy-start | bytes 1156
  40.5 23.1 %copy-start.33 = (bf16[1,192]{1,0:T(2,128)(2,1)S(1)}, bf16[1,192]{1,0:T(2,128)(2,1)}, u32[]{:S(2)}) copy-start(bf16[1,192]{1,0:T(2,128)(2,1)} %param.37) | copy-start | bytes 1156
  40.5 23.1 %copy-start.34 = (bf16[1,2,48]{2,1,0:T(2,128)(2,1)S(1)}, bf16[1,2,48]{2,1,0:T(2,128)(2,1)}, u32[]{:S(2)}) copy-start(bf16[1,2,48]{2,1,0:T(2,128)(2,1)} %param.28) | copy-start | bytes 580
  40.5 23.2 %copy-start.35 = (bf16[1,2,48]{2,1,0:T(2,128)(2,1)S(1)}, bf16[1,2,48]{2,1,0:T(2,128)(2,1)}, u32[]{:S(2)}) copy-start(bf16[1,2,48]{2,1,0:T(2,128)(2,1)} %param.35) | copy-start | bytes 580
  40.5 30.0 %copy-start.20 = (s32[2,2,256]{2,1,0:T(2,128)S(1)}, s32[2,2,256]{2,1,0:T(2,128)}, u32[]{:S(2)}) copy-start(s32[2,2,256]{2,1,0:T(2,128)} %param.20) | copy-start | bytes 12292
  40.5 30.0 %copy-start.25 = (s32[2,2]{1,0:T(2,128)S(1)}, s32[2,2]{1,0:T(2,128)}, u32[]{:S(2)}) copy-start(s32[2,2]{1,0:T(2,128)} %param.21) | copy-start | bytes 52
  40.6 298.2 %all-gather.5.cloned.1.call-start = ((), (), s32[]{:S(2)}) async-start(), calls=%async_computation.1 | async-start | bytes 12115968 | tf_op jit(solution)/shard_map/all_gather | solution.py:723
  63.9 1.2 collective-permute-start
  65.2 3.7 collective-permute-start.1
  69.0 3.9 collective-permute-start.2
  72.9 5.1 collective-permute-start.3
  132.1 3.3 copy-start.36
  134.1 34.5 %collective-permute-start.5 = (bf16[1,256,768]{2,1,0:T(8,128)(2,1)}, bf16[1,256,768]{2,1,0:T(8,128)(2,1)S(1)}, u32[]{:S(2)}, u32[]{:S(2)}) collective-permute-start(bf16[1,256,768]{2,1,0:T(8,128)(2,1)} %get-tuple-element.123), channel_id=1, source_target_pairs={{0,16},{1,17},{2,18},{3,19},{4,20},{5,21},{6,22},{7,23},{8,24},{9,... | collective-permute-start | bytes 1179656 | tf_op jit(solution)/shard_map/ppermute | solution.py:833
  139.0 77.4 %collective-permute-start.4 = (bf16[1,256,768]{2,1,0:T(8,128)(2,1)}, bf16[1,256,768]{2,1,0:T(8,128)(2,1)S(1)}, u32[]{:S(2)}, u32[]{:S(2)}) collective-permute-start(bf16[1,256,768]{2,1,0:T(8,128)(2,1)} %get-tuple-element.110), channel_id=1, source_target_pairs={{0,16},{1,17},{2,18},{3,19},{4,20},{5,21},{6,22},{7,23},{8,24},{9,... | collective-permute-start | bytes 1179656 | tf_op jit(solution)/shard_map/ppermute | solution.py:833
  215.0 49.8 %collective-permute-start.7 = (bf16[256,768]{1,0:T(8,128)(2,1)}, bf16[256,768]{1,0:T(8,128)(2,1)S(1)}, u32[]{:S(2)}, u32[]{:S(2)}) collective-permute-start(bf16[256,768]{1,0:T(8,128)(2,1)} %get-tuple-element.162), channel_id=1, source_target_pairs={{16,0},{17,1},{18,2},{19,3},{20,4},{21,5},{22,6},{23,7},{24,8},{25... | collective-permute-start | bytes 1179656 | tf_op jit(solution)/shard_map/ppermute | solution.py:840
  242.5 21.3 %copy-start = (bf16[2,2,256,768]{3,2,1,0:T(8,128)(2,1)S(1)}, bf16[2,2,256,768]{3,2,1,0:T(8,128)(2,1)}, u32[]{:S(2)}) copy-start(bf16[2,2,256,768]{3,2,1,0:T(8,128)(2,1)} %refs_5_.7) | copy-start | bytes 4718596
  242.5 21.3 %copy-start.4 = (bf16[1,256,768]{2,1,0:T(8,128)(2,1)S(1)}, bf16[1,256,768]{2,1,0:T(8,128)(2,1)}, u32[]{:S(2)}) copy-start(bf16[1,256,768]{2,1,0:T(8,128)(2,1)} %copy-done.3) | copy-start | bytes 1179652
  242.5 21.3 %copy-start.6 = (bf16[1,256,768]{2,1,0:T(8,128)(2,1)S(1)}, bf16[1,256,768]{2,1,0:T(8,128)(2,1)}, u32[]{:S(2)}) copy-start(bf16[1,256,768]{2,1,0:T(8,128)(2,1)} %copy-done.5) | copy-start | bytes 1179652
  262.5 2.4 copy-start.26
  262.5 2.4 copy-start.27
  262.5 2.3 copy-start.28
  262.5 2.3 copy-start.29
  262.5 10.0 %collective-permute-start.6 = (bf16[256,768]{1,0:T(8,128)(2,1)}, bf16[256,768]{1,0:T(8,128)(2,1)S(1)}, u32[]{:S(2)}, u32[]{:S(2)}) collective-permute-start(bf16[256,768]{1,0:T(8,128)(2,1)} %get-tuple-element.146), channel_id=1, source_target_pairs={{16,0},{17,1},{18,2},{19,3},{20,4},{21,5},{22,6},{23,7},{24,8},{25... | collective-permute-start | bytes 1179656 | tf_op jit(solution)/shard_map/ppermute | solution.py:840
  276.0 1.4 collective-permute-start.37
  277.4 11.5 %collective-permute-start.38 = (bf16[2,2,48,128]{3,2,1,0:T(8,128)(2,1)S(1)}, bf16[2,2,48,128]{3,2,1,0:T(8,128)(2,1)S(1)}, u32[]{:S(2)}, u32[]{:S(2)}) collective-permute-start(bf16[2,2,48,128]{3,2,1,0:T(8,128)(2,1)S(1)} %dynamic-slice_bitcast_fusion.13), channel_id=1, source_target_pairs={{0,2},{1,3},{2,0},{3,1},{4,6},{5,7},{6,4},{7,5},{8,10},{9,11},{10,... | collective-permute-start | bytes 147464 | tf_op jit(solution)/shard_map/ppermute | solution.py:621
  288.3 22.9 %collective-permute-start.8 = (bf16[2,2,2,48,1536]{4,3,2,1,0:T(8,128)(2,1)}, bf16[2,2,2,48,1536]{4,3,2,1,0:T(8,128)(2,1)}, u32[]{:S(2)}, u32[]{:S(2)}) collective-permute-start(bf16[2,2,2,48,1536]{4,3,2,1,0:T(8,128)(2,1)} %bitcast.235), channel_id=1, source_target_pairs={{0,1},{1,0},{2,3},{3,2},{4,5},{5,4},{6,7},{7,6},{8,9},{9,8},{10,11... | collective-permute-start | bytes 3538952 | tf_op jit(solution)/shard_map/ppermute | solution.py:621
  288.3 24.6 %collective-permute-start.9 = (bf16[2,2,2,48,1536]{4,3,2,1,0:T(8,128)(2,1)}, bf16[2,2,2,48,1536]{4,3,2,1,0:T(8,128)(2,1)}, u32[]{:S(2)}, u32[]{:S(2)}) collective-permute-start(bf16[2,2,2,48,1536]{4,3,2,1,0:T(8,128)(2,1)} %bitcast.234), channel_id=1, source_target_pairs={{0,1},{1,0},{2,3},{3,2},{4,5},{5,4},{6,7},{7,6},{8,9},{9,8},{10,11... | collective-permute-start | bytes 3538952 | tf_op jit(solution)/shard_map/ppermute | solution.py:621
  288.9 12.0 %collective-permute-start.39 = (bf16[2,48,128]{2,1,0:T(8,128)(2,1)S(1)}, bf16[2,48,128]{2,1,0:T(8,128)(2,1)S(1)}, u32[]{:S(2)}, u32[]{:S(2)}) collective-permute-start(bf16[2,48,128]{2,1,0:T(8,128)(2,1)S(1)} %dynamic-slice_bitcast_fusion.14), channel_id=1, source_target_pairs={{0,4},{1,5},{2,6},{3,7},{4,0},{5,1},{6,2},{7,3},{8,12},{9,13},{10,... | collective-permute-start | bytes 73736 | tf_op jit(solution)/shard_map/ppermute | solution.py:621
  290.9 10.9 %copy-start.1 = (f32[256,768]{1,0:T(8,128)S(1)}, f32[256,768]{1,0:T(8,128)}, u32[]{:S(2)}) copy-start(f32[256,768]{1,0:T(8,128)} %get-tuple-element.194) | copy-start | bytes 2359300
  290.9 10.9 %copy-start.2 = (f32[256,768]{1,0:T(8,128)S(1)}, f32[256,768]{1,0:T(8,128)}, u32[]{:S(2)}) copy-start(f32[256,768]{1,0:T(8,128)} %get-tuple-element.193) | copy-start | bytes 2359300
  300.3 28.0 %collective-permute-start.10 = (bf16[2,2,2,48,1536]{4,3,2,1,0:T(8,128)(2,1)}, bf16[2,2,2,48,1536]{4,3,2,1,0:T(8,128)(2,1)S(1)}, u32[]{:S(2)}, u32[]{:S(2)}) collective-permute-start(bf16[2,2,2,48,1536]{4,3,2,1,0:T(8,128)(2,1)} %bitcast.233), channel_id=1, source_target_pairs={{0,1},{1,0},{2,3},{3,2},{4,5},{5,4},{6,7},{7,6},{8,9},{9,8},{10,11... | collective-permute-start | bytes 3538952 | tf_op jit(solution)/shard_map/ppermute | solution.py:621
  300.3 28.8 %collective-permute-start.11 = (bf16[2,2,2,48,1536]{4,3,2,1,0:T(8,128)(2,1)}, bf16[2,2,2,48,1536]{4,3,2,1,0:T(8,128)(2,1)S(1)}, u32[]{:S(2)}, u32[]{:S(2)}) collective-permute-start(bf16[2,2,2,48,1536]{4,3,2,1,0:T(8,128)(2,1)} %bitcast.232), channel_id=1, source_target_pairs={{0,1},{1,0},{2,3},{3,2},{4,5},{5,4},{6,7},{7,6},{8,9},{9,8},{10,11... | collective-permute-start | bytes 3538952 | tf_op jit(solution)/shard_map/ppermute | solution.py:621
  300.9 4.7 collective-permute-start.40
  301.8 9.4 %copy-start.10 = (bf16[8,48,1536]{2,1,0:T(8,128)(2,1)S(1)}, bf16[8,48,1536]{2,1,0:T(8,128)(2,1)}, u32[]{:S(2)}) copy-start(bf16[8,48,1536]{2,1,0:T(8,128)(2,1)} %get-tuple-element.169) | copy-start | bytes 3538948
  316.5 24.5 %collective-permute-start.31 = (bf16[2,2,48,1536]{3,2,0,1:T(8,128)(2,1)}, bf16[2,2,48,1536]{3,2,0,1:T(8,128)(2,1)}, u32[]{:S(2)}, u32[]{:S(2)}) collective-permute-start(bf16[2,2,48,1536]{3,2,0,1:T(8,128)(2,1)} %bitcast.190), channel_id=1, source_target_pairs={{0,2},{1,3},{2,0},{3,1},{4,6},{5,7},{6,4},{7,5},{8,10},{9,11},{10,... | collective-permute-start | bytes 1769480 | tf_op jit(solution)/shard_map/ppermute | solution.py:621
  317.4 28.3 %collective-permute-start.34 = (bf16[2,2,48,1536]{3,2,0,1:T(8,128)(2,1)}, bf16[2,2,48,1536]{3,2,0,1:T(8,128)(2,1)}, u32[]{:S(2)}, u32[]{:S(2)}) collective-permute-start(bf16[2,2,48,1536]{3,2,0,1:T(8,128)(2,1)} %bitcast.189), channel_id=1, source_target_pairs={{0,2},{1,3},{2,0},{3,1},{4,6},{5,7},{6,4},{7,5},{8,10},{9,11},{10,... | collective-permute-start | bytes 1769480 | tf_op jit(solution)/shard_map/ppermute | solution.py:621
  318.5 10.3 %copy-start.8 = (bf16[8,48,1536]{2,1,0:T(8,128)(2,1)S(1)}, bf16[8,48,1536]{2,1,0:T(8,128)(2,1)}, u32[]{:S(2)}) copy-start(bf16[8,48,1536]{2,1,0:T(8,128)(2,1)} %get-tuple-element.175) | copy-start | bytes 3538948
  328.3 5.2 %collective-permute-start.13 = (bf16[2,2,2,48,1536]{4,3,2,1,0:T(8,128)(2,1)}, bf16[2,2,2,48,1536]{4,3,2,1,0:T(8,128)(2,1)S(1)}, u32[]{:S(2)}, u32[]{:S(2)}) collective-permute-start(bf16[2,2,2,48,1536]{4,3,2,1,0:T(8,128)(2,1)} %bitcast.237), channel_id=1, source_target_pairs={{0,1},{1,0},{2,3},{3,2},{4,5},{5,4},{6,7},{7,6},{8,9},{9,8},{10,11... | collective-permute-start | bytes 3538952 | tf_op jit(solution)/shard_map/ppermute | solution.py:621
  328.3 7.7 %collective-permute-start.12 = (bf16[2,2,2,48,1536]{4,3,2,1,0:T(8,128)(2,1)}, bf16[2,2,2,48,1536]{4,3,2,1,0:T(8,128)(2,1)S(1)}, u32[]{:S(2)}, u32[]{:S(2)}) collective-permute-start(bf16[2,2,2,48,1536]{4,3,2,1,0:T(8,128)(2,1)} %bitcast.236), channel_id=1, source_target_pairs={{0,1},{1,0},{2,3},{3,2},{4,5},{5,4},{6,7},{7,6},{8,9},{9,8},{10,11... | collective-permute-start | bytes 3538952 | tf_op jit(solution)/shard_map/ppermute | solution.py:621
  332.5 25.8 %collective-permute-start.25 = (bf16[2,2,48,1536]{3,2,0,1:T(8,128)(2,1)}, bf16[2,2,48,1536]{3,2,0,1:T(8,128)(2,1)}, u32[]{:S(2)}, u32[]{:S(2)}) collective-permute-start(bf16[2,2,48,1536]{3,2,0,1:T(8,128)(2,1)} %bitcast.188), channel_id=1, source_target_pairs={{0,2},{1,3},{2,0},{3,1},{4,6},{5,7},{6,4},{7,5},{8,10},{9,11},{10,... | collective-permute-start | bytes 1769480 | tf_op jit(solution)/shard_map/ppermute | solution.py:621
  333.5 37.4 %collective-permute-start.28 = (bf16[2,2,48,1536]{3,2,0,1:T(8,128)(2,1)}, bf16[2,2,48,1536]{3,2,0,1:T(8,128)(2,1)}, u32[]{:S(2)}, u32[]{:S(2)}) collective-permute-start(bf16[2,2,48,1536]{3,2,0,1:T(8,128)(2,1)} %bitcast.187), channel_id=1, source_target_pairs={{0,2},{1,3},{2,0},{3,1},{4,6},{5,7},{6,4},{7,5},{8,10},{9,11},{10,... | collective-permute-start | bytes 1769480 | tf_op jit(solution)/shard_map/ppermute | solution.py:621
  337.9 66.9 %collective-permute-start.19 = (bf16[2,2,48,1536]{3,2,0,1:T(8,128)(2,1)}, bf16[2,2,48,1536]{3,2,0,1:T(8,128)(2,1)}, u32[]{:S(2)}, u32[]{:S(2)}) collective-permute-start(bf16[2,2,48,1536]{3,2,0,1:T(8,128)(2,1)} %bitcast.186), channel_id=1, source_target_pairs={{0,2},{1,3},{2,0},{3,1},{4,6},{5,7},{6,4},{7,5},{8,10},{9,11},{10,... | collective-permute-start | bytes 1769480 | tf_op jit(solution)/shard_map/ppermute | solution.py:621
  341.0 141.1 %collective-permute-start.22 = (bf16[2,2,48,1536]{3,2,0,1:T(8,128)(2,1)}, bf16[2,2,48,1536]{3,2,0,1:T(8,128)(2,1)}, u32[]{:S(2)}, u32[]{:S(2)}) collective-permute-start(bf16[2,2,48,1536]{3,2,0,1:T(8,128)(2,1)} %bitcast.185), channel_id=1, source_target_pairs={{0,2},{1,3},{2,0},{3,1},{4,6},{5,7},{6,4},{7,5},{8,10},{9,11},{10,... | collective-permute-start | bytes 1769480 | tf_op jit(solution)/shard_map/ppermute | solution.py:621
  345.7 26.7 %collective-permute-start.32 = (bf16[2,48,1536]{2,1,0:T(8,128)(2,1)S(1)}, bf16[2,48,1536]{2,1,0:T(8,128)(2,1)S(1)}, u32[]{:S(2)}, u32[]{:S(2)}) collective-permute-start(bf16[2,48,1536]{2,1,0:T(8,128)(2,1)S(1)} %dynamic-slice_bitcast_fusion.1), channel_id=1, source_target_pairs={{0,4},{1,5},{2,6},{3,7},{4,0},{5,1},{6,2},{7,3},{8,12},{9,13},{10,... | collective-permute-start | bytes 884744 | tf_op jit(solution)/shard_map/ppermute | solution.py:621
  358.3 16.2 %collective-permute-start.35 = (bf16[2,48,1536]{2,1,0:T(8,128)(2,1)S(1)}, bf16[2,48,1536]{2,1,0:T(8,128)(2,1)S(1)}, u32[]{:S(2)}, u32[]{:S(2)}) collective-permute-start(bf16[2,48,1536]{2,1,0:T(8,128)(2,1)S(1)} %dynamic-slice_bitcast_fusion), channel_id=1, source_target_pairs={{0,4},{1,5},{2,6},{3,7},{4,0},{5,1},{6,2},{7,3},{8,12},{9,13},{10,... | collective-permute-start | bytes 884744 | tf_op jit(solution)/shard_map/ppermute | solution.py:621
  371.0 9.4 %collective-permute-start.26 = (bf16[2,48,1536]{2,1,0:T(8,128)(2,1)S(1)}, bf16[2,48,1536]{2,1,0:T(8,128)(2,1)S(1)}, u32[]{:S(2)}, u32[]{:S(2)}) collective-permute-start(bf16[2,48,1536]{2,1,0:T(8,128)(2,1)S(1)} %dynamic-slice_bitcast_fusion.3), channel_id=1, source_target_pairs={{0,4},{1,5},{2,6},{3,7},{4,0},{5,1},{6,2},{7,3},{8,12},{9,13},{10,... | collective-permute-start | bytes 884744 | tf_op jit(solution)/shard_map/ppermute | solution.py:621
  372.4 12.9 %collective-permute-start.29 = (bf16[2,48,1536]{2,1,0:T(8,128)(2,1)S(1)}, bf16[2,48,1536]{2,1,0:T(8,128)(2,1)S(1)}, u32[]{:S(2)}, u32[]{:S(2)}) collective-permute-start(bf16[2,48,1536]{2,1,0:T(8,128)(2,1)S(1)} %dynamic-slice_bitcast_fusion.2), channel_id=1, source_target_pairs={{0,4},{1,5},{2,6},{3,7},{4,0},{5,1},{6,2},{7,3},{8,12},{9,13},{10,... | collective-permute-start | bytes 884744 | tf_op jit(solution)/shard_map/ppermute | solution.py:621
  374.5 61.7 %collective-permute-start.14 = (bf16[2,256,768]{2,1,0:T(8,128)(2,1)}, bf16[2,256,768]{2,1,0:T(8,128)(2,1)S(1)}, u32[]{:S(2)}, u32[]{:S(2)}) collective-permute-start(bf16[2,256,768]{2,1,0:T(8,128)(2,1)} %get-tuple-element.191), channel_id=1, source_target_pairs={{0,16},{1,17},{2,18},{3,19},{4,20},{5,21},{6,22},{7,23},{8,24},{9,... | collective-permute-start | bytes 2359304 | tf_op jit(solution)/shard_map/ppermute | solution.py:925
  380.4 13.7 %collective-permute-start.33 = (bf16[48,1536]{1,0:T(8,128)(2,1)S(1)}, bf16[48,1536]{1,0:T(8,128)(2,1)S(1)}, u32[]{:S(2)}, u32[]{:S(2)}) collective-permute-start(bf16[48,1536]{1,0:T(8,128)(2,1)S(1)} %dynamic-slice_bitcast_fusion.7), channel_id=1, source_target_pairs={{0,8},{1,9},{2,10},{3,11},{4,12},{5,13},{6,14},{7,15},{8,0},{9,1},... | collective-permute-start | bytes 442376 | tf_op jit(solution)/shard_map/ppermute | solution.py:621
  385.4 11.8 %collective-permute-start.36 = (bf16[48,1536]{1,0:T(8,128)(2,1)S(1)}, bf16[48,1536]{1,0:T(8,128)(2,1)S(1)}, u32[]{:S(2)}, u32[]{:S(2)}) collective-permute-start(bf16[48,1536]{1,0:T(8,128)(2,1)S(1)} %dynamic-slice_bitcast_fusion.6), channel_id=1, source_target_pairs={{0,8},{1,9},{2,10},{3,11},{4,12},{5,13},{6,14},{7,15},{8,0},{9,1},... | collective-permute-start | bytes 442376 | tf_op jit(solution)/shard_map/ppermute | solution.py:621
  394.1 8.3 %collective-permute-start.27 = (bf16[48,1536]{1,0:T(8,128)(2,1)S(1)}, bf16[48,1536]{1,0:T(8,128)(2,1)S(1)}, u32[]{:S(2)}, u32[]{:S(2)}) collective-permute-start(bf16[48,1536]{1,0:T(8,128)(2,1)S(1)} %dynamic-slice_bitcast_fusion.9), channel_id=1, source_target_pairs={{0,8},{1,9},{2,10},{3,11},{4,12},{5,13},{6,14},{7,15},{8,0},{9,1},... | collective-permute-start | bytes 442376 | tf_op jit(solution)/shard_map/ppermute | solution.py:621
  397.2 6.7 %collective-permute-start.30 = (bf16[48,1536]{1,0:T(8,128)(2,1)S(1)}, bf16[48,1536]{1,0:T(8,128)(2,1)S(1)}, u32[]{:S(2)}, u32[]{:S(2)}) collective-permute-start(bf16[48,1536]{1,0:T(8,128)(2,1)S(1)} %dynamic-slice_bitcast_fusion.8), channel_id=1, source_target_pairs={{0,8},{1,9},{2,10},{3,11},{4,12},{5,13},{6,14},{7,15},{8,0},{9,1},... | collective-permute-start | bytes 442376 | tf_op jit(solution)/shard_map/ppermute | solution.py:621
  406.0 73.0 %copy-start.24 = (f32[2,1,768]{2,1,0:T(1,128)S(1)}, f32[2,1,768]{2,1,0:T(1,128)}, u32[]{:S(2)}) copy-start(f32[2,1,768]{2,1,0:T(1,128)} %get-tuple-element.190) | copy-start | bytes 18436
  479.8 1.2 collective-permute-start.15
  479.9 12.0 %collective-permute-start.20 = (bf16[2,48,1536]{2,1,0:T(8,128)(2,1)S(1)}, bf16[2,48,1536]{2,1,0:T(8,128)(2,1)S(1)}, u32[]{:S(2)}, u32[]{:S(2)}) collective-permute-start(bf16[2,48,1536]{2,1,0:T(8,128)(2,1)S(1)} %dynamic-slice_bitcast_fusion.5), channel_id=1, source_target_pairs={{0,4},{1,5},{2,6},{3,7},{4,0},{5,1},{6,2},{7,3},{8,12},{9,13},{10,... | collective-permute-start | bytes 884744 | tf_op jit(solution)/shard_map/ppermute | solution.py:621
  481.1 3.9 collective-permute-start.16
  485.1 5.8 %collective-permute-start.17 = (f32[8,1536]{1,0:T(8,128)S(1)}, f32[8,1536]{1,0:T(8,128)S(1)}, u32[]{:S(2)}, u32[]{:S(2)}) collective-permute-start(f32[8,1536]{1,0:T(8,128)S(1)} %pad_maximum_fusion.4), channel_id=1, source_target_pairs={{0,4},{1,5},{2,6},{3,7},{4,0},{5,1},{6,2},{7,3},{8,12},{9,13},{10,... | collective-permute-start | bytes 147464 | tf_op jit(solution)/shard_map/ppermute | solution.py:621
  486.1 14.1 %collective-permute-start.23 = (bf16[2,48,1536]{2,1,0:T(8,128)(2,1)S(1)}, bf16[2,48,1536]{2,1,0:T(8,128)(2,1)S(1)}, u32[]{:S(2)}, u32[]{:S(2)}) collective-permute-start(bf16[2,48,1536]{2,1,0:T(8,128)(2,1)S(1)} %dynamic-slice_bitcast_fusion.4), channel_id=1, source_target_pairs={{0,4},{1,5},{2,6},{3,7},{4,0},{5,1},{6,2},{7,3},{8,12},{9,13},{10,... | collective-permute-start | bytes 884744 | tf_op jit(solution)/shard_map/ppermute | solution.py:621
  490.9 15.0 %collective-permute-start.18 = (f32[16,1536]{1,0:T(8,128)S(1)}, f32[16,1536]{1,0:T(8,128)S(1)}, u32[]{:S(2)}, u32[]{:S(2)}) collective-permute-start(f32[16,1536]{1,0:T(8,128)S(1)} %pad_maximum_fusion.1), channel_id=1, source_target_pairs={{0,8},{1,9},{2,10},{3,11},{4,12},{5,13},{6,14},{7,15},{8,0},{9,1},... | collective-permute-start | bytes 294920 | tf_op jit(solution)/shard_map/ppermute | solution.py:621
  492.0 17.0 %collective-permute-start.21 = (bf16[48,1536]{1,0:T(8,128)(2,1)S(1)}, bf16[48,1536]{1,0:T(8,128)(2,1)S(1)}, u32[]{:S(2)}, u32[]{:S(2)}) collective-permute-start(bf16[48,1536]{1,0:T(8,128)(2,1)S(1)} %dynamic-slice_bitcast_fusion.11), channel_id=1, source_target_pairs={{0,8},{1,9},{2,10},{3,11},{4,12},{5,13},{6,14},{7,15},{8,0},{9,1},... | collective-permute-start | bytes 442376 | tf_op jit(solution)/shard_map/ppermute | solution.py:621
  500.3 10.3 %collective-permute-start.24 = (bf16[48,1536]{1,0:T(8,128)(2,1)S(1)}, bf16[48,1536]{1,0:T(8,128)(2,1)S(1)}, u32[]{:S(2)}, u32[]{:S(2)}) collective-permute-start(bf16[48,1536]{1,0:T(8,128)(2,1)S(1)} %dynamic-slice_bitcast_fusion.10), channel_id=1, source_target_pairs={{0,8},{1,9},{2,10},{3,11},{4,12},{5,13},{6,14},{7,15},{8,0},{9,1},... | collective-permute-start | bytes 442376 | tf_op jit(solution)/shard_map/ppermute | solution.py:621
  (16 other events, 24.2 us)
Sparse Core Ops, SparseCore 0:
  40.6 91.5 all-gather.2
  134.4 93.5 all-gather.4

commit v4 on v3

v4 whole, which is shorter than its diff:
```python
import functools

import jax
import jax.numpy as jnp
from jax import lax
from jax.experimental import pallas as pl
from jax.experimental.pallas import tpu as pltpu
from jax.sharding import PartitionSpec as P

HD = 64
BLOCK = 48
VMEM_LIMIT = 40 * 1024 * 1024

epsilon = 1e-12
SCALE = HD ** (-0.5)

ANY = pl.BlockSpec(memory_space=pl.ANY)
VMEM = pl.BlockSpec(memory_space=pltpu.VMEM)
SMEM = pl.BlockSpec(memory_space=pltpu.SMEM)
HBM = pl.BlockSpec(memory_space=pltpu.HBM)


def dot_nn(a, b):
    return jnp.dot(a, b, preferred_element_type=jnp.float32)


def dot_nt(a, b):
    return lax.dot_general(a, b, (((1,), (1,)), ((), ())), preferred_element_type=jnp.float32)


def dot_tn(a, b):
    return lax.dot_general(a, b, (((0,), (0,)), ((), ())), preferred_element_type=jnp.float32)


def gelu_parts(values):
    size = jnp.abs(values)
    inverse = 1.0 / (1.0 + (0.3275911 * 0.5**0.5) * size)
    series = 0.5 * 1.061405429
    for factor in (-1.453152027, 1.421413741, -0.284496736, 0.254829592):
        series = series * inverse + 0.5 * factor
    bell = jnp.exp(-0.5 * (values * values))
    tail = series * inverse * bell
    phi = jnp.where(values >= 0, 1.0 - tail, tail)
    return values * phi, phi + values * bell * 0.3989422804014327


def normalised(values):
    centred = values - jnp.mean(values, axis=-1, keepdims=True)
    variance = jnp.mean(centred * centred, axis=-1, keepdims=True)
    scale = lax.rsqrt(variance + epsilon)
    return centred * scale, scale


def weight_copies(layout, packs, weights, sems):
    copies = {}
    for at, (name, pack, source, width, target) in enumerate(layout):
        block = packs[pack].at[:, :, pl.ds(source, width)]
        if name == "contract":
            place = weights[name].at[:, target]
        else:
            place = weights[name].at[:, :, pl.ds(target, width)]
        copies.setdefault(name, []).append(pltpu.make_async_copy(block, place, sems.at[at]))
    return copies


NAMES = ("proj", "out", "expand", "contract")


def weight_shapes(features, hidden_size):
    blocks = features // BLOCK
    return (
        (blocks, BLOCK, 3 * features),
        (blocks, BLOCK, features),
        (blocks, BLOCK, hidden_size),
        (blocks, hidden_size // features, BLOCK, features),
    )


def in_vmem(arrays):
    return [pltpu.with_memory_space_constraint(array, pltpu.VMEM) for array in arrays]


def in_hbm(arrays):
    return [pltpu.with_memory_space_constraint(array, pltpu.HBM) for array in arrays]


def flat(block):
    return block.reshape(-1, block.shape[-1])


def two_heads(pair, head_low):
    zero = jnp.zeros_like(pair)
    return jnp.concatenate(
        [jnp.where(head_low, pair, zero), jnp.where(head_low, zero, pair)], axis=0
    )


def merged_heads(stacked, head_low):
    rows = stacked.shape[0] // 2
    return jnp.where(head_low, stacked[:rows], stacked[rows:])


def forward_kernel(layout, pack_count, view, first, crops, saved_count, kept_count, *refs):
    flag, vrow, vcol, lines, offs, x_hbm = refs[:6]
    sources = refs[6 : 6 + (pack_count or 4)]
    refs = refs[6 + (pack_count or 4) + kept_count :]
    y_out, pooled_out = refs[:2]
    refs = refs[2:]
    if pack_count:
        weights, refs = refs[:4], refs[4:]
    else:
        weights = sources
    weights = dict(zip(NAMES, weights))
    saved = refs[:saved_count]
    x_buf, mix, probs, att, low, hat1, hat2, stats, act, slope, w_sems, io_sems = refs[saved_count:]
    rows, features = x_buf.shape[1:]
    copies = {}
    if pack_count:
        copies = weight_copies(layout, sources, weights, w_sems)
        for name in NAMES:
            for copy in copies[name]:
                copy.start()

    def arrive(name):
        for copy in copies.get(name, ()):
            copy.wait()

    @pl.when(flag[0] == 1)
    def _():
        sends = []

        def keep(index, source):
            if saved_count:
                copy = pltpu.make_async_copy(source, saved[index], io_sems.at[crops + index])
                copy.start()
                sends.append(copy)

        fetches = []
        for crop in range(crops):
            source = x_hbm.at[view, first + crop] if len(x_hbm.shape) == 4 else x_hbm.at[crop]
            fetches.append(pltpu.make_async_copy(source, x_buf.at[crop], io_sems.at[crop]))
            fetches[-1].start()
        for crop in range(crops):
            fetches[crop].wait()
            x = x_buf[crop]
            if crop == 0:
                arrive("proj")
            for start, stop, line in ((0, 1, 2), (1, 2, None), (2, 3, 3)):
                columns = pl.ds(start * features, (stop - start) * features)
                part = dot_nn(x, flat(weights["proj"][:, :, columns]))
                if line is not None:
                    part = part + lines[line : line + 1, :]
                mix[:, columns] = part.astype(jnp.bfloat16)
            head_low = lax.broadcasted_iota(jnp.int32, (rows, 2 * HD), 1) < HD
            valid = jnp.broadcast_to(vrow[view, first + crop] > 0, (2 * rows, rows))
            for pair in range(features // (2 * HD)):
                at = pair * 2 * HD
                q = mix[:, at : at + 2 * HD] * jnp.asarray(SCALE, jnp.bfloat16)
                k = mix[:, features + at : features + at + 2 * HD]
                v = mix[:, 2 * features + at : 2 * features + at + 2 * HD]
                scores = jnp.where(valid, dot_nt(two_heads(q, head_low), k), -1e30)
                top = jnp.max(scores, axis=-1, keepdims=True)
                weight = jnp.exp(scores - top)
                share = 1.0 / jnp.sum(weight, axis=-1, keepdims=True)
                weight = weight.astype(jnp.bfloat16)
                if saved_count:
                    probs[2 * pair] = weight[:rows]
                    probs[2 * pair + 1] = weight[rows:]
                    stats[:, 2 + 2 * pair : 3 + 2 * pair] = share[:rows]
                    stats[:, 3 + 2 * pair : 4 + 2 * pair] = share[rows:]
                mixed = merged_heads(dot_nn(weight, v) * share, head_low)
                att[:, at : at + 2 * HD] = mixed.astype(jnp.bfloat16)
            keep(0, mix)
            keep(1, probs)
            keep(2, att)
            if crop == 0:
                arrive("out")
            total = x.astype(jnp.float32) + dot_nn(att[...], flat(weights["out"][...]))
            hat, scale = normalised(total + lines[4:5, :])
            hidden = hat * lines[0:1, :] + lines[5:6, :]
            low[...] = hidden.astype(jnp.bfloat16)
            if saved_count:
                hat1[...] = hat.astype(jnp.bfloat16)
                stats[:, 0:1] = scale
            keep(3, low)
            keep(4, hat1)
            if crop == 0:
                arrive("expand")
            groups = offs.shape[1] // features
            stack = weights["contract"].shape[0] // groups
            total = hidden + lines[6:7, :]
            for group in range(groups):
                columns = pl.ds(group * features, features)
                upward = dot_nn(low[...], flat(weights["expand"][:, :, columns]))
                value, gradient = gelu_parts(upward + offs[:, columns])
                value = value.astype(jnp.bfloat16)
                if saved_count:
                    act[:, columns] = value
                    slope[:, columns] = gradient.astype(jnp.bfloat16)
                if crop == 0 and group == 0:
                    arrive("contract")
                block = weights["contract"][group * stack : (group + 1) * stack]
                total = total + dot_nn(value, flat(block))
            keep(6, act)
            keep(7, slope)
            hat, scale = normalised(total)
            value = hat * lines[1:2, :] + lines[7:8, :]
            y_out[crop] = value.astype(jnp.bfloat16)
            if saved_count:
                hat2[...] = hat.astype(jnp.bfloat16)
                stats[:, 1:2] = scale
            count = jnp.sum(vrow[view, first + crop], axis=-1, keepdims=True)
            total = jnp.sum(value * vcol[view, first + crop], axis=0, keepdims=True)
            pooled_out[crop] = total / count
            keep(5, hat2)
            keep(8, stats)
        for copy in sends:
            copy.wait()

    if pack_count:

        @pl.when(flag[0] != 1)
        def _():
            for name in NAMES:
                arrive(name)


def forward_block(
    flag, x, vrow, vcol, lines, offs, packs, layout, save, view, first, crops, kept=()
):
    rows, features = x.shape[-2:]
    hidden_size = offs.shape[-1]
    heads = features // HD
    bf16, f32 = jnp.bfloat16, jnp.float32
    staged = bool(layout)
    shapes = []
    if staged:
        shapes = [(shape, bf16) for shape in weight_shapes(features, hidden_size)]
    first_saved = 2 + len(shapes)
    if save:
        shapes += [
            ((rows, 3 * features), bf16),
            ((heads, rows, rows), bf16),
            ((rows, features), bf16),
            ((rows, features), bf16),
            ((rows, features), bf16),
            ((rows, features), bf16),
            ((rows, hidden_size), bf16),
            ((rows, hidden_size), bf16),
            ((rows, 128), f32),
        ]
    saved_count = 9 if save else 0
    kept = tuple(kept)
    out_shape = [
        jax.ShapeDtypeStruct((crops, rows, features), bf16),
        jax.ShapeDtypeStruct((crops, 1, features), f32),
    ]
    out_shape += [pltpu.VMEM(*shape) for shape in shapes[: first_saved - 2]]
    out_shape += [pltpu.HBM(*shape) for shape in shapes[first_saved - 2 :]]
    flops = 2 * crops * rows * (4 * features * features + 2 * features * hidden_size)
    first_kept = 6 + len(packs)
    unused = (8, 128)
    result = pl.pallas_call(
        functools.partial(
            forward_kernel,
            layout,
            len(packs) if staged else 0,
            view,
            first,
            crops,
            saved_count,
            len(kept),
        ),
        out_shape=out_shape,
        in_specs=[SMEM]
        + [VMEM] * 4
        + [ANY]
        + [ANY if staged else VMEM] * len(packs)
        + [HBM] * len(kept),
        out_specs=[VMEM] * first_saved + [HBM] * saved_count,
        scratch_shapes=[
            pltpu.VMEM((crops, rows, features), bf16),
            pltpu.VMEM((rows, 3 * features), bf16),
            pltpu.VMEM((heads, rows, rows) if save else unused, bf16),
            pltpu.VMEM((rows, features), bf16),
            pltpu.VMEM((rows, features), bf16),
            pltpu.VMEM((rows, features) if save else unused, bf16),
            pltpu.VMEM((rows, features) if save else unused, bf16),
            pltpu.VMEM((rows, 128), f32),
            pltpu.VMEM((rows, hidden_size) if save else unused, bf16),
            pltpu.VMEM((rows, hidden_size) if save else unused, bf16),
            pltpu.SemaphoreType.DMA((max(1, len(layout)),)),
            pltpu.SemaphoreType.DMA((crops + 9,)),
        ],
        input_output_aliases={first_kept + i: first_saved + i for i in range(len(kept))},
        compiler_params=pltpu.CompilerParams(vmem_limit_bytes=VMEM_LIMIT),
        cost_estimate=pl.CostEstimate(flops=flops, bytes_accessed=20_000_000, transcendentals=0),
        name="forward_save" if save else "forward_only",
    )(flag, vrow, vcol, lines, offs, x, *(packs if staged else in_vmem(packs)), *in_hbm(kept))
    return result[0], result[1], tuple(result[2:first_saved]), tuple(result[first_saved:])


def backward_kernel(crop, kept_count, *refs):
    flag, vcol, lines, g_hbm = refs[:4]
    weights = dict(zip(NAMES, refs[4:8]))
    saved = refs[8:17]
    refs = refs[17 + kept_count :]
    vec_out, offs_out, dx_low = refs[:3]
    dx_out, branch_out, upward_out, output_out, mixture_out = refs[3:8]
    (
        g_buf, mix, probs, hat1, hat2, stats, slope, dbranch, dupward, doutput, datt, dmix, total,
        in_sems, out_sems,
    ) = refs[8:]
    rows, features = g_buf.shape
    hidden_size = dupward.shape[1]

    @pl.when(flag[0] == 1)
    def _():
        fetches = {}
        for at, (name, source, place) in enumerate(
            (
                ("g", g_hbm.at[crop] if len(g_hbm.shape) == 3 else g_hbm, g_buf),
                ("hat2", saved[5], hat2),
                ("stats", saved[8], stats),
                ("slope", saved[7], slope),
                ("hat1", saved[4], hat1),
                ("mix", saved[0], mix),
                ("probs", saved[1], probs),
            )
        ):
            fetches[name] = pltpu.make_async_copy(source, place, in_sems.at[at])
            fetches[name].start()

        def arrive(*names):
            for name in names:
                fetches[name].wait()

        sends = []

        def send(index, source, place):
            copy = pltpu.make_async_copy(source, place, out_sems.at[index])
            copy.start()
            sends.append(copy)

        def norm_back(gradient, hat, scale, gain):
            weighted = gradient * gain
            mean = jnp.mean(weighted, axis=-1, keepdims=True)
            slant = jnp.mean(weighted * hat, axis=-1, keepdims=True)
            return scale * (weighted - mean - hat * slant)

        def column_sum(line, values):
            vec_out[line : line + 1, :] = jnp.sum(values, axis=0, keepdims=True)

        arrive("g", "hat2", "stats")
        gradient = g_buf[...].astype(jnp.float32)
        if len(g_hbm.shape) == 3:
            gradient = gradient * vcol[0, crop]
        hat = hat2[...].astype(jnp.float32)
        column_sum(1, gradient * hat)
        column_sum(7, gradient)
        moved = norm_back(gradient, hat, stats[:, 1:2], lines[1:2, :])
        total[...] = moved
        rounded = moved.astype(jnp.bfloat16)
        dbranch[...] = rounded
        column_sum(6, rounded.astype(jnp.float32))
        send(0, dbranch, branch_out)
        arrive("slope")
        groups = hidden_size // features
        stack = weights["contract"].shape[0] // groups
        for group in range(groups):
            columns = pl.ds(group * features, features)
            block = weights["contract"][group * stack : (group + 1) * stack]
            dactive = dot_nt(rounded, flat(block))
            dup = (dactive * slope[:, columns].astype(jnp.float32)).astype(jnp.bfloat16)
            dupward[:, columns] = dup
            offs_out[:, columns] = jnp.sum(dup.astype(jnp.float32), axis=0, keepdims=True)
        send(1, dupward, upward_out)
        arrive("hat1")
        gradient = total[...] + dot_nt(dupward[...], flat(weights["expand"][...]))
        hat = hat1[...].astype(jnp.float32)
        column_sum(0, gradient * hat)
        column_sum(5, gradient)
        moved = norm_back(gradient, hat, stats[:, 0:1], lines[0:1, :])
        total[...] = moved
        rounded = moved.astype(jnp.bfloat16)
        doutput[...] = rounded
        column_sum(4, rounded.astype(jnp.float32))
        send(2, doutput, output_out)
        datt[...] = dot_nt(rounded, flat(weights["out"][...])).astype(jnp.bfloat16)
        arrive("mix", "probs")
        head_low = lax.broadcasted_iota(jnp.int32, (rows, 2 * HD), 1) < HD
        for pair in range(features // (2 * HD)):
            at = pair * 2 * HD
            q = mix[:, at : at + 2 * HD]
            k = mix[:, features + at : features + at + 2 * HD]
            v = mix[:, 2 * features + at : 2 * features + at + 2 * HD]
            share = jnp.concatenate(
                [stats[:, 2 + 2 * pair : 3 + 2 * pair], stats[:, 3 + 2 * pair : 4 + 2 * pair]], axis=0
            )
            pull = two_heads(datt[:, at : at + 2 * HD], head_low).astype(jnp.float32)
            pull = (pull * share).astype(jnp.bfloat16)
            weight = flat(probs[2 * pair : 2 * pair + 2])
            wide = weight.astype(jnp.float32)
            product = dot_nt(pull, v) * wide
            inner = jnp.sum(product, axis=-1, keepdims=True) * share
            dscores = (product - wide * inner).astype(jnp.bfloat16)
            dq = merged_heads(dot_nn(dscores, k), head_low)
            dmix[:, at : at + 2 * HD] = (dq * SCALE).astype(jnp.bfloat16)
            q_turned = q.T
            pull_turned = merged_heads(pull, head_low).T
            dk, dv = [], []
            for side in range(2):
                lanes = slice(side * HD, (side + 1) * HD)
                part = slice(side * rows, (side + 1) * rows)
                dk.append(dot_nn(q_turned[lanes], dscores[part]))
                dv.append(dot_nn(pull_turned[lanes], weight[part]))
            dk = (jnp.concatenate(dk, axis=0) * SCALE).astype(jnp.bfloat16).T
            dv = jnp.concatenate(dv, axis=0).astype(jnp.bfloat16).T
            dmix[:, features + at : features + at + 2 * HD] = dk
            dmix[:, 2 * features + at : 2 * features + at + 2 * HD] = dv
        send(3, dmix, mixture_out)
        column_sum(2, dmix[:, 0:features].astype(jnp.float32))
        column_sum(3, dmix[:, 2 * features : 3 * features].astype(jnp.float32))
        moved = total[...] + dot_nt(dmix[...], flat(weights["proj"][...]))
        total[...] = moved
        dx_low[...] = moved.astype(jnp.bfloat16)
        send(4, total, dx_out)
        for copy in sends:
            copy.wait()


def backward_block(flag, gradient, vcol, lines, weights, saved, crop, kept=()):
    rows, features = gradient.shape[-2:]
    hidden_size = saved[6].shape[-1]
    heads = features // HD
    bf16, f32 = jnp.bfloat16, jnp.float32
    kept = tuple(kept)
    out_shape = [
        jax.ShapeDtypeStruct((8, features), f32),
        jax.ShapeDtypeStruct((1, hidden_size), f32),
        jax.ShapeDtypeStruct((rows, features), bf16),
        pltpu.HBM((rows, features), f32),
        pltpu.HBM((rows, features), bf16),
        pltpu.HBM((rows, hidden_size), bf16),
        pltpu.HBM((rows, features), bf16),
        pltpu.HBM((rows, 3 * features), bf16),
    ]
    flops = 2 * rows * (4 * features * features + 2 * features * hidden_size)
    first_kept = 8 + 9
    result = pl.pallas_call(
        functools.partial(backward_kernel, crop, len(kept)),
        out_shape=out_shape,
        in_specs=[SMEM] + [VMEM] * 2 + [ANY] + [VMEM] * 4 + [HBM] * (9 + len(kept)),
        out_specs=[VMEM] * 3 + [HBM] * 5,
        scratch_shapes=[
            pltpu.VMEM((rows, features), bf16),
            pltpu.VMEM((rows, 3 * features), bf16),
            pltpu.VMEM((heads, rows, rows), bf16),
            pltpu.VMEM((rows, features), bf16),
            pltpu.VMEM((rows, features), bf16),
            pltpu.VMEM((rows, 128), f32),
            pltpu.VMEM((rows, hidden_size), bf16),
            pltpu.VMEM((rows, features), bf16),
            pltpu.VMEM((rows, hidden_size), bf16),
            pltpu.VMEM((rows, features), bf16),
            pltpu.VMEM((rows, features), bf16),
            pltpu.VMEM((rows, 3 * features), bf16),
            pltpu.VMEM((rows, features), f32),
            pltpu.SemaphoreType.DMA((7,)),
            pltpu.SemaphoreType.DMA((5,)),
        ],
        input_output_aliases={first_kept + i: 3 + i for i in range(len(kept))},
        compiler_params=pltpu.CompilerParams(vmem_limit_bytes=VMEM_LIMIT),
        cost_estimate=pl.CostEstimate(flops=flops, bytes_accessed=25_000_000, transcendentals=0),
        name="backward_data",
    )(flag, vcol, lines, gradient, *in_vmem(weights), *in_hbm(saved), *in_hbm(kept))
    return result[:3], tuple(result[3:])


def load_pairs(sources, buffers, width, sems):
    copies = {}
    for i, buffer in enumerate(buffers):
        rows = buffer.shape[0] // 2
        for column in range(0, buffer.shape[1], width):
            columns = pl.ds(column, width)
            for half in range(2):
                copies.setdefault((i, column), []).append(
                    pltpu.make_async_copy(
                        sources[2 * i + half].at[:, columns],
                        buffer.at[pl.ds(half * rows, rows), columns],
                        sems.at[2 * i + half, column // width],
                    )
                )
    waited = set()

    def arrive(which, column):
        if (which, column) not in waited:
            waited.add((which, column))
            for copy in copies[which, column]:
                copy.wait()

    return copies, arrive


def contract_kernel(core, act0, act1, grad0, grad1, *refs):
    outs, (act, grad, pieces, in_sems, out_sems) = refs[:-5], refs[-5:]
    features = grad.shape[1]
    groups = act.shape[1] // features
    span = outs[0].shape[2] // features
    copies, arrive = load_pairs((act0, act1, grad0, grad1), (act, grad), features, in_sems)
    for which in [(1, 0)] + [(0, part * features) for part in range(groups)]:
        for copy in copies[which]:
            copy.start()
    arrive(1, 0)
    sends = []
    for part in range(groups):
        columns = pl.ds(part * features, features)
        arrive(0, part * features)
        piece = dot_tn(act[:, columns], grad[...]).astype(jnp.bfloat16)
        pieces[part] = piece.reshape(pieces.shape[1:])
        count = pieces.shape[1]
        for group in range(groups):
            for side in range(2):
                source = pieces.at[part, :, core[0] ^ side, group]
                place = outs[2 * (group // span) + side].at[
                    pl.ds(part * count, count), :, pl.ds((group % span) * features, features)
                ]
                copy = pltpu.make_async_copy(source, place, out_sems.at[part, group, side])
                copy.start()
                sends.append(copy)
    for copy in sends:
        copy.wait()


def row_kernel(plan, core, *refs):
    count = 1 + max(max(entry[:2]) for entry in plan)
    sources, refs = refs[: 2 * count], refs[2 * count :]
    buffers, (pieces, in_sems, out_sems) = refs[-3 - count : -3], refs[-3:]
    outs = refs[: -3 - count]
    width = pieces.shape[-1]
    copies, arrive = load_pairs(sources, buffers, width, in_sems)
    needs = [need for entry in plan for need in ((entry[0], 0), (entry[1], entry[2]))]
    for need in dict.fromkeys(needs):
        for copy in copies[need]:
            copy.start()
    sends = []
    for part, (left, right, column, target, to) in enumerate(plan):
        arrive(left, 0)
        arrive(right, column)
        piece = dot_tn(buffers[left][...], buffers[right][:, column : column + width])
        pieces[part] = piece.astype(jnp.bfloat16).reshape(pieces.shape[1:])
        for side in range(2):
            source = pieces.at[part, :, core[0] ^ side]
            place = outs[2 * target + side].at[:, :, pl.ds(to, width)]
            copy = pltpu.make_async_copy(source, place, out_sems.at[part, side])
            copy.start()
            sends.append(copy)
    for copy in sends:
        copy.wait()


def weight_gradient(kernel, core, operands, targets, contracted, features, name):
    pairs = features // BLOCK // 2
    bf16 = jnp.bfloat16
    shape = pltpu.HBM((pairs, BLOCK, 2 * features), bf16)
    parts = 2 * targets
    buffers = [
        pltpu.VMEM((2 * operand.shape[0], operand.shape[1]), bf16) for operand in operands[::2]
    ]
    if contracted:
        pieces = pltpu.VMEM((parts, pairs // parts, 2, parts, BLOCK, features), bf16)
        out_sems = pltpu.SemaphoreType.DMA((parts, parts, 2))
    else:
        pieces = pltpu.VMEM((parts, pairs, 2, BLOCK, features), bf16)
        out_sems = pltpu.SemaphoreType.DMA((parts, 2))
    return pl.pallas_call(
        kernel,
        out_shape=[shape] * (2 * targets),
        in_specs=[SMEM] + [HBM] * len(operands),
        out_specs=[HBM] * (2 * targets),
        scratch_shapes=buffers
        + [pieces, pltpu.SemaphoreType.DMA((len(operands), parts)), out_sems],
        compiler_params=pltpu.CompilerParams(vmem_limit_bytes=VMEM_LIMIT),
        cost_estimate=pl.CostEstimate(
            flops=4 * targets * features * features * 512, bytes_accessed=9_000_000, transcendentals=0
        ),
        name=name,
    )(core, *in_hbm(operands))


def pack_kernel(plan, *refs):
    target = refs[-1]
    for source, row, column, width, place in plan:
        block = refs[source][0, row : row + target.shape[0], column : column + width]
        target[:, place : place + width] = block


def packed(arrays, pieces, rows):
    width = sum(piece[3] for piece in pieces)
    if rows % 16:
        return jnp.concatenate(
            [arrays[i][0, r : r + rows, c : c + w] for i, r, c, w in pieces], axis=1
        )
    plan, place = [], 0
    for piece in pieces:
        plan.append(piece + (place,))
        place += piece[3]
    return pl.pallas_call(
        functools.partial(pack_kernel, tuple(plan)),
        out_shape=jax.ShapeDtypeStruct((rows, width), jnp.bfloat16),
        in_specs=[VMEM] * len(arrays),
        out_specs=VMEM,
        name="pack",
    )(*arrays)


def refold(columns, shards_of, features):
    rows = features // shards_of
    if rows == BLOCK:
        return columns
    natural = jnp.moveaxis(columns.reshape(shards_of, rows, -1, features), 2, 1)
    natural = natural.reshape(features // BLOCK, -1, BLOCK, features)
    return jnp.moveaxis(natural, 1, 2).reshape(features, -1)


def unfold(blocks, shards_of, features):
    rows = features // shards_of
    if rows == BLOCK:
        return blocks
    natural = jnp.moveaxis(blocks.reshape(features // BLOCK, BLOCK, -1, features), 2, 1)
    natural = natural.reshape(shards_of, -1, rows, features)
    return jnp.moveaxis(natural, 1, 2).reshape(shards_of, rows, -1)


def swapped(block, level):
    route = [(i, i ^ (1 << level)) for i in range(lax.axis_size("dp"))]
    return lax.ppermute(block, "dp", route)


def added(first, second):
    return (first.astype(jnp.float32) + second.astype(jnp.float32)).astype(jnp.bfloat16)


def tied(value, *others):
    return lax.optimization_barrier((value,) + others)[0]


def split(block, level):
    levels = lax.axis_size("dp").bit_length() - 1
    mine = (lax.axis_index("dp") >> level) & 1
    axis = levels - 1 - level
    keep = lax.dynamic_index_in_dim(block, mine, axis, keepdims=False)
    return keep, lax.dynamic_index_in_dim(block, 1 - mine, axis, keepdims=False)


def by_bits(block, levels):
    return block.reshape((2,) * levels + block.shape[1:])


def halved(pair, level):
    keep, send = pair
    total = added(keep, swapped(send, level))
    if level + 1 == lax.axis_size("dp").bit_length() - 1:
        return total
    return split(total, level + 1)


def first_pair(keep, send, shards_of, features, contracted):
    levels = shards_of.bit_length() - 1
    if features == BLOCK * shards_of:
        return by_bits(keep, levels - 1), by_bits(send, levels - 1)
    blocks = jnp.stack([keep, send], axis=1).reshape(-1, BLOCK, keep.shape[-1])
    if contracted:
        blocks = unfold(blocks, shards_of, features)
    else:
        blocks = blocks.reshape(shards_of, features // shards_of, -1)
    return split(by_bits(blocks, levels), 0)


def doubled(block):
    here = lax.axis_index("dp")
    for level in range(lax.axis_size("dp").bit_length() - 1):
        other = swapped(block, level)
        upper = ((here >> level) & 1) == 1
        block = jnp.concatenate(
            [jnp.where(upper, other, block), jnp.where(upper, block, other)], axis=0
        )
    return block


def shards(
    inputs,
    keep_mask,
    lengths,
    slot_order,
    cotangent,
    query_projection,
    query_output,
    query_expand,
    query_contract,
    query_gains,
    query_biases,
    query_offsets,
    momentum_projection,
    momentum_output,
    momentum_expand,
    momentum_contract,
    momentum_gains,
    momentum_biases,
    momentum_offsets,
):
    first_section = lax.axis_index("section") == 0
    shards_of = lax.axis_size("dp")
    crop_count, crop_len, features = inputs.shape[1:]
    rows = features // shards_of
    hidden_size = query_expand.shape[2]
    groups = hidden_size // features
    blocks = features // BLOCK

    def folded(which):
        return [(which, i * rows, 0, features) for i in range(groups)]

    late_from, late_to = 2 * features // 3, 2 * features
    own = packed(
        (query_projection, query_output, query_expand, query_contract)
        + (momentum_output, momentum_projection),
        [(0, 0, 0, 3 * features), (1, 0, 0, features), (2, 0, 0, hidden_size)]
        + folded(3)
        + [(4, 0, 0, features), (5, 0, late_from, late_to - late_from)],
        rows,
    )
    gathered = lax.all_gather(own, "dp", axis=0, tiled=True)
    rest = packed(
        (tied(momentum_projection, own), momentum_expand, momentum_contract),
        [(0, 0, 0, late_from), (0, 0, late_to, 3 * features - late_to), (1, 0, 0, hidden_size)]
        + folded(2),
        rows,
    )
    late = lax.all_gather(rest, "dp", axis=0, tiled=True)

    sizes = (2 * rows, 6 * rows, groups * rows)
    vectors = doubled(
        jnp.concatenate(
            [
                array[0].reshape(-1)
                for array in (
                    query_gains,
                    query_biases,
                    query_offsets,
                    momentum_gains,
                    momentum_biases,
                    momentum_offsets,
                )
            ]
        )[None]
    ).astype(jnp.float32)

    def vector_rows(start):
        lines = vectors[:, start : start + 8 * rows].reshape(shards_of, 8, rows)
        marks = vectors[:, start + 8 * rows : start + sum(sizes)]
        return jnp.moveaxis(lines, 1, 0).reshape(8, features), marks.reshape(1, hidden_size)

    query_lines, query_offs = vector_rows(0)
    momentum_lines, momentum_offs = vector_rows(sum(sizes))

    inner = 4 * features + hidden_size
    vectors_at = inner + groups * features
    if rows != BLOCK:
        gathered = jnp.concatenate(
            [
                gathered[:, :inner],
                refold(gathered[:, inner:vectors_at], shards_of, features),
                gathered[:, vectors_at:],
            ],
            axis=1,
        )
        late_end = late.shape[1] - groups * features
        late = jnp.concatenate(
            [late[:, :late_end], refold(late[:, late_end:], shards_of, features)], axis=1
        )
    gathered = gathered.reshape(blocks, BLOCK, -1)
    late = late.reshape(blocks, BLOCK, -1)
    query_layout = (
        ("proj", 0, 0, 3 * features, 0),
        ("out", 0, 3 * features, features, 0),
        ("expand", 0, 4 * features, hidden_size, 0),
    ) + tuple(("contract", 0, inner + i * features, features, i) for i in range(groups))
    late_expand = 3 * features - (late_to - late_from)
    momentum_layout = (
        ("proj", 0, vectors_at + features, late_to - late_from, late_from),
        ("proj", 1, 0, late_from, 0),
        ("proj", 1, late_from, 3 * features - late_to, late_to),
        ("out", 0, vectors_at, features, 0),
        ("expand", 1, late_expand, hidden_size, 0),
    ) + tuple(
        ("contract", 1, late_expand + hidden_size + i * features, features, i)
        for i in range(groups)
    )

    positions = lax.broadcasted_iota(jnp.int32, keep_mask.shape, 2)
    validity = ((positions < lengths[:, :, None]) & ((keep_mask > 0) | (positions == 0))).astype(
        jnp.float32
    )
    across = validity[:, :, None, :]
    down = validity[:, :, :, None]
    in_first = first_section.astype(jnp.int32).reshape(1)
    in_second = 1 - in_first

    def query_forward(flag, block_in, crop, weights, layout=(), kept=()):
        return forward_block(
            flag,
            block_in,
            across,
            down,
            query_lines,
            query_offs,
            weights,
            layout,
            True,
            0,
            crop,
            1,
            kept,
        )

    def momentum_forward(flag, block_in, weights, layout=()):
        return forward_block(
            flag,
            block_in,
            across,
            down,
            momentum_lines,
            momentum_offs,
            weights,
            layout,
            False,
            1,
            0,
            crop_count,
        )[:3]

    crops = range(crop_count)
    started = [query_forward(in_first, inputs, 0, (gathered,), query_layout)]
    weights = started[0][2]
    started += [query_forward(in_first, inputs, c, weights) for c in crops[1:]]
    passed = [lax.ppermute(started[c][0], "section", [(0, 1)]) for c in crops]
    pools, saved, pulled, returned = [], [], [], []
    for c in crops:
        _, pool, _, kept = query_forward(
            in_second, passed[c], c, weights, (), started[c][3]
        )
        pools.append(jnp.where(first_section, started[c][1], pool))
        saved.append(kept)
        pulled.append(backward_block(in_second, cotangent, down, query_lines, weights, kept, c))
        returned.append(lax.ppermute(pulled[c][0][2], "section", [(1, 0)]))
    vectors, marks, terms = 0.0, 0.0, []
    for c in crops:
        ends, kept = backward_block(
            in_first, returned[c], down, query_lines, weights, saved[c], c, pulled[c][1]
        )
        terms.append(kept)
        vectors = vectors + jnp.where(first_section, ends[0], pulled[c][0][0])
        marks = marks + jnp.where(first_section, ends[1], pulled[c][0][1])
    grad_input = jnp.stack([term[0] for term in terms])[None]

    core = lax.axis_index("dp") & 1 if rows == BLOCK else jnp.int32(0)
    core = jnp.asarray(core, jnp.int32).reshape(1)
    block_ins = [jnp.where(first_section, inputs[0, c], passed[c][0]) for c in crops]

    def pairs(sums, contracted=False):
        return [
            first_pair(sums[2 * i], sums[2 * i + 1], shards_of, features, contracted)
            for i in range(len(sums) // 2)
        ]

    contract_pairs = pairs(
        weight_gradient(
            contract_kernel,
            core,
            [kept[6] for kept in saved] + [term[1] for term in terms],
            groups // 2,
            True,
            features,
            "grad_contract",
        ),
        True,
    )
    expand_pairs = pairs(
        weight_gradient(
            functools.partial(
                row_kernel,
                tuple((0, 1, i * features, i // 2, i % 2 * features) for i in range(groups)),
            ),
            core,
            [kept[3] for kept in saved] + [term[2] for term in terms],
            groups // 2,
            False,
            features,
            "grad_expand",
        )
    )
    contract_pairs = [halved(pair, 0) for pair in contract_pairs]
    project_pairs = pairs(
        weight_gradient(
            functools.partial(
                row_kernel,
                (
                    (0, 1, 0, 0, 0),
                    (2, 3, 0, 0, features),
                    (2, 3, features, 1, 0),
                    (2, 3, 2 * features, 1, features),
                ),
            ),
            tied(core, *[pair[1] for pair in contract_pairs]),
            [kept[2] for kept in saved]
            + [term[3] for term in terms]
            + block_ins
            + [term[4] for term in terms],
            2,
            False,
            features,
            "grad_projection",
        )
    )
    columns = jnp.concatenate(
        [
            vectors.T.reshape(shards_of, rows, 8),
            jnp.moveaxis(marks.reshape(shards_of, groups, rows), 1, 2),
        ],
        axis=2,
    )
    coarse = columns.astype(jnp.bfloat16)
    fine = (columns - coarse.astype(jnp.float32)).astype(jnp.bfloat16)
    both = jnp.concatenate([coarse, fine], axis=2)
    both = jnp.pad(both, ((0, 0), (0, 0), (0, 128 - both.shape[2])))
    levels = shards_of.bit_length() - 1
    small = split(by_bits(both, levels), 0)
    chunks = contract_pairs + [halved(pair, 0) for pair in expand_pairs + project_pairs]
    small = halved(small, 0)

    key_out, key_pool, key_weights = momentum_forward(
        tied(in_first, *[pair[1] for pair in chunks]), inputs, (gathered, late), momentum_layout
    )
    key_in = lax.ppermute(key_out, "section", [(0, 1)])
    chunks = [halved((tied(keep, key_pool), send), 1) for keep, send in chunks]
    small = halved(small, 1)
    for level in range(2, levels):
        chunks = [halved(pair, level) for pair in chunks]
        small = halved(small, level)
    small = small.astype(jnp.float32)
    small = (small[:, :12] + small[:, 12:24]).T

    key_pool_second = momentum_forward(in_second, key_in, key_weights)[1]
    key_pool = jnp.where(first_section, key_pool, key_pool_second)
    pooled = jnp.concatenate([jnp.concatenate(pools, axis=0)[:, None], key_pool[:, None]], axis=1)
    order = (slot_order[:, None] == jnp.arange(crop_count, dtype=jnp.int32)[None, :])[..., None]
    pooled = pooled.reshape(crop_count, -1)
    pooled = jnp.sum(jnp.where(order, pooled[None], 0.0), axis=1)
    pooled = doubled(pooled).reshape(-1, 2, features)
    pooled = jnp.moveaxis(pooled, 1, 0)[None]

    def wide(parts):
        return jnp.concatenate(parts, axis=1).astype(jnp.float32)

    half = groups // 2
    contract_sum = jnp.moveaxis(wide(chunks[:half]).reshape(rows, groups, features), 1, 0)
    expand_sum = wide(chunks[half : 2 * half])
    project_sum = wide(chunks[2 * half :])
    return (
        pooled,
        grad_input,
        project_sum[None, :, features:],
        project_sum[None, :, :features],
        expand_sum[None],
        contract_sum.reshape(1, groups * rows, features),
        small[None, :2],
        small[None, 2:8],
        small[8:].reshape(1, groups * rows),
    )


def solution(mesh):
    in_specs = (
        P(None, "dp", None, None),
        P(None, "dp", None),
        P(None, "dp"),
        P("dp"),
        P("dp", None, None),
        P("section", "dp", None),
        P("section", "dp", None),
        P("section", "dp", None),
        P("section", "dp", None),
        P("section", None, "dp"),
        P("section", None, "dp"),
        P("section", "dp"),
        P("section", "dp", None),
        P("section", "dp", None),
        P("section", "dp", None),
        P("section", "dp", None),
        P("section", None, "dp"),
        P("section", None, "dp"),
        P("section", "dp"),
    )
    out_specs = (
        P("section", None, None, None),
        P("section", "dp", None, None),
        P("section", "dp", None),
        P("section", "dp", None),
        P("section", "dp", None),
        P("section", "dp", None),
        P("section", None, "dp"),
        P("section", None, "dp"),
        P("section", "dp"),
    )
    return jax.shard_map(shards, mesh=mesh, in_specs=in_specs, out_specs=out_specs, check_vma=False)
```

time: 529 us -> 447 us (0.84)
  Pallas kernels: 228 us -> 137 us
  local copies, waits for them, and re-layouts: 25.6 us -> 55.5 us
  waiting for transfers between devices: 196 us -> 169 us
    pallas_call x2, Pallas kernels: 56 us -> 4.43 us  [packed(): pl.pallas_call(functools.partial(pack_kernel, tuple(plan)), out_shape=jax...]
    pallas_call x10, Pallas kernels: 143 us -> 111 us  [the longest x6 62 us: forward_block(): pl.pallas_call(functools.partial(forward_kernel, layout, len(packs) if st...]
    ppermute x1, waiting for transfers between devices: 30.1 us -> 0.01 us  [shards(): key_in = lax.ppermute(key_out, 'section', [(0, 1)])]
    ppermute x2, waiting for transfers between devices: 28.3 us -> 3.2 us  [shards(): passed = [lax.ppermute(started[c][0], 'section', [(0, 1)]) for c in crops]]
    unnamed x78 -> x116, local copies, waits for them, and re-layouts: 7.82 us -> 32.9 us
    all_gather x1, waiting for transfers between devices: 52.5 us -> 73.2 us  [shards(): gathered = lax.all_gather(own, 'dp', axis=0, tiled=True)]
    ppermute x36, waiting for transfers between devices: 80 us -> 89.4 us  [swapped(): return lax.ppermute(block, 'dp', route)]
    pallas_call x3, Pallas kernels: 29 us -> 20.7 us  [weight_gradient(): pl.pallas_call(kernel, out_shape=[shape] * (2 * targets), in_specs=[SMEM]...]
  transfers between devices with their start and end apart: 43 -> 43, of which waited for: 26 -> 25; matrix products, arithmetic and copies ran while one was open for 7% -> 10% of each run, Pallas kernels for 38% -> 31%
where the time goes in v4:
time: 447 us; the launch traced here: 438 us
  waiting for transfers between devices  169 us (38%)
  Pallas kernels  137 us (31%)
  local copies, waits for them, and re-layouts  55.5 us (12%)
  starting transfers between devices  38.1 us (9%)
  other arithmetic  22.9 us (5%)
  between operations  15.5 us (3%)
    ppermute x36, waiting for transfers between devices, swapped(): return lax.ppermute(block, 'dp', route)  89.4 us
    all_gather x1, waiting for transfers between devices, shards(): gathered = lax.all_gather(own, 'dp', axis=0, tiled=True)  73.2 us
    pallas_call x6, Pallas kernels, forward_block(): pl.pallas_call(functools.partial(forward_kernel, layout, len(packs) if st...  62 us
    pallas_call x4, Pallas kernels, backward_block(): pl.pallas_call(functools.partial(backward_kernel, crop, len(kept)), out_s...  49.5 us
    unnamed x116, local copies, waits for them, and re-layouts  32.9 us
    ppermute x36, starting transfers between devices, swapped(): return lax.ppermute(block, 'dp', route)  31.4 us
    pallas_call x3, Pallas kernels, weight_gradient(): pl.pallas_call(kernel, out_shape=[shape] * (2 * targets), in_specs=[SMEM]...  20.7 us
    convert_element_type x25, other arithmetic, added(): (first.astype(jnp.float32) + second.astype(jnp.float32)).astype(jnp.bfloa...  12.7 us
  transfers between devices with their start and end apart: 43, of which 25 were waited for; matrix products, arithmetic and copies ran while one was open for 10% of the time, Pallas kernels for 31%

profile of v4, /device:TPU:2, one launch (start us, length us, event | category | flops | bytes accessed | tf_op | source)
XLA Modules:
  0.0 438.0 jit_solution(321457227725997881)
XLA Ops:
  7.2 2.3 pack.2
  9.7 2.1 pack.3
  13.6 1.6 collective-permute-start.1
  15.2 2.1 collective-permute-done.1
  17.4 1.6 collective-permute-start.2
  19.1 2.0 collective-permute-done.2
  21.1 2.7 collective-permute-start.3
  28.5 73.2 %all-gather.3.cloned.1.call-done = bf16[768,11008]{1,0:T(8,128)(2,1)} async-done(((bf16[48,11008]{1,0:T(8,128)(2,1)}), bf16[768,11008]{1,0:T(8,128)(2,1)}) %all-gather.3.cloned.1.call-update) | async-done | bytes 16908304 | tf_op jit(solution)/shard_map/all_gather | solution.py:732
  102.4 7.0 %forward_save.4 = (bf16[1,256,768]{2,1,0:T(8,128)(2,1)}, f32[1,1,768]{2,1,0:T(1,128)S(1)}, bf16[16,48,2304]{2,1,0:T(8,128)(2,1)S(1)}, bf16[16,48,768]{2,1,0:T(8,...) custom-call(s32[1]{0:T(128)} %bitcast.refs_0_, ...), custom_call_target="tpu_custom_call" | custom-call | flops 3623878656 | bytes 20000000 | tf_op jit(solution)/shard_map/forward_save/pallas_call | solution.py:263
  109.4 2.1 copy-done
  111.5 2.1 copy-done.2
  117.2 1.4 reshape.207
  118.7 1.5 copy.257
  120.2 1.5 reshape.208.refs_3_
  121.7 1.4 reshape.209.refs_4_
  123.1 2.4 copy-done.1
  125.4 2.3 copy-done.3
  129.8 2.5 forward_save.6
  133.6 3.2 collective-permute-done.4.refs_5_
  136.8 2.1 copy-done.5
  139.0 14.0 %forward_save.5 = (bf16[1,256,768]{2,1,0:T(8,128)(2,1)}, f32[1,1,768]{2,1,0:T(1,128)S(1)}, bf16[256,2304]{1,0:T(8,128)(2,1)}, bf16[12,256,256]{2,1,0:T(8,128)(2,...) custom-call(s32[1]{0:T(128)S(6)} %sub.12.refs_0_, ...), custom_call_target="tpu_custom_call", output_to_operand_aliasing={{2}: (10, {}), {3}: (11, {}), {4}: (12, {}), {5}: (13, {}),... | custom-call | flops 3623878656 | bytes 20000000 | tf_op jit(solution)/shard_map/forward_save/pallas_call | solution.py:263
  153.1 2.0 copy-done.6
  155.1 13.4 %backward_data.4 = (f32[8,768]{1,0:T(8,128)S(1)}, f32[1,3072]{1,0:T(1,128)S(1)}, bf16[256,768]{1,0:T(8,128)(2,1)S(1)}, f32[256,768]{1,0:T(8,128)}, bf16[256,768]...) custom-call(s32[1]{0:T(128)S(6)} %sub.12.refs_0_, ...), custom_call_target="tpu_custom_call" | custom-call | flops 3623878656 | bytes 25000000 | tf_op jit(solution)/shard_map/backward_data/pallas_call | solution.py:450
  170.6 13.3 %forward_save.7 = (bf16[1,256,768]{2,1,0:T(8,128)(2,1)}, f32[1,1,768]{2,1,0:T(1,128)S(1)}, bf16[256,2304]{1,0:T(8,128)(2,1)}, bf16[12,256,256]{2,1,0:T(8,128)(2,...) custom-call(s32[1]{0:T(128)S(6)} %sub.12.refs_0_, ...), custom_call_target="tpu_custom_call", output_to_operand_aliasing={{2}: (10, {}), {3}: (11, {}), {4}: (12, {}), {5}: (13, {}),... | custom-call | flops 3623878656 | bytes 20000000 | tf_op jit(solution)/shard_map/forward_save/pallas_call | solution.py:263
  183.9 13.7 %backward_data.6 = (f32[8,768]{1,0:T(8,128)S(1)}, f32[1,3072]{1,0:T(1,128)S(1)}, bf16[256,768]{1,0:T(8,128)(2,1)S(1)}, f32[256,768]{1,0:T(8,128)}, bf16[256,768]...) custom-call(s32[1]{0:T(128)S(6)} %sub.12.refs_0_, ...), custom_call_target="tpu_custom_call" | custom-call | flops 3623878656 | bytes 25000000 | tf_op jit(solution)/shard_map/backward_data/pallas_call | solution.py:450
  198.9 2.0 bitcast_select_fusion
  201.7 2.1 backward_data.5
  203.8 3.7 collective-permute-done.7.refs_3_
  208.2 20.4 %backward_data.7 = (f32[8,768]{1,0:T(8,128)S(1)}, f32[1,3072]{1,0:T(1,128)S(1)}, bf16[256,768]{1,0:T(8,128)(2,1)}, f32[256,768]{1,0:T(8,128)}, bf16[256,768]{1,0...) custom-call(s32[1]{0:T(128)} %bitcast.refs_0_, ...), custom_call_target="tpu_custom_call", output_to_operand_aliasing={{3}: (17, {}), {4}: (18, {}), {5}: (19, {}), {6}: (20, {}),... | custom-call | flops 3623878656 | bytes 25000000 | tf_op jit(solution)/shard_map/backward_data/pallas_call | solution.py:450
  230.6 1.4 collective-permute-start.38
  231.9 6.9 %grad_contract.1 = (bf16[8,48,1536]{2,1,0:T(8,128)(2,1)}, bf16[8,48,1536]{2,1,0:T(8,128)(2,1)}, bf16[8,48,1536]{2,1,0:T(8,128)(2,1)}, bf16[8,48,1536]{2,1,0:T(8,128)(2,1)}) custom-call(s32[1]{0:T(128)} %bitcast.5.core, bf16[256,3072]{1,0:T(8,128)(2,1)} %get-tuple-element.141.refs_14_.act0, bf16[256,3072]{1,0:T(8,128)(2,1)} %get-tuple-element.142.refs_14_.act1, ...), custom_call_target="tpu_custom_call" | custom-call | flops 2415919104 | bytes 9000000 | tf_op jit(solution)/shard_map/grad_contract/pallas_call | solution.py:576
  239.5 1.9 collective-permute-start.39
  241.4 6.9 %grad_expand.1 = (bf16[8,48,1536]{2,1,0:T(8,128)(2,1)}, bf16[8,48,1536]{2,1,0:T(8,128)(2,1)}, bf16[8,48,1536]{2,1,0:T(8,128)(2,1)}, bf16[8,48,1536]{2,1,0:T(8,128)(2,1)}) custom-call(s32[1]{0:T(128)} %bitcast.5.core, bf16[256,768]{1,0:T(8,128)(2,1)} %get-tuple-element.146.refs_11_.refs_0_, bf16[256,768]{1,0:T(8,128)(2,1)} %get-tuple-element.161.refs_11_.refs_1_, ...), custom_call_target="tpu_custom_call" | custom-call | flops 2415919104 | bytes 9000000 | tf_op jit(solution)/shard_map/grad_expand/pallas_call | solution.py:576
  248.8 1.4 collective-permute-start.40
  251.5 2.0 collective-permute-done.40
  255.8 2.0 fusion.4
  257.8 1.6 fusion.5
  263.3 6.9 %grad_projection.1 = (bf16[8,48,1536]{2,1,0:T(8,128)(2,1)}, bf16[8,48,1536]{2,1,0:T(8,128)(2,1)}, bf16[8,48,1536]{2,1,0:T(8,128)(2,1)}, bf16[8,48,1536]{2,1,0:T(8,128)(2,1)}) custom-call(s32[1]{0:T(128)} %bitcast.5.core, bf16[256,768]{1,0:T(8,128)(2,1)} %get-tuple-element.145.refs_10_.refs_0_, bf16[256,768]{1,0:T(8,128)(2,1)} %get-tuple-element.160.refs_10_.refs_1_, ...), custom_call_target="tpu_custom_call" | custom-call | flops 2415919104 | bytes 9000000 | tf_op jit(solution)/shard_map/grad_projection/pallas_call | solution.py:576
  283.2 7.2 %forward_only.2 = (bf16[2,256,768]{2,1,0:T(8,128)(2,1)}, f32[2,1,768]{2,1,0:T(1,128)S(1)}, bf16[16,48,2304]{2,1,0:T(8,128)(2,1)S(1)}, bf16[16,48,768]{2,1,0:T(8,...) custom-call(s32[1]{0:T(128)} %bitcast.refs_0_, ...), custom_call_target="tpu_custom_call" | custom-call | flops 7247757312 | bytes 20000000 | tf_op jit(solution)/shard_map/forward_only/pallas_call | solution.py:263
  290.4 2.2 copy-done.20
  292.5 2.2 copy-done.22
  294.8 8.4 %collective-permute-done.28 = bf16[2,2,48,1536]{3,2,0,1:T(8,128)(2,1)} collective-permute-done((bf16[2,2,48,1536]{3,2,0,1:T(8,128)(2,1)}, bf16[2,2,48,1536]{3,2,0,1:T(8,128)(2,1)}, u32[]{:S(2)}, u32[]{:S(2)}) %collective-permute-start.28) | collective-permute-done | bytes 589856 | tf_op jit(solution)/shard_map/ppermute | solution.py:637
  305.2 10.6 %collective-permute-done.25 = bf16[2,2,48,1536]{3,2,0,1:T(8,128)(2,1)} collective-permute-done((bf16[2,2,48,1536]{3,2,0,1:T(8,128)(2,1)}, bf16[2,2,48,1536]{3,2,0,1:T(8,128)(2,1)}, u32[]{:S(2)}, u32[]{:S(2)}) %collective-permute-start.25) | collective-permute-done | bytes 589856 | tf_op jit(solution)/shard_map/ppermute | solution.py:637
  315.8 1.4 collective-permute-start.14
  321.1 1.9 collective-permute-start.26
  324.2 5.3 %collective-permute-done.29 = bf16[2,48,1536]{2,1,0:T(8,128)(2,1)S(1)} collective-permute-done((bf16[2,48,1536]{2,1,0:T(8,128)(2,1)S(1)}, bf16[2,48,1536]{2,1,0:T(8,128)(2,1)S(1)}, u32[]{:S(2)}, u32[]{:S(2)}) %collective-permute-start.29) | collective-permute-done | bytes 294944 | tf_op jit(solution)/shard_map/ppermute | solution.py:637
  329.9 7.6 %collective-permute-done.26 = bf16[2,48,1536]{2,1,0:T(8,128)(2,1)S(1)} collective-permute-done((bf16[2,48,1536]{2,1,0:T(8,128)(2,1)S(1)}, bf16[2,48,1536]{2,1,0:T(8,128)(2,1)S(1)}, u32[]{:S(2)}, u32[]{:S(2)}) %collective-permute-start.26) | collective-permute-done | bytes 294944 | tf_op jit(solution)/shard_map/ppermute | solution.py:637
  337.6 4.2 collective-permute-done.35
  341.8 1.4 collective-permute-start.30
  344.0 2.4 collective-permute-done.32
  346.3 2.7 collective-permute-start.27
  349.1 5.1 %collective-permute-done.30 = bf16[48,1536]{1,0:T(8,128)(2,1)S(1)} collective-permute-done((bf16[48,1536]{1,0:T(8,128)(2,1)S(1)}, bf16[48,1536]{1,0:T(8,128)(2,1)S(1)}, u32[]{:S(2)}, u32[]{:S(2)}) %collective-permute-start.30) | collective-permute-done | bytes 147488 | tf_op jit(solution)/shard_map/ppermute | solution.py:637
  354.9 7.5 %collective-permute-done.36 = bf16[48,1536]{1,0:T(8,128)(2,1)S(1)} collective-permute-done((bf16[48,1536]{1,0:T(8,128)(2,1)S(1)}, bf16[48,1536]{1,0:T(8,128)(2,1)S(1)}, u32[]{:S(2)}, u32[]{:S(2)}) %collective-permute-start.36) | collective-permute-done | bytes 147488 | tf_op jit(solution)/shard_map/ppermute | solution.py:637
  362.5 6.9 %collective-permute-done.33 = bf16[48,1536]{1,0:T(8,128)(2,1)S(1)} collective-permute-done((bf16[48,1536]{1,0:T(8,128)(2,1)S(1)}, bf16[48,1536]{1,0:T(8,128)(2,1)S(1)}, u32[]{:S(2)}, u32[]{:S(2)}) %collective-permute-start.33) | collective-permute-done | bytes 147488 | tf_op jit(solution)/shard_map/ppermute | solution.py:637
  375.8 2.3 copy-done.21
  378.1 2.3 copy-done.23
  380.4 18.0 %forward_only.3 = (bf16[2,256,768]{2,1,0:T(8,128)(2,1)}, f32[2,1,768]{2,1,0:T(1,128)S(1)}) custom-call(s32[1]{0:T(128)S(6)} %sub.12.refs_0_, f32[2,2,1,256]{3,2,1,0:T(1,128)S(1)} %broadcast_in_dim.61.refs_1_, f32[2,2,256,1]{3,2,1,0:T(8,128)} %copy.198.refs_2_.refs_1_, f32[8,768]{1,0:T(8,128)S(1)} %copy-done.14, f32[1,3072]{1,0:T(1,128)S(1)} %copy-done.15, ...), custom_call_target="tpu_custom_call" | custom-call | flops 7247757312 | bytes 20000000 | tf_op jit(solution)/shard_map/forward_only/pallas_call | solution.py:263
  402.2 1.5 collective-permute-done.16
  406.0 3.6 collective-permute-done.17
  410.0 2.8 collective-permute-start.24
  412.8 5.6 %collective-permute-done.20 = bf16[2,48,1536]{2,1,0:T(8,128)(2,1)S(1)} collective-permute-done((bf16[2,48,1536]{2,1,0:T(8,128)(2,1)S(1)}, bf16[2,48,1536]{2,1,0:T(8,128)(2,1)S(1)}, u32[]{:S(2)}, u32[]{:S(2)}) %collective-permute-start.20) | collective-permute-done | bytes 294944 | tf_op jit(solution)/shard_map/ppermute | solution.py:637
  418.9 5.8 %collective-permute-done.18 = f32[16,1536]{1,0:T(8,128)S(1)} collective-permute-done((f32[16,1536]{1,0:T(8,128)S(1)}, f32[16,1536]{1,0:T(8,128)S(1)}, u32[]{:S(2)}, u32[]{:S(2)}) %collective-permute-start.18) | collective-permute-done | bytes 98336 | tf_op jit(solution)/shard_map/ppermute | solution.py:637
  425.5 2.3 collective-permute-done.24
  427.9 1.5 collective-permute-done.21
  (289 shorter events, 67.1 us)
Async XLA Ops:
  7.2 94.5 %all-gather.3.cloned.1.call-start = ((), (), s32[]{:S(2)}) async-start(), calls=%async_computation | async-start | bytes 17965056 | tf_op jit(solution)/shard_map/all_gather | solution.py:732
  9.6 9.4 %copy-start.42 = (s32[2,2,256]{2,1,0:T(2,128)S(1)}, s32[2,2,256]{2,1,0:T(2,128)}, u32[]{:S(2)}) copy-start(s32[2,2,256]{2,1,0:T(2,128)} %param.20) | copy-start | bytes 12292
  9.7 9.3 %copy-start.43 = (s32[2,2]{1,0:T(2,128)S(1)}, s32[2,2]{1,0:T(2,128)}, u32[]{:S(2)}) copy-start(s32[2,2]{1,0:T(2,128)} %param.21) | copy-start | bytes 52
  9.7 273.5 %all-gather.5.cloned.1.call-start = ((), (), s32[]{:S(2)}) async-start(), calls=%async_computation.1 | async-start | bytes 12115968 | tf_op jit(solution)/shard_map/all_gather | solution.py:739
  12.4 1.2 collective-permute-start
  13.6 3.7 collective-permute-start.1
  17.4 3.7 collective-permute-start.2
  21.1 5.1 %collective-permute-start.3 = (bf16[8,1152]{1,0:T(8,128)(2,1)S(1)}, bf16[8,1152]{1,0:T(8,128)(2,1)S(1)}, u32[]{:S(2)}, u32[]{:S(2)}) collective-permute-start(bf16[8,1152]{1,0:T(8,128)(2,1)S(1)} %pad_maximum_fusion.6), channel_id=1, source_target_pairs={{0,8},{1,9},{2,10},{3,11},{4,12},{5,13},{6,14},{7,15},{8,0},{9,1},... | collective-permute-start | bytes 55304 | tf_op jit(solution)/shard_map/ppermute | solution.py:637
  102.4 14.2 %copy-start.51 = (s32[2]{0:T(128)S(1)}, s32[2]{0:T(128)}, u32[]{:S(2)}) copy-start(s32[2]{0:T(128)} %param.22) | copy-start | bytes 28
  115.3 17.0 %copy-start.4 = (bf16[16,48,2304]{2,1,0:T(8,128)(2,1)}, bf16[16,48,2304]{2,1,0:T(8,128)(2,1)S(1)}, u32[]{:S(2)}) copy-start(bf16[16,48,2304]{2,1,0:T(8,128)(2,1)S(1)} %get-tuple-element.115.refs_6_.refs_4_) | copy-start | bytes 10616836
  115.3 21.5 %collective-permute-start.4 = (bf16[1,256,768]{2,1,0:T(8,128)(2,1)}, bf16[1,256,768]{2,1,0:T(8,128)(2,1)}, u32[]{:S(2)}, u32[]{:S(2)}) collective-permute-start(bf16[1,256,768]{2,1,0:T(8,128)(2,1)} %get-tuple-element.114), channel_id=1, source_target_pairs={{0,16},{1,17},{2,18},{3,19},{4,20},{5,21},{6,22},{7,23},{8,24},{9,... | collective-permute-start | bytes 1179656 | tf_op jit(solution)/shard_map/ppermute | solution.py:846
  129.8 7.0 %copy-start.10 = (bf16[16,48,768]{2,1,0:T(8,128)(2,1)S(1)}, bf16[16,48,768]{2,1,0:T(8,128)(2,1)}, u32[]{:S(2)}) copy-start(bf16[16,48,768]{2,1,0:T(8,128)(2,1)} %copy-done.8) | copy-start | bytes 3538948
  132.3 4.5 %copy-start.18 = (f32[1,1,768]{2,1,0:T(1,128)}, f32[1,1,768]{2,1,0:T(1,128)S(1)}, u32[]{:S(2)}) copy-start(f32[1,1,768]{2,1,0:T(1,128)S(1)} %get-tuple-element.129) | copy-start | bytes 9220
  132.3 37.5 %collective-permute-start.5 = (bf16[1,256,768]{2,1,0:T(8,128)(2,1)}, bf16[1,256,768]{2,1,0:T(8,128)(2,1)S(1)}, u32[]{:S(2)}, u32[]{:S(2)}) collective-permute-start(bf16[1,256,768]{2,1,0:T(8,128)(2,1)} %get-tuple-element.130), channel_id=1, source_target_pairs={{0,16},{1,17},{2,18},{3,19},{4,20},{5,21},{6,22},{7,23},{8,24},{9,... | collective-permute-start | bytes 1179656 | tf_op jit(solution)/shard_map/ppermute | solution.py:846
  136.8 16.2 %slice-start = ((s8[4718592]{0:T(1024)(128)(4,1)}), s8[4194304]{0:T(1024)(128)(4,1)S(1)}, s32[]{:S(2)}) async-start(s8[4718592]{0:T(1024)(128)(4,1)} %bitcast.195), calls=%async_computation.2 | async-start | bytes 8388608
  136.8 16.2 %slice-start.2 = ((s8[4718592]{0:T(1024)(128)(4,1)}), s8[4194304]{0:T(1024)(128)(4,1)S(1)}, s32[]{:S(2)}) async-start(s8[4718592]{0:T(1024)(128)(4,1)} %bitcast.197), calls=%async_computation.4 | async-start | bytes 8388608
  139.0 14.1 %slice-start.1 = ((s8[4718592]{0:T(1024)(128)(4,1)}), s8[524288]{0:T(1024)(128)(4,1)S(1)}, s32[]{:S(2)}) async-start(s8[4718592]{0:T(1024)(128)(4,1)} %bitcast.195), calls=%async_computation.3 | async-start | bytes 1048576
  139.0 14.1 %slice-start.3 = ((s8[4718592]{0:T(1024)(128)(4,1)}), s8[524288]{0:T(1024)(128)(4,1)S(1)}, s32[]{:S(2)}) async-start(s8[4718592]{0:T(1024)(128)(4,1)} %bitcast.197), calls=%async_computation.5 | async-start | bytes 1048576
  139.0 14.1 %copy-start.13 = (f32[8,768]{1,0:T(8,128)S(1)}, f32[8,768]{1,0:T(8,128)}, u32[]{:S(2)}) copy-start(f32[8,768]{1,0:T(8,128)} %reshape.197.refs_3_.refs_2_) | copy-start | bytes 73732
  155.1 15.5 %copy-start.7 = (bf16[16,48,2304]{2,1,0:T(8,128)(2,1)S(1)}, bf16[16,48,2304]{2,1,0:T(8,128)(2,1)}, u32[]{:S(2)}) copy-start(bf16[16,48,2304]{2,1,0:T(8,128)(2,1)} %copy-done.4) | copy-start | bytes 10616836
  168.5 32.5 %collective-permute-start.6 = (bf16[256,768]{1,0:T(8,128)(2,1)S(1)}, bf16[256,768]{1,0:T(8,128)(2,1)S(1)}, u32[]{:S(2)}, u32[]{:S(2)}) collective-permute-start(bf16[256,768]{1,0:T(8,128)(2,1)S(1)} %get-tuple-element.151), channel_id=1, source_target_pairs={{16,0},{17,1},{18,2},{19,3},{20,4},{21,5},{22,6},{23,7},{24,8},{25... | collective-permute-start | bytes 1179656 | tf_op jit(solution)/shard_map/ppermute | solution.py:855
  183.8 15.1 %copy-start.26 = (bf16[2,2,256,768]{3,2,1,0:T(8,128)(2,1)S(1)}, bf16[2,2,256,768]{3,2,1,0:T(8,128)(2,1)}, u32[]{:S(2)}) copy-start(bf16[2,2,256,768]{3,2,1,0:T(8,128)(2,1)} %refs_5_.7) | copy-start | bytes 4718596
  183.9 15.1 %copy-start.33 = (bf16[1,256,768]{2,1,0:T(8,128)(2,1)S(1)}, bf16[1,256,768]{2,1,0:T(8,128)(2,1)}, u32[]{:S(2)}) copy-start(bf16[1,256,768]{2,1,0:T(8,128)(2,1)} %copy-done.32) | copy-start | bytes 1179652
  197.6 9.8 %collective-permute-start.7 = (bf16[256,768]{1,0:T(8,128)(2,1)S(1)}, bf16[256,768]{1,0:T(8,128)(2,1)S(1)}, u32[]{:S(2)}, u32[]{:S(2)}) collective-permute-start(bf16[256,768]{1,0:T(8,128)(2,1)S(1)} %get-tuple-element.166), channel_id=1, source_target_pairs={{16,0},{17,1},{18,2},{19,3},{20,4},{21,5},{22,6},{23,7},{24,8},{25... | collective-permute-start | bytes 1179656 | tf_op jit(solution)/shard_map/ppermute | solution.py:855
  229.1 1.4 collective-permute-start.37
  230.6 8.9 %collective-permute-start.38 = (bf16[2,2,48,128]{3,2,1,0:T(8,128)(2,1)S(1)}, bf16[2,2,48,128]{3,2,1,0:T(8,128)(2,1)S(1)}, u32[]{:S(2)}, u32[]{:S(2)}) collective-permute-start(bf16[2,2,48,128]{3,2,1,0:T(8,128)(2,1)S(1)} %dynamic-slice_bitcast_fusion.13), channel_id=1, source_target_pairs={{0,2},{1,3},{2,0},{3,1},{4,6},{5,7},{6,4},{7,5},{8,10},{9,11},{10,... | collective-permute-start | bytes 147464 | tf_op jit(solution)/shard_map/ppermute | solution.py:637
  238.9 16.9 %collective-permute-start.9 = (bf16[2,2,2,48,1536]{4,3,2,1,0:T(8,128)(2,1)}, bf16[2,2,2,48,1536]{4,3,2,1,0:T(8,128)(2,1)}, u32[]{:S(2)}, u32[]{:S(2)}) collective-permute-start(bf16[2,2,2,48,1536]{4,3,2,1,0:T(8,128)(2,1)} %bitcast.230), channel_id=1, source_target_pairs={{0,1},{1,0},{2,3},{3,2},{4,5},{5,4},{6,7},{7,6},{8,9},{9,8},{10,11... | collective-permute-start | bytes 3538952 | tf_op jit(solution)/shard_map/ppermute | solution.py:637
  239.0 18.8 %collective-permute-start.8 = (bf16[2,2,2,48,1536]{4,3,2,1,0:T(8,128)(2,1)}, bf16[2,2,2,48,1536]{4,3,2,1,0:T(8,128)(2,1)}, u32[]{:S(2)}, u32[]{:S(2)}) collective-permute-start(bf16[2,2,2,48,1536]{4,3,2,1,0:T(8,128)(2,1)} %bitcast.229), channel_id=1, source_target_pairs={{0,1},{1,0},{2,3},{3,2},{4,5},{5,4},{6,7},{7,6},{8,9},{9,8},{10,11... | collective-permute-start | bytes 3538952 | tf_op jit(solution)/shard_map/ppermute | solution.py:637
  239.5 9.3 %collective-permute-start.39 = (bf16[2,48,128]{2,1,0:T(8,128)(2,1)S(1)}, bf16[2,48,128]{2,1,0:T(8,128)(2,1)S(1)}, u32[]{:S(2)}, u32[]{:S(2)}) collective-permute-start(bf16[2,48,128]{2,1,0:T(8,128)(2,1)S(1)} %dynamic-slice_bitcast_fusion.14), channel_id=1, source_target_pairs={{0,4},{1,5},{2,6},{3,7},{4,0},{5,1},{6,2},{7,3},{8,12},{9,13},{10,... | collective-permute-start | bytes 73736 | tf_op jit(solution)/shard_map/ppermute | solution.py:637
  241.4 8.9 %copy-start.27 = (f32[256,768]{1,0:T(8,128)S(1)}, f32[256,768]{1,0:T(8,128)}, u32[]{:S(2)}) copy-start(f32[256,768]{1,0:T(8,128)} %get-tuple-element.201) | copy-start | bytes 2359300
  241.4 8.9 %copy-start.28 = (f32[256,768]{1,0:T(8,128)S(1)}, f32[256,768]{1,0:T(8,128)}, u32[]{:S(2)}) copy-start(f32[256,768]{1,0:T(8,128)} %get-tuple-element.202) | copy-start | bytes 2359300
  248.2 22.1 %collective-permute-start.11 = (bf16[2,2,2,48,1536]{4,3,2,1,0:T(8,128)(2,1)}, bf16[2,2,2,48,1536]{4,3,2,1,0:T(8,128)(2,1)S(1)}, u32[]{:S(2)}, u32[]{:S(2)}) collective-permute-start(bf16[2,2,2,48,1536]{4,3,2,1,0:T(8,128)(2,1)} %bitcast.228), channel_id=1, source_target_pairs={{0,1},{1,0},{2,3},{3,2},{4,5},{5,4},{6,7},{7,6},{8,9},{9,8},{10,11... | collective-permute-start | bytes 3538952 | tf_op jit(solution)/shard_map/ppermute | solution.py:637
  248.3 22.9 %collective-permute-start.10 = (bf16[2,2,2,48,1536]{4,3,2,1,0:T(8,128)(2,1)}, bf16[2,2,2,48,1536]{4,3,2,1,0:T(8,128)(2,1)S(1)}, u32[]{:S(2)}, u32[]{:S(2)}) collective-permute-start(bf16[2,2,2,48,1536]{4,3,2,1,0:T(8,128)(2,1)} %bitcast.227), channel_id=1, source_target_pairs={{0,1},{1,0},{2,3},{3,2},{4,5},{5,4},{6,7},{7,6},{8,9},{9,8},{10,11... | collective-permute-start | bytes 3538952 | tf_op jit(solution)/shard_map/ppermute | solution.py:637
  248.8 4.7 %collective-permute-start.40 = (bf16[48,128]{1,0:T(8,128)(2,1)S(1)}, bf16[48,128]{1,0:T(8,128)(2,1)S(1)}, u32[]{:S(2)}, u32[]{:S(2)}) collective-permute-start(bf16[48,128]{1,0:T(8,128)(2,1)S(1)} %dynamic-slice_bitcast_fusion.15), channel_id=1, source_target_pairs={{0,8},{1,9},{2,10},{3,11},{4,12},{5,13},{6,14},{7,15},{8,0},{9,1},... | collective-permute-start | bytes 36872 | tf_op jit(solution)/shard_map/ppermute | solution.py:637
  261.3 58.3 %collective-permute-start.34 = (bf16[2,2,48,1536]{3,2,0,1:T(8,128)(2,1)}, bf16[2,2,48,1536]{3,2,0,1:T(8,128)(2,1)}, u32[]{:S(2)}, u32[]{:S(2)}) collective-permute-start(bf16[2,2,48,1536]{3,2,0,1:T(8,128)(2,1)} %bitcast.189), channel_id=1, source_target_pairs={{0,2},{1,3},{2,0},{3,1},{4,6},{5,7},{6,4},{7,5},{8,10},{9,11},{10,... | collective-permute-start | bytes 1769480 | tf_op jit(solution)/shard_map/ppermute | solution.py:637
  262.1 59.0 %collective-permute-start.31 = (bf16[2,2,48,1536]{3,2,0,1:T(8,128)(2,1)}, bf16[2,2,48,1536]{3,2,0,1:T(8,128)(2,1)}, u32[]{:S(2)}, u32[]{:S(2)}) collective-permute-start(bf16[2,2,48,1536]{3,2,0,1:T(8,128)(2,1)} %bitcast.190), channel_id=1, source_target_pairs={{0,2},{1,3},{2,0},{3,1},{4,6},{5,7},{6,4},{7,5},{8,10},{9,11},{10,... | collective-permute-start | bytes 1769480 | tf_op jit(solution)/shard_map/ppermute | solution.py:637
  263.3 7.5 %copy-start.35 = (bf16[8,48,1536]{2,1,0:T(8,128)(2,1)S(1)}, bf16[8,48,1536]{2,1,0:T(8,128)(2,1)}, u32[]{:S(2)}) copy-start(bf16[8,48,1536]{2,1,0:T(8,128)(2,1)} %get-tuple-element.181) | copy-start | bytes 3538948
  270.3 6.0 %collective-permute-start.12 = (bf16[2,2,2,48,1536]{4,3,2,1,0:T(8,128)(2,1)}, bf16[2,2,2,48,1536]{4,3,2,1,0:T(8,128)(2,1)S(1)}, u32[]{:S(2)}, u32[]{:S(2)}) collective-permute-start(bf16[2,2,2,48,1536]{4,3,2,1,0:T(8,128)(2,1)} %bitcast.232), channel_id=1, source_target_pairs={{0,1},{1,0},{2,3},{3,2},{4,5},{5,4},{6,7},{7,6},{8,9},{9,8},{10,11... | collective-permute-start | bytes 3538952 | tf_op jit(solution)/shard_map/ppermute | solution.py:637
  270.4 9.3 %collective-permute-start.13 = (bf16[2,2,2,48,1536]{4,3,2,1,0:T(8,128)(2,1)}, bf16[2,2,2,48,1536]{4,3,2,1,0:T(8,128)(2,1)S(1)}, u32[]{:S(2)}, u32[]{:S(2)}) collective-permute-start(bf16[2,2,2,48,1536]{4,3,2,1,0:T(8,128)(2,1)} %bitcast.231), channel_id=1, source_target_pairs={{0,1},{1,0},{2,3},{3,2},{4,5},{5,4},{6,7},{7,6},{8,9},{9,8},{10,11... | collective-permute-start | bytes 3538952 | tf_op jit(solution)/shard_map/ppermute | solution.py:637
  274.4 28.8 %collective-permute-start.28 = (bf16[2,2,48,1536]{3,2,0,1:T(8,128)(2,1)}, bf16[2,2,48,1536]{3,2,0,1:T(8,128)(2,1)}, u32[]{:S(2)}, u32[]{:S(2)}) collective-permute-start(bf16[2,2,48,1536]{3,2,0,1:T(8,128)(2,1)} %bitcast.187), channel_id=1, source_target_pairs={{0,2},{1,3},{2,0},{3,1},{4,6},{5,7},{6,4},{7,5},{8,10},{9,11},{10,... | collective-permute-start | bytes 1769480 | tf_op jit(solution)/shard_map/ppermute | solution.py:637
  276.3 39.6 %collective-permute-start.25 = (bf16[2,2,48,1536]{3,2,0,1:T(8,128)(2,1)}, bf16[2,2,48,1536]{3,2,0,1:T(8,128)(2,1)}, u32[]{:S(2)}, u32[]{:S(2)}) collective-permute-start(bf16[2,2,48,1536]{3,2,0,1:T(8,128)(2,1)} %bitcast.188), channel_id=1, source_target_pairs={{0,2},{1,3},{2,0},{3,1},{4,6},{5,7},{6,4},{7,5},{8,10},{9,11},{10,... | collective-permute-start | bytes 1769480 | tf_op jit(solution)/shard_map/ppermute | solution.py:637
  282.3 92.2 %collective-permute-start.22 = (bf16[2,2,48,1536]{3,2,0,1:T(8,128)(2,1)}, bf16[2,2,48,1536]{3,2,0,1:T(8,128)(2,1)}, u32[]{:S(2)}, u32[]{:S(2)}) collective-permute-start(bf16[2,2,48,1536]{3,2,0,1:T(8,128)(2,1)} %bitcast.185), channel_id=1, source_target_pairs={{0,2},{1,3},{2,0},{3,1},{4,6},{5,7},{6,4},{7,5},{8,10},{9,11},{10,... | collective-permute-start | bytes 1769480 | tf_op jit(solution)/shard_map/ppermute | solution.py:637
  294.8 23.7 %copy-start.24 = (bf16[16,48,2304]{2,1,0:T(8,128)(2,1)}, bf16[16,48,2304]{2,1,0:T(8,128)(2,1)S(1)}, u32[]{:S(2)}) copy-start(bf16[16,48,2304]{2,1,0:T(8,128)(2,1)S(1)} %get-tuple-element.196.refs_6_) | copy-start | bytes 10616836
  303.2 97.8 %collective-permute-start.19 = (bf16[2,2,48,1536]{3,2,0,1:T(8,128)(2,1)}, bf16[2,2,48,1536]{3,2,0,1:T(8,128)(2,1)}, u32[]{:S(2)}, u32[]{:S(2)}) collective-permute-start(bf16[2,2,48,1536]{3,2,0,1:T(8,128)(2,1)} %bitcast.186), channel_id=1, source_target_pairs={{0,2},{1,3},{2,0},{3,1},{4,6},{5,7},{6,4},{7,5},{8,10},{9,11},{10,... | collective-permute-start | bytes 1769480 | tf_op jit(solution)/shard_map/ppermute | solution.py:637
  315.8 59.9 %collective-permute-start.14 = (bf16[2,256,768]{2,1,0:T(8,128)(2,1)}, bf16[2,256,768]{2,1,0:T(8,128)(2,1)}, u32[]{:S(2)}, u32[]{:S(2)}) collective-permute-start(bf16[2,256,768]{2,1,0:T(8,128)(2,1)} %get-tuple-element.195), channel_id=1, source_target_pairs={{0,16},{1,17},{2,18},{3,19},{4,20},{5,21},{6,22},{7,23},{8,24},{9,... | collective-permute-start | bytes 2359304 | tf_op jit(solution)/shard_map/ppermute | solution.py:944
  319.6 10.0 %collective-permute-start.29 = (bf16[2,48,1536]{2,1,0:T(8,128)(2,1)S(1)}, bf16[2,48,1536]{2,1,0:T(8,128)(2,1)S(1)}, u32[]{:S(2)}, u32[]{:S(2)}) collective-permute-start(bf16[2,48,1536]{2,1,0:T(8,128)(2,1)S(1)} %dynamic-slice_bitcast_fusion.2), channel_id=1, source_target_pairs={{0,4},{1,5},{2,6},{3,7},{4,0},{5,1},{6,2},{7,3},{8,12},{9,13},{10,... | collective-permute-start | bytes 884744 | tf_op jit(solution)/shard_map/ppermute | solution.py:637
  321.1 16.4 %collective-permute-start.26 = (bf16[2,48,1536]{2,1,0:T(8,128)(2,1)S(1)}, bf16[2,48,1536]{2,1,0:T(8,128)(2,1)S(1)}, u32[]{:S(2)}, u32[]{:S(2)}) collective-permute-start(bf16[2,48,1536]{2,1,0:T(8,128)(2,1)S(1)} %dynamic-slice_bitcast_fusion.3), channel_id=1, source_target_pairs={{0,4},{1,5},{2,6},{3,7},{4,0},{5,1},{6,2},{7,3},{8,12},{9,13},{10,... | collective-permute-start | bytes 884744 | tf_op jit(solution)/shard_map/ppermute | solution.py:637
  329.6 12.2 %collective-permute-start.35 = (bf16[2,48,1536]{2,1,0:T(8,128)(2,1)S(1)}, bf16[2,48,1536]{2,1,0:T(8,128)(2,1)S(1)}, u32[]{:S(2)}, u32[]{:S(2)}) collective-permute-start(bf16[2,48,1536]{2,1,0:T(8,128)(2,1)S(1)} %dynamic-slice_bitcast_fusion), channel_id=1, source_target_pairs={{0,4},{1,5},{2,6},{3,7},{4,0},{5,1},{6,2},{7,3},{8,12},{9,13},{10,... | collective-permute-start | bytes 884744 | tf_op jit(solution)/shard_map/ppermute | solution.py:637
  337.5 8.8 %collective-permute-start.32 = (bf16[2,48,1536]{2,1,0:T(8,128)(2,1)S(1)}, bf16[2,48,1536]{2,1,0:T(8,128)(2,1)S(1)}, u32[]{:S(2)}, u32[]{:S(2)}) collective-permute-start(bf16[2,48,1536]{2,1,0:T(8,128)(2,1)S(1)} %dynamic-slice_bitcast_fusion.1), channel_id=1, source_target_pairs={{0,4},{1,5},{2,6},{3,7},{4,0},{5,1},{6,2},{7,3},{8,12},{9,13},{10,... | collective-permute-start | bytes 884744 | tf_op jit(solution)/shard_map/ppermute | solution.py:637
  341.8 12.4 %collective-permute-start.30 = (bf16[48,1536]{1,0:T(8,128)(2,1)S(1)}, bf16[48,1536]{1,0:T(8,128)(2,1)S(1)}, u32[]{:S(2)}, u32[]{:S(2)}) collective-permute-start(bf16[48,1536]{1,0:T(8,128)(2,1)S(1)} %dynamic-slice_bitcast_fusion.8), channel_id=1, source_target_pairs={{0,8},{1,9},{2,10},{3,11},{4,12},{5,13},{6,14},{7,15},{8,0},{9,1},... | collective-permute-start | bytes 442376 | tf_op jit(solution)/shard_map/ppermute | solution.py:637
  346.3 26.0 %collective-permute-start.27 = (bf16[48,1536]{1,0:T(8,128)(2,1)}, bf16[48,1536]{1,0:T(8,128)(2,1)}, u32[]{:S(2)}, u32[]{:S(2)}) collective-permute-start(bf16[48,1536]{1,0:T(8,128)(2,1)} %dynamic-slice_bitcast_fusion.9), channel_id=1, source_target_pairs={{0,8},{1,9},{2,10},{3,11},{4,12},{5,13},{6,14},{7,15},{8,0},{9,1},... | collective-permute-start | bytes 442376 | tf_op jit(solution)/shard_map/ppermute | solution.py:637
  354.2 8.2 %collective-permute-start.36 = (bf16[48,1536]{1,0:T(8,128)(2,1)S(1)}, bf16[48,1536]{1,0:T(8,128)(2,1)S(1)}, u32[]{:S(2)}, u32[]{:S(2)}) collective-permute-start(bf16[48,1536]{1,0:T(8,128)(2,1)S(1)} %dynamic-slice_bitcast_fusion.6), channel_id=1, source_target_pairs={{0,8},{1,9},{2,10},{3,11},{4,12},{5,13},{6,14},{7,15},{8,0},{9,1},... | collective-permute-start | bytes 442376 | tf_op jit(solution)/shard_map/ppermute | solution.py:637
  362.4 7.0 %collective-permute-start.33 = (bf16[48,1536]{1,0:T(8,128)(2,1)S(1)}, bf16[48,1536]{1,0:T(8,128)(2,1)S(1)}, u32[]{:S(2)}, u32[]{:S(2)}) collective-permute-start(bf16[48,1536]{1,0:T(8,128)(2,1)S(1)} %dynamic-slice_bitcast_fusion.7), channel_id=1, source_target_pairs={{0,8},{1,9},{2,10},{3,11},{4,12},{5,13},{6,14},{7,15},{8,0},{9,1},... | collective-permute-start | bytes 442376 | tf_op jit(solution)/shard_map/ppermute | solution.py:637
  370.2 3.5 copy-start.39
  371.4 4.3 copy-start.25
  380.4 18.0 %copy-start.48 = (pred[2,2]{1,0:T(4,128)(4,1)S(1)}, pred[2,2]{1,0:T(4,128)(4,1)}, u32[]{:S(2)}) copy-start(pred[2,2]{1,0:T(4,128)(4,1)} %iota_compare_fusion.1) | copy-start | bytes 16
  398.6 1.2 collective-permute-start.15
  398.7 11.2 %collective-permute-start.23 = (bf16[2,48,1536]{2,1,0:T(8,128)(2,1)S(1)}, bf16[2,48,1536]{2,1,0:T(8,128)(2,1)S(1)}, u32[]{:S(2)}, u32[]{:S(2)}) collective-permute-start(bf16[2,48,1536]{2,1,0:T(8,128)(2,1)S(1)} %dynamic-slice_bitcast_fusion.4), channel_id=1, source_target_pairs={{0,4},{1,5},{2,6},{3,7},{4,0},{5,1},{6,2},{7,3},{8,12},{9,13},{10,... | collective-permute-start | bytes 884744 | tf_op jit(solution)/shard_map/ppermute | solution.py:637
  399.9 3.9 collective-permute-start.16
  403.8 5.8 %collective-permute-start.17 = (f32[8,1536]{1,0:T(8,128)S(1)}, f32[8,1536]{1,0:T(8,128)S(1)}, u32[]{:S(2)}, u32[]{:S(2)}) collective-permute-start(f32[8,1536]{1,0:T(8,128)S(1)} %pad_maximum_fusion.4), channel_id=1, source_target_pairs={{0,4},{1,5},{2,6},{3,7},{4,0},{5,1},{6,2},{7,3},{8,12},{9,13},{10,... | collective-permute-start | bytes 147464 | tf_op jit(solution)/shard_map/ppermute | solution.py:637
  404.8 13.6 %collective-permute-start.20 = (bf16[2,48,1536]{2,1,0:T(8,128)(2,1)S(1)}, bf16[2,48,1536]{2,1,0:T(8,128)(2,1)S(1)}, u32[]{:S(2)}, u32[]{:S(2)}) collective-permute-start(bf16[2,48,1536]{2,1,0:T(8,128)(2,1)S(1)} %dynamic-slice_bitcast_fusion.5), channel_id=1, source_target_pairs={{0,4},{1,5},{2,6},{3,7},{4,0},{5,1},{6,2},{7,3},{8,12},{9,13},{10,... | collective-permute-start | bytes 884744 | tf_op jit(solution)/shard_map/ppermute | solution.py:637
  409.6 15.0 %collective-permute-start.18 = (f32[16,1536]{1,0:T(8,128)S(1)}, f32[16,1536]{1,0:T(8,128)S(1)}, u32[]{:S(2)}, u32[]{:S(2)}) collective-permute-start(f32[16,1536]{1,0:T(8,128)S(1)} %pad_maximum_fusion.1), channel_id=1, source_target_pairs={{0,8},{1,9},{2,10},{3,11},{4,12},{5,13},{6,14},{7,15},{8,0},{9,1},... | collective-permute-start | bytes 294920 | tf_op jit(solution)/shard_map/ppermute | solution.py:637
  410.0 17.8 %collective-permute-start.24 = (bf16[48,1536]{1,0:T(8,128)(2,1)S(1)}, bf16[48,1536]{1,0:T(8,128)(2,1)S(1)}, u32[]{:S(2)}, u32[]{:S(2)}) collective-permute-start(bf16[48,1536]{1,0:T(8,128)(2,1)S(1)} %dynamic-slice_bitcast_fusion.10), channel_id=1, source_target_pairs={{0,8},{1,9},{2,10},{3,11},{4,12},{5,13},{6,14},{7,15},{8,0},{9,1},... | collective-permute-start | bytes 442376 | tf_op jit(solution)/shard_map/ppermute | solution.py:637
  418.5 10.9 %collective-permute-start.21 = (bf16[48,1536]{1,0:T(8,128)(2,1)S(1)}, bf16[48,1536]{1,0:T(8,128)(2,1)S(1)}, u32[]{:S(2)}, u32[]{:S(2)}) collective-permute-start(bf16[48,1536]{1,0:T(8,128)(2,1)S(1)} %dynamic-slice_bitcast_fusion.11), channel_id=1, source_target_pairs={{0,8},{1,9},{2,10},{3,11},{4,12},{5,13},{6,14},{7,15},{8,0},{9,1},... | collective-permute-start | bytes 442376 | tf_op jit(solution)/shard_map/ppermute | solution.py:637
  (35 other events, 65.7 us)
Sparse Core Ops, SparseCore 0:
  10.2 91.4 all-gather.2
  103.9 93.5 all-gather.4

commit v5 on v0

v5 whole, which is shorter than its diff:
```python
import functools

import jax
import jax.numpy as jnp
from jax import lax
from jax.experimental import pallas as pl
from jax.experimental.pallas import tpu as pltpu
from jax.sharding import PartitionSpec as P

DP, SECTION = "dp", "section"
HD = 64
BLOCK = 48
VMEM_LIMIT = 56 * 1024 * 1024

epsilon = 1e-12
SCALE = HD ** (-0.5)

ANY = pl.BlockSpec(memory_space=pl.ANY)
VMEM = pl.BlockSpec(memory_space=pltpu.VMEM)
SMEM = pl.BlockSpec(memory_space=pltpu.SMEM)


def dot_nn(a, b):
    return jnp.dot(a, b, preferred_element_type=jnp.float32)


def dot_nt(a, b):
    return lax.dot_general(a, b, (((1,), (1,)), ((), ())), preferred_element_type=jnp.float32)


def dot_tn(a, b):
    return lax.dot_general(a, b, (((0,), (0,)), ((), ())), preferred_element_type=jnp.float32)


def gelu_parts(values):
    size = jnp.abs(values)
    inverse = 1.0 / (1.0 + (0.3275911 * 0.5**0.5) * size)
    series = 0.5 * 1.061405429
    for factor in (-1.453152027, 1.421413741, -0.284496736, 0.254829592):
        series = series * inverse + 0.5 * factor
    bell = jnp.exp(-0.5 * (values * values))
    tail = series * inverse * bell
    phi = jnp.where(values >= 0, 1.0 - tail, tail)
    return values * phi, phi + values * bell * 0.3989422804014327


def normalised(values):
    centred = values - jnp.mean(values, axis=-1, keepdims=True)
    variance = jnp.mean(centred * centred, axis=-1, keepdims=True)
    scale = lax.rsqrt(variance + epsilon)
    return centred * scale, scale


(
    PROJ,
    OUT,
    EXPAND,
    CONTRACT,
    MIX,
    PROBS,
    HAT1,
    HAT2,
    SLOPE,
    STATS,
    ATT,
    LOW,
    ACT,
    TOTAL,
    DBRANCH,
    DUPWARD,
    DOUTPUT,
    DMIX,
    DATT,
    X_IN,
    G_IN,
) = range(21)
NAMES = (PROJ, OUT, EXPAND, CONTRACT)
SAVED = (MIX, PROBS, HAT1, HAT2, SLOPE, STATS, ATT, LOW, ACT)
UNROLL = 3
TERMS = (TOTAL, DBRANCH, DUPWARD, DOUTPUT, DMIX)


def flat(block):
    return block.reshape(-1, block.shape[-1])


def shape_of(name, rows, features, hidden_size):
    blocks = features // BLOCK
    bf16, f32 = jnp.bfloat16, jnp.float32
    return {
        PROJ: ((blocks, BLOCK, 3 * features), bf16),
        OUT: ((blocks, BLOCK, features), bf16),
        EXPAND: ((blocks, BLOCK, hidden_size), bf16),
        CONTRACT: ((blocks, hidden_size // features, BLOCK, features), bf16),
        MIX: ((rows, 3 * features), bf16),
        PROBS: ((features // HD, rows, rows), bf16),
        STATS: ((rows, 128), f32),
        ACT: ((rows, hidden_size), bf16),
        SLOPE: ((rows, hidden_size), bf16),
        DUPWARD: ((rows, hidden_size), bf16),
        DMIX: ((rows, 3 * features), bf16),
        TOTAL: ((rows, features), f32),
    }.get(name, ((rows, features), bf16))


def scratch_of(names, *sizes):
    return [pltpu.VMEM(*shape_of(name, *sizes)) for name in names]


def outputs_of(names, *sizes):
    return [jax.ShapeDtypeStruct(*shape_of(name, *sizes)) for name in names]


class Copier:
    def __init__(self, sems):
        self.sems, self.count, self.open = sems, 0, []

    def fetch(self, source, place):
        copy = pltpu.make_async_copy(source, place, self.sems.at[self.count])
        self.count += 1
        copy.start()
        return copy

    def send(self, source, place):
        self.open.append(self.fetch(source, place))

    def finish(self):
        for copy in self.open:
            copy.wait()


class Held:
    def __init__(self, names, buffers, copier):
        self.buffers, self.pending, self.copier = dict(zip(names, buffers)), {}, copier

    def fill(self, name, source):
        self.pending[name] = [self.copier.fetch(source, self.buffers[name])]

    def fill_weight(self, wanted, layout, packs):
        buffer = self.buffers[wanted]
        for name, pack, source, width, target in layout:
            if name == wanted:
                block = packs[pack].at[:, :, pl.ds(source, width)]
                if name == CONTRACT:
                    place = buffer.at[:, target]
                else:
                    place = buffer.at[:, :, pl.ds(target, width)]
                self.pending.setdefault(name, []).append(self.copier.fetch(block, place))

    def __contains__(self, name):
        return name in self.buffers

    def __getitem__(self, name):
        for copy in self.pending.pop(name, ()):
            copy.wait()
        return self.buffers[name]


def two_heads(pair, head_low):
    zero = jnp.zeros_like(pair)
    return jnp.concatenate(
        [jnp.where(head_low, pair, zero), jnp.where(head_low, zero, pair)], axis=0
    )


def merged_heads(stacked, head_low):
    rows = stacked.shape[0] // 2
    return jnp.where(head_low, stacked[:rows], stacked[rows:])


def low_lanes(rows):
    return lax.broadcasted_iota(jnp.int32, (rows, 2 * HD), 1) < HD


def forward_rows(x, validity, lines, offs, held, done):
    rows, features = x.shape
    saving = PROBS in held
    mix, att, low = held[MIX], held[ATT], held[LOW]
    for third, line in enumerate((2, None, 3)):
        columns = pl.ds(third * features, features)
        part = dot_nn(x, flat(held[PROJ][:, :, columns]))
        if line is not None:
            part = part + lines[line : line + 1, :]
        mix[:, columns] = part.astype(jnp.bfloat16)
    done(MIX)
    head_low = low_lanes(rows)
    valid = jnp.broadcast_to(validity > 0, (2 * rows, rows))

    def pair_step(pair, _):
        at = pl.multiple_of(pair * 2 * HD, 2 * HD)
        q = mix[:, pl.ds(at, 2 * HD)] * jnp.asarray(SCALE, jnp.bfloat16)
        k = mix[:, pl.ds(features + at, 2 * HD)]
        v = mix[:, pl.ds(2 * features + at, 2 * HD)]
        scores = jnp.where(valid, dot_nt(two_heads(q, head_low), k), -1e30)
        top = jnp.max(scores, axis=-1, keepdims=True)
        weight = jnp.exp(scores - top)
        share = 1.0 / jnp.sum(weight, axis=-1, keepdims=True)
        if saving:
            weight = (weight * share).astype(jnp.bfloat16)
            held[PROBS][pl.ds(2 * pair, 2)] = weight.reshape(2, rows, rows)
            mixed = dot_nn(weight, v)
        else:
            mixed = dot_nn(weight.astype(jnp.bfloat16), v) * share
        att[:, pl.ds(at, 2 * HD)] = merged_heads(mixed, head_low).astype(jnp.bfloat16)

    lax.fori_loop(0, features // (2 * HD), pair_step, None, unroll=UNROLL)
    done(PROBS)
    done(ATT)
    total = x.astype(jnp.float32) + dot_nn(att[...], flat(held[OUT][...]))
    hat, scale = normalised(total + lines[4:5, :])
    hidden = hat * lines[0:1, :] + lines[5:6, :]
    low[...] = hidden.astype(jnp.bfloat16)
    if saving:
        held[HAT1][...] = hat.astype(jnp.bfloat16)
        held[STATS][:, 0:1] = scale
    done(LOW)
    done(HAT1)
    groups = offs.shape[1] // features
    total = hidden + lines[6:7, :]
    for group in range(groups):
        columns = pl.ds(group * features, features)
        upward = dot_nn(low[...], flat(held[EXPAND][:, :, columns]))
        value, gradient = gelu_parts(upward + offs[:, columns])
        value = value.astype(jnp.bfloat16)
        if saving:
            held[ACT][:, columns] = value
            held[SLOPE][:, columns] = gradient.astype(jnp.bfloat16)
        contract = held[CONTRACT]
        stack = contract.shape[0] // groups
        total = total + dot_nn(value, flat(contract[group * stack : (group + 1) * stack]))
    done(ACT)
    done(SLOPE)
    hat, scale = normalised(total)
    if saving:
        held[HAT2][...] = hat.astype(jnp.bfloat16)
        held[STATS][:, 1:2] = scale
    done(HAT2)
    done(STATS)
    return hat * lines[1:2, :] + lines[7:8, :]


def pooled_rows(value, across, down):
    total = jnp.sum(value * down, axis=0, keepdims=True)
    return total / jnp.sum(across, axis=-1, keepdims=True)


def norm_back(gradient, hat, scale, gain):
    weighted = gradient * gain
    mean = jnp.mean(weighted, axis=-1, keepdims=True)
    slant = jnp.mean(weighted * hat, axis=-1, keepdims=True)
    return scale * (weighted - mean - hat * slant)


def column_sum(vec_out, line, values):
    vec_out[line : line + 1, :] = jnp.sum(values, axis=0, keepdims=True)


def backward_feed(gradient, lines, held, vec_out, offs_out, done):
    features = gradient.shape[1]
    hat = held[HAT2][...].astype(jnp.float32)
    column_sum(vec_out, 1, gradient * hat)
    column_sum(vec_out, 7, gradient)
    moved = norm_back(gradient, hat, held[STATS][:, 1:2], lines[1:2, :])
    held[TOTAL][...] = moved
    rounded = moved.astype(jnp.bfloat16)
    held[DBRANCH][...] = rounded
    column_sum(vec_out, 6, rounded.astype(jnp.float32))
    done(DBRANCH)
    groups = offs_out.shape[1] // features
    contract = held[CONTRACT]
    stack = contract.shape[0] // groups
    for group in range(groups):
        columns = pl.ds(group * features, features)
        dactive = dot_nt(rounded, flat(contract[group * stack : (group + 1) * stack]))
        slope = held[SLOPE][:, columns].astype(jnp.float32)
        dup = (dactive * slope).astype(jnp.bfloat16)
        held[DUPWARD][:, columns] = dup
        offs_out[:, columns] = jnp.sum(dup.astype(jnp.float32), axis=0, keepdims=True)
    done(DUPWARD)


def backward_rest(lines, held, vec_out, done):
    rows, features = held[TOTAL].shape
    gradient = held[TOTAL][...] + dot_nt(held[DUPWARD][...], flat(held[EXPAND][...]))
    hat = held[HAT1][...].astype(jnp.float32)
    column_sum(vec_out, 0, gradient * hat)
    column_sum(vec_out, 5, gradient)
    stats, datt, dmix = held[STATS], held[DATT], held[DMIX]
    moved = norm_back(gradient, hat, stats[:, 0:1], lines[0:1, :])
    held[TOTAL][...] = moved
    rounded = moved.astype(jnp.bfloat16)
    held[DOUTPUT][...] = rounded
    column_sum(vec_out, 4, rounded.astype(jnp.float32))
    done(DOUTPUT)
    datt[...] = dot_nt(rounded, flat(held[OUT][...])).astype(jnp.bfloat16)
    head_low = low_lanes(rows)
    mix, probs = held[MIX], held[PROBS]

    def pair_step(pair, _):
        at = pl.multiple_of(pair * 2 * HD, 2 * HD)
        q = mix[:, pl.ds(at, 2 * HD)]
        k = mix[:, pl.ds(features + at, 2 * HD)]
        v = mix[:, pl.ds(2 * features + at, 2 * HD)]
        pull = datt[:, pl.ds(at, 2 * HD)]
        weight = flat(probs[pl.ds(2 * pair, 2)])
        wide = weight.astype(jnp.float32)
        product = dot_nt(two_heads(pull, head_low), v) * wide
        inner = jnp.sum(product, axis=-1, keepdims=True)
        dscores = (product - wide * inner).astype(jnp.bfloat16)
        dq = merged_heads(dot_nn(dscores, k), head_low)
        dmix[:, pl.ds(at, 2 * HD)] = (dq * SCALE).astype(jnp.bfloat16)
        q_turned, pull_turned = q.T, pull.T
        dk, dv = [], []
        for side in range(2):
            lanes = slice(side * HD, (side + 1) * HD)
            part = slice(side * rows, (side + 1) * rows)
            dk.append(dot_nn(q_turned[lanes], dscores[part]))
            dv.append(dot_nn(pull_turned[lanes], weight[part]))
        dk = (jnp.concatenate(dk, axis=0) * SCALE).astype(jnp.bfloat16).T
        dv = jnp.concatenate(dv, axis=0).astype(jnp.bfloat16).T
        dmix[:, pl.ds(features + at, 2 * HD)] = dk
        dmix[:, pl.ds(2 * features + at, 2 * HD)] = dv

    lax.fori_loop(0, features // (2 * HD), pair_step, None, unroll=UNROLL)
    done(DMIX)
    column_sum(vec_out, 2, dmix[:, 0:features].astype(jnp.float32))
    column_sum(vec_out, 3, dmix[:, 2 * features : 3 * features].astype(jnp.float32))
    moved = held[TOTAL][...] + dot_nt(dmix[...], flat(held[PROJ][...]))
    held[TOTAL][...] = moved
    done(TOTAL)
    return moved


def taken(refs, *counts):
    parts, at = [], 0
    for count in counts:
        parts.append(refs[at : at + count])
        at += count
    return parts + [refs[at:]]


FORWARD_HELD = (MIX, ATT, LOW)


def forward_kernel(layout, pack_count, view, first, crops, save, *refs):
    names = SAVED if save else FORWARD_HELD
    (flag, vrow, vcol, lines, offs, x_hbm), packs, (y_out, pooled_out), saved, refs = taken(
        refs, 6, pack_count, 2, len(SAVED) + 1 if save else 0
    )
    buffers, (x_buf, sems) = taken(refs, len(NAMES + names))
    saved = dict(zip(SAVED, saved[1:])) | {X_IN: saved[:1]}

    @pl.when(flag[0] == 1)
    def _():
        copier = Copier(sems)
        held = Held(NAMES + names, buffers, copier)
        fetches = []
        for crop in range(crops):
            at = (view, first + crop) if len(x_hbm.shape) == 4 else (first + crop,)
            source = x_hbm.at[at]
            fetches.append(copier.fetch(source, x_buf.at[crop]))
        for name in NAMES:
            held.fill_weight(name, layout, packs)

        def done(name):
            if save:
                copier.send(held[name], saved[name])

        for crop in range(crops):
            fetches[crop].wait()
            if save:
                copier.send(x_buf.at[crop], saved[X_IN][0])
            across = vrow[view, first + crop]
            value = forward_rows(x_buf[crop], across, lines, offs, held, done)
            y_out[crop] = value.astype(jnp.bfloat16)
            pooled_out[crop] = pooled_rows(value, across, vcol[view, first + crop])
        copier.finish()


def cost_of(flops):
    return pl.CostEstimate(flops=3 * flops, bytes_accessed=0, transcendentals=0)


def params(kept, first_in, first_out, flops):
    return dict(
        input_output_aliases={first_in + i: first_out + i for i in range(kept)},
        compiler_params=pltpu.CompilerParams(vmem_limit_bytes=VMEM_LIMIT),
        cost_estimate=cost_of(flops),
    )


def block_flops(rows, features, hidden_size):
    return 2 * rows * (4 * features * features + 2 * features * hidden_size)


def forward_block(flag, x, vrow, vcol, lines, offs, packs, layout, save, view, first, crops):
    rows, features = x.shape[-2:]
    sizes = rows, features, offs.shape[-1]
    names = (X_IN,) + SAVED if save else ()
    result = pl.pallas_call(
        functools.partial(forward_kernel, layout, len(packs), view, first, crops, save),
        out_shape=[
            jax.ShapeDtypeStruct((crops, rows, features), jnp.bfloat16),
            jax.ShapeDtypeStruct((crops, 1, features), jnp.float32),
        ]
        + outputs_of(names, *sizes),
        in_specs=[SMEM] + [VMEM] * 4 + [ANY] * (1 + len(packs)),
        out_specs=[VMEM] * 2 + [ANY] * len(names),
        scratch_shapes=scratch_of(NAMES + (SAVED if save else FORWARD_HELD), *sizes)
        + [
            pltpu.VMEM((crops, rows, features), jnp.bfloat16),
            pltpu.SemaphoreType.DMA((crops + len(layout) + len(names),)),
        ],
        **params(0, 0, 0, crops * block_flops(*sizes)),
    )(flag, vrow, vcol, lines, offs, x, *packs)
    return result[0], result[1], dict(zip(names, result[2:]))


ENDS = (ATT, LOW, ACT, X_IN)
BACK_HELD = (DBRANCH, DUPWARD, DOUTPUT, DATT, DMIX, TOTAL)


def turn_kernel(layout, pack_count, crop, *refs):
    head, packs, _, outs, ends, terms, refs = taken(
        refs, 7, pack_count, len(ENDS), 4, len(ENDS), len(TERMS)
    )
    flag, vrow, vcol, lines, offs, x_hbm, g_hbm = head
    pooled_out, vec_out, offs_out, dx_low = outs
    names = NAMES + SAVED + BACK_HELD + (X_IN, G_IN)
    buffers, (sems,) = taken(refs, len(names))
    places = dict(zip(ENDS + TERMS, ends + terms))

    @pl.when(flag[0] == 1)
    def _():
        copier = Copier(sems)
        held = Held(names, buffers, copier)
        held.fill(X_IN, x_hbm.at[0])
        for name in NAMES:
            held.fill_weight(name, layout, packs)
        held.fill(G_IN, g_hbm.at[crop])

        def done(name):
            if name in places:
                copier.send(held[name], places[name])

        done(X_IN)
        value = forward_rows(held[X_IN][...], vrow[0, crop], lines, offs, held, done)
        pooled_out[0] = pooled_rows(value, vrow[0, crop], vcol[0, crop])
        gradient = held[G_IN][...].astype(jnp.float32) * vcol[0, crop]
        backward_feed(gradient, lines, held, vec_out, offs_out, done)
        dx_low[...] = backward_rest(lines, held, vec_out, done).astype(jnp.bfloat16)
        copier.finish()


def turn_block(flag, x, gradient, vrow, vcol, lines, offs, packs, layout, crop, saved):
    rows, features = x.shape[-2:]
    sizes = rows, features, offs.shape[-1]
    result = pl.pallas_call(
        functools.partial(turn_kernel, layout, len(packs), crop),
        out_shape=[
            jax.ShapeDtypeStruct((1, 1, features), jnp.float32),
            jax.ShapeDtypeStruct((8, features), jnp.float32),
            jax.ShapeDtypeStruct(offs.shape, jnp.float32),
            jax.ShapeDtypeStruct((rows, features), jnp.bfloat16),
        ]
        + outputs_of(ENDS + TERMS, *sizes),
        in_specs=[SMEM] + [VMEM] * 4 + [ANY] * (2 + len(packs) + len(ENDS)),
        out_specs=[VMEM] * 4 + [ANY] * len(ENDS + TERMS),
        scratch_shapes=scratch_of(NAMES + SAVED + BACK_HELD + (X_IN, G_IN), *sizes)
        + [pltpu.SemaphoreType.DMA((2 + len(layout) + len(ENDS + TERMS),))],
        **params(len(ENDS), 7 + len(packs), 4, 2 * block_flops(*sizes)),
    )(flag, vrow, vcol, lines, offs, x, gradient, *packs, *[saved[name] for name in ENDS])
    return result[:4], dict(zip(ENDS + TERMS, result[4:]))


BACK_SAVED = (HAT2, STATS, SLOPE, HAT1, MIX, PROBS)
BACK_ORDER = (G_IN, HAT2, STATS, CONTRACT, SLOPE, EXPAND, HAT1, OUT, MIX, PROBS, PROJ)


def backward_kernel(layout, pack_count, *refs):
    (flag, lines, g_hbm), packs, saved, _, outs, terms, refs = taken(
        refs, 3, pack_count, len(BACK_SAVED), len(TERMS), 2, len(TERMS)
    )
    vec_out, offs_out = outs
    names = NAMES + BACK_SAVED + BACK_HELD + (G_IN,)
    buffers, (sems,) = taken(refs, len(names))
    places = dict(zip(TERMS, terms))
    saved = dict(zip(BACK_SAVED, saved)) | {G_IN: g_hbm}

    @pl.when(flag[0] == 1)
    def _():
        copier = Copier(sems)
        held = Held(names, buffers, copier)
        for name in BACK_ORDER:
            if name in NAMES:
                held.fill_weight(name, layout, packs)
            else:
                held.fill(name, saved[name])

        def done(name):
            copier.send(held[name], places[name])

        gradient = held[G_IN][...].astype(jnp.float32)
        backward_feed(gradient, lines, held, vec_out, offs_out, done)
        backward_rest(lines, held, vec_out, done)
        copier.finish()


def backward_block(flag, gradient, lines, packs, layout, saved, terms):
    rows, features = gradient.shape
    hidden_size = saved[SLOPE].shape[-1]
    sizes = rows, features, hidden_size
    result = pl.pallas_call(
        functools.partial(backward_kernel, layout, len(packs)),
        out_shape=[
            jax.ShapeDtypeStruct((8, features), jnp.float32),
            jax.ShapeDtypeStruct((1, hidden_size), jnp.float32),
        ]
        + outputs_of(TERMS, *sizes),
        in_specs=[SMEM, VMEM] + [ANY] * (1 + len(packs) + len(BACK_SAVED) + len(TERMS)),
        out_specs=[VMEM] * 2 + [ANY] * len(TERMS),
        scratch_shapes=scratch_of(NAMES + BACK_SAVED + BACK_HELD + (G_IN,), *sizes)
        + [pltpu.SemaphoreType.DMA((1 + len(layout) + len(BACK_SAVED) + len(TERMS),))],
        **params(
            len(TERMS), 3 + len(packs) + len(BACK_SAVED), 2, block_flops(*sizes)
        ),
    )(
        flag,
        lines,
        gradient,
        *packs,
        *[saved[name] for name in BACK_SAVED],
        *[terms[name] for name in TERMS],
    )
    return result[:2], dict(zip(TERMS, result[2:]))


FEED_SAVED = (HAT2, STATS, SLOPE)
FEED_TERMS = (DBRANCH, DUPWARD)


def feed_kernel(layout, pack_count, *refs):
    (flag, lines, g_hbm), packs, saved, _, outs, refs = taken(
        refs, 3, pack_count, len(FEED_SAVED), len(FEED_TERMS), 5
    )
    vec_out, offs_out, total_out, branch_out, upward_out = outs
    names = (CONTRACT,) + FEED_SAVED + FEED_TERMS + (TOTAL, G_IN)
    buffers, (sems,) = taken(refs, len(names))
    places = {DBRANCH: branch_out, DUPWARD: upward_out}

    @pl.when(flag[0] == 1)
    def _():
        copier = Copier(sems)
        held = Held(names, buffers, copier)
        held.fill(G_IN, g_hbm)
        held.fill(HAT2, saved[0])
        held.fill(STATS, saved[1])
        held.fill_weight(CONTRACT, layout, packs)
        held.fill(SLOPE, saved[2])

        def done(name):
            copier.send(held[name], places[name])

        vec_out[...] = jnp.zeros_like(vec_out)
        gradient = held[G_IN][...].astype(jnp.float32)
        backward_feed(gradient, lines, held, vec_out, offs_out, done)
        copier.send(held[TOTAL], total_out)
        copier.finish()


def feed_block(flag, gradient, lines, packs, layout, saved, terms):
    rows, features = gradient.shape
    hidden_size = saved[SLOPE].shape[-1]
    sizes = rows, features, hidden_size
    names = (TOTAL,) + FEED_TERMS
    result = pl.pallas_call(
        functools.partial(feed_kernel, layout, len(packs)),
        out_shape=[
            jax.ShapeDtypeStruct((8, features), jnp.float32),
            jax.ShapeDtypeStruct((1, hidden_size), jnp.float32),
        ]
        + outputs_of(names, *sizes),
        in_specs=[SMEM, VMEM] + [ANY] * (1 + len(packs) + len(FEED_SAVED) + len(FEED_TERMS)),
        out_specs=[VMEM] * 2 + [ANY] * len(names),
        scratch_shapes=scratch_of(
            (CONTRACT,) + FEED_SAVED + FEED_TERMS + (TOTAL, G_IN), *sizes
        )
        + [pltpu.SemaphoreType.DMA((1 + len(layout) + len(FEED_SAVED) + len(names),))],
        **params(
            len(FEED_TERMS),
            3 + len(packs) + len(FEED_SAVED),
            3,
            block_flops(*sizes) // 3,
        ),
    )(
        flag,
        lines,
        gradient,
        *packs,
        *[saved[name] for name in FEED_SAVED],
        *[terms[name] for name in FEED_TERMS],
    )
    return result[:2], dict(zip(names, result[2:]))


REST_IN = (DUPWARD, TOTAL, HAT1, STATS, MIX, PROBS)
REST_ORDER = (DUPWARD, EXPAND, TOTAL, HAT1, STATS, OUT, MIX, PROBS, PROJ)
REST_TERMS = (TOTAL, DOUTPUT, DMIX)


REST_WEIGHTS = (PROJ, OUT, EXPAND)


def closing_kernel(plan, layout, pack_count, *refs):
    (flag, core, lines), parts, packs, sources, _, operands, terms, outs, refs = taken(
        refs, 3, 8, pack_count, len(REST_IN), len(REST_TERMS), 6, len(REST_TERMS), 4
    )
    names = REST_WEIGHTS + REST_IN + (DOUTPUT, DMIX, DATT)
    held_buffers, buffers, (vec, sems, *scratch) = taken(refs, len(names), 4)
    places = dict(zip(REST_TERMS, terms))
    sources = dict(zip(REST_IN, sources))

    @pl.when(flag[0] == 1)
    def _():
        copier = Copier(sems)
        held = Held(names, held_buffers, copier)
        for name in REST_ORDER:
            if name in NAMES:
                held.fill_weight(name, layout, packs)
            else:
                held.fill(name, sources[name])

        def done(name):
            copier.send(held[name], places[name])

        vec[...] = jnp.zeros_like(vec)
        backward_rest(lines, held, vec, done)
        copier.finish()

    att0, att1, dout0, x0, x1, dmix0 = operands
    pairs = (att0, att1, dout0, places[DOUTPUT], x0, x1, dmix0, places[DMIX])
    own = (parts[4], parts[5], vec, parts[6], parts[7])
    row_products(plan, core, (flag, tuple(parts[:4]) + own), pairs, outs, buffers, *scratch)


def closing_block(plan, flag, core, lines, parts, packs, layout, saved, feed, terms, operands):
    rows, features = feed[TOTAL].shape
    sizes = rows, features, feed[DUPWARD].shape[-1]
    sources = dict(saved) | {DUPWARD: feed[DUPWARD], TOTAL: feed[TOTAL]}
    names = REST_WEIGHTS + REST_IN + (DOUTPUT, DMIX, DATT)
    pairs = [
        pltpu.VMEM((2 * rows, operand.shape[1]), jnp.bfloat16)
        for operand in (operands[0], operands[2], operands[3], operands[5])
    ]
    result = pl.pallas_call(
        functools.partial(closing_kernel, plan, layout, len(packs)),
        out_shape=outputs_of(REST_TERMS, *sizes) + sum_shapes(4, features, 128),
        in_specs=[SMEM] * 2
        + [VMEM] * (1 + len(parts))
        + [ANY] * (len(packs) + len(REST_IN) + len(REST_TERMS) + len(operands)),
        out_specs=[ANY] * (len(REST_TERMS) + 4),
        scratch_shapes=scratch_of(names, *sizes)
        + pairs
        + [
            pltpu.VMEM((8, features), jnp.float32),
            pltpu.SemaphoreType.DMA((len(layout) + len(REST_IN) + len(REST_TERMS),)),
        ]
        + row_scratch(4, 4, features),
        **params(
            len(REST_TERMS),
            3 + len(parts) + len(packs) + len(REST_IN),
            0,
            block_flops(*sizes) * 3 // 2,
        ),
    )(
        flag,
        core,
        lines,
        *parts,
        *packs,
        *[sources[name] for name in REST_IN],
        *[terms[name] for name in REST_TERMS],
        *operands,
    )
    return dict(zip(REST_TERMS, result)), result[len(REST_TERMS) :]


def load_pairs(sources, buffers, width, sems):
    copies = {}
    for i, buffer in enumerate(buffers):
        rows = buffer.shape[0] // 2
        for column in range(0, buffer.shape[1], width):
            columns = pl.ds(column, width)
            for half in range(2):
                copies.setdefault((i, column), []).append(
                    pltpu.make_async_copy(
                        sources[2 * i + half].at[:, columns],
                        buffer.at[pl.ds(half * rows, rows), columns],
                        sems.at[2 * i + half, column // width],
                    )
                )
    waited = set()

    def arrive(which, column):
        if (which, column) not in waited:
            waited.add((which, column))
            for copy in copies[which, column]:
                copy.wait()

    return copies, arrive


def contract_kernel(core, act0, act1, grad0, grad1, *refs):
    outs, (act, grad, pieces, in_sems, out_sems) = refs[:-5], refs[-5:]
    features = grad.shape[1]
    groups = act.shape[1] // features
    span = outs[0].shape[-1] // features
    copies, arrive = load_pairs((act0, act1, grad0, grad1), (act, grad), features, in_sems)
    for which in [(1, 0)] + [(0, part * features) for part in range(groups)]:
        for copy in copies[which]:
            copy.start()
    arrive(1, 0)
    sends = []
    for part in range(groups):
        columns = pl.ds(part * features, features)
        arrive(0, part * features)
        piece = dot_tn(act[:, columns], grad[...]).astype(jnp.bfloat16)
        pieces[part] = piece.reshape(pieces.shape[1:])
        for group in range(groups):
            for side in range(2):
                source = pieces.at[part, :, core[0] ^ side, group]
                place = outs[2 * (group // span) + side].at[
                    :, part % 2, part // 2, :, pl.ds((group % span) * features, features)
                ]
                copy = pltpu.make_async_copy(source, place, out_sems.at[part, group, side])
                copy.start()
                sends.append(copy)
    for copy in sends:
        copy.wait()


def vector_columns(flag, parts, target):
    turned, own, _ = taken(parts, 4, 5)
    chosen = flag[0] == 1
    vec = jnp.where(chosen, own[0][...] + own[1][...] + own[2][...], turned[0][...] + turned[1][...])
    marks = jnp.where(chosen, own[3][...] + own[4][...], turned[2][...] + turned[3][...])
    features = vec.shape[1]
    lane = lax.broadcasted_iota(jnp.int32, (features, 128), 1)
    column = jnp.concatenate([vec.T, jnp.zeros((features, 120), jnp.float32)], axis=1)
    marks = jnp.broadcast_to(marks, (8, marks.shape[1])).T.reshape(features // BLOCK, -1, BLOCK, 8)
    for group in range(marks.shape[1]):
        part = jnp.broadcast_to(marks[:, group].reshape(features, 8)[:, 0:1], column.shape)
        column = jnp.where(lane == 8 + group, part, column)
    coarse = column.astype(jnp.bfloat16)
    fine = pltpu.roll(column - coarse.astype(jnp.float32), 12, 1)
    both = jnp.where(lane < 12, column, jnp.where(lane < 24, fine, 0.0)).astype(jnp.bfloat16)
    for block in range(features // BLOCK):
        place = tuple((block >> level) & 1 for level in range(4))
        target[place] = both[block * BLOCK : (block + 1) * BLOCK]


def row_products(plan, core, vectors, sources, outs, buffers, pieces, small, in_sems, out_sems):
    width = pieces.shape[-1]
    copies, arrive = load_pairs(sources, buffers, width, in_sems)
    needs = [need for entry in plan for need in ((entry[0], 0), (entry[1], entry[2]))]
    for need in dict.fromkeys(needs):
        for copy in copies[need]:
            copy.start()
    sends = []

    def send(source, place, sem):
        copy = pltpu.make_async_copy(source, place, sem)
        copy.start()
        sends.append(copy)

    if vectors:
        vector_columns(*vectors, small)
        for side in range(2):
            place = outs[side].at[:, :, :, :, pl.ds(outs[side].shape[-1] - 128, 128)]
            send(small.at[core[0] ^ side], place, out_sems.at[len(plan), side, 0, 0])
    for part, (left, right, column, target, to) in enumerate(plan):
        arrive(left, 0)
        arrive(right, column)
        piece = dot_tn(buffers[left][...], buffers[right][:, column : column + width])
        pieces[part] = piece.astype(jnp.bfloat16).reshape(pieces.shape[1:])
        for side in range(2):
            for low, high in ((0, 0), (0, 1), (1, 0), (1, 1)):
                source = pieces.at[part, :, high, low, core[0] ^ side]
                place = outs[2 * target + side].at[low, high, :, :, pl.ds(to, width)]
                send(source, place, out_sems.at[part, side, low, high])
    for copy in sends:
        copy.wait()


def row_kernel(plan, core, *refs):
    sources, outs, buffers, refs = taken(refs, 4, len(refs) - 10, 2)
    row_products(plan, core, (), sources, outs, buffers, *refs)


def row_scratch(parts, pairs, features):
    return [
        pltpu.VMEM((parts, 2, 2, 2, 2, BLOCK, features), jnp.bfloat16),
        pltpu.VMEM((2, 2, 2, 2, BLOCK, 128), jnp.bfloat16),
        pltpu.SemaphoreType.DMA((2 * pairs, parts)),
        pltpu.SemaphoreType.DMA((parts + 1, 2, 2, 2)),
    ]


def sum_shapes(count, features, extra):
    widths = [2 * features + (extra if i < 2 else 0) for i in range(count)]
    return [jax.ShapeDtypeStruct((2, 2, 2, BLOCK, width), jnp.bfloat16) for width in widths]


def weight_gradient(kernel, core, operands, targets, contracted, features):
    pairs = features // BLOCK // 2
    bf16 = jnp.bfloat16
    parts = 2 * targets
    buffers = [
        pltpu.VMEM((2 * operand.shape[0], operand.shape[1]), bf16) for operand in operands[::2]
    ]
    if contracted:
        scratch = [
            pltpu.VMEM((parts, pairs // parts, 2, parts, BLOCK, features), bf16),
            pltpu.SemaphoreType.DMA((len(operands), parts)),
            pltpu.SemaphoreType.DMA((parts, parts, 2)),
        ]
    else:
        scratch = row_scratch(parts, len(operands) // 2, features)
    return pl.pallas_call(
        kernel,
        out_shape=sum_shapes(2 * targets, features, 0),
        in_specs=[SMEM] + [ANY] * len(operands),
        out_specs=[ANY] * (2 * targets),
        scratch_shapes=buffers + scratch,
        **params(0, 0, 0, 8 * targets * features * features * 512),
    )(core, *operands)


def pack_kernel(plan, *refs):
    target = refs[-1]
    for source, row, column, width, place in plan:
        block = refs[source][0, row : row + target.shape[0], column : column + width]
        target[:, place : place + width] = block


def packed(arrays, pieces, rows):
    width = sum(piece[3] for piece in pieces)
    if rows % 16:
        return jnp.concatenate(
            [arrays[i][0, r : r + rows, c : c + w] for i, r, c, w in pieces], axis=1
        )
    plan, place = [], 0
    for piece in pieces:
        plan.append(piece + (place,))
        place += piece[3]
    return pl.pallas_call(
        functools.partial(pack_kernel, tuple(plan)),
        out_shape=jax.ShapeDtypeStruct((rows, width), jnp.bfloat16),
        in_specs=[VMEM] * len(arrays),
        out_specs=VMEM,
    )(*arrays)


def refold(columns, shards_of, features):
    rows = features // shards_of
    if rows == BLOCK:
        return columns
    natural = jnp.moveaxis(columns.reshape(shards_of, rows, -1, features), 2, 1)
    natural = natural.reshape(features // BLOCK, -1, BLOCK, features)
    return jnp.moveaxis(natural, 1, 2).reshape(features, -1)


def unfold(blocks, shards_of, features):
    rows = features // shards_of
    if rows == BLOCK:
        return blocks
    natural = jnp.moveaxis(blocks.reshape(features // BLOCK, BLOCK, -1, features), 2, 1)
    natural = natural.reshape(shards_of, -1, rows, features)
    return jnp.moveaxis(natural, 1, 2).reshape(shards_of, rows, -1)


def swapped(block, level):
    route = [(i, i ^ (1 << level)) for i in range(lax.axis_size(DP))]
    return lax.ppermute(block, DP, route)


def added(first, second):
    return (first.astype(jnp.float32) + second.astype(jnp.float32)).astype(jnp.bfloat16)


def tied(value, *others):
    return lax.optimization_barrier((value,) + others)[0]


def bit(level):
    return (lax.axis_index(DP) >> level) & 1


def by_bits(block, levels):
    block = block.reshape((2,) * levels + block.shape[1:])
    return jnp.transpose(block, tuple(range(levels))[::-1] + tuple(range(levels, block.ndim)))


def outgoing(block, level):
    return lax.dynamic_index_in_dim(block, 1 - bit(level), 0, keepdims=False)


def joined(state, got, level):
    block = state[0]
    if isinstance(block, tuple):
        keep = block[0]
    else:
        keep = lax.dynamic_index_in_dim(block, bit(level), 0, keepdims=False)
    total = added(keep, got)
    if level + 1 == lax.axis_size(DP).bit_length() - 1:
        return total, total
    return total, outgoing(total, level + 1)


def halved(state, level):
    return joined(state, swapped(state[1], level), level)


def first_state(keep, send, shards_of, features, contracted, small):
    levels = shards_of.bit_length() - 1
    if features == BLOCK * shards_of:
        return (keep,), send
    blocks = jnp.transpose(jnp.stack([keep, send]), (3, 2, 1, 0, 4, 5))
    blocks = blocks.reshape((-1,) + blocks.shape[4:])
    if contracted:
        blocks = unfold(blocks, shards_of, features)
    else:
        blocks = blocks.reshape(shards_of, features // shards_of, -1)
    if small:
        lines = blocks[:, :, 2 * features :].reshape(features, 128)
        marks = jnp.stack([lines[:, 8:12], lines[:, 20:24]]).reshape(2, -1, BLOCK, 4)
        marks = jnp.moveaxis(marks, 3, 2).reshape(2, shards_of, 4, -1)
        marks = jnp.moveaxis(marks, 2, 3).reshape(2, features, 4)
        lines = jnp.concatenate([lines[:, :8], marks[0], lines[:, 12:20], marks[1]], axis=1)
        lines = jnp.pad(lines, ((0, 0), (0, 104))).reshape(shards_of, -1, 128)
        blocks = jnp.concatenate([blocks[:, :, : 2 * features], lines], axis=2)
    blocks = by_bits(blocks, levels)
    return blocks, outgoing(blocks, 0)


def doubled(block, level, other):
    upper = bit(level) == 1
    return jnp.concatenate(
        [jnp.where(upper, other, block), jnp.where(upper, block, other)], axis=0
    )


def shards(
    inputs,
    keep_mask,
    lengths,
    slot_order,
    cotangent,
    query_projection,
    query_output,
    query_expand,
    query_contract,
    query_gains,
    query_biases,
    query_offsets,
    momentum_projection,
    momentum_output,
    momentum_expand,
    momentum_contract,
    momentum_gains,
    momentum_biases,
    momentum_offsets,
):
    first_section = lax.axis_index(SECTION) == 0
    shards_of = lax.axis_size(DP)
    crop_count, crop_len, features = inputs.shape[1:]
    rows = features // shards_of
    hidden_size = query_expand.shape[2]
    groups = hidden_size // features
    blocks = features // BLOCK

    def folded(which):
        return [(which, i * rows, 0, features) for i in range(groups)]

    late_from, late_to = 2 * features // 3, 2 * features
    own = packed(
        (query_projection, query_output, query_expand, query_contract)
        + (momentum_output, momentum_projection),
        [(0, 0, 0, 3 * features), (1, 0, 0, features), (2, 0, 0, hidden_size)]
        + folded(3)
        + [(4, 0, 0, features), (5, 0, late_from, late_to - late_from)],
        rows,
    )
    gathered = lax.all_gather(own, DP, axis=0, tiled=True)
    rest = packed(
        (tied(momentum_projection, own), momentum_expand, momentum_contract),
        [(0, 0, 0, late_from), (0, 0, late_to, 3 * features - late_to), (1, 0, 0, hidden_size)]
        + folded(2),
        rows,
    )
    late = lax.all_gather(rest, DP, axis=0, tiled=True)

    sizes = (2 * rows, 6 * rows, groups * rows)
    vectors = jnp.concatenate(
        [
            array[0].reshape(-1)
            for array in (
                query_gains,
                query_biases,
                query_offsets,
                momentum_gains,
                momentum_biases,
                momentum_offsets,
            )
        ]
    )[None]
    levels = shards_of.bit_length() - 1
    for level in range(levels):
        vectors = doubled(vectors, level, swapped(vectors, level))
    vectors = vectors.astype(jnp.float32)

    def vector_rows(start):
        lines = vectors[:, start : start + 8 * rows].reshape(shards_of, 8, rows)
        marks = vectors[:, start + 8 * rows : start + sum(sizes)]
        return jnp.moveaxis(lines, 1, 0).reshape(8, features), marks.reshape(1, hidden_size)

    query_lines, query_offs = vector_rows(0)
    momentum_lines, momentum_offs = vector_rows(sum(sizes))

    inner = 4 * features + hidden_size
    vectors_at = inner + groups * features
    if rows != BLOCK:
        gathered = jnp.concatenate(
            [
                gathered[:, :inner],
                refold(gathered[:, inner:vectors_at], shards_of, features),
                gathered[:, vectors_at:],
            ],
            axis=1,
        )
        late_end = late.shape[1] - groups * features
        late = jnp.concatenate(
            [late[:, :late_end], refold(late[:, late_end:], shards_of, features)], axis=1
        )
    gathered = gathered.reshape(blocks, BLOCK, -1)
    late = late.reshape(blocks, BLOCK, -1)
    query_layout = (
        (PROJ, 0, 0, 3 * features, 0),
        (OUT, 0, 3 * features, features, 0),
        (EXPAND, 0, 4 * features, hidden_size, 0),
    ) + tuple((CONTRACT, 0, inner + i * features, features, i) for i in range(groups))
    late_expand = 3 * features - (late_to - late_from)
    momentum_layout = (
        (PROJ, 0, vectors_at + features, late_to - late_from, late_from),
        (PROJ, 1, 0, late_from, 0),
        (PROJ, 1, late_from, 3 * features - late_to, late_to),
        (OUT, 0, vectors_at, features, 0),
        (EXPAND, 1, late_expand, hidden_size, 0),
    ) + tuple(
        (CONTRACT, 1, late_expand + hidden_size + i * features, features, i)
        for i in range(groups)
    )

    positions = lax.broadcasted_iota(jnp.int32, keep_mask.shape, 2)
    validity = ((positions < lengths[:, :, None]) & ((keep_mask > 0) | (positions == 0))).astype(
        jnp.float32
    )
    across = validity[:, :, None, :]
    down = validity[:, :, :, None]
    in_first = first_section.astype(jnp.int32).reshape(1)
    in_second = 1 - in_first

    def momentum_forward(flag, block_in, crop, count):
        return forward_block(
            flag,
            block_in,
            across,
            down,
            momentum_lines,
            momentum_offs,
            (gathered, late),
            momentum_layout,
            False,
            1,
            crop,
            count,
        )[:2]

    crops = range(crop_count)
    last = crop_count - 1
    started, turned, before = [], [], [momentum_lines, momentum_offs]
    for c in crops:
        started.append(
            forward_block(
                tied(in_first, *before),
                inputs,
                across,
                down,
                query_lines,
                query_offs,
                (gathered,),
                query_layout,
                True,
                0,
                c,
                1,
            )
        )
        before = [started[c][1]]
    passed = [lax.ppermute(started[c][0], SECTION, [(0, 1)]) for c in crops]
    for c in crops:
        turned.append(
            turn_block(
                tied(in_second, *before),
                passed[c],
                cotangent,
                across,
                down,
                query_lines,
                query_offs,
                (gathered,),
                query_layout,
                c,
                started[c][2],
            )
        )
        before = [turned[c][0][0]]
    returned = [lax.ppermute(turned[c][0][3], SECTION, [(1, 0)]) for c in crops]
    ended = [
        backward_block(
            in_first,
            returned[c],
            query_lines,
            (gathered,),
            query_layout,
            started[c][2],
            turned[c][1],
        )
        for c in crops[:last]
    ]
    feed_ends, feed_terms = feed_block(
        tied(in_first, *[end[0][0] for end in ended]),
        returned[last],
        query_lines,
        (gathered,),
        query_layout,
        started[last][2],
        turned[last][1],
    )
    ends = [turned[c][1] | ended[c][1] for c in crops[:last]] + [turned[last][1] | feed_terms]

    core = lax.axis_index(DP) & 1 if rows == BLOCK else jnp.int32(0)
    core = jnp.asarray(core, jnp.int32).reshape(1)
    def pairs(sums, contracted=False, small=False):
        return [
            first_state(
                sums[2 * i], sums[2 * i + 1], shards_of, features, contracted, small and not i
            )
            for i in range(len(sums) // 2)
        ]

    def operands(*names):
        return [ends[c][name] for name in names for c in crops]

    chunks = pairs(
        weight_gradient(
            contract_kernel,
            core,
            operands(ACT, DBRANCH),
            groups // 2,
            True,
            features,
        ),
        True,
    )
    half = len(chunks)
    level_of = [0] * 6

    key_pools, key_seconds, key_ways, key_ins = [], [], [], []

    def advance(i, got):
        chunks[i] = joined(chunks[i], got, level_of[i])
        level_of[i] += 1

    def step(moving, kernel):
        gots = [swapped(chunks[i][1], level_of[i]) for i in moving]
        passing, key_ways[:] = list(key_ways), []
        done = kernel(*[chunks[i][1] for i in moving])
        done, *gots = lax.optimization_barrier((done, *gots, *passing))
        key_ins.extend(gots[len(moving) :])
        for i, got in zip(moving, gots):
            advance(i, got)
        return done

    def expand_gradient(*before):
        sums = weight_gradient(
            functools.partial(
                row_kernel,
                tuple((0, 1, i * features, i // 2, i % 2 * features) for i in range(groups)),
            ),
            tied(core, *before),
            operands(LOW, DUPWARD),
            groups // 2,
            False,
            features,
        )
        chunks.extend(pairs(sums))
        return sums[0]

    def closing(*before):
        turned_parts = [turned[c][0][1] for c in crops] + [turned[c][0][2] for c in crops]
        own_parts = [ended[0][0][0], feed_ends[0], ended[0][0][1], feed_ends[1]]
        terms, sums = closing_block(
            (
                (0, 1, 0, 0, 0),
                (2, 3, 0, 0, features),
                (2, 3, features, 1, 0),
                (2, 3, 2 * features, 1, features),
            ),
            tied(in_first, *before),
            core,
            query_lines,
            turned_parts + own_parts,
            (gathered,),
            query_layout,
            started[last][2],
            feed_terms,
            turned[last][1],
            operands(ATT) + [ends[0][DOUTPUT]] + operands(X_IN) + [ends[0][DMIX]],
        )
        ends[last] = ends[last] | terms
        chunks.extend(pairs(sums, False, True))
        return sums[2]

    def key_first(*before):
        key_out, pool = momentum_forward(tied(in_first, *before), inputs, 0, crop_count)
        key_ways.append(lax.ppermute(key_out, SECTION, [(0, 1)]))
        key_pools.append(pool)
        return pool

    def key_second(c, *before):
        return momentum_forward(tied(in_second, *before), key_ins[0], c, 1)[1]

    def unfinished(*second):
        return [
            i
            for i in range(len(chunks))
            if level_of[i] < levels and (level_of[i] != 1 or i in second)
        ]

    step([0, 1], expand_gradient)
    step(unfinished(0, 1), key_first)
    step(unfinished(2, 3), closing)
    for i in (4, 5):
        advance(i, swapped(chunks[i][1], 0))
    key_seconds.append(step(unfinished(4), functools.partial(key_second, 0)))
    chunks[5] = chunks[5][0], tied(chunks[5][1], key_seconds[0])
    done = step(unfinished(5), functools.partial(key_second, 1))
    key_seconds.append(done)

    key_pool = jnp.where(first_section, key_pools[0], jnp.concatenate(key_seconds, axis=0))
    pools = [jnp.where(first_section, started[c][1], turned[c][0][0]) for c in crops]
    pooled = jnp.concatenate([jnp.concatenate(pools, axis=0)[:, None], key_pool[:, None]], axis=1)
    order = (slot_order[:, None] == jnp.arange(crop_count, dtype=jnp.int32)[None, :])[..., None]
    pooled = jnp.sum(jnp.where(order, pooled.reshape(crop_count, -1)[None], 0.0), axis=1)
    for level in range(levels):
        moving = unfinished(*range(6))
        gots = [swapped(chunks[i][1], level_of[i]) for i in moving]
        other, *gots = lax.optimization_barrier((swapped(pooled, level), *gots))
        pooled = doubled(pooled, level, other)
        for i, got in zip(moving, gots):
            advance(i, got)
    pooled = jnp.moveaxis(pooled.reshape(-1, 2, features), 1, 0)[None]
    chunks[:4] = [(tied(chunk[0], done),) for chunk in chunks[:4]]
    small = chunks[4][0][:, half * features :]
    chunks[4] = (chunks[4][0][:, : half * features],)
    grad_input = jnp.stack([tied(end[TOTAL], done) for end in ends])[None]
    chunks = [chunk[0] for chunk in chunks]
    small = small.astype(jnp.float32)
    small = (small[:, :12] + small[:, 12:24]).T

    def wide(parts):
        return jnp.concatenate(parts, axis=1).astype(jnp.float32)

    contract_sum = jnp.moveaxis(wide(chunks[:half]).reshape(rows, groups, features), 1, 0)
    expand_sum = wide(chunks[half : 2 * half])
    project_sum = wide(chunks[2 * half :])
    return (
        pooled,
        grad_input,
        project_sum[None, :, features:],
        project_sum[None, :, :features],
        expand_sum[None],
        contract_sum.reshape(1, groups * rows, features),
        small[None, :2],
        small[None, 2:8],
        small[8:].reshape(1, groups * rows),
    )


def solution(mesh):
    in_specs = (
        P(None, DP, None, None),
        P(None, DP, None),
        P(None, DP),
        P(DP),
        P(DP, None, None),
        P(SECTION, DP, None),
        P(SECTION, DP, None),
        P(SECTION, DP, None),
        P(SECTION, DP, None),
        P(SECTION, None, DP),
        P(SECTION, None, DP),
        P(SECTION, DP),
        P(SECTION, DP, None),
        P(SECTION, DP, None),
        P(SECTION, DP, None),
        P(SECTION, DP, None),
        P(SECTION, None, DP),
        P(SECTION, None, DP),
        P(SECTION, DP),
    )
    out_specs = (
        P(SECTION, None, None, None),
        P(SECTION, DP, None, None),
        P(SECTION, DP, None),
        P(SECTION, DP, None),
        P(SECTION, DP, None),
        P(SECTION, DP, None),
        P(SECTION, None, DP),
        P(SECTION, None, DP),
        P(SECTION, DP),
    )
    return jax.shard_map(shards, mesh=mesh, in_specs=in_specs, out_specs=out_specs, check_vma=False)
```

time: 1220 us -> 365 us (0.30)
  the two profiles are of different devices: /device:TPU:2 before, /device:TPU:0 now
where the time goes in v5:
time: 365 us; the launch traced here: 360 us
  waiting for transfers between devices  143 us (39%)
  Pallas kernels  131 us (36%)
  starting transfers between devices  41.3 us (11%)
  local copies, waits for them, and re-layouts  17.3 us (5%)
  between operations  15.2 us (4%)
  other arithmetic  11.9 us (3%)
    all_gather x1, waiting for transfers between devices, shards(): gathered = lax.all_gather(own, DP, axis=0, tiled=True)  72.5 us
    pallas_call x5, Pallas kernels, forward_block(): pl.pallas_call(functools.partial(forward_kernel, layout, len(packs), view...  54.1 us
    ppermute x32, waiting for transfers between devices, swapped(): return lax.ppermute(block, DP, route)  42.2 us
    ppermute x32, starting transfers between devices, swapped(): return lax.ppermute(block, DP, route)  33.7 us
    ppermute x2, waiting for transfers between devices, shards(): returned = [lax.ppermute(turned[c][0][3], SECTION, [(1, 0)]) for c in crops]  28.7 us
    pallas_call x1, Pallas kernels, closing_block(): pl.pallas_call(functools.partial(closing_kernel, plan, layout, len(packs)...  19.7 us
    pallas_call x2, Pallas kernels, turn_block(): pl.pallas_call(functools.partial(turn_kernel, layout, len(packs), crop),...  16 us
    pallas_call x1, Pallas kernels, backward_block(): pl.pallas_call(functools.partial(backward_kernel, layout, len(packs)), ou...  14.8 us
  transfers between devices with their start and end apart: 39, of which 20 were waited for; matrix products, arithmetic and copies ran while one was open for 6% of the time, Pallas kernels for 36%

profile of v5, /device:TPU:0, one launch (start us, length us, event | category | flops | bytes accessed | tf_op | source)
XLA Modules:
  0.0 359.9 jit_solution(14385725598265592864)
XLA Ops:
  7.2 2.3 shard_map.250
  9.7 2.1 shard_map.259
  12.9 0.8 collective-permute-done
  13.7 2.9 collective-permute-start.1
  16.7 1.5 collective-permute-done.1
  18.3 2.1 collective-permute-start.2
  20.5 1.6 collective-permute-done.2
  22.1 3.1 collective-permute-start.3
  25.8 1.1 copy.74.refs_2_
  30.6 72.5 %all-gather.3.cloned.1.call-done = bf16[768,11008]{1,0:T(8,128)(2,1)} async-done(((bf16[48,11008]{1,0:T(8,128)(2,1)}), bf16[768,11008]{1,0:T(8,128)(2,1)}) %all-gather.3.cloned.1.call-update) | async-done | bytes 16908304 | tf_op jit(solution)/shard_map/all_gather | solution.py:994
  103.1 14.6 %shard_map.251 = (bf16[1,256,768]{2,1,0:T(8,128)(2,1)}, f32[1,1,768]{2,1,0:T(1,128)}, bf16[256,768]{1,0:T(8,128)(2,1)}, bf16[256,2304]{1,0:T(8,128)(2,1)}, bf16[...) custom-call(s32[1]{0:T(128)} %bitcast.refs_0_, ...), custom_call_target="tpu_custom_call" | custom-call | flops 10871635968 | tf_op jit(solution)/shard_map/pallas_call | solution.py:400
  117.7 1.3 collective-permute-start.4
  119.0 14.8 %shard_map.252 = (bf16[1,256,768]{2,1,0:T(8,128)(2,1)}, f32[1,1,768]{2,1,0:T(1,128)}, bf16[256,768]{1,0:T(8,128)(2,1)}, bf16[256,2304]{1,0:T(8,128)(2,1)}, bf16[...) custom-call(s32[1]{0:T(128)} %bitcast.refs_0_, ...), custom_call_target="tpu_custom_call" | custom-call | flops 10871635968 | tf_op jit(solution)/shard_map/pallas_call | solution.py:400
  133.8 1.3 collective-permute-start.5
  135.9 11.2 %shard_map.253 = (f32[1,1,768]{2,1,0:T(1,128)}, f32[8,768]{1,0:T(8,128)}, f32[1,3072]{1,0:T(1,128)}, bf16[256,768]{1,0:T(8,128)(2,1)}, bf16[256,768]{1,0:T(8,128...) custom-call(s32[1]{0:T(128)S(6)} %sub.8.refs_0_, ...), custom_call_target="tpu_custom_call", output_to_operand_aliasing={{4}: (8, {}), {5}: (9, {}), {6}: (10, {}), {7}: (11, {})} | custom-call | flops 21743271936 | tf_op jit(solution)/shard_map/pallas_call | solution.py:458
  147.2 1.3 collective-permute-start.6
  149.2 4.8 %shard_map.254 = (f32[1,1,768]{2,1,0:T(1,128)}, f32[8,768]{1,0:T(8,128)}, f32[1,3072]{1,0:T(1,128)}, bf16[256,768]{1,0:T(8,128)(2,1)}, bf16[256,768]{1,0:T(8,128...) custom-call(s32[1]{0:T(128)S(6)} %sub.8.refs_0_, ...), custom_call_target="tpu_custom_call", output_to_operand_aliasing={{4}: (8, {}), {5}: (9, {}), {6}: (10, {}), {7}: (11, {})} | custom-call | flops 21743271936 | tf_op jit(solution)/shard_map/pallas_call | solution.py:458
  154.1 1.3 collective-permute-start.7
  155.4 18.8 %collective-permute-done.6.refs_2_ = bf16[256,768]{1,0:T(8,128)(2,1)S(1)} collective-permute-done((bf16[256,768]{1,0:T(8,128)(2,1)}, bf16[256,768]{1,0:T(8,128)(2,1)S(1)}, u32[]{:S(2)}, u32[]{:S(2)}) %collective-permute-start.6) | collective-permute-done | bytes 393248 | tf_op jit(solution)/shard_map/ppermute | solution.py:1128
  175.0 14.8 %shard_map.255 = (f32[8,768]{1,0:T(8,128)}, f32[1,3072]{1,0:T(1,128)}, f32[256,768]{1,0:T(8,128)}, bf16[256,768]{1,0:T(8,128)(2,1)}, bf16[256,3072]{1,0:T(8,128)...) custom-call(s32[1]{0:T(128)} %bitcast.refs_0_, ...), custom_call_target="tpu_custom_call", output_to_operand_aliasing={{2}: (10, {}), {3}: (11, {}), {4}: (12, {}), {5}: (13, {}),... | custom-call | flops 10871635968 | tf_op jit(solution)/shard_map/pallas_call | solution.py:513
  189.8 9.9 %collective-permute-done.7.refs_2_ = bf16[256,768]{1,0:T(8,128)(2,1)S(1)} collective-permute-done((bf16[256,768]{1,0:T(8,128)(2,1)}, bf16[256,768]{1,0:T(8,128)(2,1)S(1)}, u32[]{:S(2)}, u32[]{:S(2)}) %collective-permute-start.7) | collective-permute-done | bytes 393248 | tf_op jit(solution)/shard_map/ppermute | solution.py:1128
  200.4 7.7 %shard_map.256 = (f32[8,768]{1,0:T(8,128)}, f32[1,3072]{1,0:T(1,128)}, f32[256,768]{1,0:T(8,128)}, bf16[256,768]{1,0:T(8,128)(2,1)}, bf16[256,3072]{1,0:T(8,128)(2,1)}) custom-call(s32[1]{0:T(128)} %bitcast.refs_0_, f32[8,768]{1,0:T(8,128)} %reshape.159.refs_3_.refs_1_.refs_2_, ...), custom_call_target="tpu_custom_call", output_to_operand_aliasing={{3}: (7, {}), {4}: (8, {})} | custom-call | flops 3623878656 | tf_op jit(solution)/shard_map/pallas_call | solution.py:576
  208.2 6.9 %shard_map.257 = (bf16[2,2,2,48,1536]{4,3,2,1,0:T(8,128)(2,1)}, bf16[2,2,2,48,1536]{4,3,2,1,0:T(8,128)(2,1)}, bf16[2,2,2,48,1536]{4,3,2,1,0:T(8,128)(2,1)}, bf16[2,2,2,48,1536]{4,3,2,1,0:T(8,128)(2,1)}) custom-call(s32[1]{0:T(128)} %bitcast.6.core.refs_1_, bf16[256,3072]{1,0:T(8,128)(2,1)} %get-tuple-element.151.act0, ...), custom_call_target="tpu_custom_call" | custom-call | flops 14495514624 | tf_op jit(solution)/shard_map/pallas_call | solution.py:829
  215.7 7.1 %shard_map.258 = (bf16[2,2,2,48,1536]{4,3,2,1,0:T(8,128)(2,1)}, bf16[2,2,2,48,1536]{4,3,2,1,0:T(8,128)(2,1)}, bf16[2,2,2,48,1536]{4,3,2,1,0:T(8,128)(2,1)}, bf16[2,2,2,48,1536]{4,3,2,1,0:T(8,128)(2,1)}) custom-call(s32[1]{0:T(128)} %bitcast.6.core.refs_1_, bf16[256,768]{1,0:T(8,128)(2,1)} %get-tuple-element.179.refs_0_, ...), custom_call_target="tpu_custom_call" | custom-call | flops 14495514624 | tf_op jit(solution)/shard_map/pallas_call | solution.py:829
  223.7 0.9 dynamic-slice_bitcast_fusion.4
  224.6 1.3 collective-permute-start.11
  226.2 0.9 dynamic-slice_bitcast_fusion.5
  227.8 20.6 %shard_map.260 = (bf16[2,256,768]{2,1,0:T(8,128)(2,1)}, f32[2,1,768]{2,1,0:T(1,128)}) custom-call(s32[1]{0:T(128)} %bitcast.refs_0_, f32[2,2,1,256]{3,2,1,0:T(1,128)} %broadcast_in_dim.62.refs_1_, f32[2,2,256,1]{3,2,1,0:T(8,128)} %copy.74.refs_2_, f32[8,768]{1,0:T(8,128)} %reshape.156.refs_3_, f32[1,3072]{1,0:T(1,128)} %reshape.157.refs_4_, ...), custom_call_target="tpu_custom_call" | custom-call | flops 21743271936 | tf_op jit(solution)/shard_map/pallas_call | solution.py:400
  248.4 2.2 collective-permute-start.18
  250.6 2.2 collective-permute-done.10
  252.9 1.6 add_convert_fusion.2
  254.5 1.2 copy-done.2
  256.1 1.2 fusion.4
  257.3 1.2 fusion.5
  258.6 1.4 collective-permute-start.17
  260.7 1.8 collective-permute-start.15
  262.7 19.7 %shard_map.261 = (f32[256,768]{1,0:T(8,128)}, bf16[256,768]{1,0:T(8,128)(2,1)}, bf16[256,2304]{1,0:T(8,128)(2,1)}, bf16[2,2,2,48,1664]{4,3,2,1,0:T(8,128)(2,1)},...) custom-call(s32[1]{0:T(128)} %bitcast.refs_0_, ...), custom_call_target="tpu_custom_call", output_to_operand_aliasing={{0}: (18, {}), {1}: (19, {}), {2}: (20, {})} | custom-call | flops 16307453952 | tf_op jit(solution)/shard_map/pallas_call | solution.py:655
  283.0 2.8 collective-permute-done.16
  286.1 1.8 collective-permute-start.23
  288.3 2.3 collective-permute-start.21
  291.9 0.9 copy-done
  293.2 1.4 collective-permute-start.24
  294.5 2.0 shard_map.262
  296.6 7.2 %collective-permute-done.21 = bf16[48,1536]{1,0:T(8,128)(2,1)S(1)} collective-permute-done((bf16[48,1536]{1,0:T(8,128)(2,1)S(1)}, bf16[48,1536]{1,0:T(8,128)(2,1)S(1)}, u32[]{:S(2)}, u32[]{:S(2)}) %collective-permute-start.21) | collective-permute-done | bytes 147488 | tf_op jit(solution)/shard_map/ppermute | solution.py:884
  303.8 1.6 collective-permute-done.20
  306.1 1.7 collective-permute-done.24
  307.8 1.3 collective-permute-start.29
  310.3 2.0 collective-permute-start.27
  312.3 0.9 collective-permute-start.26
  313.2 2.1 shard_map.263
  315.4 3.7 %collective-permute-done.27 = bf16[48,1536]{1,0:T(8,128)(2,1)S(1)} collective-permute-done((bf16[48,1536]{1,0:T(8,128)(2,1)S(1)}, bf16[48,1536]{1,0:T(8,128)(2,1)S(1)}, u32[]{:S(2)}, u32[]{:S(2)}) %collective-permute-start.27) | collective-permute-done | bytes 147488 | tf_op jit(solution)/shard_map/ppermute | solution.py:884
  319.1 4.3 %collective-permute-done.26 = bf16[48,1536]{1,0:T(8,128)(2,1)S(1)} collective-permute-done((bf16[48,1536]{1,0:T(8,128)(2,1)S(1)}, bf16[48,1536]{1,0:T(8,128)(2,1)S(1)}, u32[]{:S(2)}, u32[]{:S(2)}) %collective-permute-start.26) | collective-permute-done | bytes 147488 | tf_op jit(solution)/shard_map/ppermute | solution.py:884
  324.8 2.2 collective-permute-start.31
  327.2 0.9 maximum_convert_fusion.1
  328.1 1.2 maximum_bitcast_fusion
  329.7 0.9 copy.81
  331.1 1.8 collective-permute-done.32
  333.1 1.3 collective-permute-start.34
  334.4 0.9 collective-permute-start.33
  338.3 2.9 collective-permute-done.34
  341.4 0.8 slice_bitcast_fusion
  342.2 3.2 collective-permute-done.35
  345.4 1.0 collective-permute-start.36
  347.1 4.9 %collective-permute-done.36 = f32[16,1536]{1,0:T(8,128)S(1)} collective-permute-done((f32[16,1536]{1,0:T(8,128)S(1)}, f32[16,1536]{1,0:T(8,128)S(1)}, u32[]{:S(2)}, u32[]{:S(2)}) %collective-permute-start.36) | collective-permute-done | bytes 98336 | tf_op jit(solution)/shard_map/ppermute | solution.py:884
  (191 shorter events, 24.8 us)
Async XLA Ops:
  7.2 95.9 %all-gather.3.cloned.1.call-start = ((), (), s32[]{:S(2)}) async-start(), calls=%async_computation | async-start | bytes 17965056 | tf_op jit(solution)/shard_map/all_gather | solution.py:994
  9.6 2.3 copy-start.16
  9.6 2.3 copy-start.17
  9.6 2.4 copy-start.18
  9.6 2.4 copy-start.19
  9.6 2.4 copy-start.24
  9.6 2.5 copy-start.25
  9.6 7.0 %copy-start.9 = (s32[2,2,256]{2,1,0:T(2,128)S(1)}, s32[2,2,256]{2,1,0:T(2,128)}, u32[]{:S(2)}) copy-start(s32[2,2,256]{2,1,0:T(2,128)} %param.20) | copy-start | bytes 12292
  9.7 7.0 %copy-start.11 = (s32[2,2]{1,0:T(2,128)S(1)}, s32[2,2]{1,0:T(2,128)}, u32[]{:S(2)}) copy-start(s32[2,2]{1,0:T(2,128)} %param.21) | copy-start | bytes 52
  9.7 15.5 %copy-start.26 = (s32[2]{0:T(128)S(1)}, s32[2]{0:T(128)}, u32[]{:S(2)}) copy-start(s32[2]{0:T(128)} %param.22) | copy-start | bytes 28
  9.7 218.1 %all-gather.5.cloned.1.call-start = ((), (), s32[]{:S(2)}) async-start(), calls=%async_computation.1 | async-start | bytes 12115968 | tf_op jit(solution)/shard_map/all_gather | solution.py:1001
  12.3 1.3 collective-permute-start
  13.7 4.5 %collective-permute-start.1 = (bf16[2,1152]{1,0:T(2,128)(2,1)S(1)}, bf16[2,1152]{1,0:T(2,128)(2,1)S(1)}, u32[]{:S(2)}, u32[]{:S(2)}) collective-permute-start(bf16[2,1152]{1,0:T(2,128)(2,1)S(1)} %pad_maximum_fusion.6), channel_id=1, source_target_pairs={{0,2},{1,3},{2,0},{3,1},{4,6},{5,7},{6,4},{7,5},{8,10},{9,11},{10,... | collective-permute-start | bytes 13832 | tf_op jit(solution)/shard_map/ppermute | solution.py:884
  18.3 3.8 %collective-permute-start.2 = (bf16[4,1152]{1,0:T(4,128)(2,1)S(1)}, bf16[4,1152]{1,0:T(4,128)(2,1)S(1)}, u32[]{:S(2)}, u32[]{:S(2)}) collective-permute-start(bf16[4,1152]{1,0:T(4,128)(2,1)S(1)} %pad_maximum_fusion.5), channel_id=1, source_target_pairs={{0,4},{1,5},{2,6},{3,7},{4,0},{5,1},{6,2},{7,3},{8,12},{9,13},{10,... | collective-permute-start | bytes 27656 | tf_op jit(solution)/shard_map/ppermute | solution.py:884
  22.1 5.3 %collective-permute-start.3 = (bf16[8,1152]{1,0:T(8,128)(2,1)S(1)}, bf16[8,1152]{1,0:T(8,128)(2,1)S(1)}, u32[]{:S(2)}, u32[]{:S(2)}) collective-permute-start(bf16[8,1152]{1,0:T(8,128)(2,1)S(1)} %pad_maximum_fusion.4), channel_id=1, source_target_pairs={{0,8},{1,9},{2,10},{3,11},{4,12},{5,13},{6,14},{7,15},{8,0},{9,1},... | collective-permute-start | bytes 55304 | tf_op jit(solution)/shard_map/ppermute | solution.py:884
  117.7 17.5 %collective-permute-start.4 = (bf16[1,256,768]{2,1,0:T(8,128)(2,1)}, bf16[1,256,768]{2,1,0:T(8,128)(2,1)S(1)}, u32[]{:S(2)}, u32[]{:S(2)}) collective-permute-start(bf16[1,256,768]{2,1,0:T(8,128)(2,1)} %get-tuple-element.138), channel_id=1, source_target_pairs={{0,16},{1,17},{2,18},{3,19},{4,20},{5,21},{6,22},{7,23},{8,24},{9,... | collective-permute-start | bytes 1179656 | tf_op jit(solution)/shard_map/ppermute | solution.py:1110
  133.8 14.6 %collective-permute-start.5 = (bf16[1,256,768]{2,1,0:T(8,128)(2,1)}, bf16[1,256,768]{2,1,0:T(8,128)(2,1)S(1)}, u32[]{:S(2)}, u32[]{:S(2)}) collective-permute-start(bf16[1,256,768]{2,1,0:T(8,128)(2,1)} %get-tuple-element.145), channel_id=1, source_target_pairs={{0,16},{1,17},{2,18},{3,19},{4,20},{5,21},{6,22},{7,23},{8,24},{9,... | collective-permute-start | bytes 1179656 | tf_op jit(solution)/shard_map/ppermute | solution.py:1110
  135.2 0.8 copy-start.23
  147.2 27.1 %collective-permute-start.6 = (bf16[256,768]{1,0:T(8,128)(2,1)}, bf16[256,768]{1,0:T(8,128)(2,1)S(1)}, u32[]{:S(2)}, u32[]{:S(2)}) collective-permute-start(bf16[256,768]{1,0:T(8,128)(2,1)} %get-tuple-element.153), channel_id=1, source_target_pairs={{16,0},{17,1},{18,2},{19,3},{20,4},{21,5},{22,6},{23,7},{24,8},{25... | collective-permute-start | bytes 1179656 | tf_op jit(solution)/shard_map/ppermute | solution.py:1128
  148.5 0.7 copy-start.22
  149.2 4.8 %copy-start.13 = (f32[1,1,768]{2,1,0:T(1,128)S(1)}, f32[1,1,768]{2,1,0:T(1,128)}, u32[]{:S(2)}) copy-start(f32[1,1,768]{2,1,0:T(1,128)} %get-tuple-element.134) | copy-start | bytes 9220
  149.2 4.8 %copy-start.15 = (f32[1,1,768]{2,1,0:T(1,128)S(1)}, f32[1,1,768]{2,1,0:T(1,128)}, u32[]{:S(2)}) copy-start(f32[1,1,768]{2,1,0:T(1,128)} %get-tuple-element.143) | copy-start | bytes 9220
  149.2 6.2 %copy-start.14 = (f32[1,1,768]{2,1,0:T(1,128)S(1)}, f32[1,1,768]{2,1,0:T(1,128)}, u32[]{:S(2)}) copy-start(f32[1,1,768]{2,1,0:T(1,128)} %get-tuple-element.136) | copy-start | bytes 9220
  154.1 45.6 %collective-permute-start.7 = (bf16[256,768]{1,0:T(8,128)(2,1)}, bf16[256,768]{1,0:T(8,128)(2,1)S(1)}, u32[]{:S(2)}, u32[]{:S(2)}) collective-permute-start(bf16[256,768]{1,0:T(8,128)(2,1)} %get-tuple-element.168), channel_id=1, source_target_pairs={{16,0},{17,1},{18,2},{19,3},{20,4},{21,5},{22,6},{23,7},{24,8},{25... | collective-permute-start | bytes 1179656 | tf_op jit(solution)/shard_map/ppermute | solution.py:1128
  215.1 8.3 %collective-permute-start.8 = (bf16[2,2,2,48,1536]{4,3,2,1,0:T(8,128)(2,1)}, bf16[2,2,2,48,1536]{4,3,2,1,0:T(8,128)(2,1)S(1)}, u32[]{:S(2)}, u32[]{:S(2)}) collective-permute-start(bf16[2,2,2,48,1536]{4,3,2,1,0:T(8,128)(2,1)} %get-tuple-element.176), channel_id=1, source_target_pairs={{0,1},{1,0},{2,3},{3,2},{4,5},{5,4},{6,7},{7,6},{8,9},{9,8},{10,11... | collective-permute-start | bytes 3538952 | tf_op jit(solution)/shard_map/ppermute | solution.py:884
  215.2 8.2 %collective-permute-start.9 = (bf16[2,2,2,48,1536]{4,3,2,1,0:T(8,128)(2,1)}, bf16[2,2,2,48,1536]{4,3,2,1,0:T(8,128)(2,1)S(1)}, u32[]{:S(2)}, u32[]{:S(2)}) collective-permute-start(bf16[2,2,2,48,1536]{4,3,2,1,0:T(8,128)(2,1)} %get-tuple-element.177), channel_id=1, source_target_pairs={{0,1},{1,0},{2,3},{3,2},{4,5},{5,4},{6,7},{7,6},{8,9},{9,8},{10,11... | collective-permute-start | bytes 3538952 | tf_op jit(solution)/shard_map/ppermute | solution.py:884
  215.7 7.7 %copy-start.5 = (bf16[2,2,2,48,1536]{4,3,2,1,0:T(8,128)(2,1)S(1)}, bf16[2,2,2,48,1536]{4,3,2,1,0:T(8,128)(2,1)}, u32[]{:S(2)}) copy-start(bf16[2,2,2,48,1536]{4,3,2,1,0:T(8,128)(2,1)} %get-tuple-element.185) | copy-start | bytes 3538948
  222.8 27.8 %collective-permute-start.12 = (bf16[2,2,2,48,1536]{4,3,2,1,0:T(8,128)(2,1)}, bf16[2,2,2,48,1536]{4,3,2,1,0:T(8,128)(2,1)S(1)}, u32[]{:S(2)}, u32[]{:S(2)}) collective-permute-start(bf16[2,2,2,48,1536]{4,3,2,1,0:T(8,128)(2,1)} %get-tuple-element.187), channel_id=1, source_target_pairs={{0,1},{1,0},{2,3},{3,2},{4,5},{5,4},{6,7},{7,6},{8,9},{9,8},{10,11... | collective-permute-start | bytes 3538952 | tf_op jit(solution)/shard_map/ppermute | solution.py:884
  223.0 27.7 %collective-permute-start.13 = (bf16[2,2,2,48,1536]{4,3,2,1,0:T(8,128)(2,1)}, bf16[2,2,2,48,1536]{4,3,2,1,0:T(8,128)(2,1)}, u32[]{:S(2)}, u32[]{:S(2)}) collective-permute-start(bf16[2,2,2,48,1536]{4,3,2,1,0:T(8,128)(2,1)} %get-tuple-element.188), channel_id=1, source_target_pairs={{0,1},{1,0},{2,3},{3,2},{4,5},{5,4},{6,7},{7,6},{8,9},{9,8},{10,11... | collective-permute-start | bytes 3538952 | tf_op jit(solution)/shard_map/ppermute | solution.py:884
  223.7 2.2 copy-start.4
  224.6 26.0 %collective-permute-start.11 = (bf16[2,2,48,1536]{3,2,1,0:T(8,128)(2,1)}, bf16[2,2,48,1536]{3,2,1,0:T(8,128)(2,1)}, u32[]{:S(2)}, u32[]{:S(2)}) collective-permute-start(bf16[2,2,48,1536]{3,2,1,0:T(8,128)(2,1)} %dynamic-slice_bitcast_fusion.4), channel_id=1, source_target_pairs={{0,2},{1,3},{2,0},{3,1},{4,6},{5,7},{6,4},{7,5},{8,10},{9,11},{10,... | collective-permute-start | bytes 1769480 | tf_op jit(solution)/shard_map/ppermute | solution.py:884
  227.1 25.8 %collective-permute-start.10 = (bf16[2,2,48,1536]{3,2,1,0:T(8,128)(2,1)}, bf16[2,2,48,1536]{3,2,1,0:T(8,128)(2,1)}, u32[]{:S(2)}, u32[]{:S(2)}) collective-permute-start(bf16[2,2,48,1536]{3,2,1,0:T(8,128)(2,1)} %dynamic-slice_bitcast_fusion.5), channel_id=1, source_target_pairs={{0,2},{1,3},{2,0},{3,1},{4,6},{5,7},{6,4},{7,5},{8,10},{9,11},{10,... | collective-permute-start | bytes 1769480 | tf_op jit(solution)/shard_map/ppermute | solution.py:884
  227.8 25.1 %copy-start.3 = (bf16[2,2,2,48,1536]{4,3,2,1,0:T(8,128)(2,1)S(1)}, bf16[2,2,2,48,1536]{4,3,2,1,0:T(8,128)(2,1)}, u32[]{:S(2)}) copy-start(bf16[2,2,2,48,1536]{4,3,2,1,0:T(8,128)(2,1)} %get-tuple-element.195) | copy-start | bytes 3538948
  248.4 34.0 %collective-permute-start.18 = (bf16[2,256,768]{2,1,0:T(8,128)(2,1)}, bf16[2,256,768]{2,1,0:T(8,128)(2,1)}, u32[]{:S(2)}, u32[]{:S(2)}) collective-permute-start(bf16[2,256,768]{2,1,0:T(8,128)(2,1)} %get-tuple-element.219), channel_id=1, source_target_pairs={{0,16},{1,17},{2,18},{3,19},{4,20},{5,21},{6,22},{7,23},{8,24},{9,... | collective-permute-start | bytes 2359304 | tf_op jit(solution)/shard_map/ppermute | solution.py:1237
  254.4 1.3 copy-start.2
  258.6 24.4 %collective-permute-start.17 = (bf16[2,2,48,1536]{3,2,1,0:T(8,128)(2,1)S(1)}, bf16[2,2,48,1536]{3,2,1,0:T(8,128)(2,1)S(1)}, u32[]{:S(2)}, u32[]{:S(2)}) collective-permute-start(bf16[2,2,48,1536]{3,2,1,0:T(8,128)(2,1)S(1)} %dynamic-slice_bitcast_fusion.2), channel_id=1, source_target_pairs={{0,2},{1,3},{2,0},{3,1},{4,6},{5,7},{6,4},{7,5},{8,10},{9,11},{10,... | collective-permute-start | bytes 1769480 | tf_op jit(solution)/shard_map/ppermute | solution.py:884
  259.9 25.8 %collective-permute-start.16 = (bf16[2,2,48,1536]{3,2,1,0:T(8,128)(2,1)S(1)}, bf16[2,2,48,1536]{3,2,1,0:T(8,128)(2,1)S(1)}, u32[]{:S(2)}, u32[]{:S(2)}) collective-permute-start(bf16[2,2,48,1536]{3,2,1,0:T(8,128)(2,1)S(1)} %dynamic-slice_bitcast_fusion.3), channel_id=1, source_target_pairs={{0,2},{1,3},{2,0},{3,1},{4,6},{5,7},{6,4},{7,5},{8,10},{9,11},{10,... | collective-permute-start | bytes 1769480 | tf_op jit(solution)/shard_map/ppermute | solution.py:884
  260.7 21.8 %collective-permute-start.15 = (bf16[2,48,1536]{2,1,0:T(8,128)(2,1)S(1)}, bf16[2,48,1536]{2,1,0:T(8,128)(2,1)S(1)}, u32[]{:S(2)}, u32[]{:S(2)}) collective-permute-start(bf16[2,48,1536]{2,1,0:T(8,128)(2,1)S(1)} %dynamic-slice_bitcast_fusion.10), channel_id=1, source_target_pairs={{0,4},{1,5},{2,6},{3,7},{4,0},{5,1},{6,2},{7,3},{8,12},{9,13},{10,... | collective-permute-start | bytes 884744 | tf_op jit(solution)/shard_map/ppermute | solution.py:884
  262.4 20.5 %collective-permute-start.14 = (bf16[2,48,1536]{2,1,0:T(8,128)(2,1)S(1)}, bf16[2,48,1536]{2,1,0:T(8,128)(2,1)S(1)}, u32[]{:S(2)}, u32[]{:S(2)}) collective-permute-start(bf16[2,48,1536]{2,1,0:T(8,128)(2,1)S(1)} %dynamic-slice_bitcast_fusion.11), channel_id=1, source_target_pairs={{0,4},{1,5},{2,6},{3,7},{4,0},{5,1},{6,2},{7,3},{8,12},{9,13},{10,... | collective-permute-start | bytes 884744 | tf_op jit(solution)/shard_map/ppermute | solution.py:884
  282.4 9.5 %collective-permute-start.19 = (bf16[2,2,2,48,1664]{4,3,2,1,0:T(8,128)(2,1)}, bf16[2,2,2,48,1664]{4,3,2,1,0:T(8,128)(2,1)S(1)}, u32[]{:S(2)}, u32[]{:S(2)}) collective-permute-start(bf16[2,2,2,48,1664]{4,3,2,1,0:T(8,128)(2,1)} %get-tuple-element.225), channel_id=1, source_target_pairs={{0,1},{1,0},{2,3},{3,2},{4,5},{5,4},{6,7},{7,6},{8,9},{9,8},{10,11... | collective-permute-start | bytes 3833864 | tf_op jit(solution)/shard_map/ppermute | solution.py:884
  282.5 8.3 %collective-permute-start.25 = (bf16[2,2,2,48,1536]{4,3,2,1,0:T(8,128)(2,1)}, bf16[2,2,2,48,1536]{4,3,2,1,0:T(8,128)(2,1)S(1)}, u32[]{:S(2)}, u32[]{:S(2)}) collective-permute-start(bf16[2,2,2,48,1536]{4,3,2,1,0:T(8,128)(2,1)} %get-tuple-element.233), channel_id=1, source_target_pairs={{0,1},{1,0},{2,3},{3,2},{4,5},{5,4},{6,7},{7,6},{8,9},{9,8},{10,11... | collective-permute-start | bytes 3538952 | tf_op jit(solution)/shard_map/ppermute | solution.py:884
  286.1 5.4 %copy-start.1 = (bf16[2,2,2,48,1536]{4,3,2,1,0:T(8,128)(2,1)S(1)}, bf16[2,2,2,48,1536]{4,3,2,1,0:T(8,128)(2,1)}, u32[]{:S(2)}) copy-start(bf16[2,2,2,48,1536]{4,3,2,1,0:T(8,128)(2,1)} %get-tuple-element.218) | copy-start | bytes 3538948
  286.1 19.2 %collective-permute-start.23 = (bf16[2,48,1536]{2,1,0:T(8,128)(2,1)S(1)}, bf16[2,48,1536]{2,1,0:T(8,128)(2,1)S(1)}, u32[]{:S(2)}, u32[]{:S(2)}) collective-permute-start(bf16[2,48,1536]{2,1,0:T(8,128)(2,1)S(1)} %dynamic-slice_bitcast_fusion.8), channel_id=1, source_target_pairs={{0,4},{1,5},{2,6},{3,7},{4,0},{5,1},{6,2},{7,3},{8,12},{9,13},{10,... | collective-permute-start | bytes 884744 | tf_op jit(solution)/shard_map/ppermute | solution.py:884
  288.0 18.1 %collective-permute-start.22 = (bf16[2,48,1536]{2,1,0:T(8,128)(2,1)S(1)}, bf16[2,48,1536]{2,1,0:T(8,128)(2,1)S(1)}, u32[]{:S(2)}, u32[]{:S(2)}) collective-permute-start(bf16[2,48,1536]{2,1,0:T(8,128)(2,1)S(1)} %dynamic-slice_bitcast_fusion.9), channel_id=1, source_target_pairs={{0,4},{1,5},{2,6},{3,7},{4,0},{5,1},{6,2},{7,3},{8,12},{9,13},{10,... | collective-permute-start | bytes 884744 | tf_op jit(solution)/shard_map/ppermute | solution.py:884
  288.3 15.4 %collective-permute-start.21 = (bf16[48,1536]{1,0:T(8,128)(2,1)S(1)}, bf16[48,1536]{1,0:T(8,128)(2,1)S(1)}, u32[]{:S(2)}, u32[]{:S(2)}) collective-permute-start(bf16[48,1536]{1,0:T(8,128)(2,1)S(1)} %dynamic-slice_bitcast_fusion.16), channel_id=1, source_target_pairs={{0,8},{1,9},{2,10},{3,11},{4,12},{5,13},{6,14},{7,15},{8,0},{9,1},... | collective-permute-start | bytes 442376 | tf_op jit(solution)/shard_map/ppermute | solution.py:884
  290.8 14.6 %collective-permute-start.20 = (bf16[48,1536]{1,0:T(8,128)(2,1)S(1)}, bf16[48,1536]{1,0:T(8,128)(2,1)S(1)}, u32[]{:S(2)}, u32[]{:S(2)}) collective-permute-start(bf16[48,1536]{1,0:T(8,128)(2,1)S(1)} %dynamic-slice_bitcast_fusion.17), channel_id=1, source_target_pairs={{0,8},{1,9},{2,10},{3,11},{4,12},{5,13},{6,14},{7,15},{8,0},{9,1},... | collective-permute-start | bytes 442376 | tf_op jit(solution)/shard_map/ppermute | solution.py:884
  291.5 1.3 copy-start
  293.2 14.6 %collective-permute-start.24 = (bf16[2,2,48,1664]{3,2,1,0:T(8,128)(2,1)S(1)}, bf16[2,2,48,1664]{3,2,1,0:T(8,128)(2,1)S(1)}, u32[]{:S(2)}, u32[]{:S(2)}) collective-permute-start(bf16[2,2,48,1664]{3,2,1,0:T(8,128)(2,1)S(1)} %dynamic-slice_bitcast_fusion), channel_id=1, source_target_pairs={{0,2},{1,3},{2,0},{3,1},{4,6},{5,7},{6,4},{7,5},{8,10},{9,11},{10,... | collective-permute-start | bytes 1916936 | tf_op jit(solution)/shard_map/ppermute | solution.py:884
  307.8 15.6 %collective-permute-start.29 = (bf16[2,2,48,1536]{3,2,1,0:T(8,128)(2,1)S(1)}, bf16[2,2,48,1536]{3,2,1,0:T(8,128)(2,1)S(1)}, u32[]{:S(2)}, u32[]{:S(2)}) collective-permute-start(bf16[2,2,48,1536]{3,2,1,0:T(8,128)(2,1)S(1)} %dynamic-slice_bitcast_fusion.1), channel_id=1, source_target_pairs={{0,2},{1,3},{2,0},{3,1},{4,6},{5,7},{6,4},{7,5},{8,10},{9,11},{10,... | collective-permute-start | bytes 1769480 | tf_op jit(solution)/shard_map/ppermute | solution.py:884
  309.5 13.9 %copy-start.10 = (f32[2,1,768]{2,1,0:T(1,128)S(1)}, f32[2,1,768]{2,1,0:T(1,128)}, u32[]{:S(2)}) copy-start(f32[2,1,768]{2,1,0:T(1,128)} %get-tuple-element.191) | copy-start | bytes 18436
  309.5 13.9 %copy-start.12 = (f32[1,1,768]{2,1,0:T(1,128)S(1)}, f32[1,1,768]{2,1,0:T(1,128)}, u32[]{:S(2)}) copy-start(f32[1,1,768]{2,1,0:T(1,128)} %get-tuple-element.229) | copy-start | bytes 9220
  309.5 13.9 %collective-permute-start.28 = (bf16[2,48,1664]{2,1,0:T(8,128)(2,1)S(1)}, bf16[2,48,1664]{2,1,0:T(8,128)(2,1)S(1)}, u32[]{:S(2)}, u32[]{:S(2)}) collective-permute-start(bf16[2,48,1664]{2,1,0:T(8,128)(2,1)S(1)} %dynamic-slice_bitcast_fusion.6), channel_id=1, source_target_pairs={{0,4},{1,5},{2,6},{3,7},{4,0},{5,1},{6,2},{7,3},{8,12},{9,13},{10,... | collective-permute-start | bytes 958472 | tf_op jit(solution)/shard_map/ppermute | solution.py:884
  310.3 8.8 %collective-permute-start.27 = (bf16[48,1536]{1,0:T(8,128)(2,1)S(1)}, bf16[48,1536]{1,0:T(8,128)(2,1)S(1)}, u32[]{:S(2)}, u32[]{:S(2)}) collective-permute-start(bf16[48,1536]{1,0:T(8,128)(2,1)S(1)} %dynamic-slice_bitcast_fusion.14), channel_id=1, source_target_pairs={{0,8},{1,9},{2,10},{3,11},{4,12},{5,13},{6,14},{7,15},{8,0},{9,1},... | collective-permute-start | bytes 442376 | tf_op jit(solution)/shard_map/ppermute | solution.py:884
  312.3 11.1 %collective-permute-start.26 = (bf16[48,1536]{1,0:T(8,128)(2,1)S(1)}, bf16[48,1536]{1,0:T(8,128)(2,1)S(1)}, u32[]{:S(2)}, u32[]{:S(2)}) collective-permute-start(bf16[48,1536]{1,0:T(8,128)(2,1)S(1)} %dynamic-slice_bitcast_fusion.15), channel_id=1, source_target_pairs={{0,8},{1,9},{2,10},{3,11},{4,12},{5,13},{6,14},{7,15},{8,0},{9,1},... | collective-permute-start | bytes 442376 | tf_op jit(solution)/shard_map/ppermute | solution.py:884
  324.4 2.7 copy-start.20
  324.4 3.7 %copy-start.6 = (f32[256,768]{1,0:T(8,128)S(1)}, f32[256,768]{1,0:T(8,128)}, u32[]{:S(2)}) copy-start(f32[256,768]{1,0:T(8,128)} %get-tuple-element.246) | copy-start | bytes 2359300
  324.4 3.7 %copy-start.7 = (f32[256,768]{1,0:T(8,128)S(1)}, f32[256,768]{1,0:T(8,128)}, u32[]{:S(2)}) copy-start(f32[256,768]{1,0:T(8,128)} %get-tuple-element.244) | copy-start | bytes 2359300
  324.4 8.5 %collective-permute-start.32 = (bf16[2,48,1536]{2,1,0:T(8,128)(2,1)S(1)}, bf16[2,48,1536]{2,1,0:T(8,128)(2,1)S(1)}, u32[]{:S(2)}, u32[]{:S(2)}) collective-permute-start(bf16[2,48,1536]{2,1,0:T(8,128)(2,1)S(1)} %dynamic-slice_bitcast_fusion.7), channel_id=1, source_target_pairs={{0,4},{1,5},{2,6},{3,7},{4,0},{5,1},{6,2},{7,3},{8,12},{9,13},{10,... | collective-permute-start | bytes 884744 | tf_op jit(solution)/shard_map/ppermute | solution.py:884
  324.8 6.3 %collective-permute-start.31 = (bf16[48,1664]{1,0:T(8,128)(2,1)S(1)}, bf16[48,1664]{1,0:T(8,128)(2,1)S(1)}, u32[]{:S(2)}, u32[]{:S(2)}) collective-permute-start(bf16[48,1664]{1,0:T(8,128)(2,1)S(1)} %dynamic-slice_bitcast_fusion.12), channel_id=1, source_target_pairs={{0,8},{1,9},{2,10},{3,11},{4,12},{5,13},{6,14},{7,15},{8,0},{9,1},... | collective-permute-start | bytes 479240 | tf_op jit(solution)/shard_map/ppermute | solution.py:884
  327.1 3.5 collective-permute-start.30
  333.1 8.1 %collective-permute-start.34 = (bf16[48,1536]{1,0:T(8,128)(2,1)S(1)}, bf16[48,1536]{1,0:T(8,128)(2,1)S(1)}, u32[]{:S(2)}, u32[]{:S(2)}) collective-permute-start(bf16[48,1536]{1,0:T(8,128)(2,1)S(1)} %dynamic-slice_bitcast_fusion.13), channel_id=1, source_target_pairs={{0,8},{1,9},{2,10},{3,11},{4,12},{5,13},{6,14},{7,15},{8,0},{9,1},... | collective-permute-start | bytes 442376 | tf_op jit(solution)/shard_map/ppermute | solution.py:884
  334.4 3.9 %collective-permute-start.33 = (f32[4,1536]{1,0:T(4,128)S(1)}, f32[4,1536]{1,0:T(4,128)S(1)}, u32[]{:S(2)}, u32[]{:S(2)}) collective-permute-start(f32[4,1536]{1,0:T(4,128)S(1)} %pad_maximum_fusion.3), channel_id=1, source_target_pairs={{0,2},{1,3},{2,0},{3,1},{4,6},{5,7},{6,4},{7,5},{8,10},{9,11},{10,... | collective-permute-start | bytes 73736 | tf_op jit(solution)/shard_map/ppermute | solution.py:884
  341.3 4.2 %collective-permute-start.35 = (f32[8,1536]{1,0:T(8,128)S(1)}, f32[8,1536]{1,0:T(8,128)S(1)}, u32[]{:S(2)}, u32[]{:S(2)}) collective-permute-start(f32[8,1536]{1,0:T(8,128)S(1)} %pad_maximum_fusion.2), channel_id=1, source_target_pairs={{0,4},{1,5},{2,6},{3,7},{4,0},{5,1},{6,2},{7,3},{8,12},{9,13},{10,... | collective-permute-start | bytes 147464 | tf_op jit(solution)/shard_map/ppermute | solution.py:884
  345.4 6.5 %collective-permute-start.36 = (f32[16,1536]{1,0:T(8,128)S(1)}, f32[16,1536]{1,0:T(8,128)S(1)}, u32[]{:S(2)}, u32[]{:S(2)}) collective-permute-start(f32[16,1536]{1,0:T(8,128)S(1)} %pad_maximum_fusion.1), channel_id=1, source_target_pairs={{0,8},{1,9},{2,10},{3,11},{4,12},{5,13},{6,14},{7,15},{8,0},{9,1},... | collective-permute-start | bytes 294920 | tf_op jit(solution)/shard_map/ppermute | solution.py:884
  (2 other events, 1.5 us)
Sparse Core Ops, SparseCore 0:
  10.2 92.8 all-gather.2
  105.4 93.5 all-gather.4
